TPU v7x, 32 devices: a whole 2x2x4 slice. The times are simulated.
32 devices in a mesh: dom: 8 (over y, x, core), grp: 4 (over z).
Axes of the slice: x: 2, y: 2, z: 4, core: 2. Of those that a mesh axis runs over, the one named last changes fastest.
Arguments:
- feats: bfloat16 [8, 4, 1024, 256], P('dom', 'grp'), may hold values from -6 to 6
- hop_noise: bfloat16 [2, 8, 4, 1024, 256], P(None, 'dom', 'grp'), may hold values from -4 to 4
- send_rows: int32 [8, 4, 8, 32], P('dom', 'grp'), may hold values from 0 to 1023
- tile_block: int32 [8, 4, 64], P('dom', 'grp'), may hold values from 0 to 7
- tile_src: int32 [8, 4, 64, 256], P('dom', 'grp'), may hold values from 0 to 1279
- tile_dst: int32 [8, 4, 64, 256], P('dom', 'grp'), may hold values from 0 to 128
- tile_count: int32 [8, 4], P('dom', 'grp'), may hold values from 1 to 64, as said below
- labels: int32 [8, 4, 32], P('dom', 'grp'), may hold values from 0 to 171
- w_first: bfloat16 [768, 1024], replicated, may hold values from -6 to 6
- w_second: bfloat16 [1024, 1024], replicated, may hold values from -0.75 to 0.75
- w_third: bfloat16 [1024, 172], replicated, may hold values from -2.5 to 2.5
- noise_first: float32 [768, 1024], P('dom'), may hold values from -0.75 to 0.75
- noise_second: float32 [1024, 1024], P('dom'), may hold values from -0.75 to 0.75
- noise_third: float32 [1024, 172], P('dom'), may hold values from -0.75 to 0.75
Outputs:
- hop_feats: bfloat16 [2, 8, 4, 1024, 256], P(None, 'dom', 'grp')
- grad_first: float32 [768, 1024], P('dom')
- grad_second: float32 [1024, 1024], P('dom')
- grad_third: float32 [1024, 172], P('dom')
Inputs may be any that keep to these rules, and one draw needn't show every extreme that they name: `tile_count`: tiles at positions of a partition's count and beyond are ignored; the count 64 is reached by some partition in every draw. `tile_dst`: A value of 128 marks an empty slot. `tile_src`: values below 1024 are the partition's own nodes; value 1024 + p * 32 + j is the j-th row received from partition p of the group.
All inputs are finite; a program needn't handle non-finite values.
Results may differ from a plain program's by a relative error of at most 0.0044.
Values may be sent and summed in bfloat16 or wider, within the bound.
No kernel may reach another device: no remote copies, remote signals or barrier semaphores. Data moves between devices by JAX's collectives and lax.ppermute only.
A program may use at most 64 MiB of HBM per device.

v0:
```python
import jax
import jax.numpy as jnp
from jax import lax
from jax.sharding import PartitionSpec as P

HOPS = 2
BLOCK = 128


clip_bound = 4.0
noise_mult = 1.0
tile_batch = 8


def normalize(values):
    return (values * lax.rsqrt(jnp.sum(values * values, -1, keepdims=True) + 1e-06)).astype(
        jnp.bfloat16
    )


def silu_slope(values):
    sigma = jax.nn.sigmoid(values)
    return sigma * (1.0 + values * (1.0 - sigma))


def squares(values):
    wide = values.astype(jnp.float32)
    return jnp.sum(wide * wide, -1)


def aggregate(table, blocks, sources, targets, count, node_count):
    width = table.shape[1]
    positions = jnp.arange(BLOCK, dtype=jnp.int32)
    nb_count = node_count // BLOCK
    block_ids = jnp.arange(nb_count, dtype=jnp.int32)

    def turn(step, totals):
        first = step * tile_batch
        picked = lax.dynamic_slice_in_dim(sources, first, tile_batch, 0)
        places = lax.dynamic_slice_in_dim(targets, first, tile_batch, 0)
        owners = lax.dynamic_slice_in_dim(blocks, first, tile_batch, 0)
        live = first + jnp.arange(tile_batch, dtype=jnp.int32) < count
        gathered = table[picked]
        onehot = ((places[:, None, :] == positions[None, :, None]) & live[:, None, None]).astype(
            jnp.bfloat16
        )
        parts = jnp.einsum("gbe,gef->gbf", onehot, gathered, preferred_element_type=jnp.float32)
        choose = (owners[:, None] == block_ids[None, :]).astype(jnp.float32)
        placed = jnp.einsum(
            "gk,gbf->kbf",
            choose,
            parts,
            precision=lax.Precision.HIGHEST,
            preferred_element_type=jnp.float32,
        )
        return totals + placed

    start = jnp.zeros((nb_count, BLOCK, width), jnp.float32)
    totals = lax.fori_loop(0, sources.shape[0] // tile_batch, turn, start)
    return totals.reshape(node_count, width)


def local(
    feats,
    hop_noise,
    send_rows,
    tile_block,
    tile_src,
    tile_dst,
    tile_count,
    labels,
    w_first,
    w_second,
    w_third,
    noise_first,
    noise_second,
    noise_third,
):
    node_count = feats.shape[2]
    width = feats.shape[3]
    train_count = labels.shape[2]
    count = tile_count[0, 0]
    current = normalize(feats[0, 0].astype(jnp.float32))
    states = [current]
    for hop in range(HOPS):
        outgoing = current[send_rows[0, 0]]
        ghosts = lax.all_to_all(outgoing, "dom", split_axis=0, concat_axis=0, tiled=True)
        table = jnp.concatenate([current, ghosts.reshape(-1, width)], 0)
        summed = aggregate(
            table, tile_block[0, 0], tile_src[0, 0], tile_dst[0, 0], count, node_count
        )
        current = normalize(summed + hop_noise[hop, 0, 0].astype(jnp.float32))
        states.append(current)
    hop_feats = jnp.stack(states[1:])[:, None, None]
    inputs = jnp.concatenate([state[:train_count] for state in states], -1)
    z_one = jnp.dot(inputs, w_first, preferred_element_type=jnp.float32)
    h_one = jax.nn.silu(z_one).astype(jnp.bfloat16)
    z_two = jnp.dot(h_one, w_second, preferred_element_type=jnp.float32)
    h_two = jax.nn.silu(z_two).astype(jnp.bfloat16)
    logits = jnp.dot(h_two, w_third, preferred_element_type=jnp.float32)
    expo = jnp.exp(logits)
    probs = expo / jnp.sum(expo, -1, keepdims=True)
    classes = w_third.shape[1]
    onehot = (labels[0, 0][:, None] == jnp.arange(classes, dtype=jnp.int32)[None, :]).astype(
        jnp.float32
    )
    d_three = (probs - onehot).astype(jnp.bfloat16)
    d_two = (
        jnp.dot(d_three, w_third.T, preferred_element_type=jnp.float32) * silu_slope(z_two)
    ).astype(jnp.bfloat16)
    d_one = (
        jnp.dot(d_two, w_second.T, preferred_element_type=jnp.float32) * silu_slope(z_one)
    ).astype(jnp.bfloat16)
    norm = jnp.sqrt(
        squares(inputs) * squares(d_one)
        + squares(h_one) * squares(d_two)
        + squares(h_two) * squares(d_three)
    )
    factor = (clip_bound / jnp.maximum(norm, clip_bound))[:, None]
    e_one = (d_one.astype(jnp.float32) * factor).astype(jnp.bfloat16)
    e_two = (d_two.astype(jnp.float32) * factor).astype(jnp.bfloat16)
    e_three = (d_three.astype(jnp.float32) * factor).astype(jnp.bfloat16)
    scale = noise_mult * clip_bound
    g_one = jnp.dot(inputs.T, e_one, preferred_element_type=jnp.float32)
    g_two = jnp.dot(h_one.T, e_two, preferred_element_type=jnp.float32)
    g_three = jnp.dot(h_two.T, e_three, preferred_element_type=jnp.float32)
    p_one, p_two, p_three = (
        lax.psum_scatter(g_one, "dom", scatter_dimension=0, tiled=True),
        lax.psum_scatter(g_two, "dom", scatter_dimension=0, tiled=True),
        lax.psum_scatter(g_three, "dom", scatter_dimension=0, tiled=True),
    )
    s_one, s_two, s_three = lax.psum((p_one, p_two, p_three), "grp")
    grad_first = s_one + scale * noise_first
    grad_second = s_two + scale * noise_second
    grad_third = s_three + scale * noise_third
    return (hop_feats, grad_first, grad_second, grad_third)


def solution(mesh):
    in_specs = (
        P("dom", "grp", None, None),
        P(None, "dom", "grp", None, None),
        P("dom", "grp", None, None),
        P("dom", "grp", None),
        P("dom", "grp", None, None),
        P("dom", "grp", None, None),
        P("dom", "grp"),
        P("dom", "grp", None),
        P(),
        P(),
        P(),
        P("dom", None),
        P("dom", None),
        P("dom", None),
    )
    out_specs = (P(None, "dom", "grp", None, None), P("dom", None), P("dom", None), P("dom", None))
    return jax.shard_map(local, mesh=mesh, in_specs=in_specs, out_specs=out_specs, check_vma=False)
```

profile of v0, /device:TPU:0, one launch (start us, length us, event | category | flops | bytes accessed | tf_op | source)
XLA Modules:
  0.0 497.4 jit_solution(12594437065878632755)
XLA Ops:
  10.6 1.8 gather_fusion.2
  12.4 5.2 %all-to-all-start = ((bf16[8,32,256]{2,1,0:T(8,128)(2,1)}), bf16[8,32,256]{2,1,0:T(8,128)(2,1)S(1)}, u32[]{:S(2)}, u32[]{:S(2)}) async-start(bf16[8,32,256]{2,1,0:T(8,128)(2,1)} %bitcast.7), calls=%async_computation | async-start | bytes 262144 | tf_op jit(solution)/shard_map/all_to_all | solution.py:87
  17.6 3.0 convert_bitcast_fusion
  20.6 2.5 all-to-all-done
  23.2 121.8 %while.28 = (s32[]{:T(128)}, f32[8,128,256]{2,0,1:T(8,128)}, s32[64]{0:T(128)S(1)}, s32[64,256]{1,0:T(8,128)}, s32[]{:T(128)}, /*index=5*/s32[64,256]{1,0:T(8,12...) while((s32[]{:T(128)}, f32[8,128,256]{2,0,1:T(8,128)}, ...), condition=%wide.region_2.0_spmd.clone, body=%wide.region_1.0_spmd.clone.sunk | while | flops 160440400 | bytes 15810921 | solution.py:59
  25.4 9.0 %gather_fusion = bf16[2048,256]{1,0:T(8,128)(2,1)} fusion(bf16[1280,256]{1,0:T(8,128)(2,1)S(1)} %get-tuple-element.550, s32[2048]{0:T(1024)S(1)} %broadcast_clamp_fusion.4), kind=kCustom, calls=%fused_computation.clone.clone.1 | custom fusion | bytes 2105344 | tf_op jit(solution)/shard_map/while/body/eval_jaxpr/gather | solution.py:43
  34.4 1.7 fusion.89
  40.6 9.0 %gather_fusion = bf16[2048,256]{1,0:T(8,128)(2,1)} fusion(bf16[1280,256]{1,0:T(8,128)(2,1)S(1)} %get-tuple-element.550, s32[2048]{0:T(1024)S(1)} %broadcast_clamp_fusion.4), kind=kCustom, calls=%fused_computation.clone.clone.1 | custom fusion | bytes 2105344 | tf_op jit(solution)/shard_map/while/body/eval_jaxpr/gather | solution.py:43
  49.6 1.7 fusion.89
  51.3 1.4 convolution_add_fusion.4
  55.8 9.0 %gather_fusion = bf16[2048,256]{1,0:T(8,128)(2,1)} fusion(bf16[1280,256]{1,0:T(8,128)(2,1)S(1)} %get-tuple-element.550, s32[2048]{0:T(1024)S(1)} %broadcast_clamp_fusion.4), kind=kCustom, calls=%fused_computation.clone.clone.1 | custom fusion | bytes 2105344 | tf_op jit(solution)/shard_map/while/body/eval_jaxpr/gather | solution.py:43
  64.8 1.7 fusion.89
  66.5 1.4 convolution_add_fusion.4
  71.1 9.0 %gather_fusion = bf16[2048,256]{1,0:T(8,128)(2,1)} fusion(bf16[1280,256]{1,0:T(8,128)(2,1)S(1)} %get-tuple-element.550, s32[2048]{0:T(1024)S(1)} %broadcast_clamp_fusion.4), kind=kCustom, calls=%fused_computation.clone.clone.1 | custom fusion | bytes 2105344 | tf_op jit(solution)/shard_map/while/body/eval_jaxpr/gather | solution.py:43
  80.1 1.7 fusion.89
  86.3 9.0 %gather_fusion = bf16[2048,256]{1,0:T(8,128)(2,1)} fusion(bf16[1280,256]{1,0:T(8,128)(2,1)S(1)} %get-tuple-element.550, s32[2048]{0:T(1024)S(1)} %broadcast_clamp_fusion.4), kind=kCustom, calls=%fused_computation.clone.clone.1 | custom fusion | bytes 2105344 | tf_op jit(solution)/shard_map/while/body/eval_jaxpr/gather | solution.py:43
  95.3 1.7 fusion.89
  97.0 1.4 convolution_add_fusion.4
  101.5 9.0 %gather_fusion = bf16[2048,256]{1,0:T(8,128)(2,1)} fusion(bf16[1280,256]{1,0:T(8,128)(2,1)S(1)} %get-tuple-element.550, s32[2048]{0:T(1024)S(1)} %broadcast_clamp_fusion.4), kind=kCustom, calls=%fused_computation.clone.clone.1 | custom fusion | bytes 2105344 | tf_op jit(solution)/shard_map/while/body/eval_jaxpr/gather | solution.py:43
  110.5 1.7 fusion.89
  116.7 9.0 %gather_fusion = bf16[2048,256]{1,0:T(8,128)(2,1)} fusion(bf16[1280,256]{1,0:T(8,128)(2,1)S(1)} %get-tuple-element.550, s32[2048]{0:T(1024)S(1)} %broadcast_clamp_fusion.4), kind=kCustom, calls=%fused_computation.clone.clone.1 | custom fusion | bytes 2105344 | tf_op jit(solution)/shard_map/while/body/eval_jaxpr/gather | solution.py:43
  125.7 1.7 fusion.89
  127.4 1.4 convolution_add_fusion.4
  131.9 9.0 %gather_fusion = bf16[2048,256]{1,0:T(8,128)(2,1)} fusion(bf16[1280,256]{1,0:T(8,128)(2,1)S(1)} %get-tuple-element.550, s32[2048]{0:T(1024)S(1)} %broadcast_clamp_fusion.4), kind=kCustom, calls=%fused_computation.clone.clone.1 | custom fusion | bytes 2105344 | tf_op jit(solution)/shard_map/while/body/eval_jaxpr/gather | solution.py:43
  140.9 1.7 fusion.89
  142.7 1.4 convolution_add_fusion.4
  145.0 1.7 copy.45
  147.6 2.2 fusion.36
  149.8 2.7 gather_fusion.3
  152.5 3.4 all-to-all-start.1
  157.4 4.0 all-to-all-done.1
  162.4 121.8 %while.29 = (s32[]{:T(128)}, f32[8,128,256]{2,0,1:T(8,128)}, s32[64]{0:T(128)S(1)}, s32[64,256]{1,0:T(8,128)}, s32[]{:T(128)}, /*index=5*/s32[64,256]{1,0:T(8,12...) while((s32[]{:T(128)}, f32[8,128,256]{2,0,1:T(8,128)}, ...), condition=%wide.region_5.0_spmd.clone, body=%wide.region_4.0_spmd.clone.sunk | while | flops 160440400 | bytes 15810921 | solution.py:59
  164.6 9.0 %gather_fusion.1 = bf16[2048,256]{1,0:T(8,128)(2,1)} fusion(bf16[1280,256]{1,0:T(8,128)(2,1)S(1)} %get-tuple-element.583, s32[2048]{0:T(1024)S(1)} %broadcast_clamp_fusion.5), kind=kCustom, calls=%fused_computation.1.clone.clone.1 | custom fusion | bytes 2105344 | tf_op jit(solution)/shard_map/while/body/eval_jaxpr/gather | solution.py:43
  173.6 1.7 fusion.95
  175.3 1.4 convolution_add_fusion.5
  179.8 9.0 %gather_fusion.1 = bf16[2048,256]{1,0:T(8,128)(2,1)} fusion(bf16[1280,256]{1,0:T(8,128)(2,1)S(1)} %get-tuple-element.583, s32[2048]{0:T(1024)S(1)} %broadcast_clamp_fusion.5), kind=kCustom, calls=%fused_computation.1.clone.clone.1 | custom fusion | bytes 2105344 | tf_op jit(solution)/shard_map/while/body/eval_jaxpr/gather | solution.py:43
  188.8 1.7 fusion.95
  195.1 9.0 %gather_fusion.1 = bf16[2048,256]{1,0:T(8,128)(2,1)} fusion(bf16[1280,256]{1,0:T(8,128)(2,1)S(1)} %get-tuple-element.583, s32[2048]{0:T(1024)S(1)} %broadcast_clamp_fusion.5), kind=kCustom, calls=%fused_computation.1.clone.clone.1 | custom fusion | bytes 2105344 | tf_op jit(solution)/shard_map/while/body/eval_jaxpr/gather | solution.py:43
  204.1 1.7 fusion.95
  205.8 1.4 convolution_add_fusion.5
  210.3 9.0 %gather_fusion.1 = bf16[2048,256]{1,0:T(8,128)(2,1)} fusion(bf16[1280,256]{1,0:T(8,128)(2,1)S(1)} %get-tuple-element.583, s32[2048]{0:T(1024)S(1)} %broadcast_clamp_fusion.5), kind=kCustom, calls=%fused_computation.1.clone.clone.1 | custom fusion | bytes 2105344 | tf_op jit(solution)/shard_map/while/body/eval_jaxpr/gather | solution.py:43
  219.3 1.7 fusion.95
  225.5 9.0 %gather_fusion.1 = bf16[2048,256]{1,0:T(8,128)(2,1)} fusion(bf16[1280,256]{1,0:T(8,128)(2,1)S(1)} %get-tuple-element.583, s32[2048]{0:T(1024)S(1)} %broadcast_clamp_fusion.5), kind=kCustom, calls=%fused_computation.1.clone.clone.1 | custom fusion | bytes 2105344 | tf_op jit(solution)/shard_map/while/body/eval_jaxpr/gather | solution.py:43
  234.5 1.7 fusion.95
  236.2 1.4 convolution_add_fusion.5
  240.7 9.0 %gather_fusion.1 = bf16[2048,256]{1,0:T(8,128)(2,1)} fusion(bf16[1280,256]{1,0:T(8,128)(2,1)S(1)} %get-tuple-element.583, s32[2048]{0:T(1024)S(1)} %broadcast_clamp_fusion.5), kind=kCustom, calls=%fused_computation.1.clone.clone.1 | custom fusion | bytes 2105344 | tf_op jit(solution)/shard_map/while/body/eval_jaxpr/gather | solution.py:43
  249.7 1.7 fusion.95
  255.9 9.0 %gather_fusion.1 = bf16[2048,256]{1,0:T(8,128)(2,1)} fusion(bf16[1280,256]{1,0:T(8,128)(2,1)S(1)} %get-tuple-element.583, s32[2048]{0:T(1024)S(1)} %broadcast_clamp_fusion.5), kind=kCustom, calls=%fused_computation.1.clone.clone.1 | custom fusion | bytes 2105344 | tf_op jit(solution)/shard_map/while/body/eval_jaxpr/gather | solution.py:43
  264.9 1.7 fusion.95
  266.6 1.4 convolution_add_fusion.5
  271.2 9.0 %gather_fusion.1 = bf16[2048,256]{1,0:T(8,128)(2,1)} fusion(bf16[1280,256]{1,0:T(8,128)(2,1)S(1)} %get-tuple-element.583, s32[2048]{0:T(1024)S(1)} %broadcast_clamp_fusion.5), kind=kCustom, calls=%fused_computation.1.clone.clone.1 | custom fusion | bytes 2105344 | tf_op jit(solution)/shard_map/while/body/eval_jaxpr/gather | solution.py:43
  280.2 1.7 fusion.95
  284.2 1.7 copy.49
  287.8 2.0 multiply_reduce_fusion.1
  293.4 2.3 fusion.45
  295.8 2.7 fusion.46
  298.5 28.3 %reduce-scatter.8.cloned.1.call-done = f32[128,172]{0,1:T(8,128)} async-done(((f32[1024,172]{0,1:T(8,128)}), f32[128,172]{0,1:T(8,128)}) %reduce-scatter.8.cloned.1.call-update) | async-done | bytes 88080 | tf_op jit(solution)/shard_map/reduce_scatter | solution.py:130
  326.8 50.0 %reduce-scatter.4.cloned.1.call-done = f32[96,1024]{1,0:T(8,128)} async-done(((f32[768,1024]{1,0:T(8,128)}), f32[96,1024]{1,0:T(8,128)}) %reduce-scatter.4.cloned.1.call-update) | async-done | bytes 393232 | tf_op jit(solution)/shard_map/reduce_scatter | solution.py:128
  376.9 54.7 %reduce-scatter.6.cloned.1.call-done = f32[128,1024]{1,0:T(8,128)} async-done(((f32[1024,1024]{1,0:T(8,128)}), f32[128,1024]{1,0:T(8,128)}) %reduce-scatter.6.cloned.1.call-update) | async-done | bytes 524304 | tf_op jit(solution)/shard_map/reduce_scatter | solution.py:129
  431.6 1.9 fusion.38
  434.6 51.1 %all-reduce.3.cloned.1.call-done = (f32[96,1024]{1,0:T(8,128)}, f32[128,1024]{1,0:T(8,128)}, f32[128,172]{0,1:T(8,128)}) async-done(((f32[96,1024]{1,0:T(8,128)}, f32[128,1024]{1,0:T(8,128)}, f32[128,172]{0,1:T(8,128)}), (f32[96,1024]{1,0:T(8,128)}, f32[128,1024]{1,0:T(8,128)}, f32[128,172]{0,1:T(8,128)})) %all-reduce.3.cloned.1.call-update) | async-done | bytes 1005584 | tf_op jit(solution)/shard_map/psum | solution.py:132
  485.7 1.8 multiply_add_fusion.1
  487.5 1.5 multiply_add_fusion.2
  489.0 1.9 multiply_add_fusion
  (234 shorter events, 73.0 us)
Async XLA Ops:
  7.2 282.6 %copy-start = (bf16[1024,1024]{1,0:T(8,128)(2,1)S(1)}, bf16[1024,1024]{1,0:T(8,128)(2,1)}, u32[]{:S(2)}) copy-start(bf16[1024,1024]{1,0:T(8,128)(2,1)} %param.27) | copy-start | bytes 6291460
  10.6 12.5 %copy-start.9 = (bf16[1024,256]{1,0:T(8,128)(2,1)}, bf16[1024,256]{1,0:T(8,128)(2,1)S(1)}, u32[]{:S(2)}) copy-start(bf16[1024,256]{1,0:T(8,128)(2,1)S(1)} %fusion.32) | copy-start | bytes 1572868
  12.4 10.7 %all-to-all-start = ((bf16[8,32,256]{2,1,0:T(8,128)(2,1)}), bf16[8,32,256]{2,1,0:T(8,128)(2,1)S(1)}, u32[]{:S(2)}, u32[]{:S(2)}) async-start(bf16[8,32,256]{2,1,0:T(8,128)(2,1)} %bitcast.7), calls=%async_computation | async-start | bytes 262144 | tf_op jit(solution)/shard_map/all_to_all | solution.py:87
  17.6 5.6 %copy-start.18 = (s32[1,1,64]{2,1,0:T(1,128)S(1)}, s32[1,1,64]{2,1,0:T(1,128)}, u32[]{:S(2)}) copy-start(s32[1,1,64]{2,1,0:T(1,128)} %param.21) | copy-start | bytes 772
  34.4 1.7 copy-start.4
  37.5 1.0 copy-start.5
  49.6 1.7 copy-start.4
  52.7 1.0 copy-start.5
  64.8 1.7 copy-start.4
  67.9 1.0 copy-start.5
  80.1 1.7 copy-start.4
  83.2 1.0 copy-start.5
  95.3 1.7 copy-start.4
  98.4 1.0 copy-start.5
  110.5 1.7 copy-start.4
  113.6 1.0 copy-start.5
  125.7 1.7 copy-start.4
  128.8 1.0 copy-start.5
  140.9 1.7 copy-start.4
  144.0 1.0 copy-start.5
  145.0 1.7 copy-start.6
  145.0 1.9 copy-start.12
  146.7 3.1 copy-start.7
  152.5 8.8 %all-to-all-start.1 = ((bf16[8,32,256]{2,1,0:T(8,128)(2,1)}), bf16[8,32,256]{2,1,0:T(8,128)(2,1)S(1)}, u32[]{:S(2)}, u32[]{:S(2)}) async-start(bf16[8,32,256]{2,1,0:T(8,128)(2,1)} %bitcast.15), calls=%async_computation.1 | async-start | bytes 262144 | tf_op jit(solution)/shard_map/all_to_all | solution.py:87
  155.9 170.9 %reduce-scatter.8.cloned.1.call-start = ((), (), s32[]{:S(2)}) async-start(), calls=%async_computation.7 | async-start | bytes 811008 | tf_op jit(solution)/shard_map/reduce_scatter | solution.py:130
  173.6 1.7 copy-start.1
  176.7 1.0 copy-start.2
  188.8 1.7 copy-start.1
  191.9 1.0 copy-start.2
  204.1 1.7 copy-start.1
  207.2 1.0 copy-start.2
  219.3 1.7 copy-start.1
  222.4 1.0 copy-start.2
  234.5 1.7 copy-start.1
  237.6 1.0 copy-start.2
  249.7 1.7 copy-start.1
  252.8 1.0 copy-start.2
  264.9 1.7 copy-start.1
  268.0 1.0 copy-start.2
  280.2 1.7 copy-start.1
  283.2 1.0 copy-start.2
  284.2 1.7 copy-start.3
  284.2 1.9 copy-start.11
  285.9 3.8 copy-start.10
  287.8 2.6 copy-start.15
  287.8 2.9 copy-start.17
  293.4 83.5 %reduce-scatter.4.cloned.1.call-start = ((), (), s32[]{:S(2)}) async-start(), calls=%async_computation.5 | async-start | bytes 3538944 | tf_op jit(solution)/shard_map/reduce_scatter | solution.py:128
  295.7 135.9 %reduce-scatter.6.cloned.1.call-start = ((), (), s32[]{:S(2)}) async-start(), calls=%async_computation.6 | async-start | bytes 4718592 | tf_op jit(solution)/shard_map/reduce_scatter | solution.py:129
  298.5 133.2 %copy-start.8 = (f32[8,128,256]{2,1,0:T(8,128)S(1)}, f32[8,128,256]{2,1,0:T(8,128)}, u32[]{:S(2)}) copy-start(f32[8,128,256]{2,1,0:T(8,128)} %copy-done.7) | copy-start | bytes 3145732
  298.5 187.2 %all-reduce.3.cloned.1.call-start = ((), (), s32[]{:S(2)}) async-start(), calls=%async_computation.8 | async-start | bytes 2015232 | tf_op jit(solution)/shard_map/psum | solution.py:132
  433.5 52.2 %copy-start.14 = (f32[96,1024]{1,0:T(8,128)S(1)}, f32[96,1024]{1,0:T(8,128)}, u32[]{:S(2)}) copy-start(f32[96,1024]{1,0:T(8,128)} %param.29) | copy-start | bytes 1179652
  433.5 53.9 %copy-start.16 = (f32[128,172]{0,1:T(8,128)S(1)}, f32[128,172]{0,1:T(8,128)}, u32[]{:S(2)}) copy-start(f32[128,172]{0,1:T(8,128)} %param.31) | copy-start | bytes 264196
  433.5 55.5 %copy-start.13 = (f32[128,1024]{1,0:T(8,128)S(1)}, f32[128,1024]{1,0:T(8,128)}, u32[]{:S(2)}) copy-start(f32[128,1024]{1,0:T(8,128)} %param.30) | copy-start | bytes 1572868
Sparse Core Ops, SparseCore 0:
  293.5 33.3 reduce-scatter.7
  330.6 46.2 reduce-scatter.3
  380.2 51.3 reduce-scatter.5
  434.2 51.3 all-reduce.2
where the time goes:
time: 500 us; the launch traced here: 497 us
  waiting for transfers between devices  191 us (38%)
  local copies, waits for them, and re-layouts  182 us (36%)
  matrix products  59.3 us (12%)
  other arithmetic  42.1 us (8%)
  between operations  14 us (3%)
  starting transfers between devices  8.71 us (2%)
    gather x16, local copies, waits for them, and re-layouts, turn(): gathered = table[picked]  144 us
    reduce_scatter x1, waiting for transfers between devices, local(): lax.psum_scatter(g_two, 'dom', scatter_dimension=0, tiled=True)  54.7 us
    psum x1, waiting for transfers between devices, local(): s_one, s_two, s_three = lax.psum((p_one, p_two, p_three), 'grp')  51.1 us
    reduce_scatter x1, waiting for transfers between devices, local(): lax.psum_scatter(g_one, 'dom', scatter_dimension=0, tiled=True)  50 us
    reduce_scatter x1, waiting for transfers between devices, local(): lax.psum_scatter(g_three, 'dom', scatter_dimension=0, tiled=True)  28.3 us
    dot_general x16, matrix products, turn(): jnp.einsum('gbe,gef->gbf', onehot, gathered, preferred_element_type=jnp.f...  27.1 us
    dot_general x16, matrix products, turn(): jnp.einsum('gk,gbf->kbf', choose, parts, precision=lax.Precision.HIGHEST,...  22 us
    while x80, local copies, waits for them, and re-layouts  15.6 us
  transfers between devices with their start and end apart: 6, of which 6 were waited for; matrix products, arithmetic and copies ran while one was open for 2% of the time, Pallas kernels for 0%

commit v1 on v0

v1 whole, which is shorter than its diff:
```python
import functools

import jax
import jax.numpy as jnp
from jax import lax
from jax.experimental import pallas as pl
from jax.experimental.pallas import tpu as pltpu
from jax.sharding import PartitionSpec as P

BLOCK = 128
LOW = 256
GROUP = 4
clip_bound = 4.0
noise_mult = 1.0

f32 = jnp.float32
bf16 = jnp.bfloat16
VMEM = pltpu.VMEM
SMEM = pltpu.SMEM


def params():
    return pltpu.CompilerParams(vmem_limit_bytes=56 * 1024 * 1024)


def normalize(values):
    return (values * lax.rsqrt(jnp.sum(values * values, -1, keepdims=True) + 1e-06)).astype(bf16)


def dot(left, right):
    return jnp.dot(left, right, preferred_element_type=f32)


def dot_nt(left, right):
    return lax.dot_general(left, right, (((1,), (1,)), ((), ())), preferred_element_type=f32)


def dot_tn(left, right):
    return lax.dot_general(left, right, (((0,), (0,)), ((), ())), preferred_element_type=f32)


def send(start, rows_ref, out_ref, turn_ref, pick_ref):
    parts, each = rows_ref.shape
    nodes = start.shape[0]
    turn_ref[:parts, :each] = rows_ref[...]
    columns = turn_ref[...].T
    spots = lax.broadcasted_iota(jnp.int32, (each, nodes), 1)
    for part in range(parts):
        wanted = columns[:each, part : part + 1]
        pick_ref[part * each : (part + 1) * each, :] = jnp.where(wanted == spots, 1.0, 0.0).astype(
            bf16
        )
    out = dot(pick_ref[...], start).astype(bf16)
    out_ref[...] = out.reshape(out_ref.shape)


def first_kernel(feats_ref, rows_ref, start_ref, out_ref, turn_ref, pick_ref):
    start = normalize(feats_ref[...].astype(f32))
    start_ref[...] = start
    send(start, rows_ref, out_ref, turn_ref, pick_ref)


def build_kernel(
    blocks_ref,
    count_ref,
    src_ref,
    dst_ref,
    start_ref,
    noise_ref,
    own_ref,
    ghost_ref,
    part_ref,
    flag_ref,
    own_rest_ref,
    ghost_rest_ref,
    sums_ref,
    rest_ref,
):
    nodes, cols = sums_ref.shape
    pieces = cols // LOW
    slots = src_ref.shape[1]
    count = count_ref[0]
    sums_ref[...] = jnp.zeros_like(sums_ref)
    low_ids = lax.broadcasted_iota(jnp.int32, (LOW, slots), 0)
    spot_ids = lax.broadcasted_iota(jnp.int32, (pieces * BLOCK, slots), 0)

    def turn(step, carry):
        for inner in range(GROUP):
            tile = step * GROUP + inner
            src = src_ref[pl.ds(tile, 1), :]
            dst = dst_ref[pl.ds(tile, 1), :]
            live = (dst < BLOCK) & (tile < count)
            spot = jnp.where(live, (src // LOW) * BLOCK + dst, -1)
            low = src % LOW
            low_hot = jnp.where(low_ids == low, 1.0, 0.0).astype(bf16)
            spot_hot = jnp.where(spot_ids == spot, 1.0, 0.0).astype(bf16)
            out = dot_nt(spot_hot, low_hot)
            base = pl.multiple_of(blocks_ref[tile] * BLOCK, BLOCK)
            for piece in range(pieces):
                sums_ref[pl.ds(base, BLOCK), piece * LOW : (piece + 1) * LOW] += out[
                    piece * BLOCK : (piece + 1) * BLOCK
                ]
        return carry

    lax.fori_loop(0, (count + GROUP - 1) // GROUP, turn, 0)
    own_ref[...] = sums_ref[:, :nodes].astype(bf16)
    ghost_ref[...] = sums_ref[:, nodes:].astype(bf16)
    part_ref[...] = dot(own_ref[...], start_ref[...]) + noise_ref[...].astype(f32)
    big = jnp.max(sums_ref[...]) > 256.0
    flag_ref[0] = big.astype(jnp.int32)

    @pl.when(big)
    def _():
        own_rest = (sums_ref[:, :nodes] - own_ref[...].astype(f32)).astype(bf16)
        part_ref[...] += dot(own_rest, start_ref[...])
        rest_ref[...] = own_rest
        pltpu.sync_copy(rest_ref, own_rest_ref)
        rest_ref[:, : cols - nodes] = (sums_ref[:, nodes:] - ghost_ref[...].astype(f32)).astype(bf16)
        pltpu.sync_copy(rest_ref.at[:, : cols - nodes], ghost_rest_ref)


def aggregate(flag_ref, part_ref, count_ref, rest_hbm, table, sums_ref, rest_ref):
    rows = sums_ref.shape[0]
    sums_ref[...] = part_ref[...] + dot(count_ref[...], table)

    @pl.when(flag_ref[0] > 0)
    def _():
        pltpu.sync_copy(rest_hbm.at[:rows], rest_ref)
        sums_ref[...] += dot(rest_ref[...], table)


def hop_kernel(
    flag_ref,
    part_ref,
    ghost_ref,
    rest_hbm,
    table_ref,
    rows_ref,
    start_ref,
    out_ref,
    sums_ref,
    rest_ref,
    turn_ref,
    pick_ref,
):
    width = start_ref.shape[1]
    table = table_ref[...].reshape(-1, width)
    aggregate(flag_ref, part_ref, ghost_ref, rest_hbm, table, sums_ref, rest_ref)
    start = normalize(sums_ref[...])
    start_ref[...] = start
    send(start, rows_ref, out_ref, turn_ref, pick_ref)


def own_kernel(flag_ref, own_ref, rest_hbm, start_ref, noise_ref, part_ref, rest_ref):
    start = start_ref[...]
    aggregate(flag_ref, noise_ref, own_ref, rest_hbm, start, part_ref, rest_ref)


def train_kernel(flag_ref, part_ref, ghost_ref, rest_hbm, table_ref, out_ref, sums_ref, rest_ref):
    table = table_ref[...].reshape(-1, out_ref.shape[1])
    aggregate(flag_ref, part_ref, ghost_ref, rest_hbm, table, sums_ref, rest_ref)
    out_ref[...] = normalize(sums_ref[...])


def last_kernel(
    flag_ref, part_ref, ghost_ref, rest_hbm, table_ref, start_ref, out_ref, sums_ref, rest_ref
):
    table = table_ref[...].reshape(-1, out_ref.shape[-1])
    aggregate(flag_ref, part_ref, ghost_ref, rest_hbm, table, sums_ref, rest_ref)
    out_ref[0, 0, 0] = start_ref[...]
    out_ref[1, 0, 0] = normalize(sums_ref[...])


def shares(ref, first, share):
    if share % 128 == 0:
        return ref[:, pl.ds(pl.multiple_of(first, 128), share)].astype(f32)
    length = ref.shape[1]
    rows = lax.broadcasted_iota(jnp.int32, (length, share), 0)
    cols = lax.broadcasted_iota(jnp.int32, (length, share), 1)
    return dot(ref[...], jnp.where(rows == cols + first, 1.0, 0.0).astype(bf16))


def lanes_sum(values):
    total = None
    for piece in range(values.shape[1] // 128):
        part = values[:, piece * 128 : (piece + 1) * 128].astype(f32)
        total = part * part if total is None else total + part * part
    return total


def classify_kernel(
    place_ref,
    label_ref,
    zero_ref,
    one_ref,
    two_ref,
    w_first_ref,
    w_second_ref,
    w_third_ref,
    n_first_ref,
    n_second_ref,
    n_third_ref,
    g_first_ref,
    g_second_ref,
    g_third_ref,
    in_ref,
    w_third_pad_ref,
    turn_ref,
    column_ref,
    h_one_ref,
    h_two_ref,
    slope_one_ref,
    slope_two_ref,
    d_one_ref,
    d_two_ref,
):
    classes = w_third_ref.shape[0]
    hid = w_second_ref.shape[0]
    width = zero_ref.shape[1]
    wide = w_third_pad_ref.shape[0]
    groups, train = label_ref.shape
    scale = noise_mult * clip_bound
    place = place_ref[0]

    @pl.when(pl.program_id(0) == 0)
    def _():
        g_first_ref[...] = scale * n_first_ref[...]
        g_second_ref[...] = scale * n_second_ref[...]
        g_third_ref[...] = scale * n_third_ref[...]
        w_third_pad_ref[...] = jnp.zeros_like(w_third_pad_ref)
        w_third_pad_ref[:classes, :] = w_third_ref[...]

    turn_ref[:groups, :train] = label_ref[...]
    turned = turn_ref[...].T
    for group in range(groups):
        column_ref[group * train : (group + 1) * train, :] = jnp.broadcast_to(
            turned[:train, group : group + 1], (train, 128)
        )
    for hop, ref in enumerate((zero_ref, one_ref, two_ref)):
        in_ref[:, hop * width : (hop + 1) * width] = ref[...]

    def activate(values, h_ref, slope_ref, cols):
        sigma = 0.5 + 0.5 * jnp.tanh(0.5 * values)
        out = values * sigma
        slope_ref[:, cols] = sigma + out * (1.0 - sigma)
        rounded = out.astype(bf16)
        h_ref[:, cols] = rounded
        return lanes_sum(rounded)

    step = 256
    cuts = [slice(at, at + step) for at in range(0, hid, step)]
    sq_in = lanes_sum(in_ref[...])
    sq_one = sum(
        activate(dot(in_ref[...], w_first_ref[:, cut]), h_one_ref, slope_one_ref, cut)
        for cut in cuts
    )
    sq_two = sum(
        activate(dot(h_one_ref[...], w_second_ref[:, cut]), h_two_ref, slope_two_ref, cut)
        for cut in cuts
    )
    logits = dot_nt(h_two_ref[...], w_third_pad_ref[...])
    ids = lax.broadcasted_iota(jnp.int32, (logits.shape[0], wide), 1)
    expo = jnp.where(ids < classes, jnp.exp(logits), 0.0)
    probs = expo / jnp.sum(expo, -1, keepdims=True)
    label = column_ref[:, :1]
    d_three = (probs - jnp.where(ids == label, 1.0, 0.0)).astype(bf16)
    sq_dthree = lanes_sum(d_three)

    def back(values, slope_ref, d_ref, cut):
        rounded = (values * slope_ref[:, cut]).astype(bf16)
        d_ref[:, cut] = rounded
        return lanes_sum(rounded)

    sq_dtwo = sum(
        back(dot(d_three, w_third_pad_ref[:, cut]), slope_two_ref, d_two_ref, cut)
        for cut in cuts
    )
    sq_done = sum(
        back(dot_nt(d_two_ref[...], w_second_ref[cut, :]), slope_one_ref, d_one_ref, cut)
        for cut in cuts
    )

    def total(values):
        return jnp.sum(values, -1, keepdims=True)

    norm = jnp.sqrt(
        total(sq_in) * total(sq_done)
        + total(sq_one) * total(sq_dtwo)
        + total(sq_two) * total(sq_dthree)
    )
    factor = clip_bound / jnp.maximum(norm, clip_bound)

    def left(ref, share):
        return (shares(ref, place * share, share) * factor).astype(bf16)

    share = g_second_ref.shape[0]
    g_first_ref[...] += dot_tn(left(in_ref, g_first_ref.shape[0]), d_one_ref[...])
    g_second_ref[...] += dot_tn(left(h_one_ref, share), d_two_ref[...])
    g_third_ref[...] += dot_tn(d_three, left(h_two_ref, share))[:classes, :]


def call(kernel, outs, ins, scratch, **more):
    return pl.pallas_call(
        kernel,
        out_shape=[jax.ShapeDtypeStruct(shape, dtype) for shape, dtype, _ in outs],
        in_specs=[pl.BlockSpec(memory_space=space) for _, space in ins],
        out_specs=[pl.BlockSpec(memory_space=space) for _, _, space in outs],
        scratch_shapes=scratch,
        compiler_params=params(),
        **more,
    )(*[value for value, _ in ins])


def local(
    feats,
    hop_noise,
    send_rows,
    tile_block,
    tile_src,
    tile_dst,
    tile_count,
    labels,
    w_first,
    w_second,
    w_third,
    noise_first,
    noise_second,
    noise_third,
):
    nodes, width = feats.shape[2:]
    parts, each = send_rows.shape[2:]
    ghosts = parts * each
    tiles = tile_src.shape[2]
    slots = tile_src.shape[3]
    train = labels.shape[2]
    classes = w_third.shape[1]
    hid = w_second.shape[0]
    d_in = w_first.shape[0]
    cols = nodes + ghosts
    rows = send_rows.reshape(parts, each)
    turn = VMEM((128, 128), jnp.int32)
    pick = VMEM((ghosts, nodes), bf16)

    def gather(value):
        return lax.all_gather(value, ("dom", "grp"), axis=0, tiled=True)

    every_label = gather(labels.reshape(1, train))
    start0, out0 = call(
        first_kernel,
        [((nodes, width), bf16, VMEM), ((parts, each, width), bf16, VMEM)],
        [(feats.reshape(nodes, width), VMEM), (rows, VMEM)],
        [turn, pick],
    )
    every0 = gather(start0[:train])
    table0 = lax.all_to_all(out0, "dom", split_axis=0, concat_axis=0, tiled=True)
    own, ghost, part1, flag, own_rest, ghost_rest = call(
        build_kernel,
        [
            ((nodes, nodes), bf16, VMEM),
            ((nodes, ghosts), bf16, VMEM),
            ((nodes, width), f32, VMEM),
            ((1,), jnp.int32, SMEM),
            ((nodes, nodes), bf16, pl.ANY),
            ((nodes, ghosts), bf16, pl.ANY),
        ],
        [
            (tile_block.reshape(tiles), SMEM),
            (tile_count.reshape(1), SMEM),
            (tile_src.reshape(tiles, slots), VMEM),
            (tile_dst.reshape(tiles, slots), VMEM),
            (start0, VMEM),
            (hop_noise[0, 0, 0], VMEM),
        ],
        [VMEM((nodes, cols), f32), VMEM((nodes, max(nodes, ghosts)), bf16)],
    )
    start1, out1 = call(
        hop_kernel,
        [
            ((nodes, width), bf16, VMEM),
            ((parts, each, width), bf16, VMEM),
        ],
        [
            (flag, SMEM),
            (part1, VMEM),
            (ghost, VMEM),
            (ghost_rest, pl.ANY),
            (table0, VMEM),
            (rows, VMEM),
        ],
        [VMEM((nodes, width), f32), VMEM((nodes, ghosts), bf16), turn, pick],
    )
    table1 = lax.all_to_all(out1, "dom", split_axis=0, concat_axis=0, tiled=True)
    every1 = gather(start1[:train])
    (part2,) = call(
        own_kernel,
        [((nodes, width), f32, VMEM)],
        [
            (flag, SMEM),
            (own, VMEM),
            (own_rest, pl.ANY),
            (start1, VMEM),
            (hop_noise[1, 0, 0], VMEM),
        ],
        [VMEM((nodes, nodes), bf16)],
    )
    (last,) = pl.pallas_call(
        train_kernel,
        grid=(1,),
        out_shape=[jax.ShapeDtypeStruct((train, width), bf16)],
        in_specs=[
            pl.BlockSpec(memory_space=SMEM),
            pl.BlockSpec((train, width), lambda i: (0, 0)),
            pl.BlockSpec((train, ghosts), lambda i: (0, 0)),
            pl.BlockSpec(memory_space=pl.ANY),
            pl.BlockSpec((parts, each, width), lambda i: (0, 0, 0)),
        ],
        out_specs=[pl.BlockSpec((train, width), lambda i: (0, 0))],
        scratch_shapes=[VMEM((train, width), f32), VMEM((train, ghosts), bf16)],
        compiler_params=params(),
    )(flag, part2, ghost, ghost_rest, table1)
    every2 = gather(last)
    (hop_feats,) = call(
        last_kernel,
        [((2, 1, 1, nodes, width), bf16, VMEM)],
        [
            (flag, SMEM),
            (part2, VMEM),
            (ghost, VMEM),
            (ghost_rest, pl.ANY),
            (table1, VMEM),
            (start1, VMEM),
        ],
        [VMEM((nodes, width), f32), VMEM((nodes, ghosts), bf16)],
    )
    total = every2.shape[0]
    chunk = min(total, 1024)
    wide = (classes + 255) // 256 * 256

    def fixed(value):
        return pl.BlockSpec(value.shape, lambda i: (0, 0))

    grads = pl.pallas_call(
        classify_kernel,
        grid=(total // chunk,),
        out_shape=[
            jax.ShapeDtypeStruct(value.shape, f32)
            for value in (noise_first, noise_second, noise_third.T)
        ],
        in_specs=[
            pl.BlockSpec(memory_space=SMEM),
            pl.BlockSpec((chunk // train, train), lambda i: (i, 0)),
        ]
        + [pl.BlockSpec((chunk, width), lambda i: (i, 0))] * 3
        + [
            fixed(value)
            for value in (w_first, w_second, w_third.T, noise_first, noise_second, noise_third.T)
        ],
        out_specs=[fixed(value) for value in (noise_first, noise_second, noise_third.T)],
        scratch_shapes=[
            VMEM((chunk, d_in), bf16),
            VMEM((wide, hid), bf16),
            VMEM((128, 128), jnp.int32),
            VMEM((chunk, 128), jnp.int32),
            VMEM((chunk, hid), bf16),
            VMEM((chunk, hid), bf16),
            VMEM((chunk, hid), f32),
            VMEM((chunk, hid), f32),
            VMEM((chunk, hid), bf16),
            VMEM((chunk, hid), bf16),
        ],
        compiler_params=params(),
    )(
        lax.axis_index("dom").reshape(1).astype(jnp.int32),
        every_label,
        every0,
        every1,
        every2,
        w_first,
        w_second,
        w_third.T,
        noise_first,
        noise_second,
        noise_third.T,
    )
    return (hop_feats, grads[0], grads[1], grads[2].T)


def solution(mesh):
    in_specs = (
        P("dom", "grp", None, None),
        P(None, "dom", "grp", None, None),
        P("dom", "grp", None, None),
        P("dom", "grp", None),
        P("dom", "grp", None, None),
        P("dom", "grp", None, None),
        P("dom", "grp"),
        P("dom", "grp", None),
        P(),
        P(),
        P(),
        P("dom", None),
        P("dom", None),
        P("dom", None),
    )
    out_specs = (P(None, "dom", "grp", None, None), P("dom", None), P("dom", None), P("dom", None))
    return jax.shard_map(local, mesh=mesh, in_specs=in_specs, out_specs=out_specs, check_vma=False)
```

time: 500 us -> 352 us (0.70)
  blocking collectives: 0 us -> 299 us
  waiting for transfers between devices: 191 us -> 0.01 us
  local copies, waits for them, and re-layouts: 182 us -> 5 us
  matrix products: 59.3 us -> 0 us
  other arithmetic: 42.1 us -> 0 us
  Pallas kernels: 0 us -> 37.3 us
  between operations: 14 us -> 1.31 us
    all_gather x0 -> x4, blocking collectives: none -> 299 us  [gather(): return lax.all_gather(value, ('dom', 'grp'), axis=0, tiled=True)]
    gather x18 -> x0, local copies, waits for them, and re-layouts: 149 us -> none  [the longest x16 144 us: turn(): gathered = table[picked]]
    reduce_scatter x3 -> x0, waiting for transfers between devices: 133 us -> none  [the longest x1 54.7 us: local(): lax.psum_scatter(g_two, 'dom', scatter_dimension=0, tiled=True)]
    dot_general x40 -> x0, matrix products: 59.3 us -> none  [the longest x16 27.1 us: turn(): jnp.einsum('gbe,gef->gbf', onehot, gathered, preferred_element_type=jnp.f...]
    psum x1 -> x0, waiting for transfers between devices: 51.1 us -> none  [local(): s_one, s_two, s_three = lax.psum((p_one, p_two, p_three), 'grp')]
    pallas_call x0 -> x7, Pallas kernels: none -> 37.3 us  [the longest x5 19.9 us: call(): pl.pallas_call(kernel, out_shape=[jax.ShapeDtypeStruct(shape, dtype) for...]
    while x82 -> x0, local copies, waits for them, and re-layouts: 19 us -> none
    dynamic_slice x32 -> x0, local copies, waits for them, and re-layouts: 12.5 us -> none  [the longest x16 11.2 us: turn(): places = lax.dynamic_slice_in_dim(targets, first, tile_batch, 0)]
  transfers between devices with their start and end apart: 6 -> 2, of which waited for: 6 -> 0; matrix products, arithmetic and copies ran while one was open for 2% -> 1% of each run, Pallas kernels for 0% -> 3%
where the time goes in v1:
time: 352 us
  blocking collectives  299 us (85%)
  Pallas kernels  37.3 us (11%)
  starting transfers between devices  8.98 us (3%)
  local copies, waits for them, and re-layouts  5 us (1%)
    all_gather x4, blocking collectives, gather(): return lax.all_gather(value, ('dom', 'grp'), axis=0, tiled=True)  299 us
    pallas_call x5, Pallas kernels, call(): pl.pallas_call(kernel, out_shape=[jax.ShapeDtypeStruct(shape, dtype) for...  19.9 us
    pallas_call x1, Pallas kernels, local(): pl.pallas_call(classify_kernel, grid=(total // chunk,), out_shape=[jax.Sh...  15 us
  transfers between devices with their start and end apart: 2, of which 0 were waited for; matrix products, arithmetic and copies ran while one was open for 1% of the time, Pallas kernels for 3%

profile of v1, /device:TPU:0, one launch (start us, length us, event | category | flops | bytes accessed | tf_op | source)
XLA Modules:
  0.0 351.9 jit_solution(11065770359756902283)
XLA Ops:
  0.6 2.4 shard_map.165
  3.0 0.0 copy-start.2
  3.0 5.3 %all-to-all-start = ((bf16[8,32,256]{2,1,0:T(8,128)(2,1)}), bf16[8,32,256]{2,1,0:T(8,128)(2,1)S(1)}, u32[]{:S(2)}, u32[]{:S(2)}) async-start(bf16[8,32,256]{2,1,0:T(8,128)(2,1)} %get-tuple-element.24), calls=%async_computation | async-start | bytes 262144 | tf_op jit(solution)/shard_map/all_to_all | solution.py:355
  8.3 2.3 slice_bitcast_fusion
  10.6 0.7 slice.14
  11.3 78.1 %all_gather.13.zero_ref = bf16[1024,256]{1,0:T(8,128)(2,1)} all-gather(bf16[32,256]{1,0:T(8,128)(2,1)S(1)} %slice.14), channel_id=1, replica_groups=mesh['dom'=8,'grp'=4] {'dom','grp'}, dimensions={0}, use_global_device_ids=true | all-gather | bytes 540672 | tf_op jit(solution)/shard_map/all_gather | solution.py:345
  90.1 5.8 %shard_map.166 = (bf16[1024,1024]{1,0:T(8,128)(2,1)}, bf16[1024,256]{1,0:T(8,128)(2,1)}, f32[1024,256]{1,0:T(8,128)}, s32[1]{0:T(128)}, bf16[1024,1024]{1,0:T(8,128)(2,1)}, /*index=5*/bf16[1024,256]{1,0:T(8,128)(2,1)}) custom-call(s32[64]{0:T(128)} %bitcast.24, s32[1]{0:T(128)} %bitcast.15.count_ref, s32[64,256]{1,0:T(8,128)} %bitcast.20, ...), custom_call_target="tpu_custom_call" | custom-call | tf_op jit(solution)/shard_map/pallas_call | solution.py:303
  95.8 0.0 copy-done.2
  95.9 73.1 %all-gather = s32[32,1,32]{2,1,0:T(1,128)} all-gather(s32[1,1,32]{2,1,0:T(1,128)S(1)} %copy-done.2), channel_id=2, replica_groups=mesh['dom'=8,'grp'=4] {'dom','grp'}, dimensions={0}, use_global_device_ids=true | all-gather | bytes 4224 | tf_op jit(solution)/shard_map/all_gather | solution.py:345
  168.9 0.0 all-to-all-done.table_ref
  168.9 0.0 copy-start.1
  168.9 0.7 copy-done.1
  169.6 3.7 %shard_map.167 = (bf16[1024,256]{1,0:T(8,128)(2,1)}, bf16[8,32,256]{2,1,0:T(8,128)(2,1)}) custom-call(s32[1]{0:T(128)} %get-tuple-element.18.flag_ref, f32[1024,256]{1,0:T(8,128)} %get-tuple-element.21.part_ref, bf16[1024,256]{1,0:T(8,128)(2,1)} %get-tuple-element.22.ghost_ref, bf16[1024,256]{1,0:T(8,128)(2,1)} %get-tuple-element.23.rest_hbm, ...), custom_call_target="tpu_custom_call" | custom-call | tf_op jit(solution)/shard_map/pallas_call | solution.py:303
  173.3 3.7 %all-to-all-start.1 = ((bf16[8,32,256]{2,1,0:T(8,128)(2,1)}), bf16[8,32,256]{2,1,0:T(8,128)(2,1)S(1)}, u32[]{:S(2)}, u32[]{:S(2)}) async-start(bf16[8,32,256]{2,1,0:T(8,128)(2,1)} %get-tuple-element.26), calls=%async_computation.1 | async-start | bytes 262144 | tf_op jit(solution)/shard_map/all_to_all | solution.py:392
  177.0 0.7 slice.15
  177.7 73.5 %all_gather.14.one_ref = bf16[1024,256]{1,0:T(8,128)(2,1)} all-gather(bf16[32,256]{1,0:T(8,128)(2,1)S(1)} %slice.15), channel_id=1, replica_groups=mesh['dom'=8,'grp'=4] {'dom','grp'}, dimensions={0}, use_global_device_ids=true | all-gather | bytes 540672 | tf_op jit(solution)/shard_map/all_gather | solution.py:345
  251.2 4.2 %shard_map.168.part_ref = f32[1024,256]{1,0:T(8,128)} custom-call(s32[1]{0:T(128)} %get-tuple-element.18.flag_ref, bf16[1024,1024]{1,0:T(8,128)(2,1)} %get-tuple-element.19.own_ref, bf16[1024,1024]{1,0:T(8,128)(2,1)} %get-tuple-element.20.rest_hbm, bf16[1024,256]{1,0:T(8,128)(2,1)} %get-tuple-element.25.start_ref, bf16[1024,256]{1,0:T(8,128)(2,1)} %get-tuple-element.30.noise_ref), custom_call_target="tpu_custom_call" | custom-call | tf_op jit(solution)/shard_map/pallas_call | solution.py:303
  255.4 0.0 all-to-all-done.1.table_ref
  255.4 0.0 copy-start
  255.4 0.6 copy-done
  256.1 2.5 shard_map.170
  258.5 74.7 %all_gather.15.two_ref = bf16[1024,256]{1,0:T(8,128)(2,1)} all-gather(bf16[32,256]{1,0:T(8,128)(2,1)} %shard_map.170), channel_id=1, replica_groups=mesh['dom'=8,'grp'=4] {'dom','grp'}, dimensions={0}, use_global_device_ids=true | all-gather | bytes 540672 | tf_op jit(solution)/shard_map/all_gather | solution.py:345
  333.2 15.0 %shard_map.171 = (f32[96,1024]{1,0:T(8,128)}, f32[128,1024]{1,0:T(8,128)}, f32[172,128]{1,0:T(8,128)}) custom-call(s32[1]{0:T(128)} %bitcast.8.place_ref, s32[32,32]{1,0:T(8,128)} %bitcast.19, bf16[1024,256]{1,0:T(8,128)(2,1)} %all_gather.13.zero_ref, bf16[1024,256]{1,0:T(8,128)(2,1)} %all_gather.14.one_ref, bf16[1024,256]{1,0:T(8,128)(2,1)} %all_gather.15.two_ref, ...), custom_call_target="tpu_custom_call" | custom-call | tf_op jit(solution)/shard_map/pallas_call | solution.py:442
  348.2 3.7 %shard_map.169 = bf16[2,1,1,1024,256]{4,3,2,1,0:T(8,128)(2,1)} custom-call(s32[1]{0:T(128)} %get-tuple-element.18.flag_ref, f32[1024,256]{1,0:T(8,128)} %shard_map.168.part_ref, bf16[1024,256]{1,0:T(8,128)(2,1)} %get-tuple-element.22.ghost_ref, bf16[1024,256]{1,0:T(8,128)(2,1)} %get-tuple-element.23.rest_hbm, bf16[8,32,256]{2,1,0:T(8,128)(2,1)} %copy-done, ...), custom_call_target="tpu_custom_call" | custom-call | tf_op jit(solution)/shard_map/pallas_call | solution.py:303
Async XLA Ops:
  3.0 92.8 %copy-start.2 = (s32[1,1,32]{2,1,0:T(1,128)S(1)}, s32[1,1,32]{2,1,0:T(1,128)}, u32[]{:S(2)}) copy-start(s32[1,1,32]{2,1,0:T(1,128)} %param.21) | copy-start | bytes 388
  3.0 165.9 %all-to-all-start = ((bf16[8,32,256]{2,1,0:T(8,128)(2,1)}), bf16[8,32,256]{2,1,0:T(8,128)(2,1)S(1)}, u32[]{:S(2)}, u32[]{:S(2)}) async-start(bf16[8,32,256]{2,1,0:T(8,128)(2,1)} %get-tuple-element.24), calls=%async_computation | async-start | bytes 262144 | tf_op jit(solution)/shard_map/all_to_all | solution.py:355
  168.9 0.7 copy-start.1
  173.3 82.1 %all-to-all-start.1 = ((bf16[8,32,256]{2,1,0:T(8,128)(2,1)}), bf16[8,32,256]{2,1,0:T(8,128)(2,1)S(1)}, u32[]{:S(2)}, u32[]{:S(2)}) async-start(bf16[8,32,256]{2,1,0:T(8,128)(2,1)} %get-tuple-element.26), calls=%async_computation.1 | async-start | bytes 262144 | tf_op jit(solution)/shard_map/all_to_all | solution.py:392
  255.4 0.6 copy-start

commit v2 on v1

--- a/solution.py
+++ b/solution.py
@@ -19,8 +19,11 @@
 SMEM = pltpu.SMEM
 
 
-def params():
-    return pltpu.CompilerParams(vmem_limit_bytes=56 * 1024 * 1024)
+FEW = 64
+
+
+def params(mib):
+    return pltpu.CompilerParams(vmem_limit_bytes=mib * 1024 * 1024)
 
 
 def normalize(values):
@@ -54,10 +57,23 @@
     out_ref[...] = out.reshape(out_ref.shape)
 
 
-def first_kernel(feats_ref, rows_ref, start_ref, out_ref, turn_ref, pick_ref):
+def spread(rows, out_ref):
+    out_ref[...] = jnp.broadcast_to(rows[None], out_ref.shape)
+
+
+def first_kernel(
+    feats_ref, rows_ref, labels_ref, start_ref, out_ref, side_ref, turn_ref, pick_ref
+):
     start = normalize(feats_ref[...].astype(f32))
     start_ref[...] = start
     send(start, rows_ref, out_ref, turn_ref, pick_ref)
+    train = labels_ref.shape[1]
+    turn_ref[:1, :train] = labels_ref[...]
+    side_ref[:, :train, :] = jnp.broadcast_to(
+        start[None, :train], (side_ref.shape[0], train, start.shape[1])
+    )
+    label = turn_ref[:16, :].astype(f32).astype(bf16)
+    side_ref[:, train:, :128] = jnp.broadcast_to(label[None], (side_ref.shape[0], 16, 128))
 
 
 def build_kernel(
@@ -105,7 +121,7 @@
     lax.fori_loop(0, (count + GROUP - 1) // GROUP, turn, 0)
     own_ref[...] = sums_ref[:, :nodes].astype(bf16)
     ghost_ref[...] = sums_ref[:, nodes:].astype(bf16)
-    part_ref[...] = dot(own_ref[...], start_ref[...]) + noise_ref[...].astype(f32)
+    part_ref[...] = dot(own_ref[...], start_ref[...]) + noise_ref[0, 0, 0].astype(f32)
     big = jnp.max(sums_ref[...]) > 256.0
     flag_ref[0] = big.astype(jnp.int32)
 
@@ -121,7 +137,7 @@
 
 def aggregate(flag_ref, part_ref, count_ref, rest_hbm, table, sums_ref, rest_ref):
     rows = sums_ref.shape[0]
-    sums_ref[...] = part_ref[...] + dot(count_ref[...], table)
+    sums_ref[...] = part_ref.astype(f32) + dot(count_ref, table)
 
     @pl.when(flag_ref[0] > 0)
     def _():
@@ -138,6 +154,7 @@
     rows_ref,
     start_ref,
     out_ref,
+    side_ref,
     sums_ref,
     rest_ref,
     turn_ref,
@@ -145,28 +162,32 @@
 ):
     width = start_ref.shape[1]
     table = table_ref[...].reshape(-1, width)
-    aggregate(flag_ref, part_ref, ghost_ref, rest_hbm, table, sums_ref, rest_ref)
+    aggregate(flag_ref, part_ref[...], ghost_ref[...], rest_hbm, table, sums_ref, rest_ref)
     start = normalize(sums_ref[...])
     start_ref[...] = start
     send(start, rows_ref, out_ref, turn_ref, pick_ref)
+    spread(start[: side_ref.shape[1]], side_ref)
 
 
 def own_kernel(flag_ref, own_ref, rest_hbm, start_ref, noise_ref, part_ref, rest_ref):
     start = start_ref[...]
-    aggregate(flag_ref, noise_ref, own_ref, rest_hbm, start, part_ref, rest_ref)
+    aggregate(flag_ref, noise_ref[1, 0, 0], own_ref[...], rest_hbm, start, part_ref, rest_ref)
 
 
 def train_kernel(flag_ref, part_ref, ghost_ref, rest_hbm, table_ref, out_ref, sums_ref, rest_ref):
-    table = table_ref[...].reshape(-1, out_ref.shape[1])
-    aggregate(flag_ref, part_ref, ghost_ref, rest_hbm, table, sums_ref, rest_ref)
-    out_ref[...] = normalize(sums_ref[...])
+    train, width = sums_ref.shape
+    table = table_ref[...].reshape(-1, width)
+    aggregate(
+        flag_ref, part_ref[:train], ghost_ref[:train], rest_hbm, table, sums_ref, rest_ref
+    )
+    spread(normalize(sums_ref[...]), out_ref)
 
 
 def last_kernel(
     flag_ref, part_ref, ghost_ref, rest_hbm, table_ref, start_ref, out_ref, sums_ref, rest_ref
 ):
     table = table_ref[...].reshape(-1, out_ref.shape[-1])
-    aggregate(flag_ref, part_ref, ghost_ref, rest_hbm, table, sums_ref, rest_ref)
+    aggregate(flag_ref, part_ref[...], ghost_ref[...], rest_hbm, table, sums_ref, rest_ref)
     out_ref[0, 0, 0] = start_ref[...]
     out_ref[1, 0, 0] = normalize(sums_ref[...])
 
@@ -189,6 +210,7 @@
 
 
 def classify_kernel(
+    many,
     place_ref,
     label_ref,
     zero_ref,
@@ -216,20 +238,23 @@
 ):
     classes = w_third_ref.shape[0]
     hid = w_second_ref.shape[0]
-    width = zero_ref.shape[1]
+    width = zero_ref.shape[2]
     wide = w_third_pad_ref.shape[0]
     groups, train = label_ref.shape
     scale = noise_mult * clip_bound
     place = place_ref[0]
 
-    @pl.when(pl.program_id(0) == 0)
-    def _():
+    def begin():
         g_first_ref[...] = scale * n_first_ref[...]
         g_second_ref[...] = scale * n_second_ref[...]
         g_third_ref[...] = scale * n_third_ref[...]
         w_third_pad_ref[...] = jnp.zeros_like(w_third_pad_ref)
         w_third_pad_ref[:classes, :] = w_third_ref[...]
 
+    if many:
+        pl.when(pl.program_id(0) == 0)(begin)
+    else:
+        begin()
     turn_ref[:groups, :train] = label_ref[...]
     turned = turn_ref[...].T
     for group in range(groups):
@@ -237,7 +262,7 @@
             turned[:train, group : group + 1], (train, 128)
         )
     for hop, ref in enumerate((zero_ref, one_ref, two_ref)):
-        in_ref[:, hop * width : (hop + 1) * width] = ref[...]
+        in_ref[:, hop * width : (hop + 1) * width] = ref[:, :train, :].reshape(-1, width)
 
     def activate(values, h_ref, slope_ref, cols):
         sigma = 0.5 + 0.5 * jnp.tanh(0.5 * values)
@@ -299,16 +324,26 @@
     g_third_ref[...] += dot_tn(d_three, left(h_two_ref, share))[:classes, :]
 
 
-def call(kernel, outs, ins, scratch, **more):
+def call(kernel, mib, outs, ins, scratch):
+    def shape_of(shape, dtype, space):
+        return VMEM(shape, dtype) if space is None else jax.ShapeDtypeStruct(shape, dtype)
+
+    def block(space):
+        return pl.BlockSpec(memory_space=VMEM if space is None else space)
+
     return pl.pallas_call(
         kernel,
-        out_shape=[jax.ShapeDtypeStruct(shape, dtype) for shape, dtype, _ in outs],
-        in_specs=[pl.BlockSpec(memory_space=space) for _, space in ins],
-        out_specs=[pl.BlockSpec(memory_space=space) for _, _, space in outs],
+        out_shape=[shape_of(*out) for out in outs],
+        in_specs=[block(space) for _, space in ins],
+        out_specs=[block(space) for _, _, space in outs],
         scratch_shapes=scratch,
-        compiler_params=params(),
-        **more,
-    )(*[value for value, _ in ins])
+        compiler_params=params(mib),
+    )(
+        *[
+            pltpu.with_memory_space_constraint(value, VMEM) if space is None else value
+            for value, space in ins
+        ]
+    )
 
 
 def local(
@@ -340,25 +375,42 @@
     rows = send_rows.reshape(parts, each)
     turn = VMEM((128, 128), jnp.int32)
     pick = VMEM((ghosts, nodes), bf16)
+    axes = ("dom", "grp")
+    members = lax.axis_size(axes)
+    few = members <= FEW
+    copies = members if few else 1
 
     def gather(value):
-        return lax.all_gather(value, ("dom", "grp"), axis=0, tiled=True)
-
-    every_label = gather(labels.reshape(1, train))
-    start0, out0 = call(
+        if few:
+            return lax.all_to_all(value, axes, split_axis=0, concat_axis=0, tiled=True)
+        return lax.all_gather(value, axes, axis=0, tiled=True)
+
+    label_rows = labels.reshape(1, train)
+    start0, out0, side0 = call(
         first_kernel,
-        [((nodes, width), bf16, VMEM), ((parts, each, width), bf16, VMEM)],
-        [(feats.reshape(nodes, width), VMEM), (rows, VMEM)],
+        16,
+        [
+            ((nodes, width), bf16, None),
+            ((parts, each, width), bf16, VMEM),
+            ((copies, train + 16, width), bf16, VMEM),
+        ],
+        [(feats.reshape(nodes, width), VMEM), (rows, VMEM), (label_rows, VMEM)],
         [turn, pick],
     )
-    every0 = gather(start0[:train])
     table0 = lax.all_to_all(out0, "dom", split_axis=0, concat_axis=0, tiled=True)
+    if few:
+        every0 = gather(side0)
+        every_label = every0[:, train, :train].astype(jnp.int32)
+    else:
+        every0 = gather(side0[:, :train])
+        every_label = gather(label_rows)
     own, ghost, part1, flag, own_rest, ghost_rest = call(
         build_kernel,
-        [
-            ((nodes, nodes), bf16, VMEM),
-            ((nodes, ghosts), bf16, VMEM),
-            ((nodes, width), f32, VMEM),
+        24,
+        [
+            ((nodes, nodes), bf16, None),
+            ((nodes, ghosts), bf16, None),
+            ((nodes, width), f32, None),
             ((1,), jnp.int32, SMEM),
             ((nodes, nodes), bf16, pl.ANY),
             ((nodes, ghosts), bf16, pl.ANY),
@@ -368,121 +420,120 @@
             (tile_count.reshape(1), SMEM),
             (tile_src.reshape(tiles, slots), VMEM),
             (tile_dst.reshape(tiles, slots), VMEM),
-            (start0, VMEM),
-            (hop_noise[0, 0, 0], VMEM),
+            (start0, None),
+            (hop_noise, None),
         ],
         [VMEM((nodes, cols), f32), VMEM((nodes, max(nodes, ghosts)), bf16)],
     )
-    start1, out1 = call(
+    start1, out1, side1 = call(
         hop_kernel,
-        [
-            ((nodes, width), bf16, VMEM),
+        16,
+        [
+            ((nodes, width), bf16, None),
             ((parts, each, width), bf16, VMEM),
+            ((copies, train, width), bf16, VMEM),
         ],
         [
             (flag, SMEM),
-            (part1, VMEM),
-            (ghost, VMEM),
+            (part1, None),
+            (ghost, None),
             (ghost_rest, pl.ANY),
-            (table0, VMEM),
+            (table0, None),
             (rows, VMEM),
         ],
         [VMEM((nodes, width), f32), VMEM((nodes, ghosts), bf16), turn, pick],
     )
     table1 = lax.all_to_all(out1, "dom", split_axis=0, concat_axis=0, tiled=True)
-    every1 = gather(start1[:train])
+    every1 = gather(side1)
     (part2,) = call(
         own_kernel,
-        [((nodes, width), f32, VMEM)],
+        12,
+        [((nodes, width), f32, None)],
         [
             (flag, SMEM),
-            (own, VMEM),
+            (own, None),
             (own_rest, pl.ANY),
-            (start1, VMEM),
-            (hop_noise[1, 0, 0], VMEM),
+            (start1, None),
+            (hop_noise, None),
         ],
         [VMEM((nodes, nodes), bf16)],
     )
-    (last,) = pl.pallas_call(
+    (last,) = call(
         train_kernel,
-        grid=(1,),
-        out_shape=[jax.ShapeDtypeStruct((train, width), bf16)],
-        in_specs=[
-            pl.BlockSpec(memory_space=SMEM),
-            pl.BlockSpec((train, width), lambda i: (0, 0)),
-            pl.BlockSpec((train, ghosts), lambda i: (0, 0)),
-            pl.BlockSpec(memory_space=pl.ANY),
-            pl.BlockSpec((parts, each, width), lambda i: (0, 0, 0)),
-        ],
-        out_specs=[pl.BlockSpec((train, width), lambda i: (0, 0))],
-        scratch_shapes=[VMEM((train, width), f32), VMEM((train, ghosts), bf16)],
-        compiler_params=params(),
-    )(flag, part2, ghost, ghost_rest, table1)
+        8,
+        [((copies, train, width), bf16, VMEM)],
+        [
+            (flag, SMEM),
+            (part2, None),
+            (ghost, None),
+            (ghost_rest, pl.ANY),
+            (table1, None),
+        ],
+        [VMEM((train, width), f32), VMEM((train, ghosts), bf16)],
+    )
     every2 = gather(last)
     (hop_feats,) = call(
         last_kernel,
+        12,
         [((2, 1, 1, nodes, width), bf16, VMEM)],
         [
             (flag, SMEM),
-            (part2, VMEM),
-            (ghost, VMEM),
+            (part2, None),
+            (ghost, None),
             (ghost_rest, pl.ANY),
-            (table1, VMEM),
-            (start1, VMEM),
+            (table1, None),
+            (start1, None),
         ],
         [VMEM((nodes, width), f32), VMEM((nodes, ghosts), bf16)],
     )
-    total = every2.shape[0]
-    chunk = min(total, 1024)
+    chunk = train * min(members, 32)
+    groups = chunk // train
     wide = (classes + 255) // 256 * 256
-
-    def fixed(value):
-        return pl.BlockSpec(value.shape, lambda i: (0, 0))
-
-    grads = pl.pallas_call(
-        classify_kernel,
-        grid=(total // chunk,),
-        out_shape=[
-            jax.ShapeDtypeStruct(value.shape, f32)
-            for value in (noise_first, noise_second, noise_third.T)
-        ],
-        in_specs=[
-            pl.BlockSpec(memory_space=SMEM),
-            pl.BlockSpec((chunk // train, train), lambda i: (i, 0)),
-        ]
-        + [pl.BlockSpec((chunk, width), lambda i: (i, 0))] * 3
-        + [
-            fixed(value)
-            for value in (w_first, w_second, w_third.T, noise_first, noise_second, noise_third.T)
-        ],
-        out_specs=[fixed(value) for value in (noise_first, noise_second, noise_third.T)],
-        scratch_shapes=[
-            VMEM((chunk, d_in), bf16),
-            VMEM((wide, hid), bf16),
-            VMEM((128, 128), jnp.int32),
-            VMEM((chunk, 128), jnp.int32),
-            VMEM((chunk, hid), bf16),
-            VMEM((chunk, hid), bf16),
-            VMEM((chunk, hid), f32),
-            VMEM((chunk, hid), f32),
-            VMEM((chunk, hid), bf16),
-            VMEM((chunk, hid), bf16),
-        ],
-        compiler_params=params(),
-    )(
-        lax.axis_index("dom").reshape(1).astype(jnp.int32),
-        every_label,
-        every0,
-        every1,
-        every2,
-        w_first,
-        w_second,
-        w_third.T,
-        noise_first,
-        noise_second,
-        noise_third.T,
-    )
-    return (hop_feats, grads[0], grads[1], grads[2].T)
+    fixed = (w_first, w_second, w_third.T, noise_first, noise_second, noise_third.T)
+    scratch = [
+        VMEM((chunk, d_in), bf16),
+        VMEM((wide, hid), bf16),
+        VMEM((128, 128), jnp.int32),
+        VMEM((chunk, 128), jnp.int32),
+        VMEM((chunk, hid), bf16),
+        VMEM((chunk, hid), bf16),
+        VMEM((chunk, hid), f32),
+        VMEM((chunk, hid), f32),
+        VMEM((chunk, hid), bf16),
+        VMEM((chunk, hid), bf16),
+    ]
+    place = lax.axis_index("dom").reshape(1).astype(jnp.int32)
+    ins = (every_label, every0, every1, every2)
+    if members == groups:
+        first, second, third = call(
+            functools.partial(classify_kernel, False),
+            36,
+            [(value.shape, f32, VMEM) for value in fixed[3:]],
+            [(place, SMEM)] + [(value, None) for value in ins + fixed],
+            scratch,
+        )
+    else:
+
+        def whole(value):
+            return pl.BlockSpec(value.shape, lambda i: (0, 0))
+
+        def piece(value):
+            return pl.BlockSpec(
+                (groups,) + value.shape[1:], lambda i: (i,) + (0,) * (value.ndim - 1)
+            )
+
+        first, second, third = pl.pallas_call(
+            functools.partial(classify_kernel, True),
+            grid=(members // groups,),
+            out_shape=[jax.ShapeDtypeStruct(value.shape, f32) for value in fixed[3:]],
+            in_specs=[pl.BlockSpec(memory_space=SMEM)]
+            + [piece(value) for value in ins]
+            + [whole(value) for value in fixed],
+            out_specs=[whole(value) for value in fixed[3:]],
+            scratch_shapes=scratch,
+            compiler_params=params(56),
+        )(place, *ins, *fixed)
+    return (hop_feats, first, second, third.T)
 
 
 def solution(mesh):

time: 352 us -> 123 us (0.35)
  the two profiles are of different devices: /device:TPU:0 before, /device:TPU:1 now
where the time goes in v2:
time: 123 us; the launch traced here: 121 us
  Pallas kernels  31.1 us (25%)
  blocking collectives  30 us (24%)
  waiting for transfers between devices  24.8 us (20%)
  local copies, waits for them, and re-layouts  21.6 us (18%)
  starting transfers between devices  11.6 us (9%)
  between operations  1.42 us (1%)
    pallas_call x7, Pallas kernels, call(): pl.pallas_call(kernel, out_shape=[shape_of(*out) for out in outs], in_spe...  31.1 us
    all_to_all x2, waiting for transfers between devices, gather(): return lax.all_to_all(value, axes, split_axis=0, concat_axis=0, tiled=True)  24.8 us
    unnamed x48, local copies, waits for them, and re-layouts  21.6 us
    all_to_all x1, blocking collectives, gather(): return lax.all_to_all(value, axes, split_axis=0, concat_axis=0, tiled=True)  18.3 us
    all_to_all x1, blocking collectives, local(): lax.all_to_all(out1, 'dom', split_axis=0, concat_axis=0, tiled=True)  11.7 us
    all_to_all x2, starting transfers between devices, gather(): return lax.all_to_all(value, axes, split_axis=0, concat_axis=0, tiled=True)  6.35 us
    all_to_all x1, starting transfers between devices, local(): lax.all_to_all(out0, 'dom', split_axis=0, concat_axis=0, tiled=True)  5.22 us
  transfers between devices with their start and end apart: 3, of which 2 were waited for; matrix products, arithmetic and copies ran while one was open for 1% of the time, Pallas kernels for 12%

profile of v2, /device:TPU:1, one launch (start us, length us, event | category | flops | bytes accessed | tf_op | source)
XLA Modules:
  0.0 121.4 jit_solution(15240127166681910940)
XLA Ops:
  0.6 0.0 copy-start.21
  0.6 0.0 copy-start.13
  0.7 1.0 copy-done.13
  1.7 0.0 copy-start.20
  1.7 0.7 copy-done.20
  2.4 0.0 copy-start.22
  2.4 0.7 copy-done.22
  3.0 1.4 %shard_map.165 = (bf16[1024,256]{1,0:T(8,128)(2,1)S(1)}, bf16[8,32,256]{2,1,0:T(8,128)(2,1)}, bf16[32,48,256]{2,1,0:T(8,128)(2,1)S(1)}) custom-call(bf16[1024,256]{1,0:T(8,128)(2,1)S(1)} %bitcast.13, s32[8,32]{1,0:T(8,128)S(1)} %bitcast.19, s32[1,32]{1,0:T(1,128)S(1)} %bitcast.21), custom_call_target="tpu_custom_call" | custom-call | tf_op jit(solution)/shard_map/pallas_call | solution.py:334
  4.4 0.0 copy-start.12
  4.4 0.9 copy-done.12
  5.3 5.2 %all-to-all-start = ((bf16[8,32,256]{2,1,0:T(8,128)(2,1)}), bf16[8,32,256]{2,1,0:T(8,128)(2,1)S(1)}, u32[]{:S(2)}, u32[]{:S(2)}) async-start(bf16[8,32,256]{2,1,0:T(8,128)(2,1)} %get-tuple-element.26), calls=%async_computation | async-start | bytes 262144 | tf_op jit(solution)/shard_map/all_to_all | solution.py:400
  11.2 0.0 copy-start
  11.2 1.2 %copy-done = bf16[2,1,1,1024,256]{4,3,2,1,0:T(8,128)(2,1)S(1)} copy-done((bf16[2,1,1,1024,256]{4,3,2,1,0:T(8,128)(2,1)S(1)}, bf16[2,1,1,1024,256]{4,3,2,1,0:T(8,128)(2,1)}, u32[]{:S(2)}) %copy-start) | copy-done | bytes 1048600
  12.4 0.0 copy-start.18
  12.4 0.8 copy-done.18
  13.3 0.0 copy-start.19
  13.3 0.8 copy-done.19
  14.1 0.0 copy-start.23
  14.1 0.7 copy-done.23
  14.8 9.6 %shard_map.166 = (bf16[1024,1024]{1,0:T(8,128)(2,1)S(1)}, bf16[1024,256]{1,0:T(8,128)(2,1)S(1)}, f32[1024,256]{1,0:T(8,128)S(1)}, s32[1]{0:T(128)}, bf16[1024,10...) custom-call(s32[64]{0:T(128)S(1)} %bitcast.22, s32[1]{0:T(128)} %bitcast.12.count_ref, s32[64,256]{1,0:T(8,128)S(1)} %bitcast.17, ...), custom_call_target="tpu_custom_call" | custom-call | tf_op jit(solution)/shard_map/pallas_call | solution.py:334
  24.4 0.0 copy-start.2
  24.4 1.3 %copy-done.2 = bf16[1024,1024]{1,0:T(8,128)(2,1)} copy-done((bf16[1024,1024]{1,0:T(8,128)(2,1)}, bf16[1024,1024]{1,0:T(8,128)(2,1)S(1)}, u32[]{:S(2)}) %copy-start.2) | copy-done | bytes 2097176
  25.7 0.0 copy-start.4
  25.7 1.3 %copy-done.4 = bf16[1024,1024]{1,0:T(8,128)(2,1)} copy-done((bf16[1024,1024]{1,0:T(8,128)(2,1)}, bf16[1024,1024]{1,0:T(8,128)(2,1)S(1)}, u32[]{:S(2)}) %copy-start.4) | copy-done | bytes 2097176
  27.0 0.0 all-to-all-done.table_ref
  27.1 0.0 copy-done.21
  27.1 0.0 copy-start.1
  27.1 1.7 %shard_map.167 = (bf16[1024,256]{1,0:T(8,128)(2,1)S(1)}, bf16[8,32,256]{2,1,0:T(8,128)(2,1)S(1)}, bf16[32,32,256]{2,1,0:T(8,128)(2,1)S(1)}) custom-call(s32[1]{0:T(128)} %get-tuple-element.20.flag_ref, f32[1024,256]{1,0:T(8,128)S(1)} %get-tuple-element.23.part_ref, bf16[1024,256]{1,0:T(8,128)(2,1)S(1)} %get-tuple-element.24.ghost_ref, ...), custom_call_target="tpu_custom_call" | custom-call | tf_op jit(solution)/shard_map/pallas_call | solution.py:334
  28.8 0.0 copy-start.8
  28.8 0.8 copy-done.8
  29.6 11.7 %all_to_all.25.table_ref = bf16[8,32,256]{2,1,0:T(8,128)(2,1)S(1)} all-to-all(bf16[8,32,256]{2,1,0:T(8,128)(2,1)S(1)} %get-tuple-element.28), channel_id=1, replica_groups=mesh['dom'=8,'grp'=4] {'dom'}, dimensions={0} | all-to-all | bytes 262144 | tf_op jit(solution)/shard_map/all_to_all | solution.py:446
  41.3 18.3 %all_to_all.26.one_ref = bf16[32,32,256]{2,1,0:T(8,128)(2,1)} all-to-all(bf16[32,32,256]{2,1,0:T(8,128)(2,1)S(1)} %get-tuple-element.30), channel_id=1, replica_groups=mesh['dom'=8,'grp'=4] {'dom','grp'}, dimensions={0} | all-to-all | bytes 1048576 | tf_op jit(solution)/shard_map/all_to_all | solution.py:385
  59.6 3.2 %all-to-all-start.2 = ((bf16[32,48,256]{2,1,0:T(8,128)(2,1)}), bf16[32,48,256]{2,1,0:T(8,128)(2,1)}, u32[]{:S(2)}, u32[]{:S(2)}) async-start(bf16[32,48,256]{2,1,0:T(8,128)(2,1)} %copy-done.12), calls=%async_computation.2 | async-start | bytes 1572864 | tf_op jit(solution)/shard_map/all_to_all | solution.py:385
  62.8 0.0 copy-done.1
  62.8 0.0 copy-start.3
  62.8 1.6 %copy-done.3 = bf16[1024,1024]{1,0:T(8,128)(2,1)S(1)} copy-done((bf16[1024,1024]{1,0:T(8,128)(2,1)S(1)}, bf16[1024,1024]{1,0:T(8,128)(2,1)}, u32[]{:S(2)}) %copy-start.3) | copy-done | bytes 2097176
  64.4 0.0 copy-start.5
  64.4 1.6 %copy-done.5 = bf16[1024,1024]{1,0:T(8,128)(2,1)S(1)} copy-done((bf16[1024,1024]{1,0:T(8,128)(2,1)S(1)}, bf16[1024,1024]{1,0:T(8,128)(2,1)}, u32[]{:S(2)}) %copy-start.5) | copy-done | bytes 2097176
  66.0 0.0 copy-start.9
  66.0 1.0 copy-done.9
  67.0 1.3 %shard_map.168.part_ref = f32[1024,256]{1,0:T(8,128)S(1)} custom-call(s32[1]{0:T(128)} %get-tuple-element.20.flag_ref, bf16[1024,1024]{1,0:T(8,128)(2,1)S(1)} %copy-done.3, bf16[1024,1024]{1,0:T(8,128)(2,1)S(1)} %copy-done.5, bf16[1024,256]{1,0:T(8,128)(2,1)S(1)} %copy-done.9, bf16[2,1,1,1024,256]{4,3,2,1,0:T(8,128)(2,1)S(1)} %copy-done.1), custom_call_target="tpu_custom_call" | custom-call | tf_op jit(solution)/shard_map/pallas_call | solution.py:334
  68.3 1.7 %shard_map.170 = bf16[32,32,256]{2,1,0:T(8,128)(2,1)} custom-call(s32[1]{0:T(128)} %get-tuple-element.20.flag_ref, f32[1024,256]{1,0:T(8,128)S(1)} %shard_map.168.part_ref, bf16[1024,256]{1,0:T(8,128)(2,1)S(1)} %get-tuple-element.24.ghost_ref, bf16[1024,256]{1,0:T(8,128)(2,1)S(1)} %get-tuple-element.25.rest_hbm, bf16[8,32,256]{2,1,0:T(8,128)(2,1)S(1)} %all_to_all.25.table_ref), custom_call_target="tpu_custom_call" | custom-call | tf_op jit(solution)/shard_map/pallas_call | solution.py:334
  69.9 13.7 %all-to-all-done.2.zero_ref = bf16[32,48,256]{2,1,0:T(8,128)(2,1)} async-done(((bf16[32,48,256]{2,1,0:T(8,128)(2,1)}), bf16[32,48,256]{2,1,0:T(8,128)(2,1)}, u32[]{:S(2)}, u32[]{:S(2)}) %all-to-all-start.2) | async-done | bytes 786464 | tf_op jit(solution)/shard_map/all_to_all | solution.py:385
  83.7 0.0 copy-start.17
  83.7 3.2 %all-to-all-start.4 = ((bf16[32,32,256]{2,1,0:T(8,128)(2,1)}), bf16[32,32,256]{2,1,0:T(8,128)(2,1)S(1)}, u32[]{:S(2)}, u32[]{:S(2)}) async-start(bf16[32,32,256]{2,1,0:T(8,128)(2,1)} %shard_map.170), calls=%async_computation.4 | async-start | bytes 1048576 | tf_op jit(solution)/shard_map/all_to_all | solution.py:385
  86.8 0.0 copy-start.7
  86.8 0.0 copy-start.10
  86.9 1.1 copy-done.10
  87.9 2.2 %shard_map.169 = bf16[2,1,1,1024,256]{4,3,2,1,0:T(8,128)(2,1)} custom-call(s32[1]{0:T(128)} %get-tuple-element.20.flag_ref, f32[1024,256]{1,0:T(8,128)S(1)} %shard_map.168.part_ref, bf16[1024,256]{1,0:T(8,128)(2,1)S(1)} %get-tuple-element.24.ghost_ref, bf16[1024,256]{1,0:T(8,128)(2,1)S(1)} %get-tuple-element.25.rest_hbm, ...), custom_call_target="tpu_custom_call" | custom-call | tf_op jit(solution)/shard_map/pallas_call | solution.py:334
  90.2 0.9 slice_convert_fusion
  91.0 11.1 %all-to-all-done.4.two_ref = bf16[32,32,256]{2,1,0:T(8,128)(2,1)S(1)} async-done(((bf16[32,32,256]{2,1,0:T(8,128)(2,1)}), bf16[32,32,256]{2,1,0:T(8,128)(2,1)S(1)}, u32[]{:S(2)}, u32[]{:S(2)}) %all-to-all-start.4) | async-done | bytes 524320 | tf_op jit(solution)/shard_map/all_to_all | solution.py:385
  102.1 0.0 copy-done.17
  102.1 0.0 copy-done.7
  102.1 0.0 copy-start.6
  102.1 1.6 %copy-done.6 = bf16[1024,1024]{1,0:T(8,128)(2,1)S(1)} copy-done((bf16[1024,1024]{1,0:T(8,128)(2,1)S(1)}, bf16[1024,1024]{1,0:T(8,128)(2,1)}, u32[]{:S(2)}) %copy-start.6) | copy-done | bytes 2097176
  103.7 0.0 copy-start.11
  103.7 1.4 %copy-done.11 = bf16[768,1024]{1,0:T(8,128)(2,1)S(1)} copy-done((bf16[768,1024]{1,0:T(8,128)(2,1)S(1)}, bf16[768,1024]{1,0:T(8,128)(2,1)}, u32[]{:S(2)}) %copy-start.11) | copy-done | bytes 1572888
  105.1 0.0 copy-start.14
  105.1 1.0 copy-done.14
  106.2 0.0 copy-start.15
  106.2 1.0 copy-done.15
  107.2 0.0 copy-start.16
  107.2 1.0 copy-done.16
  108.2 13.3 %shard_map.171 = (f32[96,1024]{1,0:T(8,128)}, f32[128,1024]{1,0:T(8,128)}, f32[172,128]{1,0:T(8,128)}) custom-call(s32[1]{0:T(128)} %bitcast.7.place_ref, s32[32,32]{1,0:T(8,128)S(1)} %bitcast.16, bf16[32,48,256]{2,1,0:T(8,128)(2,1)} %all-to-all-done.2.zero_ref, bf16[32,32,256]{2,1,0:T(8,128)(2,1)S(1)} %copy-done.7, ...), custom_call_target="tpu_custom_call" | custom-call | tf_op jit(solution)/shard_map/pallas_call | solution.py:334
Async XLA Ops:
  0.6 26.4 %copy-start.21 = (s32[1,1,8,32]{3,2,1,0:T(8,128)S(1)}, s32[1,1,8,32]{3,2,1,0:T(8,128)}, u32[]{:S(2)}) copy-start(s32[1,1,8,32]{3,2,1,0:T(8,128)} %param.16) | copy-start | bytes 3076
  0.6 1.0 copy-start.13
  1.7 0.7 copy-start.20
  2.4 0.7 copy-start.22
  4.4 0.9 copy-start.12
  5.3 21.7 %all-to-all-start = ((bf16[8,32,256]{2,1,0:T(8,128)(2,1)}), bf16[8,32,256]{2,1,0:T(8,128)(2,1)S(1)}, u32[]{:S(2)}, u32[]{:S(2)}) async-start(bf16[8,32,256]{2,1,0:T(8,128)(2,1)} %get-tuple-element.26), calls=%async_computation | async-start | bytes 262144 | tf_op jit(solution)/shard_map/all_to_all | solution.py:400
  11.2 1.2 %copy-start = (bf16[2,1,1,1024,256]{4,3,2,1,0:T(8,128)(2,1)S(1)}, bf16[2,1,1,1024,256]{4,3,2,1,0:T(8,128)(2,1)}, u32[]{:S(2)}) copy-start(bf16[2,1,1,1024,256]{4,3,2,1,0:T(8,128)(2,1)} %noise_ref.3) | copy-start | bytes 3145732
  12.4 0.8 copy-start.18
  13.3 0.8 copy-start.19
  14.1 0.7 copy-start.23
  24.4 1.4 %copy-start.2 = (bf16[1024,1024]{1,0:T(8,128)(2,1)}, bf16[1024,1024]{1,0:T(8,128)(2,1)S(1)}, u32[]{:S(2)}) copy-start(bf16[1024,1024]{1,0:T(8,128)(2,1)S(1)} %get-tuple-element.21.own_ref) | copy-start | bytes 6291460
  25.7 1.3 %copy-start.4 = (bf16[1024,1024]{1,0:T(8,128)(2,1)}, bf16[1024,1024]{1,0:T(8,128)(2,1)S(1)}, u32[]{:S(2)}) copy-start(bf16[1024,1024]{1,0:T(8,128)(2,1)S(1)} %get-tuple-element.22.rest_hbm) | copy-start | bytes 6291460
  27.1 35.7 %copy-start.1 = (bf16[2,1,1,1024,256]{4,3,2,1,0:T(8,128)(2,1)S(1)}, bf16[2,1,1,1024,256]{4,3,2,1,0:T(8,128)(2,1)}, u32[]{:S(2)}) copy-start(bf16[2,1,1,1024,256]{4,3,2,1,0:T(8,128)(2,1)} %noise_ref.3) | copy-start | bytes 3145732
  28.8 0.8 copy-start.8
  59.6 24.1 %all-to-all-start.2 = ((bf16[32,48,256]{2,1,0:T(8,128)(2,1)}), bf16[32,48,256]{2,1,0:T(8,128)(2,1)}, u32[]{:S(2)}, u32[]{:S(2)}) async-start(bf16[32,48,256]{2,1,0:T(8,128)(2,1)} %copy-done.12), calls=%async_computation.2 | async-start | bytes 1572864 | tf_op jit(solution)/shard_map/all_to_all | solution.py:385
  62.8 1.6 %copy-start.3 = (bf16[1024,1024]{1,0:T(8,128)(2,1)S(1)}, bf16[1024,1024]{1,0:T(8,128)(2,1)}, u32[]{:S(2)}) copy-start(bf16[1024,1024]{1,0:T(8,128)(2,1)} %copy-done.2) | copy-start | bytes 6291460
  64.4 1.6 %copy-start.5 = (bf16[1024,1024]{1,0:T(8,128)(2,1)S(1)}, bf16[1024,1024]{1,0:T(8,128)(2,1)}, u32[]{:S(2)}) copy-start(bf16[1024,1024]{1,0:T(8,128)(2,1)} %copy-done.4) | copy-start | bytes 6291460
  66.0 1.0 copy-start.9
  83.7 18.5 %copy-start.17 = (f32[128,172]{0,1:T(8,128)S(1)}, f32[128,172]{0,1:T(8,128)}, u32[]{:S(2)}) copy-start(f32[128,172]{0,1:T(8,128)} %param.27) | copy-start | bytes 264196
  83.7 18.5 %all-to-all-start.4 = ((bf16[32,32,256]{2,1,0:T(8,128)(2,1)}), bf16[32,32,256]{2,1,0:T(8,128)(2,1)S(1)}, u32[]{:S(2)}, u32[]{:S(2)}) async-start(bf16[32,32,256]{2,1,0:T(8,128)(2,1)} %shard_map.170), calls=%async_computation.4 | async-start | bytes 1048576 | tf_op jit(solution)/shard_map/all_to_all | solution.py:385
  86.8 15.3 %copy-start.7 = (bf16[32,32,256]{2,1,0:T(8,128)(2,1)S(1)}, bf16[32,32,256]{2,1,0:T(8,128)(2,1)}, u32[]{:S(2)}) copy-start(bf16[32,32,256]{2,1,0:T(8,128)(2,1)} %all_to_all.26.one_ref) | copy-start | bytes 1572868
  86.8 1.1 copy-start.10
  102.1 1.6 %copy-start.6 = (bf16[1024,1024]{1,0:T(8,128)(2,1)S(1)}, bf16[1024,1024]{1,0:T(8,128)(2,1)}, u32[]{:S(2)}) copy-start(bf16[1024,1024]{1,0:T(8,128)(2,1)} %w_second_ref.1) | copy-start | bytes 6291460
  103.7 1.4 %copy-start.11 = (bf16[768,1024]{1,0:T(8,128)(2,1)S(1)}, bf16[768,1024]{1,0:T(8,128)(2,1)}, u32[]{:S(2)}) copy-start(bf16[768,1024]{1,0:T(8,128)(2,1)} %w_first_ref.1) | copy-start | bytes 4718596
  105.1 1.0 copy-start.14
  106.2 1.0 copy-start.15
  107.2 1.0 copy-start.16

commit v3 on v2

--- a/solution.py
+++ b/solution.py
@@ -17,6 +17,8 @@
 bf16 = jnp.bfloat16
 VMEM = pltpu.VMEM
 SMEM = pltpu.SMEM
+HBM = pltpu.HBM
+DMA = pltpu.SemaphoreType.DMA
 
 
 FEW = 64
@@ -24,6 +26,13 @@
 
 def params(mib):
     return pltpu.CompilerParams(vmem_limit_bytes=mib * 1024 * 1024)
+
+
+def fetch(pairs, sems):
+    copies = [pltpu.make_async_copy(*pair, sems.at[at]) for at, pair in enumerate(pairs)]
+    for copy in copies:
+        copy.start()
+    return copies
 
 
 def normalize(values):
@@ -62,56 +71,100 @@
 
 
 def first_kernel(
-    feats_ref, rows_ref, labels_ref, start_ref, out_ref, side_ref, turn_ref, pick_ref
+    feats_hbm,
+    rows_hbm,
+    labels_hbm,
+    start_ref,
+    out_ref,
+    side_ref,
+    feats_ref,
+    rows_ref,
+    labels_ref,
+    turn_ref,
+    pick_ref,
+    sems,
 ):
+    sources = (feats_hbm.at[0, 0], rows_hbm.at[0, 0], labels_hbm.at[0])
+    copies = fetch(zip(sources, (feats_ref, rows_ref, labels_ref)), sems)
+    for copy in copies:
+        copy.wait()
     start = normalize(feats_ref[...].astype(f32))
     start_ref[...] = start
     send(start, rows_ref, out_ref, turn_ref, pick_ref)
     train = labels_ref.shape[1]
+    side_ref[:train, :] = start[:train]
     turn_ref[:1, :train] = labels_ref[...]
-    side_ref[:, :train, :] = jnp.broadcast_to(
-        start[None, :train], (side_ref.shape[0], train, start.shape[1])
-    )
-    label = turn_ref[:16, :].astype(f32).astype(bf16)
-    side_ref[:, train:, :128] = jnp.broadcast_to(label[None], (side_ref.shape[0], 16, 128))
+    side_ref[train:, :128] = turn_ref[:16, :].astype(f32).astype(bf16)
 
 
 def build_kernel(
     blocks_ref,
     count_ref,
-    src_ref,
-    dst_ref,
+    src_hbm,
+    dst_hbm,
+    noise_hbm,
     start_ref,
-    noise_ref,
-    own_ref,
+    own_hbm,
     ghost_ref,
     part_ref,
     flag_ref,
     own_rest_ref,
     ghost_rest_ref,
+    src_ref,
+    dst_ref,
+    noise_ref,
+    low_ref,
+    high_ref,
+    spot_ref,
     sums_ref,
     rest_ref,
+    own_ref,
+    sems,
 ):
+    copies = fetch(
+        (
+            (src_hbm.at[0, 0], src_ref),
+            (dst_hbm.at[0, 0], dst_ref),
+            (noise_hbm.at[0, 0, 0], noise_ref),
+        ),
+        sems,
+    )
     nodes, cols = sums_ref.shape
     pieces = cols // LOW
-    slots = src_ref.shape[1]
-    count = count_ref[0]
+    tiles, slots = src_ref.shape
+    count = count_ref[0, 0]
     sums_ref[...] = jnp.zeros_like(sums_ref)
-    low_ids = lax.broadcasted_iota(jnp.int32, (LOW, slots), 0)
-    spot_ids = lax.broadcasted_iota(jnp.int32, (pieces * BLOCK, slots), 0)
+    for copy in copies:
+        copy.wait()
+
+    def sixteen(values):
+        wide = jnp.broadcast_to(values.astype(f32)[:, None, :], (tiles, 16, slots))
+        return wide.reshape(tiles * 16, slots).astype(bf16)
+
+    src = src_ref[...]
+    dst = dst_ref[...]
+    tile_ids = lax.broadcasted_iota(jnp.int32, (tiles, slots), 0)
+    low_ref[...] = sixteen(src % LOW)
+    high_ref[...] = sixteen(src // LOW)
+    spot_ref[...] = sixteen(jnp.where((dst < BLOCK) & (tile_ids < count), dst, -1))
+    ids = lax.broadcasted_iota(jnp.int32, (LOW, slots), 0).astype(f32).astype(bf16)
+    one = jnp.ones((), bf16)
+    zero = jnp.zeros((), bf16)
+
+    def hot(values, length):
+        tall = jnp.concatenate([values] * (length // 16), 0)
+        return jnp.where(ids[:length] == tall, one, zero)
 
     def turn(step, carry):
         for inner in range(GROUP):
             tile = step * GROUP + inner
-            src = src_ref[pl.ds(tile, 1), :]
-            dst = dst_ref[pl.ds(tile, 1), :]
-            live = (dst < BLOCK) & (tile < count)
-            spot = jnp.where(live, (src // LOW) * BLOCK + dst, -1)
-            low = src % LOW
-            low_hot = jnp.where(low_ids == low, 1.0, 0.0).astype(bf16)
-            spot_hot = jnp.where(spot_ids == spot, 1.0, 0.0).astype(bf16)
-            out = dot_nt(spot_hot, low_hot)
-            base = pl.multiple_of(blocks_ref[tile] * BLOCK, BLOCK)
+            rows = pl.ds(pl.multiple_of(tile * 16, 16), 16)
+            low, high, spot = low_ref[rows, :], high_ref[rows, :], spot_ref[rows, :]
+            spots = [
+                hot(jnp.where(high == piece, spot, -one), BLOCK) for piece in range(pieces)
+            ]
+            out = dot_nt(jnp.concatenate(spots, 0), hot(low, LOW))
+            base = pl.multiple_of(blocks_ref[0, 0, tile] * BLOCK, BLOCK)
             for piece in range(pieces):
                 sums_ref[pl.ds(base, BLOCK), piece * LOW : (piece + 1) * LOW] += out[
                     piece * BLOCK : (piece + 1) * BLOCK
@@ -119,20 +172,33 @@
         return carry
 
     lax.fori_loop(0, (count + GROUP - 1) // GROUP, turn, 0)
-    own_ref[...] = sums_ref[:, :nodes].astype(bf16)
-    ghost_ref[...] = sums_ref[:, nodes:].astype(bf16)
-    part_ref[...] = dot(own_ref[...], start_ref[...]) + noise_ref[0, 0, 0].astype(f32)
-    big = jnp.max(sums_ref[...]) > 256.0
+    top = jnp.zeros((BLOCK, LOW), f32)
+    for first in range(0, nodes, BLOCK):
+        for piece in range(pieces):
+            values = sums_ref[first : first + BLOCK, piece * LOW : (piece + 1) * LOW]
+            top = jnp.maximum(top, values)
+            at = piece * LOW
+            if at < nodes:
+                own_ref[first : first + BLOCK, at : at + LOW] = values.astype(bf16)
+            else:
+                at -= nodes
+                ghost_ref[first : first + BLOCK, at : at + LOW] = values.astype(bf16)
+    own_copy = pltpu.make_async_copy(own_ref, own_hbm, sems.at[3])
+    own_copy.start()
+    part_ref[...] = dot(own_ref[...], start_ref[...]) + noise_ref[...].astype(f32)
+    big = jnp.max(top) > 256.0
     flag_ref[0] = big.astype(jnp.int32)
 
     @pl.when(big)
     def _():
         own_rest = (sums_ref[:, :nodes] - own_ref[...].astype(f32)).astype(bf16)
         part_ref[...] += dot(own_rest, start_ref[...])
-        rest_ref[...] = own_rest
-        pltpu.sync_copy(rest_ref, own_rest_ref)
+        rest_ref[:, :nodes] = own_rest
+        pltpu.sync_copy(rest_ref.at[:, :nodes], own_rest_ref)
         rest_ref[:, : cols - nodes] = (sums_ref[:, nodes:] - ghost_ref[...].astype(f32)).astype(bf16)
         pltpu.sync_copy(rest_ref.at[:, : cols - nodes], ghost_rest_ref)
+
+    own_copy.wait()
 
 
 def aggregate(flag_ref, part_ref, count_ref, rest_hbm, table, sums_ref, rest_ref):
@@ -154,7 +220,6 @@
     rows_ref,
     start_ref,
     out_ref,
-    side_ref,
     sums_ref,
     rest_ref,
     turn_ref,
@@ -166,21 +231,43 @@
     start = normalize(sums_ref[...])
     start_ref[...] = start
     send(start, rows_ref, out_ref, turn_ref, pick_ref)
-    spread(start[: side_ref.shape[1]], side_ref)
-
-
-def own_kernel(flag_ref, own_ref, rest_hbm, start_ref, noise_ref, part_ref, rest_ref):
+
+
+def own_kernel(
+    flag_ref, own_hbm, rest_hbm, noise_hbm, start_ref, part_ref, own_ref, noise_ref, rest_ref, sems
+):
+    copies = fetch(((own_hbm, own_ref), (noise_hbm.at[1, 0, 0], noise_ref)), sems)
+    for copy in copies:
+        copy.wait()
     start = start_ref[...]
-    aggregate(flag_ref, noise_ref[1, 0, 0], own_ref[...], rest_hbm, start, part_ref, rest_ref)
-
-
-def train_kernel(flag_ref, part_ref, ghost_ref, rest_hbm, table_ref, out_ref, sums_ref, rest_ref):
+    noise = noise_ref[...].astype(f32)
+    aggregate(flag_ref, noise, own_ref[...], rest_hbm, start, part_ref, rest_ref)
+
+
+def train_kernel(
+    flag_ref,
+    place_ref,
+    part_ref,
+    ghost_ref,
+    rest_hbm,
+    table_ref,
+    start_ref,
+    *refs,
+):
+    *piece_refs, out_ref, side_ref, sums_ref, rest_ref = refs
     train, width = sums_ref.shape
     table = table_ref[...].reshape(-1, width)
     aggregate(
         flag_ref, part_ref[:train], ghost_ref[:train], rest_hbm, table, sums_ref, rest_ref
     )
     spread(normalize(sums_ref[...]), out_ref)
+    group, groups = place_ref[1], side_ref.shape[1] // train
+    for shift in range(len(piece_refs) + 1):
+        rows = piece_refs[shift - 1][...] if shift else start_ref[:train, :]
+        at = pl.multiple_of(lax.rem(group + shift, groups) * train, train)
+        side_ref[:, pl.ds(at, train), :] = jnp.broadcast_to(
+            rows[None], (side_ref.shape[0], train, width)
+        )
 
 
 def last_kernel(
@@ -213,18 +300,26 @@
     many,
     place_ref,
     label_ref,
-    zero_ref,
-    one_ref,
+    zero_in,
+    one_in,
     two_ref,
+    w_first_hbm,
+    w_second_hbm,
+    w_third_hbm,
+    n_first_hbm,
+    n_second_hbm,
+    n_third_hbm,
+    g_first_ref,
+    g_second_ref,
+    g_third_ref,
+    zero_own,
+    one_own,
     w_first_ref,
     w_second_ref,
     w_third_ref,
     n_first_ref,
     n_second_ref,
     n_third_ref,
-    g_first_ref,
-    g_second_ref,
-    g_third_ref,
     in_ref,
     w_third_pad_ref,
     turn_ref,
@@ -235,32 +330,56 @@
     slope_two_ref,
     d_one_ref,
     d_two_ref,
+    sems,
 ):
     classes = w_third_ref.shape[0]
     hid = w_second_ref.shape[0]
-    width = zero_ref.shape[2]
+    width = two_ref.shape[2]
     wide = w_third_pad_ref.shape[0]
     groups, train = label_ref.shape
     scale = noise_mult * clip_bound
     place = place_ref[0]
-
-    def begin():
+    pairs = (
+        (w_first_hbm, w_first_ref),
+        (w_second_hbm, w_second_ref),
+        (w_third_hbm, w_third_ref),
+        (n_first_hbm, n_first_ref),
+        (n_second_hbm, n_second_ref),
+        (n_third_hbm, n_third_ref),
+    )
+
+    def set_noise():
         g_first_ref[...] = scale * n_first_ref[...]
         g_second_ref[...] = scale * n_second_ref[...]
         g_third_ref[...] = scale * n_third_ref[...]
+
+    def pad():
         w_third_pad_ref[...] = jnp.zeros_like(w_third_pad_ref)
         w_third_pad_ref[:classes, :] = w_third_ref[...]
 
     if many:
-        pl.when(pl.program_id(0) == 0)(begin)
+
+        @pl.when(pl.program_id(0) == 0)
+        def _():
+            for copy in fetch(pairs, sems):
+                copy.wait()
+            set_noise()
+            pad()
+
+        zero_ref, one_ref = zero_in, one_in
     else:
-        begin()
+        zero_ref, one_ref = zero_own, one_own
+        copies = fetch(((zero_in, zero_own), (one_in, one_own)) + pairs, sems)
+
     turn_ref[:groups, :train] = label_ref[...]
     turned = turn_ref[...].T
     for group in range(groups):
         column_ref[group * train : (group + 1) * train, :] = jnp.broadcast_to(
             turned[:train, group : group + 1], (train, 128)
         )
+    if not many:
+        for copy in copies[:3]:
+            copy.wait()
     for hop, ref in enumerate((zero_ref, one_ref, two_ref)):
         in_ref[:, hop * width : (hop + 1) * width] = ref[:, :train, :].reshape(-1, width)
 
@@ -279,10 +398,15 @@
         activate(dot(in_ref[...], w_first_ref[:, cut]), h_one_ref, slope_one_ref, cut)
         for cut in cuts
     )
+    if not many:
+        copies[3].wait()
     sq_two = sum(
         activate(dot(h_one_ref[...], w_second_ref[:, cut]), h_two_ref, slope_two_ref, cut)
         for cut in cuts
     )
+    if not many:
+        copies[4].wait()
+        pad()
     logits = dot_nt(h_two_ref[...], w_third_pad_ref[...])
     ids = lax.broadcasted_iota(jnp.int32, (logits.shape[0], wide), 1)
     expo = jnp.where(ids < classes, jnp.exp(logits), 0.0)
@@ -318,6 +442,10 @@
     def left(ref, share):
         return (shares(ref, place * share, share) * factor).astype(bf16)
 
+    if not many:
+        for copy in copies[5:]:
+            copy.wait()
+        set_noise()
     share = g_second_ref.shape[0]
     g_first_ref[...] += dot_tn(left(in_ref, g_first_ref.shape[0]), d_one_ref[...])
     g_second_ref[...] += dot_tn(left(h_one_ref, share), d_two_ref[...])
@@ -326,10 +454,17 @@
 
 def call(kernel, mib, outs, ins, scratch):
     def shape_of(shape, dtype, space):
-        return VMEM(shape, dtype) if space is None else jax.ShapeDtypeStruct(shape, dtype)
+        if space is None or space is HBM:
+            return (space or VMEM)(shape, dtype)
+        return jax.ShapeDtypeStruct(shape, dtype)
 
     def block(space):
         return pl.BlockSpec(memory_space=VMEM if space is None else space)
+
+    def held(value, space):
+        if space is None or space is HBM:
+            return pltpu.with_memory_space_constraint(value, space or VMEM)
+        return value
 
     return pl.pallas_call(
         kernel,
@@ -338,12 +473,7 @@
         out_specs=[block(space) for _, _, space in outs],
         scratch_shapes=scratch,
         compiler_params=params(mib),
-    )(
-        *[
-            pltpu.with_memory_space_constraint(value, VMEM) if space is None else value
-            for value, space in ins
-        ]
-    )
+    )(*[held(value, space) for value, space in ins])
 
 
 def local(
@@ -380,98 +510,132 @@
     few = members <= FEW
     copies = members if few else 1
 
-    def gather(value):
-        if few:
-            return lax.all_to_all(value, axes, split_axis=0, concat_axis=0, tiled=True)
-        return lax.all_gather(value, axes, axis=0, tiled=True)
-
-    label_rows = labels.reshape(1, train)
+    def every(value, *names):
+        for name in names:
+            value = lax.all_gather(value, name, axis=0, tiled=True)
+        return value
+
     start0, out0, side0 = call(
         first_kernel,
         16,
         [
             ((nodes, width), bf16, None),
             ((parts, each, width), bf16, VMEM),
-            ((copies, train + 16, width), bf16, VMEM),
-        ],
-        [(feats.reshape(nodes, width), VMEM), (rows, VMEM), (label_rows, VMEM)],
-        [turn, pick],
+            ((train + 16, width), bf16, VMEM),
+        ],
+        [(feats, HBM), (send_rows, HBM), (labels, HBM)],
+        [
+            VMEM((nodes, width), bf16),
+            VMEM((parts, each), jnp.int32),
+            VMEM((1, train), jnp.int32),
+            turn,
+            pick,
+            DMA((3,)),
+        ],
     )
     table0 = lax.all_to_all(out0, "dom", split_axis=0, concat_axis=0, tiled=True)
     if few:
-        every0 = gather(side0)
+        every0 = every(side0[None], "grp", "dom")
         every_label = every0[:, train, :train].astype(jnp.int32)
     else:
-        every0 = gather(side0[:, :train])
-        every_label = gather(label_rows)
+        every0 = every(side0[None, :train], axes)
+        every_label = every(labels.reshape(1, train), axes)
     own, ghost, part1, flag, own_rest, ghost_rest = call(
         build_kernel,
-        24,
-        [
-            ((nodes, nodes), bf16, None),
+        28,
+        [
+            ((nodes, nodes), bf16, HBM),
             ((nodes, ghosts), bf16, None),
             ((nodes, width), f32, None),
             ((1,), jnp.int32, SMEM),
-            ((nodes, nodes), bf16, pl.ANY),
-            ((nodes, ghosts), bf16, pl.ANY),
-        ],
-        [
-            (tile_block.reshape(tiles), SMEM),
-            (tile_count.reshape(1), SMEM),
-            (tile_src.reshape(tiles, slots), VMEM),
-            (tile_dst.reshape(tiles, slots), VMEM),
+            ((nodes, nodes), bf16, HBM),
+            ((nodes, ghosts), bf16, HBM),
+        ],
+        [
+            (tile_block, SMEM),
+            (tile_count, SMEM),
+            (tile_src, HBM),
+            (tile_dst, HBM),
+            (hop_noise, HBM),
             (start0, None),
-            (hop_noise, None),
-        ],
-        [VMEM((nodes, cols), f32), VMEM((nodes, max(nodes, ghosts)), bf16)],
-    )
-    start1, out1, side1 = call(
+        ],
+        [
+            VMEM((tiles, slots), jnp.int32),
+            VMEM((tiles, slots), jnp.int32),
+            VMEM((nodes, width), bf16),
+            VMEM((tiles * 16, slots), bf16),
+            VMEM((tiles * 16, slots), bf16),
+            VMEM((tiles * 16, slots), bf16),
+            VMEM((nodes, cols), f32),
+            VMEM((nodes, max(nodes, ghosts)), bf16),
+            VMEM((nodes, nodes), bf16),
+            DMA((4,)),
+        ],
+    )
+    start1, out1 = call(
         hop_kernel,
         16,
         [
             ((nodes, width), bf16, None),
             ((parts, each, width), bf16, VMEM),
-            ((copies, train, width), bf16, VMEM),
         ],
         [
             (flag, SMEM),
             (part1, None),
             (ghost, None),
-            (ghost_rest, pl.ANY),
+            (ghost_rest, HBM),
             (table0, None),
             (rows, VMEM),
         ],
         [VMEM((nodes, width), f32), VMEM((nodes, ghosts), bf16), turn, pick],
     )
     table1 = lax.all_to_all(out1, "dom", split_axis=0, concat_axis=0, tiled=True)
-    every1 = gather(side1)
     (part2,) = call(
         own_kernel,
+        16,
+        [((nodes, width), f32, None)],
+        [(flag, SMEM), (own, HBM), (own_rest, HBM), (hop_noise, HBM), (start1, None)],
+        [
+            VMEM((nodes, nodes), bf16),
+            VMEM((nodes, width), bf16),
+            VMEM((nodes, nodes), bf16),
+            DMA((2,)),
+        ],
+    )
+    place = jnp.stack([lax.axis_index("dom"), lax.axis_index("grp")]).astype(jnp.int32)
+    grp = lax.axis_size("grp")
+    pieces1 = []
+    if few:
+        pieces1 = [
+            lax.ppermute(start1[:train], "grp", [((at + shift) % grp, at) for at in range(grp)])
+            for shift in range(1, grp)
+        ]
+    last, side1 = call(
+        train_kernel,
         12,
-        [((nodes, width), f32, None)],
+        [
+            ((copies, train, width), bf16, VMEM),
+            ((parts, (grp if few else 1) * train, width), bf16, VMEM),
+        ],
         [
             (flag, SMEM),
-            (own, None),
-            (own_rest, pl.ANY),
-            (start1, None),
-            (hop_noise, None),
-        ],
-        [VMEM((nodes, nodes), bf16)],
-    )
-    (last,) = call(
-        train_kernel,
-        8,
-        [((copies, train, width), bf16, VMEM)],
-        [
-            (flag, SMEM),
+            (place, SMEM),
             (part2, None),
             (ghost, None),
-            (ghost_rest, pl.ANY),
+            (ghost_rest, HBM),
             (table1, None),
-        ],
+            (start1, None),
+        ]
+        + [(piece, None) for piece in pieces1],
         [VMEM((train, width), f32), VMEM((train, ghosts), bf16)],
     )
-    every2 = gather(last)
+    if few:
+        every2 = lax.all_to_all(last, axes, split_axis=0, concat_axis=0, tiled=True)
+        every1 = lax.all_to_all(side1, "dom", split_axis=0, concat_axis=0, tiled=True)
+        every1 = every1.reshape(members, train, width)
+    else:
+        every2 = every(last, axes)
+        every1 = every(start1[None, :train], axes)
     (hop_feats,) = call(
         last_kernel,
         12,
@@ -480,7 +644,7 @@
             (flag, SMEM),
             (part2, None),
             (ghost, None),
-            (ghost_rest, pl.ANY),
+            (ghost_rest, HBM),
             (table1, None),
             (start1, None),
         ],
@@ -490,7 +654,13 @@
     groups = chunk // train
     wide = (classes + 255) // 256 * 256
     fixed = (w_first, w_second, w_third.T, noise_first, noise_second, noise_third.T)
-    scratch = [
+    scratch = (
+        [VMEM(value.shape, bf16) for value in (every0, every1)]
+        if few
+        else [VMEM((16, 128), bf16)] * 2
+    )
+    scratch += [VMEM(value.shape, value.dtype) for value in fixed]
+    scratch += [
         VMEM((chunk, d_in), bf16),
         VMEM((wide, hid), bf16),
         VMEM((128, 128), jnp.int32),
@@ -501,15 +671,16 @@
         VMEM((chunk, hid), f32),
         VMEM((chunk, hid), bf16),
         VMEM((chunk, hid), bf16),
+        DMA((8,)),
     ]
-    place = lax.axis_index("dom").reshape(1).astype(jnp.int32)
     ins = (every_label, every0, every1, every2)
     if members == groups:
         first, second, third = call(
             functools.partial(classify_kernel, False),
-            36,
+            44,
             [(value.shape, f32, VMEM) for value in fixed[3:]],
-            [(place, SMEM)] + [(value, None) for value in ins + fixed],
+            [(place, SMEM), (every_label, VMEM), (every0, HBM), (every1, HBM), (every2, None)]
+            + [(value, HBM) for value in fixed],
             scratch,
         )
     else:
@@ -528,7 +699,7 @@
             out_shape=[jax.ShapeDtypeStruct(value.shape, f32) for value in fixed[3:]],
             in_specs=[pl.BlockSpec(memory_space=SMEM)]
             + [piece(value) for value in ins]
-            + [whole(value) for value in fixed],
+            + [pl.BlockSpec(memory_space=HBM) for value in fixed],
             out_specs=[whole(value) for value in fixed[3:]],
             scratch_shapes=scratch,
             compiler_params=params(56),

time: 123 us -> 109 us (0.89)
  the two profiles are of different devices: /device:TPU:1 before, /device:TPU:0 now
where the time goes in v3:
time: 109 us
  blocking collectives  44.9 us (41%)
  Pallas kernels  43.3 us (40%)
  starting transfers between devices  16 us (15%)
  waiting for transfers between devices  1.77 us (2%)
  local copies, waits for them, and re-layouts  1.57 us (1%)
  between operations  1.56 us (1%)
    pallas_call x7, Pallas kernels, call(): pl.pallas_call(kernel, out_shape=[shape_of(*out) for out in outs], in_spe...  43.3 us
    all_gather x2, blocking collectives, every(): value = lax.all_gather(value, name, axis=0, tiled=True)  31.1 us
    all_to_all x1, blocking collectives, local(): lax.all_to_all(side1, 'dom', split_axis=0, concat_axis=0, tiled=True)  13.8 us
    all_to_all x1, starting transfers between devices, local(): lax.all_to_all(out0, 'dom', split_axis=0, concat_axis=0, tiled=True)  5.18 us
    ppermute x3, starting transfers between devices, local(): lax.ppermute(start1[:train], 'grp', [((at + shift) % grp, at) for at in r...  4.85 us
    all_to_all x1, starting transfers between devices, local(): lax.all_to_all(out1, 'dom', split_axis=0, concat_axis=0, tiled=True)  3.37 us
    all_to_all x1, starting transfers between devices, local(): every2 = lax.all_to_all(last, axes, split_axis=0, concat_axis=0, tiled=True)  2.6 us
  transfers between devices with their start and end apart: 6, of which 2 were waited for; matrix products, arithmetic and copies ran while one was open for 0% of the time, Pallas kernels for 18%

profile of v3, /device:TPU:0, one launch (start us, length us, event | category | flops | bytes accessed | tf_op | source)
XLA Modules:
  0.0 109.1 jit_solution(5161818950948727466)
XLA Ops:
  0.6 0.0 copy-start
  0.6 2.4 %shard_map.165 = (bf16[1024,256]{1,0:T(8,128)(2,1)S(1)}, bf16[8,32,256]{2,1,0:T(8,128)(2,1)}, bf16[48,256]{1,0:T(8,128)(2,1)S(1)}) custom-call(bf16[1,1,1024,256]{3,2,1,0:T(8,128)(2,1)} %feats_hbm.1, s32[1,1,8,32]{3,2,1,0:T(8,128)} %rows_hbm.1, s32[1,1,32]{2,1,0:T(1,128)} %labels_hbm.1), custom_call_target="tpu_custom_call" | custom-call | tf_op jit(solution)/shard_map/pallas_call | solution.py:469
  3.1 5.2 %all-to-all-start = ((bf16[8,32,256]{2,1,0:T(8,128)(2,1)}), bf16[8,32,256]{2,1,0:T(8,128)(2,1)S(1)}, u32[]{:S(2)}, u32[]{:S(2)}) async-start(bf16[8,32,256]{2,1,0:T(8,128)(2,1)} %get-tuple-element.27), calls=%async_computation | async-start | bytes 262144 | tf_op jit(solution)/shard_map/all_to_all | solution.py:536
  8.9 0.0 copy-start.1
  8.9 0.6 copy-done.1
  9.6 14.5 %shard_map.166 = (bf16[1024,1024]{1,0:T(8,128)(2,1)}, bf16[1024,256]{1,0:T(8,128)(2,1)S(1)}, f32[1024,256]{1,0:T(8,128)S(1)}, s32[1]{0:T(128)}, bf16[1024,1024]{1,0:T(8,128)(2,1)}, /*index=5*/bf16[1024,256]{1,0:T(8,128)(2,1)}) custom-call(s32[1,1,64]{2,1,0:T(1,128)S(1)} %copy-done.1, s32[1,1]{1,0:T(1,128)S(6)} %copy.23.count_ref, s32[1,1,64,256]{3,2,1,0:T(8,128)} %src_hbm.1, ...), custom_call_target="tpu_custom_call" | custom-call | tf_op jit(solution)/shard_map/pallas_call | solution.py:469
  24.1 0.0 all-to-all-done.table_ref
  24.1 0.0 copy-done
  24.1 2.3 %shard_map.167 = (bf16[1024,256]{1,0:T(8,128)(2,1)S(1)}, bf16[8,32,256]{2,1,0:T(8,128)(2,1)}) custom-call(s32[1]{0:T(128)} %get-tuple-element.21.flag_ref, f32[1024,256]{1,0:T(8,128)S(1)} %get-tuple-element.24.part_ref, bf16[1024,256]{1,0:T(8,128)(2,1)S(1)} %get-tuple-element.25.ghost_ref, bf16[1024,256]{1,0:T(8,128)(2,1)} %get-tuple-element.26.rest_hbm, ...), custom_call_target="tpu_custom_call" | custom-call | tf_op jit(solution)/shard_map/pallas_call | solution.py:469
  26.4 3.4 %all-to-all-start.1 = ((bf16[8,32,256]{2,1,0:T(8,128)(2,1)}), bf16[8,32,256]{2,1,0:T(8,128)(2,1)S(1)}, u32[]{:S(2)}, u32[]{:S(2)}) async-start(bf16[8,32,256]{2,1,0:T(8,128)(2,1)} %get-tuple-element.29), calls=%async_computation.1 | async-start | bytes 262144 | tf_op jit(solution)/shard_map/all_to_all | solution.py:592
  29.8 4.2 %collective-permute-start = (bf16[32,256]{1,0:T(8,128)(2,1)S(1)}, bf16[32,256]{1,0:T(8,128)(2,1)S(1)}, u32[]{:S(2)}, u32[]{:S(2)}) collective-permute-start(bf16[32,256]{1,0:T(8,128)(2,1)S(1)} %slice.9), channel_id=1, source_target_pairs={{1,0},{2,1},{3,2},{0,3},{5,4},{6,5},{7,6},{4,7},{9,8},{10,9},{11,1... | collective-permute-start | bytes 49160 | tf_op jit(solution)/shard_map/ppermute | solution.py:610
  34.0 0.0 collective-permute-start.1
  34.0 0.6 collective-permute-start.2
  34.7 0.1 pad_add_fusion.place_ref
  34.8 3.0 %shard_map.168.part_ref = f32[1024,256]{1,0:T(8,128)S(1)} custom-call(s32[1]{0:T(128)} %get-tuple-element.21.flag_ref, bf16[1024,1024]{1,0:T(8,128)(2,1)} %get-tuple-element.22.own_hbm, bf16[1024,1024]{1,0:T(8,128)(2,1)} %get-tuple-element.23.rest_hbm, bf16[2,1,1,1024,256]{4,3,2,1,0:T(8,128)(2,1)} %noise_hbm.3, bf16[1024,256]{1,0:T(8,128)(2,1)S(1)} %get-tuple-element.28.start_ref), custom_call_target="tpu_custom_call" | custom-call | tf_op jit(solution)/shard_map/pallas_call | solution.py:469
  37.8 0.0 collective-permute-done.refs_0_
  37.8 0.9 collective-permute-done.1.refs_1_
  38.7 0.9 collective-permute-done.2.refs_2_
  39.6 0.0 all-to-all-done.1.table_ref
  39.6 2.3 %shard_map.170 = (bf16[32,32,256]{2,1,0:T(8,128)(2,1)}, bf16[8,128,256]{2,1,0:T(8,128)(2,1)S(1)}) custom-call(s32[1]{0:T(128)} %get-tuple-element.21.flag_ref, s32[2]{0:T(128)S(1)} %pad_add_fusion.place_ref, f32[1024,256]{1,0:T(8,128)S(1)} %shard_map.168.part_ref, bf16[1024,256]{1,0:T(8,128)(2,1)S(1)} %get-tuple-element.25.ghost_ref, ...), custom_call_target="tpu_custom_call" | custom-call | tf_op jit(solution)/shard_map/pallas_call | solution.py:469
  41.9 13.8 %all_to_all.20 = bf16[8,128,256]{2,1,0:T(8,128)(2,1)} all-to-all(bf16[8,128,256]{2,1,0:T(8,128)(2,1)S(1)} %get-tuple-element.31), channel_id=1, replica_groups=mesh['dom'=8,'grp'=4] {'dom'}, dimensions={0} | all-to-all | bytes 1048576 | tf_op jit(solution)/shard_map/all_to_all | solution.py:634
  55.7 2.6 %all-to-all-start.3 = ((bf16[32,32,256]{2,1,0:T(8,128)(2,1)}), bf16[32,32,256]{2,1,0:T(8,128)(2,1)S(1)}, u32[]{:S(2)}, u32[]{:S(2)}) async-start(bf16[32,32,256]{2,1,0:T(8,128)(2,1)} %get-tuple-element.32), calls=%async_computation.3 | async-start | bytes 1048576 | tf_op jit(solution)/shard_map/all_to_all | solution.py:633
  58.3 20.7 %all-gather = bf16[192,256]{1,0:T(8,128)(2,1)S(1)} all-gather(bf16[48,256]{1,0:T(8,128)(2,1)S(1)} %get-tuple-element.30), channel_id=2, replica_groups=mesh['dom'=8,'grp'=4] {'grp'}, dimensions={0}, use_global_device_ids=true | all-gather | bytes 122880 | tf_op jit(solution)/shard_map/all_gather | solution.py:515
  79.0 10.4 %all_gather.7.zero_in = bf16[32,48,256]{2,1,0:T(8,128)(2,1)S(1)} all-gather(bf16[4,48,256]{2,1,0:T(8,128)(2,1)S(1)} %bitcast.15), channel_id=1, replica_groups=mesh['dom'=8,'grp'=4] {'dom'}, dimensions={0}, use_global_device_ids=true | all-gather | bytes 884736 | tf_op jit(solution)/shard_map/all_gather | solution.py:515
  89.4 0.0 copy-start.2
  89.4 0.9 copy-done.2
  90.3 2.3 %shard_map.169 = bf16[2,1,1,1024,256]{4,3,2,1,0:T(8,128)(2,1)} custom-call(s32[1]{0:T(128)} %get-tuple-element.21.flag_ref, f32[1024,256]{1,0:T(8,128)S(1)} %shard_map.168.part_ref, bf16[1024,256]{1,0:T(8,128)(2,1)S(1)} %get-tuple-element.25.ghost_ref, bf16[1024,256]{1,0:T(8,128)(2,1)} %get-tuple-element.26.rest_hbm, ...), custom_call_target="tpu_custom_call" | custom-call | tf_op jit(solution)/shard_map/pallas_call | solution.py:469
  92.6 0.0 all-to-all-done.3.two_ref
  92.6 16.3 %shard_map.171 = (f32[96,1024]{1,0:T(8,128)}, f32[128,1024]{1,0:T(8,128)}, f32[172,128]{1,0:T(8,128)}) custom-call(s32[2]{0:T(128)S(1)} %pad_add_fusion.place_ref, s32[32,32]{1,0:T(8,128)S(1)} %fusion.label_ref, bf16[32,48,256]{2,1,0:T(8,128)(2,1)} %copy-done.2, bf16[32,32,256]{2,1,0:T(8,128)(2,1)} %bitcast.14, ...), custom_call_target="tpu_custom_call" | custom-call | tf_op jit(solution)/shard_map/pallas_call | solution.py:469
  (3 shorter events, 0.0 us)
Async XLA Ops:
  0.6 23.5 %copy-start = (s32[1,1,8,32]{3,2,1,0:T(8,128)S(1)}, s32[1,1,8,32]{3,2,1,0:T(8,128)}, u32[]{:S(2)}) copy-start(s32[1,1,8,32]{3,2,1,0:T(8,128)} %rows_hbm.1) | copy-start | bytes 3076
  3.1 21.0 %all-to-all-start = ((bf16[8,32,256]{2,1,0:T(8,128)(2,1)}), bf16[8,32,256]{2,1,0:T(8,128)(2,1)S(1)}, u32[]{:S(2)}, u32[]{:S(2)}) async-start(bf16[8,32,256]{2,1,0:T(8,128)(2,1)} %get-tuple-element.27), calls=%async_computation | async-start | bytes 262144 | tf_op jit(solution)/shard_map/all_to_all | solution.py:536
  8.9 0.7 copy-start.1
  26.4 13.2 %all-to-all-start.1 = ((bf16[8,32,256]{2,1,0:T(8,128)(2,1)}), bf16[8,32,256]{2,1,0:T(8,128)(2,1)S(1)}, u32[]{:S(2)}, u32[]{:S(2)}) async-start(bf16[8,32,256]{2,1,0:T(8,128)(2,1)} %get-tuple-element.29), calls=%async_computation.1 | async-start | bytes 262144 | tf_op jit(solution)/shard_map/all_to_all | solution.py:592
  29.8 8.0 %collective-permute-start = (bf16[32,256]{1,0:T(8,128)(2,1)S(1)}, bf16[32,256]{1,0:T(8,128)(2,1)S(1)}, u32[]{:S(2)}, u32[]{:S(2)}) collective-permute-start(bf16[32,256]{1,0:T(8,128)(2,1)S(1)} %slice.9), channel_id=1, source_target_pairs={{1,0},{2,1},{3,2},{0,3},{5,4},{6,5},{7,6},{4,7},{9,8},{10,9},{11,1... | collective-permute-start | bytes 49160 | tf_op jit(solution)/shard_map/ppermute | solution.py:610
  34.0 4.6 %collective-permute-start.1 = (bf16[32,256]{1,0:T(8,128)(2,1)S(1)}, bf16[32,256]{1,0:T(8,128)(2,1)S(1)}, u32[]{:S(2)}, u32[]{:S(2)}) collective-permute-start(bf16[32,256]{1,0:T(8,128)(2,1)S(1)} %slice.9), channel_id=1, source_target_pairs={{2,0},{3,1},{0,2},{1,3},{6,4},{7,5},{4,6},{5,7},{10,8},{11,9},{8,1... | collective-permute-start | bytes 49160 | tf_op jit(solution)/shard_map/ppermute | solution.py:610
  34.0 5.5 %collective-permute-start.2 = (bf16[32,256]{1,0:T(8,128)(2,1)S(1)}, bf16[32,256]{1,0:T(8,128)(2,1)S(1)}, u32[]{:S(2)}, u32[]{:S(2)}) collective-permute-start(bf16[32,256]{1,0:T(8,128)(2,1)S(1)} %slice.9), channel_id=1, source_target_pairs={{3,0},{0,1},{1,2},{2,3},{7,4},{4,5},{5,6},{6,7},{11,8},{8,9},{9,10... | collective-permute-start | bytes 49160 | tf_op jit(solution)/shard_map/ppermute | solution.py:610
  55.7 37.0 %all-to-all-start.3 = ((bf16[32,32,256]{2,1,0:T(8,128)(2,1)}), bf16[32,32,256]{2,1,0:T(8,128)(2,1)S(1)}, u32[]{:S(2)}, u32[]{:S(2)}) async-start(bf16[32,32,256]{2,1,0:T(8,128)(2,1)} %get-tuple-element.32), calls=%async_computation.3 | async-start | bytes 1048576 | tf_op jit(solution)/shard_map/all_to_all | solution.py:633
  89.4 0.9 copy-start.2

commit v4 on v3

--- a/solution.py
+++ b/solution.py
@@ -21,7 +21,7 @@
 DMA = pltpu.SemaphoreType.DMA
 
 
-FEW = 64
+FEW = 32
 
 
 def params(mib):
@@ -73,28 +73,22 @@
 def first_kernel(
     feats_hbm,
     rows_hbm,
-    labels_hbm,
     start_ref,
     out_ref,
-    side_ref,
     feats_ref,
     rows_ref,
-    labels_ref,
     turn_ref,
     pick_ref,
     sems,
 ):
-    sources = (feats_hbm.at[0, 0], rows_hbm.at[0, 0], labels_hbm.at[0])
-    copies = fetch(zip(sources, (feats_ref, rows_ref, labels_ref)), sems)
+    copies = fetch(
+        ((feats_hbm.at[0, 0], feats_ref), (rows_hbm.at[0, 0], rows_ref)), sems
+    )
     for copy in copies:
         copy.wait()
     start = normalize(feats_ref[...].astype(f32))
     start_ref[...] = start
     send(start, rows_ref, out_ref, turn_ref, pick_ref)
-    train = labels_ref.shape[1]
-    side_ref[:train, :] = start[:train]
-    turn_ref[:1, :train] = labels_ref[...]
-    side_ref[train:, :128] = turn_ref[:16, :].astype(f32).astype(bf16)
 
 
 def build_kernel(
@@ -133,7 +127,8 @@
     pieces = cols // LOW
     tiles, slots = src_ref.shape
     count = count_ref[0, 0]
-    sums_ref[...] = jnp.zeros_like(sums_ref)
+    own_ref[...] = jnp.zeros_like(own_ref)
+    ghost_ref[...] = jnp.zeros_like(ghost_ref)
     for copy in copies:
         copy.wait()
 
@@ -144,50 +139,62 @@
     src = src_ref[...]
     dst = dst_ref[...]
     tile_ids = lax.broadcasted_iota(jnp.int32, (tiles, slots), 0)
-    low_ref[...] = sixteen(src % LOW)
     high_ref[...] = sixteen(src // LOW)
     spot_ref[...] = sixteen(jnp.where((dst < BLOCK) & (tile_ids < count), dst, -1))
-    ids = lax.broadcasted_iota(jnp.int32, (LOW, slots), 0).astype(f32).astype(bf16)
+    low = (src % LOW).astype(f32).T
+    for tile in range(tiles):
+        low_ref[tile] = jnp.broadcast_to(low[:, tile : tile + 1], (slots, 128)).astype(bf16)
+    ids = lax.broadcasted_iota(jnp.int32, (BLOCK, slots), 0).astype(f32).astype(bf16)
+    lanes = lax.broadcasted_iota(jnp.int32, (slots, 128), 1).astype(f32)
+    lanes = [(lanes + first).astype(bf16) for first in range(0, LOW, 128)]
     one = jnp.ones((), bf16)
     zero = jnp.zeros((), bf16)
 
-    def hot(values, length):
-        tall = jnp.concatenate([values] * (length // 16), 0)
-        return jnp.where(ids[:length] == tall, one, zero)
-
-    def turn(step, carry):
+    def turn(add, step, carry):
         for inner in range(GROUP):
             tile = step * GROUP + inner
             rows = pl.ds(pl.multiple_of(tile * 16, 16), 16)
-            low, high, spot = low_ref[rows, :], high_ref[rows, :], spot_ref[rows, :]
-            spots = [
-                hot(jnp.where(high == piece, spot, -one), BLOCK) for piece in range(pieces)
-            ]
-            out = dot_nt(jnp.concatenate(spots, 0), hot(low, LOW))
+            high, spot = high_ref[rows, :], spot_ref[rows, :]
+            spots = []
+            for piece in range(pieces):
+                wanted = jnp.where(high == piece, spot, -one)
+                tall = jnp.concatenate([wanted] * (BLOCK // 16), 0)
+                spots.append(jnp.where(ids == tall, one, zero))
+            low = low_ref[tile]
+            low_hot = jnp.concatenate([jnp.where(low == ids, one, zero) for ids in lanes], 1)
+            out = dot(jnp.concatenate(spots, 0), low_hot)
             base = pl.multiple_of(blocks_ref[0, 0, tile] * BLOCK, BLOCK)
             for piece in range(pieces):
-                sums_ref[pl.ds(base, BLOCK), piece * LOW : (piece + 1) * LOW] += out[
-                    piece * BLOCK : (piece + 1) * BLOCK
-                ]
+                add(pl.ds(base, BLOCK), piece * LOW, out[piece * BLOCK : (piece + 1) * BLOCK])
         return carry
 
-    lax.fori_loop(0, (count + GROUP - 1) // GROUP, turn, 0)
-    top = jnp.zeros((BLOCK, LOW), f32)
+    def add_short(rows, at, values):
+        ref, at = (own_ref, at) if at < nodes else (ghost_ref, at - nodes)
+        ref[rows, at : at + LOW] += values.astype(bf16)
+
+    def add_long(rows, at, values):
+        sums_ref[rows, at : at + LOW] += values
+
+    steps = (count + GROUP - 1) // GROUP
+    lax.fori_loop(0, steps, functools.partial(turn, add_short), 0)
+    top = ghost_ref[:BLOCK, :LOW]
     for first in range(0, nodes, BLOCK):
-        for piece in range(pieces):
-            values = sums_ref[first : first + BLOCK, piece * LOW : (piece + 1) * LOW]
-            top = jnp.maximum(top, values)
-            at = piece * LOW
-            if at < nodes:
-                own_ref[first : first + BLOCK, at : at + LOW] = values.astype(bf16)
-            else:
-                at -= nodes
-                ghost_ref[first : first + BLOCK, at : at + LOW] = values.astype(bf16)
+        for ref in (own_ref, ghost_ref):
+            for at in range(0, ref.shape[1], LOW):
+                top = jnp.maximum(top, ref[first : first + BLOCK, at : at + LOW])
+    big = jnp.max(top.astype(f32)) >= 256.0
+    flag_ref[0] = big.astype(jnp.int32)
+
+    @pl.when(big)
+    def _():
+        sums_ref[...] = jnp.zeros_like(sums_ref)
+        lax.fori_loop(0, steps, functools.partial(turn, add_long), 0)
+        own_ref[...] = sums_ref[:, :nodes].astype(bf16)
+        ghost_ref[...] = sums_ref[:, nodes:].astype(bf16)
+
     own_copy = pltpu.make_async_copy(own_ref, own_hbm, sems.at[3])
     own_copy.start()
     part_ref[...] = dot(own_ref[...], start_ref[...]) + noise_ref[...].astype(f32)
-    big = jnp.max(top) > 256.0
-    flag_ref[0] = big.astype(jnp.int32)
 
     @pl.when(big)
     def _():
@@ -218,8 +225,11 @@
     rest_hbm,
     table_ref,
     rows_ref,
+    old_ref,
+    labels_ref,
     start_ref,
     out_ref,
+    side_ref,
     sums_ref,
     rest_ref,
     turn_ref,
@@ -231,6 +241,11 @@
     start = normalize(sums_ref[...])
     start_ref[...] = start
     send(start, rows_ref, out_ref, turn_ref, pick_ref)
+    train = labels_ref.shape[1]
+    side_ref[:train, :] = old_ref[:train, :]
+    side_ref[train : 2 * train, :] = start[:train]
+    turn_ref[:1, :train] = labels_ref[...]
+    side_ref[2 * train :, :128] = turn_ref[:16, :].astype(f32).astype(bf16)
 
 
 def own_kernel(
@@ -245,8 +260,21 @@
 
 
 def train_kernel(
+    flag_ref, part_ref, ghost_ref, rest_hbm, table_ref, out_ref, token_ref, sums_ref, rest_ref
+):
+    train, width = sums_ref.shape
+    table = table_ref[...].reshape(-1, width)
+    aggregate(
+        flag_ref, part_ref[:train], ghost_ref[:train], rest_hbm, table, sums_ref, rest_ref
+    )
+    spread(normalize(sums_ref[...]), out_ref)
+    token_ref[...] = sums_ref[:8, :128]
+
+
+def last_kernel(
     flag_ref,
     place_ref,
+    token_ref,
     part_ref,
     ghost_ref,
     rest_hbm,
@@ -254,29 +282,20 @@
     start_ref,
     *refs,
 ):
-    *piece_refs, out_ref, side_ref, sums_ref, rest_ref = refs
-    train, width = sums_ref.shape
-    table = table_ref[...].reshape(-1, width)
-    aggregate(
-        flag_ref, part_ref[:train], ghost_ref[:train], rest_hbm, table, sums_ref, rest_ref
-    )
-    spread(normalize(sums_ref[...]), out_ref)
-    group, groups = place_ref[1], side_ref.shape[1] // train
-    for shift in range(len(piece_refs) + 1):
-        rows = piece_refs[shift - 1][...] if shift else start_ref[:train, :]
-        at = pl.multiple_of(lax.rem(group + shift, groups) * train, train)
-        side_ref[:, pl.ds(at, train), :] = jnp.broadcast_to(
-            rows[None], (side_ref.shape[0], train, width)
-        )
-
-
-def last_kernel(
-    flag_ref, part_ref, ghost_ref, rest_hbm, table_ref, start_ref, out_ref, sums_ref, rest_ref
-):
+    *piece_refs, out_ref, side_ref, sums_ref, rest_ref, turn_ref = refs
     table = table_ref[...].reshape(-1, out_ref.shape[-1])
     aggregate(flag_ref, part_ref[...], ghost_ref[...], rest_hbm, table, sums_ref, rest_ref)
     out_ref[0, 0, 0] = start_ref[...]
     out_ref[1, 0, 0] = normalize(sums_ref[...])
+    length = piece_refs[0].shape[0] - 16
+    groups = len(piece_refs)
+    if groups > 1:
+        for shift, ref in enumerate(piece_refs):
+            group = lax.rem(place_ref[1] + shift, groups)
+            at = pl.multiple_of(group * length, length)
+            side_ref[pl.ds(at, length), :] = ref[:length, :]
+            turn_ref[pl.ds(group, 1), :] = ref[length:, :128].astype(f32)[:1]
+        side_ref[groups * length :, :128] = turn_ref[:16, :].astype(bf16)
 
 
 def shares(ref, first, share):
@@ -300,9 +319,10 @@
     many,
     place_ref,
     label_ref,
-    zero_in,
-    one_in,
+    zero_ref,
+    one_ref,
     two_ref,
+    side_refs,
     w_first_hbm,
     w_second_hbm,
     w_third_hbm,
@@ -312,8 +332,6 @@
     g_first_ref,
     g_second_ref,
     g_third_ref,
-    zero_own,
-    one_own,
     w_first_ref,
     w_second_ref,
     w_third_ref,
@@ -336,7 +354,7 @@
     hid = w_second_ref.shape[0]
     width = two_ref.shape[2]
     wide = w_third_pad_ref.shape[0]
-    groups, train = label_ref.shape
+    train = two_ref.shape[1]
     scale = noise_mult * clip_bound
     place = place_ref[0]
     pairs = (
@@ -357,6 +375,11 @@
         w_third_pad_ref[...] = jnp.zeros_like(w_third_pad_ref)
         w_third_pad_ref[:classes, :] = w_third_ref[...]
 
+    def column(row, turned, lane):
+        column_ref[row : row + train, :] = jnp.broadcast_to(
+            turned[:train, lane : lane + 1], (train, 128)
+        ).astype(jnp.int32)
+
     if many:
 
         @pl.when(pl.program_id(0) == 0)
@@ -366,22 +389,36 @@
             set_noise()
             pad()
 
-        zero_ref, one_ref = zero_in, one_in
+        groups = label_ref.shape[0]
+        turn_ref[:groups, :train] = label_ref[...].astype(f32)
+        turned = turn_ref[...].T
+        for group in range(groups):
+            column(group * train, turned, group)
+        for hop, ref in enumerate((zero_ref, one_ref)):
+            in_ref[:, hop * width : (hop + 1) * width] = ref[...].reshape(-1, width)
     else:
-        zero_ref, one_ref = zero_own, one_own
-        copies = fetch(((zero_in, zero_own), (one_in, one_own)) + pairs, sems)
-
-    turn_ref[:groups, :train] = label_ref[...]
-    turned = turn_ref[...].T
-    for group in range(groups):
-        column_ref[group * train : (group + 1) * train, :] = jnp.broadcast_to(
-            turned[:train, group : group + 1], (train, 128)
-        )
+        copies = fetch(pairs[:1], sems)
+        parts = len(side_refs)
+        groups = two_ref.shape[0] // parts
+        rows = groups * train
+        for shift, ref in enumerate(side_refs):
+            part = lax.rem(place - shift + parts, parts)
+            at = pl.multiple_of(part * rows, rows)
+            for group in range(groups):
+                for hop in range(2):
+                    first = (2 * group + hop) * train
+                    in_ref[pl.ds(at + group * train, train), hop * width : (hop + 1) * width] = ref[
+                        first : first + train, :
+                    ]
+            turn_ref[pl.ds(pl.multiple_of(part * 16, 16), 16), :] = ref[2 * rows :, :128].astype(f32)
+        turned = turn_ref[...].T
+        for part in range(parts):
+            for group in range(groups):
+                column((part * groups + group) * train, turned, part * 16 + group)
+    in_ref[:, 2 * width :] = two_ref[...].reshape(-1, width)
     if not many:
-        for copy in copies[:3]:
-            copy.wait()
-    for hop, ref in enumerate((zero_ref, one_ref, two_ref)):
-        in_ref[:, hop * width : (hop + 1) * width] = ref[:, :train, :].reshape(-1, width)
+        copies[0].wait()
+        copies = fetch(pairs[1:], sems)
 
     def activate(values, h_ref, slope_ref, cols):
         sigma = 0.5 + 0.5 * jnp.tanh(0.5 * values)
@@ -399,13 +436,13 @@
         for cut in cuts
     )
     if not many:
-        copies[3].wait()
+        copies[0].wait()
     sq_two = sum(
         activate(dot(h_one_ref[...], w_second_ref[:, cut]), h_two_ref, slope_two_ref, cut)
         for cut in cuts
     )
     if not many:
-        copies[4].wait()
+        copies[1].wait()
         pad()
     logits = dot_nt(h_two_ref[...], w_third_pad_ref[...])
     ids = lax.broadcasted_iota(jnp.int32, (logits.shape[0], wide), 1)
@@ -443,7 +480,7 @@
         return (shares(ref, place * share, share) * factor).astype(bf16)
 
     if not many:
-        for copy in copies[5:]:
+        for copy in copies[2:]:
             copy.wait()
         set_noise()
     share = g_second_ref.shape[0]
@@ -507,7 +544,7 @@
     pick = VMEM((ghosts, nodes), bf16)
     axes = ("dom", "grp")
     members = lax.axis_size(axes)
-    few = members <= FEW
+    few = members <= FEW and parts <= 8
     copies = members if few else 1
 
     def every(value, *names):
@@ -515,31 +552,14 @@
             value = lax.all_gather(value, name, axis=0, tiled=True)
         return value
 
-    start0, out0, side0 = call(
+    start0, out0 = call(
         first_kernel,
         16,
-        [
-            ((nodes, width), bf16, None),
-            ((parts, each, width), bf16, VMEM),
-            ((train + 16, width), bf16, VMEM),
-        ],
-        [(feats, HBM), (send_rows, HBM), (labels, HBM)],
-        [
-            VMEM((nodes, width), bf16),
-            VMEM((parts, each), jnp.int32),
-            VMEM((1, train), jnp.int32),
-            turn,
-            pick,
-            DMA((3,)),
-        ],
+        [((nodes, width), bf16, None), ((parts, each, width), bf16, None)],
+        [(feats, HBM), (send_rows, HBM)],
+        [VMEM((nodes, width), bf16), VMEM((parts, each), jnp.int32), turn, pick, DMA((2,))],
     )
     table0 = lax.all_to_all(out0, "dom", split_axis=0, concat_axis=0, tiled=True)
-    if few:
-        every0 = every(side0[None], "grp", "dom")
-        every_label = every0[:, train, :train].astype(jnp.int32)
-    else:
-        every0 = every(side0[None, :train], axes)
-        every_label = every(labels.reshape(1, train), axes)
     own, ghost, part1, flag, own_rest, ghost_rest = call(
         build_kernel,
         28,
@@ -563,7 +583,7 @@
             VMEM((tiles, slots), jnp.int32),
             VMEM((tiles, slots), jnp.int32),
             VMEM((nodes, width), bf16),
-            VMEM((tiles * 16, slots), bf16),
+            VMEM((tiles, slots, 128), bf16),
             VMEM((tiles * 16, slots), bf16),
             VMEM((tiles * 16, slots), bf16),
             VMEM((nodes, cols), f32),
@@ -572,12 +592,13 @@
             DMA((4,)),
         ],
     )
-    start1, out1 = call(
+    start1, out1, side = call(
         hop_kernel,
         16,
         [
             ((nodes, width), bf16, None),
-            ((parts, each, width), bf16, VMEM),
+            ((parts, each, width), bf16, None),
+            ((2 * train + 16, width), bf16, None),
         ],
         [
             (flag, SMEM),
@@ -586,6 +607,8 @@
             (ghost_rest, HBM),
             (table0, None),
             (rows, VMEM),
+            (start0, None),
+            (labels.reshape(1, train), VMEM),
         ],
         [VMEM((nodes, width), f32), VMEM((nodes, ghosts), bf16), turn, pick],
     )
@@ -604,66 +627,58 @@
     )
     place = jnp.stack([lax.axis_index("dom"), lax.axis_index("grp")]).astype(jnp.int32)
     grp = lax.axis_size("grp")
-    pieces1 = []
-    if few:
-        pieces1 = [
-            lax.ppermute(start1[:train], "grp", [((at + shift) % grp, at) for at in range(grp)])
-            for shift in range(1, grp)
+
+    def shifted(value, name, size, step):
+        return [
+            lax.ppermute(value, name, [((at + step * shift) % size, at) for at in range(size)])
+            for shift in range(1, size)
         ]
-    last, side1 = call(
+
+    sides = [side] + (shifted(side, "grp", grp, 1) if few else [])
+    last, token = call(
         train_kernel,
         12,
+        [((copies, train, width), bf16, None), ((8, 128), f32, None)],
+        [(flag, SMEM), (part2, None), (ghost, None), (ghost_rest, HBM), (table1, None)],
+        [VMEM((train, width), f32), VMEM((train, ghosts), bf16)],
+    )
+    if few:
+        every2 = lax.all_to_all(last, axes, split_axis=0, concat_axis=0, tiled=True)
+    else:
+        every0, every1, every2 = (
+            every(value, axes) for value in (start0[None, :train], start1[None, :train], last)
+        )
+        every_label = every(labels.reshape(1, train), axes)
+    hop_feats, side = call(
+        last_kernel,
+        12,
         [
-            ((copies, train, width), bf16, VMEM),
-            ((parts, (grp if few else 1) * train, width), bf16, VMEM),
+            ((2, 1, 1, nodes, width), bf16, VMEM),
+            ((len(sides) * 2 * train + 16, width), bf16, None),
         ],
         [
             (flag, SMEM),
             (place, SMEM),
+            (token, None),
             (part2, None),
             (ghost, None),
             (ghost_rest, HBM),
             (table1, None),
             (start1, None),
         ]
-        + [(piece, None) for piece in pieces1],
-        [VMEM((train, width), f32), VMEM((train, ghosts), bf16)],
-    )
-    if few:
-        every2 = lax.all_to_all(last, axes, split_axis=0, concat_axis=0, tiled=True)
-        every1 = lax.all_to_all(side1, "dom", split_axis=0, concat_axis=0, tiled=True)
-        every1 = every1.reshape(members, train, width)
-    else:
-        every2 = every(last, axes)
-        every1 = every(start1[None, :train], axes)
-    (hop_feats,) = call(
-        last_kernel,
-        12,
-        [((2, 1, 1, nodes, width), bf16, VMEM)],
-        [
-            (flag, SMEM),
-            (part2, None),
-            (ghost, None),
-            (ghost_rest, HBM),
-            (table1, None),
-            (start1, None),
-        ],
-        [VMEM((nodes, width), f32), VMEM((nodes, ghosts), bf16)],
-    )
+        + [(value, None) for value in sides],
+        [VMEM((nodes, width), f32), VMEM((nodes, ghosts), bf16), VMEM((128, 128), f32)],
+    )
+    sides = [side] + (shifted(side, "dom", parts, -1) if few else [])
     chunk = train * min(members, 32)
     groups = chunk // train
     wide = (classes + 255) // 256 * 256
     fixed = (w_first, w_second, w_third.T, noise_first, noise_second, noise_third.T)
-    scratch = (
-        [VMEM(value.shape, bf16) for value in (every0, every1)]
-        if few
-        else [VMEM((16, 128), bf16)] * 2
-    )
-    scratch += [VMEM(value.shape, value.dtype) for value in fixed]
+    scratch = [VMEM(value.shape, value.dtype) for value in fixed]
     scratch += [
         VMEM((chunk, d_in), bf16),
         VMEM((wide, hid), bf16),
-        VMEM((128, 128), jnp.int32),
+        VMEM((128, 128), f32),
         VMEM((chunk, 128), jnp.int32),
         VMEM((chunk, hid), bf16),
         VMEM((chunk, hid), bf16),
@@ -671,20 +686,33 @@
         VMEM((chunk, hid), f32),
         VMEM((chunk, hid), bf16),
         VMEM((chunk, hid), bf16),
-        DMA((8,)),
+        DMA((6,)),
     ]
-    ins = (every_label, every0, every1, every2)
-    if members == groups:
+    if few:
+
+        def classify(place_ref, *refs):
+            sides_in, rest = refs[:parts], refs[parts:]
+            classify_kernel(False, place_ref, None, None, None, rest[0], sides_in, *rest[1:])
+
         first, second, third = call(
-            functools.partial(classify_kernel, False),
+            classify,
             44,
             [(value.shape, f32, VMEM) for value in fixed[3:]],
-            [(place, SMEM), (every_label, VMEM), (every0, HBM), (every1, HBM), (every2, None)]
+            [(place, SMEM)]
+            + [(value, None) for value in sides]
+            + [(every2, None)]
             + [(value, HBM) for value in fixed],
             scratch,
         )
     else:
 
+        ins = (every_label, every0, every1, every2)
+
+        def classify(place_ref, label_ref, zero_ref, one_ref, two_ref, *rest):
+            classify_kernel(
+                True, place_ref, label_ref, zero_ref, one_ref, two_ref, None, *rest
+            )
+
         def whole(value):
             return pl.BlockSpec(value.shape, lambda i: (0, 0))
 
@@ -694,7 +722,7 @@
             )
 
         first, second, third = pl.pallas_call(
-            functools.partial(classify_kernel, True),
+            classify,
             grid=(members // groups,),
             out_shape=[jax.ShapeDtypeStruct(value.shape, f32) for value in fixed[3:]],
             in_specs=[pl.BlockSpec(memory_space=SMEM)]

time: 109 us -> 97 us (0.89); the launches traced: 109 us -> 95.7 us
  blocking collectives: 44.9 us -> 0 us
  waiting for transfers between devices: 1.77 us -> 22.4 us
  starting transfers between devices: 16 us -> 29.9 us
  Pallas kernels: 43.3 us -> 38.9 us
  local copies, waits for them, and re-layouts: 1.57 us -> 2.84 us
    all_gather x2 -> x0, blocking collectives: 31.1 us -> none  [every(): value = lax.all_gather(value, name, axis=0, tiled=True)]
    ppermute x3 -> x10, waiting for transfers between devices: 1.76 us -> 20 us  [shifted(): lax.ppermute(value, name, [((at + step * shift) % size, at) for at in ran...]
    all_to_all x1 -> x0, blocking collectives: 13.8 us -> none  [local(): lax.all_to_all(side1, 'dom', split_axis=0, concat_axis=0, tiled=True)]
    ppermute x3 -> x10, starting transfers between devices: 4.85 us -> 13.3 us  [shifted(): lax.ppermute(value, name, [((at + step * shift) % size, at) for at in ran...]
    pallas_call x7, Pallas kernels: 43.3 us -> 38.9 us  [call(): pl.pallas_call(kernel, out_shape=[shape_of(*out) for out in outs], in_spe...]
    all_to_all x1, starting transfers between devices: 3.37 us -> 6.25 us  [local(): lax.all_to_all(out1, 'dom', split_axis=0, concat_axis=0, tiled=True)]
    all_to_all x1, starting transfers between devices: 2.6 us -> 5.15 us  [local(): every2 = lax.all_to_all(last, axes, split_axis=0, concat_axis=0, tiled=True)]
    all_to_all x1, waiting for transfers between devices: 0.01 us -> 2.48 us  [local(): lax.all_to_all(out1, 'dom', split_axis=0, concat_axis=0, tiled=True)]
  transfers between devices with their start and end apart: 6 -> 13, of which waited for: 2 -> 7; matrix products, arithmetic and copies ran while one was open for 0% -> 0% of each run, Pallas kernels for 18% -> 17%
where the time goes in v4:
time: 97 us; the launch traced here: 95.7 us
  Pallas kernels  38.9 us (40%)
  starting transfers between devices  29.9 us (31%)
  waiting for transfers between devices  22.4 us (23%)
  local copies, waits for them, and re-layouts  2.84 us (3%)
  between operations  1.54 us (2%)
    pallas_call x7, Pallas kernels, call(): pl.pallas_call(kernel, out_shape=[shape_of(*out) for out in outs], in_spe...  38.9 us
    ppermute x10, waiting for transfers between devices, shifted(): lax.ppermute(value, name, [((at + step * shift) % size, at) for at in ran...  20 us
    ppermute x10, starting transfers between devices, shifted(): lax.ppermute(value, name, [((at + step * shift) % size, at) for at in ran...  13.3 us
    all_to_all x1, starting transfers between devices, local(): lax.all_to_all(out1, 'dom', split_axis=0, concat_axis=0, tiled=True)  6.25 us
    all_to_all x1, starting transfers between devices, local(): lax.all_to_all(out0, 'dom', split_axis=0, concat_axis=0, tiled=True)  5.18 us
    all_to_all x1, starting transfers between devices, local(): every2 = lax.all_to_all(last, axes, split_axis=0, concat_axis=0, tiled=True)  5.15 us
    unnamed x10, local copies, waits for them, and re-layouts  2.84 us
    all_to_all x1, waiting for transfers between devices, local(): lax.all_to_all(out1, 'dom', split_axis=0, concat_axis=0, tiled=True)  2.48 us
  transfers between devices with their start and end apart: 13, of which 7 were waited for; matrix products, arithmetic and copies ran while one was open for 0% of the time, Pallas kernels for 17%

profile of v4, /device:TPU:0, one launch (start us, length us, event | category | flops | bytes accessed | tf_op | source)
XLA Modules:
  0.0 95.7 jit_solution(15328109727579071955)
XLA Ops:
  0.6 0.0 copy-start.2
  0.6 0.0 copy-start.4
  0.7 2.4 %shard_map.165 = (bf16[1024,256]{1,0:T(8,128)(2,1)S(1)}, bf16[8,32,256]{2,1,0:T(8,128)(2,1)}) custom-call(bf16[1,1,1024,256]{3,2,1,0:T(8,128)(2,1)} %feats_hbm.1, s32[1,1,8,32]{3,2,1,0:T(8,128)} %rows_hbm.1), custom_call_target="tpu_custom_call" | custom-call | tf_op jit(solution)/shard_map/pallas_call | solution.py:506
  3.1 5.2 %all-to-all-start = ((bf16[8,32,256]{2,1,0:T(8,128)(2,1)}), bf16[8,32,256]{2,1,0:T(8,128)(2,1)S(1)}, u32[]{:S(2)}, u32[]{:S(2)}) async-start(bf16[8,32,256]{2,1,0:T(8,128)(2,1)} %get-tuple-element.29), calls=%async_computation | async-start | bytes 262144 | tf_op jit(solution)/shard_map/all_to_all | solution.py:562
  8.9 0.0 copy-start.3
  8.9 0.6 copy-done.3
  9.6 10.6 %shard_map.166 = (bf16[1024,1024]{1,0:T(8,128)(2,1)}, bf16[1024,256]{1,0:T(8,128)(2,1)S(1)}, f32[1024,256]{1,0:T(8,128)S(1)}, s32[1]{0:T(128)}, bf16[1024,1024]{1,0:T(8,128)(2,1)}, /*index=5*/bf16[1024,256]{1,0:T(8,128)(2,1)}) custom-call(s32[1,1,64]{2,1,0:T(1,128)S(1)} %copy-done.3, s32[1,1]{1,0:T(1,128)S(6)} %copy.18.count_ref, s32[1,1,64,256]{3,2,1,0:T(8,128)} %src_hbm.1, ...), custom_call_target="tpu_custom_call" | custom-call | tf_op jit(solution)/shard_map/pallas_call | solution.py:506
  20.2 0.0 copy-start
  20.2 1.0 %copy-done = f32[1024,256]{1,0:T(8,128)} copy-done((f32[1024,256]{1,0:T(8,128)}, f32[1024,256]{1,0:T(8,128)S(1)}, u32[]{:S(2)}) %copy-start) | copy-done | bytes 1048600
  21.2 0.0 all-to-all-done.table_ref
  21.2 0.0 copy-done.2
  21.2 0.0 copy-done.4
  21.2 0.0 copy-start.1
  21.2 1.2 %copy-done.1 = f32[1024,256]{1,0:T(8,128)S(1)} copy-done((f32[1024,256]{1,0:T(8,128)S(1)}, f32[1024,256]{1,0:T(8,128)}, u32[]{:S(2)}) %copy-start.1) | copy-done | bytes 1048600
  22.4 2.3 %shard_map.167 = (bf16[1024,256]{1,0:T(8,128)(2,1)S(1)}, bf16[8,32,256]{2,1,0:T(8,128)(2,1)}, bf16[80,256]{1,0:T(8,128)(2,1)S(1)}) custom-call(s32[1]{0:T(128)} %get-tuple-element.23.flag_ref, f32[1024,256]{1,0:T(8,128)S(1)} %copy-done.1, bf16[1024,256]{1,0:T(8,128)(2,1)S(1)} %get-tuple-element.27.ghost_ref, bf16[1024,256]{1,0:T(8,128)(2,1)} %get-tuple-element.28.rest_hbm, ...), custom_call_target="tpu_custom_call" | custom-call | tf_op jit(solution)/shard_map/pallas_call | solution.py:506
  24.7 6.3 %all-to-all-start.1 = ((bf16[8,32,256]{2,1,0:T(8,128)(2,1)}), bf16[8,32,256]{2,1,0:T(8,128)(2,1)S(1)}, u32[]{:S(2)}, u32[]{:S(2)}) async-start(bf16[8,32,256]{2,1,0:T(8,128)(2,1)} %get-tuple-element.31), calls=%async_computation.1 | async-start | bytes 262144 | tf_op jit(solution)/shard_map/all_to_all | solution.py:615
  31.0 3.0 %shard_map.168.part_ref = f32[1024,256]{1,0:T(8,128)S(1)} custom-call(s32[1]{0:T(128)} %get-tuple-element.23.flag_ref, bf16[1024,1024]{1,0:T(8,128)(2,1)} %get-tuple-element.24.own_hbm, bf16[1024,1024]{1,0:T(8,128)(2,1)} %get-tuple-element.25.rest_hbm, bf16[2,1,1,1024,256]{4,3,2,1,0:T(8,128)(2,1)} %noise_hbm.3, bf16[1024,256]{1,0:T(8,128)(2,1)S(1)} %get-tuple-element.30.start_ref), custom_call_target="tpu_custom_call" | custom-call | tf_op jit(solution)/shard_map/pallas_call | solution.py:506
  34.0 2.5 %all-to-all-done.1.table_ref = bf16[8,32,256]{2,1,0:T(8,128)(2,1)S(1)} async-done(((bf16[8,32,256]{2,1,0:T(8,128)(2,1)}), bf16[8,32,256]{2,1,0:T(8,128)(2,1)S(1)}, u32[]{:S(2)}, u32[]{:S(2)}) %all-to-all-start.1) | async-done | bytes 131104 | tf_op jit(solution)/shard_map/all_to_all | solution.py:615
  36.5 1.7 %shard_map.169 = (bf16[32,32,256]{2,1,0:T(8,128)(2,1)}, f32[8,128]{1,0:T(8,128)S(1)}) custom-call(s32[1]{0:T(128)} %get-tuple-element.23.flag_ref, f32[1024,256]{1,0:T(8,128)S(1)} %shard_map.168.part_ref, bf16[1024,256]{1,0:T(8,128)(2,1)S(1)} %get-tuple-element.27.ghost_ref, bf16[1024,256]{1,0:T(8,128)(2,1)} %get-tuple-element.28.rest_hbm, ...), custom_call_target="tpu_custom_call" | custom-call | tf_op jit(solution)/shard_map/pallas_call | solution.py:506
  38.3 5.1 %all-to-all-start.2 = ((bf16[32,32,256]{2,1,0:T(8,128)(2,1)}), bf16[32,32,256]{2,1,0:T(8,128)(2,1)S(1)}, u32[]{:S(2)}, u32[]{:S(2)}) async-start(bf16[32,32,256]{2,1,0:T(8,128)(2,1)} %get-tuple-element.36), calls=%async_computation.2 | async-start | bytes 1048576 | tf_op jit(solution)/shard_map/all_to_all | solution.py:646
  43.4 3.7 %collective-permute-start = (bf16[80,256]{1,0:T(8,128)(2,1)S(1)}, bf16[80,256]{1,0:T(8,128)(2,1)S(1)}, u32[]{:S(2)}, u32[]{:S(2)}) collective-permute-start(bf16[80,256]{1,0:T(8,128)(2,1)S(1)} %get-tuple-element.33.refs_0_), channel_id=1, source_target_pairs={{1,0},{2,1},{3,2},{0,3},{5,4},{6,5},{7,6},{4,7},{9,8},{10,9},{11,1... | collective-permute-start | bytes 122888 | tf_op jit(solution)/shard_map/ppermute | solution.py:633
  47.1 0.0 collective-permute-start.1
  47.1 1.1 %collective-permute-start.2 = (bf16[80,256]{1,0:T(8,128)(2,1)S(1)}, bf16[80,256]{1,0:T(8,128)(2,1)S(1)}, u32[]{:S(2)}, u32[]{:S(2)}) collective-permute-start(bf16[80,256]{1,0:T(8,128)(2,1)S(1)} %get-tuple-element.33.refs_0_), channel_id=1, source_target_pairs={{3,0},{0,1},{1,2},{2,3},{7,4},{4,5},{5,6},{6,7},{11,8},{8,9},{9,10... | collective-permute-start | bytes 122888 | tf_op jit(solution)/shard_map/ppermute | solution.py:633
  48.2 0.1 pad_add_fusion.place_ref
  48.2 5.5 %collective-permute-done.refs_1_ = bf16[80,256]{1,0:T(8,128)(2,1)S(1)} collective-permute-done((bf16[80,256]{1,0:T(8,128)(2,1)S(1)}, bf16[80,256]{1,0:T(8,128)(2,1)S(1)}, u32[]{:S(2)}, u32[]{:S(2)}) %collective-permute-start) | collective-permute-done | bytes 40992 | tf_op jit(solution)/shard_map/ppermute | solution.py:633
  53.8 8.2 %collective-permute-done.1.refs_2_ = bf16[80,256]{1,0:T(8,128)(2,1)S(1)} collective-permute-done((bf16[80,256]{1,0:T(8,128)(2,1)S(1)}, bf16[80,256]{1,0:T(8,128)(2,1)S(1)}, u32[]{:S(2)}, u32[]{:S(2)}) %collective-permute-start.1) | collective-permute-done | bytes 40992 | tf_op jit(solution)/shard_map/ppermute | solution.py:633
  61.9 0.0 collective-permute-done.2.refs_3_
  61.9 2.7 %shard_map.170 = (bf16[2,1,1,1024,256]{4,3,2,1,0:T(8,128)(2,1)}, bf16[272,256]{1,0:T(8,128)(2,1)S(1)}) custom-call(s32[1]{0:T(128)} %get-tuple-element.23.flag_ref, s32[2]{0:T(128)S(1)} %pad_add_fusion.place_ref, f32[8,128]{1,0:T(8,128)S(1)} %get-tuple-element.32.token_ref, f32[1024,256]{1,0:T(8,128)S(1)} %shard_map.168.part_ref, ...), custom_call_target="tpu_custom_call" | custom-call | tf_op jit(solution)/shard_map/pallas_call | solution.py:506
  64.6 0.0 collective-permute-start.3
  64.6 1.5 %collective-permute-start.4 = (bf16[272,256]{1,0:T(8,128)(2,1)S(1)}, bf16[272,256]{1,0:T(8,128)(2,1)S(1)}, u32[]{:S(2)}, u32[]{:S(2)}) collective-permute-start(bf16[272,256]{1,0:T(8,128)(2,1)S(1)} %get-tuple-element.35.refs_0_), channel_id=1, source_target_pairs={{24,0},{28,4},{0,8},{4,12},{8,16},{12,20},{16,24},{20,28},{25,1},{... | collective-permute-start | bytes 417800 | tf_op jit(solution)/shard_map/ppermute | solution.py:633
  66.1 2.4 %collective-permute-start.5 = (bf16[272,256]{1,0:T(8,128)(2,1)S(1)}, bf16[272,256]{1,0:T(8,128)(2,1)S(1)}, u32[]{:S(2)}, u32[]{:S(2)}) collective-permute-start(bf16[272,256]{1,0:T(8,128)(2,1)S(1)} %get-tuple-element.35.refs_0_), channel_id=1, source_target_pairs={{20,0},{24,4},{28,8},{0,12},{4,16},{8,20},{12,24},{16,28},{21,1},{... | collective-permute-start | bytes 417800 | tf_op jit(solution)/shard_map/ppermute | solution.py:633
  68.5 0.5 collective-permute-start.6
  69.0 0.1 collective-permute-start.7
  69.1 2.0 %collective-permute-done.3.refs_1_ = bf16[272,256]{1,0:T(8,128)(2,1)S(1)} collective-permute-done((bf16[272,256]{1,0:T(8,128)(2,1)S(1)}, bf16[272,256]{1,0:T(8,128)(2,1)S(1)}, u32[]{:S(2)}, u32[]{:S(2)}) %collective-permute-start.3) | collective-permute-done | bytes 139296 | tf_op jit(solution)/shard_map/ppermute | solution.py:633
  71.0 1.4 %collective-permute-start.8 = (bf16[272,256]{1,0:T(8,128)(2,1)S(1)}, bf16[272,256]{1,0:T(8,128)(2,1)S(1)}, u32[]{:S(2)}, u32[]{:S(2)}) collective-permute-start(bf16[272,256]{1,0:T(8,128)(2,1)S(1)} %get-tuple-element.35.refs_0_), channel_id=1, source_target_pairs={{8,0},{12,4},{16,8},{20,12},{24,16},{28,20},{0,24},{4,28},{9,1},{1... | collective-permute-start | bytes 417800 | tf_op jit(solution)/shard_map/ppermute | solution.py:633
  72.4 0.0 collective-permute-done.4.refs_2_
  72.4 2.7 %collective-permute-start.9 = (bf16[272,256]{1,0:T(8,128)(2,1)S(1)}, bf16[272,256]{1,0:T(8,128)(2,1)S(1)}, u32[]{:S(2)}, u32[]{:S(2)}) collective-permute-start(bf16[272,256]{1,0:T(8,128)(2,1)S(1)} %get-tuple-element.35.refs_0_), channel_id=1, source_target_pairs={{4,0},{8,4},{12,8},{16,12},{20,16},{24,20},{28,24},{0,28},{5,1},{9... | collective-permute-start | bytes 417800 | tf_op jit(solution)/shard_map/ppermute | solution.py:633
  75.1 2.2 %collective-permute-done.5.refs_3_ = bf16[272,256]{1,0:T(8,128)(2,1)S(1)} collective-permute-done((bf16[272,256]{1,0:T(8,128)(2,1)S(1)}, bf16[272,256]{1,0:T(8,128)(2,1)S(1)}, u32[]{:S(2)}, u32[]{:S(2)}) %collective-permute-start.5) | collective-permute-done | bytes 139296 | tf_op jit(solution)/shard_map/ppermute | solution.py:633
  77.3 0.2 collective-permute-done.6.refs_4_
  77.5 1.9 %collective-permute-done.7.refs_5_ = bf16[272,256]{1,0:T(8,128)(2,1)S(1)} collective-permute-done((bf16[272,256]{1,0:T(8,128)(2,1)S(1)}, bf16[272,256]{1,0:T(8,128)(2,1)S(1)}, u32[]{:S(2)}, u32[]{:S(2)}) %collective-permute-start.7) | collective-permute-done | bytes 139296 | tf_op jit(solution)/shard_map/ppermute | solution.py:633
  79.4 0.0 collective-permute-done.8.refs_6_
  79.4 0.0 collective-permute-done.9.refs_7_
  79.4 0.0 all-to-all-done.2.refs_8_
  79.4 16.1 %shard_map.171 = (f32[96,1024]{1,0:T(8,128)}, f32[128,1024]{1,0:T(8,128)}, f32[172,128]{1,0:T(8,128)}) custom-call(s32[2]{0:T(128)S(1)} %pad_add_fusion.place_ref, bf16[272,256]{1,0:T(8,128)(2,1)S(1)} %get-tuple-element.35.refs_0_, bf16[272,256]{1,0:T(8,128)(2,1)S(1)} %collective-permute-done.3.refs_1_, bf16[272,256]{1,0:T(8,128)(2,1)S(1)} %collective-permute-done.4.refs_2_, ...), custom_call_target="tpu_custom_call" | custom-call | tf_op jit(solution)/shard_map/pallas_call | solution.py:506
Async XLA Ops:
  0.6 20.6 %copy-start.2 = (s32[1,1,8,32]{3,2,1,0:T(8,128)S(1)}, s32[1,1,8,32]{3,2,1,0:T(8,128)}, u32[]{:S(2)}) copy-start(s32[1,1,8,32]{3,2,1,0:T(8,128)} %rows_hbm.1) | copy-start | bytes 3076
  0.6 20.6 %copy-start.4 = (s32[1,1,32]{2,1,0:T(1,128)S(1)}, s32[1,1,32]{2,1,0:T(1,128)}, u32[]{:S(2)}) copy-start(s32[1,1,32]{2,1,0:T(1,128)} %param.21) | copy-start | bytes 388
  3.1 18.1 %all-to-all-start = ((bf16[8,32,256]{2,1,0:T(8,128)(2,1)}), bf16[8,32,256]{2,1,0:T(8,128)(2,1)S(1)}, u32[]{:S(2)}, u32[]{:S(2)}) async-start(bf16[8,32,256]{2,1,0:T(8,128)(2,1)} %get-tuple-element.29), calls=%async_computation | async-start | bytes 262144 | tf_op jit(solution)/shard_map/all_to_all | solution.py:562
  8.9 0.7 copy-start.3
  20.2 1.0 %copy-start = (f32[1024,256]{1,0:T(8,128)}, f32[1024,256]{1,0:T(8,128)S(1)}, u32[]{:S(2)}) copy-start(f32[1024,256]{1,0:T(8,128)S(1)} %get-tuple-element.26.part_ref) | copy-start | bytes 3145732
  21.2 1.2 %copy-start.1 = (f32[1024,256]{1,0:T(8,128)S(1)}, f32[1024,256]{1,0:T(8,128)}, u32[]{:S(2)}) copy-start(f32[1024,256]{1,0:T(8,128)} %copy-done) | copy-start | bytes 3145732
  24.7 11.8 %all-to-all-start.1 = ((bf16[8,32,256]{2,1,0:T(8,128)(2,1)}), bf16[8,32,256]{2,1,0:T(8,128)(2,1)S(1)}, u32[]{:S(2)}, u32[]{:S(2)}) async-start(bf16[8,32,256]{2,1,0:T(8,128)(2,1)} %get-tuple-element.31), calls=%async_computation.1 | async-start | bytes 262144 | tf_op jit(solution)/shard_map/all_to_all | solution.py:615
  38.3 41.2 %all-to-all-start.2 = ((bf16[32,32,256]{2,1,0:T(8,128)(2,1)}), bf16[32,32,256]{2,1,0:T(8,128)(2,1)S(1)}, u32[]{:S(2)}, u32[]{:S(2)}) async-start(bf16[32,32,256]{2,1,0:T(8,128)(2,1)} %get-tuple-element.36), calls=%async_computation.2 | async-start | bytes 1048576 | tf_op jit(solution)/shard_map/all_to_all | solution.py:646
  43.4 10.3 %collective-permute-start = (bf16[80,256]{1,0:T(8,128)(2,1)S(1)}, bf16[80,256]{1,0:T(8,128)(2,1)S(1)}, u32[]{:S(2)}, u32[]{:S(2)}) collective-permute-start(bf16[80,256]{1,0:T(8,128)(2,1)S(1)} %get-tuple-element.33.refs_0_), channel_id=1, source_target_pairs={{1,0},{2,1},{3,2},{0,3},{5,4},{6,5},{7,6},{4,7},{9,8},{10,9},{11,1... | collective-permute-start | bytes 122888 | tf_op jit(solution)/shard_map/ppermute | solution.py:633
  47.1 14.8 %collective-permute-start.1 = (bf16[80,256]{1,0:T(8,128)(2,1)S(1)}, bf16[80,256]{1,0:T(8,128)(2,1)S(1)}, u32[]{:S(2)}, u32[]{:S(2)}) collective-permute-start(bf16[80,256]{1,0:T(8,128)(2,1)S(1)} %get-tuple-element.33.refs_0_), channel_id=1, source_target_pairs={{2,0},{3,1},{0,2},{1,3},{6,4},{7,5},{4,6},{5,7},{10,8},{11,9},{8,1... | collective-permute-start | bytes 122888 | tf_op jit(solution)/shard_map/ppermute | solution.py:633
  47.1 14.8 %collective-permute-start.2 = (bf16[80,256]{1,0:T(8,128)(2,1)S(1)}, bf16[80,256]{1,0:T(8,128)(2,1)S(1)}, u32[]{:S(2)}, u32[]{:S(2)}) collective-permute-start(bf16[80,256]{1,0:T(8,128)(2,1)S(1)} %get-tuple-element.33.refs_0_), channel_id=1, source_target_pairs={{3,0},{0,1},{1,2},{2,3},{7,4},{4,5},{5,6},{6,7},{11,8},{8,9},{9,10... | collective-permute-start | bytes 122888 | tf_op jit(solution)/shard_map/ppermute | solution.py:633
  64.6 6.4 %collective-permute-start.3 = (bf16[272,256]{1,0:T(8,128)(2,1)S(1)}, bf16[272,256]{1,0:T(8,128)(2,1)S(1)}, u32[]{:S(2)}, u32[]{:S(2)}) collective-permute-start(bf16[272,256]{1,0:T(8,128)(2,1)S(1)} %get-tuple-element.35.refs_0_), channel_id=1, source_target_pairs={{28,0},{0,4},{4,8},{8,12},{12,16},{16,20},{20,24},{24,28},{29,1},{... | collective-permute-start | bytes 417800 | tf_op jit(solution)/shard_map/ppermute | solution.py:633
  64.6 7.8 %collective-permute-start.4 = (bf16[272,256]{1,0:T(8,128)(2,1)S(1)}, bf16[272,256]{1,0:T(8,128)(2,1)S(1)}, u32[]{:S(2)}, u32[]{:S(2)}) collective-permute-start(bf16[272,256]{1,0:T(8,128)(2,1)S(1)} %get-tuple-element.35.refs_0_), channel_id=1, source_target_pairs={{24,0},{28,4},{0,8},{4,12},{8,16},{12,20},{16,24},{20,28},{25,1},{... | collective-permute-start | bytes 417800 | tf_op jit(solution)/shard_map/ppermute | solution.py:633
  66.1 11.2 %collective-permute-start.5 = (bf16[272,256]{1,0:T(8,128)(2,1)S(1)}, bf16[272,256]{1,0:T(8,128)(2,1)S(1)}, u32[]{:S(2)}, u32[]{:S(2)}) collective-permute-start(bf16[272,256]{1,0:T(8,128)(2,1)S(1)} %get-tuple-element.35.refs_0_), channel_id=1, source_target_pairs={{20,0},{24,4},{28,8},{0,12},{4,16},{8,20},{12,24},{16,28},{21,1},{... | collective-permute-start | bytes 417800 | tf_op jit(solution)/shard_map/ppermute | solution.py:633
  68.5 9.1 %collective-permute-start.6 = (bf16[272,256]{1,0:T(8,128)(2,1)S(1)}, bf16[272,256]{1,0:T(8,128)(2,1)S(1)}, u32[]{:S(2)}, u32[]{:S(2)}) collective-permute-start(bf16[272,256]{1,0:T(8,128)(2,1)S(1)} %get-tuple-element.35.refs_0_), channel_id=1, source_target_pairs={{16,0},{20,4},{24,8},{28,12},{0,16},{4,20},{8,24},{12,28},{17,1},{... | collective-permute-start | bytes 417800 | tf_op jit(solution)/shard_map/ppermute | solution.py:633
  69.0 10.4 %collective-permute-start.7 = (bf16[272,256]{1,0:T(8,128)(2,1)S(1)}, bf16[272,256]{1,0:T(8,128)(2,1)S(1)}, u32[]{:S(2)}, u32[]{:S(2)}) collective-permute-start(bf16[272,256]{1,0:T(8,128)(2,1)S(1)} %get-tuple-element.35.refs_0_), channel_id=1, source_target_pairs={{12,0},{16,4},{20,8},{24,12},{28,16},{0,20},{4,24},{8,28},{13,1},{... | collective-permute-start | bytes 417800 | tf_op jit(solution)/shard_map/ppermute | solution.py:633
  71.0 8.4 %collective-permute-start.8 = (bf16[272,256]{1,0:T(8,128)(2,1)S(1)}, bf16[272,256]{1,0:T(8,128)(2,1)S(1)}, u32[]{:S(2)}, u32[]{:S(2)}) collective-permute-start(bf16[272,256]{1,0:T(8,128)(2,1)S(1)} %get-tuple-element.35.refs_0_), channel_id=1, source_target_pairs={{8,0},{12,4},{16,8},{20,12},{24,16},{28,20},{0,24},{4,28},{9,1},{1... | collective-permute-start | bytes 417800 | tf_op jit(solution)/shard_map/ppermute | solution.py:633
  72.4 7.0 %collective-permute-start.9 = (bf16[272,256]{1,0:T(8,128)(2,1)S(1)}, bf16[272,256]{1,0:T(8,128)(2,1)S(1)}, u32[]{:S(2)}, u32[]{:S(2)}) collective-permute-start(bf16[272,256]{1,0:T(8,128)(2,1)S(1)} %get-tuple-element.35.refs_0_), channel_id=1, source_target_pairs={{4,0},{8,4},{12,8},{16,12},{20,16},{24,20},{28,24},{0,28},{5,1},{9... | collective-permute-start | bytes 417800 | tf_op jit(solution)/shard_map/ppermute | solution.py:633

commit v5 on v4

--- a/solution.py
+++ b/solution.py
@@ -8,7 +8,7 @@
 from jax.sharding import PartitionSpec as P
 
 BLOCK = 128
-LOW = 256
+LOW = 512
 GROUP = 4
 clip_bound = 4.0
 noise_mult = 1.0
@@ -75,6 +75,7 @@
     rows_hbm,
     start_ref,
     out_ref,
+    own_ref,
     feats_ref,
     rows_ref,
     turn_ref,
@@ -88,6 +89,7 @@
         copy.wait()
     start = normalize(feats_ref[...].astype(f32))
     start_ref[...] = start
+    own_ref[...] = start[: own_ref.shape[0]]
     send(start, rows_ref, out_ref, turn_ref, pick_ref)
 
 
@@ -124,7 +126,7 @@
         sems,
     )
     nodes, cols = sums_ref.shape
-    pieces = cols // LOW
+    pieces = -(-cols // LOW)
     tiles, slots = src_ref.shape
     count = count_ref[0, 0]
     own_ref[...] = jnp.zeros_like(own_ref)
@@ -141,12 +143,12 @@
     tile_ids = lax.broadcasted_iota(jnp.int32, (tiles, slots), 0)
     high_ref[...] = sixteen(src // LOW)
     spot_ref[...] = sixteen(jnp.where((dst < BLOCK) & (tile_ids < count), dst, -1))
-    low = (src % LOW).astype(f32).T
+    low = (src % LOW - LOW // 2).astype(f32).T
     for tile in range(tiles):
         low_ref[tile] = jnp.broadcast_to(low[:, tile : tile + 1], (slots, 128)).astype(bf16)
     ids = lax.broadcasted_iota(jnp.int32, (BLOCK, slots), 0).astype(f32).astype(bf16)
     lanes = lax.broadcasted_iota(jnp.int32, (slots, 128), 1).astype(f32)
-    lanes = [(lanes + first).astype(bf16) for first in range(0, LOW, 128)]
+    lanes = [(lanes + first).astype(bf16) for first in range(-LOW // 2, LOW // 2, 128)]
     one = jnp.ones((), bf16)
     zero = jnp.zeros((), bf16)
 
@@ -170,18 +172,20 @@
 
     def add_short(rows, at, values):
         ref, at = (own_ref, at) if at < nodes else (ghost_ref, at - nodes)
-        ref[rows, at : at + LOW] += values.astype(bf16)
+        size = min(LOW, ref.shape[1] - at)
+        ref[rows, at : at + size] += values[:, :size].astype(bf16)
 
     def add_long(rows, at, values):
-        sums_ref[rows, at : at + LOW] += values
+        size = min(LOW, cols - at)
+        sums_ref[rows, at : at + size] += values[:, :size]
 
     steps = (count + GROUP - 1) // GROUP
     lax.fori_loop(0, steps, functools.partial(turn, add_short), 0)
-    top = ghost_ref[:BLOCK, :LOW]
+    top = ghost_ref[:BLOCK, :256]
     for first in range(0, nodes, BLOCK):
         for ref in (own_ref, ghost_ref):
-            for at in range(0, ref.shape[1], LOW):
-                top = jnp.maximum(top, ref[first : first + BLOCK, at : at + LOW])
+            for at in range(0, ref.shape[1], 256):
+                top = jnp.maximum(top, ref[first : first + BLOCK, at : at + 256])
     big = jnp.max(top.astype(f32)) >= 256.0
     flag_ref[0] = big.astype(jnp.int32)
 
@@ -242,7 +246,7 @@
     start_ref[...] = start
     send(start, rows_ref, out_ref, turn_ref, pick_ref)
     train = labels_ref.shape[1]
-    side_ref[:train, :] = old_ref[:train, :]
+    side_ref[:train, :] = old_ref[...]
     side_ref[train : 2 * train, :] = start[:train]
     turn_ref[:1, :train] = labels_ref[...]
     side_ref[2 * train :, :128] = turn_ref[:16, :].astype(f32).astype(bf16)
@@ -259,34 +263,14 @@
     aggregate(flag_ref, noise, own_ref[...], rest_hbm, start, part_ref, rest_ref)
 
 
-def train_kernel(
-    flag_ref, part_ref, ghost_ref, rest_hbm, table_ref, out_ref, token_ref, sums_ref, rest_ref
-):
+def train_kernel(flag_ref, place_ref, part_ref, ghost_ref, rest_hbm, table_ref, *refs):
+    *piece_refs, out_ref, side_ref, sums_ref, rest_ref, turn_ref = refs
     train, width = sums_ref.shape
     table = table_ref[...].reshape(-1, width)
     aggregate(
         flag_ref, part_ref[:train], ghost_ref[:train], rest_hbm, table, sums_ref, rest_ref
     )
     spread(normalize(sums_ref[...]), out_ref)
-    token_ref[...] = sums_ref[:8, :128]
-
-
-def last_kernel(
-    flag_ref,
-    place_ref,
-    token_ref,
-    part_ref,
-    ghost_ref,
-    rest_hbm,
-    table_ref,
-    start_ref,
-    *refs,
-):
-    *piece_refs, out_ref, side_ref, sums_ref, rest_ref, turn_ref = refs
-    table = table_ref[...].reshape(-1, out_ref.shape[-1])
-    aggregate(flag_ref, part_ref[...], ghost_ref[...], rest_hbm, table, sums_ref, rest_ref)
-    out_ref[0, 0, 0] = start_ref[...]
-    out_ref[1, 0, 0] = normalize(sums_ref[...])
     length = piece_refs[0].shape[0] - 16
     groups = len(piece_refs)
     if groups > 1:
@@ -296,6 +280,24 @@
             side_ref[pl.ds(at, length), :] = ref[:length, :]
             turn_ref[pl.ds(group, 1), :] = ref[length:, :128].astype(f32)[:1]
         side_ref[groups * length :, :128] = turn_ref[:16, :].astype(bf16)
+
+
+def last_kernel(
+    flag_ref,
+    token_ref,
+    part_ref,
+    ghost_ref,
+    rest_hbm,
+    table_ref,
+    start_ref,
+    out_ref,
+    sums_ref,
+    rest_ref,
+):
+    table = table_ref[...].reshape(-1, out_ref.shape[-1])
+    aggregate(flag_ref, part_ref[...], ghost_ref[...], rest_hbm, table, sums_ref, rest_ref)
+    out_ref[0, 0, 0] = start_ref[...]
+    out_ref[1, 0, 0] = normalize(sums_ref[...])
 
 
 def shares(ref, first, share):
@@ -401,8 +403,10 @@
         parts = len(side_refs)
         groups = two_ref.shape[0] // parts
         rows = groups * train
-        for shift, ref in enumerate(side_refs):
-            part = lax.rem(place - shift + parts, parts)
+        chips = parts // 2
+        for at, ref in enumerate(side_refs):
+            core = place % 2 if at < chips else 1 - place % 2
+            part = 2 * lax.rem(place // 2 - at % chips + chips, chips) + core
             at = pl.multiple_of(part * rows, rows)
             for group in range(groups):
                 for hop in range(2):
@@ -428,7 +432,7 @@
         h_ref[:, cols] = rounded
         return lanes_sum(rounded)
 
-    step = 256
+    step = 512
     cuts = [slice(at, at + step) for at in range(0, hid, step)]
     sq_in = lanes_sum(in_ref[...])
     sq_one = sum(
@@ -544,7 +548,7 @@
     pick = VMEM((ghosts, nodes), bf16)
     axes = ("dom", "grp")
     members = lax.axis_size(axes)
-    few = members <= FEW and parts <= 8
+    few = members <= FEW and parts <= 8 and parts % 2 == 0
     copies = members if few else 1
 
     def every(value, *names):
@@ -552,10 +556,14 @@
             value = lax.all_gather(value, name, axis=0, tiled=True)
         return value
 
-    start0, out0 = call(
+    start0, out0, own0 = call(
         first_kernel,
         16,
-        [((nodes, width), bf16, None), ((parts, each, width), bf16, None)],
+        [
+            ((nodes, width), bf16, None),
+            ((parts, each, width), bf16, None),
+            ((train, width), bf16, None),
+        ],
         [(feats, HBM), (send_rows, HBM)],
         [VMEM((nodes, width), bf16), VMEM((parts, each), jnp.int32), turn, pick, DMA((2,))],
     )
@@ -607,7 +615,7 @@
             (ghost_rest, HBM),
             (table0, None),
             (rows, VMEM),
-            (start0, None),
+            (own0, None),
             (labels.reshape(1, train), VMEM),
         ],
         [VMEM((nodes, width), f32), VMEM((nodes, ghosts), bf16), turn, pick],
@@ -635,41 +643,57 @@
         ]
 
     sides = [side] + (shifted(side, "grp", grp, 1) if few else [])
-    last, token = call(
+    last, side = call(
         train_kernel,
         12,
-        [((copies, train, width), bf16, None), ((8, 128), f32, None)],
-        [(flag, SMEM), (part2, None), (ghost, None), (ghost_rest, HBM), (table1, None)],
-        [VMEM((train, width), f32), VMEM((train, ghosts), bf16)],
+        [
+            ((copies, train, width), bf16, None),
+            ((len(sides) * 2 * train + 16, width), bf16, None),
+        ],
+        [
+            (flag, SMEM),
+            (place, SMEM),
+            (part2, None),
+            (ghost, None),
+            (ghost_rest, HBM),
+            (table1, None),
+        ]
+        + [(value, None) for value in sides],
+        [VMEM((train, width), f32), VMEM((train, ghosts), bf16), VMEM((128, 128), f32)],
     )
     if few:
         every2 = lax.all_to_all(last, axes, split_axis=0, concat_axis=0, tiled=True)
+        chips = parts // 2
+        sides = [side]
+        for shift in range(1, chips):
+            pairs = [
+                (2 * ((chip - shift) % chips) + core, 2 * chip + core)
+                for chip in range(chips)
+                for core in range(2)
+            ]
+            sides.append(lax.ppermute(side, "dom", pairs))
+        swap = [(at, at ^ 1) for at in range(parts)]
+        sides += [lax.ppermute(value, "dom", swap) for value in sides]
     else:
         every0, every1, every2 = (
-            every(value, axes) for value in (start0[None, :train], start1[None, :train], last)
+            every(value, axes) for value in (own0[None], start1[None, :train], last)
         )
         every_label = every(labels.reshape(1, train), axes)
-    hop_feats, side = call(
+    (hop_feats,) = call(
         last_kernel,
         12,
-        [
-            ((2, 1, 1, nodes, width), bf16, VMEM),
-            ((len(sides) * 2 * train + 16, width), bf16, None),
-        ],
+        [((2, 1, 1, nodes, width), bf16, VMEM)],
         [
             (flag, SMEM),
-            (place, SMEM),
-            (token, None),
+            (side, None),
             (part2, None),
             (ghost, None),
             (ghost_rest, HBM),
             (table1, None),
             (start1, None),
-        ]
-        + [(value, None) for value in sides],
-        [VMEM((nodes, width), f32), VMEM((nodes, ghosts), bf16), VMEM((128, 128), f32)],
-    )
-    sides = [side] + (shifted(side, "dom", parts, -1) if few else [])
+        ],
+        [VMEM((nodes, width), f32), VMEM((nodes, ghosts), bf16)],
+    )
     chunk = train * min(members, 32)
     groups = chunk // train
     wide = (classes + 255) // 256 * 256

time: 97 us -> 84.2 us (0.87); the launches traced: 95.7 us -> 83.9 us
  waiting for transfers between devices: 22.4 us -> 10.8 us
  Pallas kernels: 38.9 us -> 35.1 us
  local copies, waits for them, and re-layouts: 2.84 us -> 5.35 us
  starting transfers between devices: 29.9 us -> 31 us
    ppermute x10 -> x3, waiting for transfers between devices: 20 us -> 1.06 us  [shifted(): lax.ppermute(value, name, [((at + step * shift) % size, at) for at in ran...]
    ppermute x0 -> x7, waiting for transfers between devices: none -> 9.72 us  [the longest x3 9.71 us: local(): sides.append(lax.ppermute(side, 'dom', pairs))]
    ppermute x10 -> x3, starting transfers between devices: 13.3 us -> 5.82 us  [shifted(): lax.ppermute(value, name, [((at + step * shift) % size, at) for at in ran...]
    ppermute x0 -> x7, starting transfers between devices: none -> 5.26 us  [the longest x3 4.75 us: local(): sides.append(lax.ppermute(side, 'dom', pairs))]
    all_to_all x1, starting transfers between devices: 6.25 us -> 10.6 us  [local(): lax.all_to_all(out1, 'dom', split_axis=0, concat_axis=0, tiled=True)]
    pallas_call x7, Pallas kernels: 38.9 us -> 35.1 us  [call(): pl.pallas_call(kernel, out_shape=[shape_of(*out) for out in outs], in_spe...]
    unnamed x10 -> x18, local copies, waits for them, and re-layouts: 2.84 us -> 5.35 us
    all_to_all x1, waiting for transfers between devices: 2.48 us -> 0.01 us  [local(): lax.all_to_all(out1, 'dom', split_axis=0, concat_axis=0, tiled=True)]
  transfers between devices with their start and end apart: 13 -> 13, of which waited for: 7 -> 4; matrix products, arithmetic and copies ran while one was open for 0% -> 0% of each run, Pallas kernels for 17% -> 14%
where the time goes in v5:
time: 84.2 us; the launch traced here: 83.9 us
  Pallas kernels  35.1 us (42%)
  starting transfers between devices  31 us (37%)
  waiting for transfers between devices  10.8 us (13%)
  local copies, waits for them, and re-layouts  5.35 us (6%)
  between operations  1.55 us (2%)
    pallas_call x7, Pallas kernels, call(): pl.pallas_call(kernel, out_shape=[shape_of(*out) for out in outs], in_spe...  35.1 us
    all_to_all x1, starting transfers between devices, local(): lax.all_to_all(out1, 'dom', split_axis=0, concat_axis=0, tiled=True)  10.6 us
    ppermute x3, waiting for transfers between devices, local(): sides.append(lax.ppermute(side, 'dom', pairs))  9.71 us
    ppermute x3, starting transfers between devices, shifted(): lax.ppermute(value, name, [((at + step * shift) % size, at) for at in ran...  5.82 us
    unnamed x18, local copies, waits for them, and re-layouts  5.35 us
    all_to_all x1, starting transfers between devices, local(): lax.all_to_all(out0, 'dom', split_axis=0, concat_axis=0, tiled=True)  5.18 us
    ppermute x3, starting transfers between devices, local(): sides.append(lax.ppermute(side, 'dom', pairs))  4.75 us
    all_to_all x1, starting transfers between devices, local(): every2 = lax.all_to_all(last, axes, split_axis=0, concat_axis=0, tiled=True)  4.19 us
  transfers between devices with their start and end apart: 13, of which 4 were waited for; matrix products, arithmetic and copies ran while one was open for 0% of the time, Pallas kernels for 14%

profile of v5, /device:TPU:0, one launch (start us, length us, event | category | flops | bytes accessed | tf_op | source)
XLA Modules:
  0.0 83.9 jit_solution(1124073904619046711)
XLA Ops:
  0.6 0.0 copy-start.6
  0.6 0.0 copy-start.8
  0.7 2.4 %shard_map.165 = (bf16[1024,256]{1,0:T(8,128)(2,1)S(1)}, bf16[8,32,256]{2,1,0:T(8,128)(2,1)}, bf16[32,256]{1,0:T(8,128)(2,1)S(1)}) custom-call(bf16[1,1,1024,256]{3,2,1,0:T(8,128)(2,1)} %feats_hbm.1, s32[1,1,8,32]{3,2,1,0:T(8,128)} %rows_hbm.1), custom_call_target="tpu_custom_call" | custom-call | tf_op jit(solution)/shard_map/pallas_call | solution.py:510
  3.1 5.2 %all-to-all-start = ((bf16[8,32,256]{2,1,0:T(8,128)(2,1)}), bf16[8,32,256]{2,1,0:T(8,128)(2,1)S(1)}, u32[]{:S(2)}, u32[]{:S(2)}) async-start(bf16[8,32,256]{2,1,0:T(8,128)(2,1)} %get-tuple-element.28), calls=%async_computation | async-start | bytes 262144 | tf_op jit(solution)/shard_map/all_to_all | solution.py:570
  8.9 0.0 copy-start.7
  8.9 0.6 copy-done.7
  9.6 6.5 %shard_map.166 = (bf16[1024,1024]{1,0:T(8,128)(2,1)}, bf16[1024,256]{1,0:T(8,128)(2,1)S(1)}, f32[1024,256]{1,0:T(8,128)S(1)}, s32[1]{0:T(128)}, bf16[1024,1024]{1,0:T(8,128)(2,1)}, /*index=5*/bf16[1024,256]{1,0:T(8,128)(2,1)}) custom-call(s32[1,1,64]{2,1,0:T(1,128)S(1)} %copy-done.7, s32[1,1]{1,0:T(1,128)S(6)} %copy.18.count_ref, s32[1,1,64,256]{3,2,1,0:T(8,128)} %src_hbm.1, ...), custom_call_target="tpu_custom_call" | custom-call | tf_op jit(solution)/shard_map/pallas_call | solution.py:510
  16.1 0.0 all-to-all-done.table_ref
  16.1 0.0 copy-done.6
  16.1 0.0 copy-done.8
  16.1 2.3 %shard_map.167 = (bf16[1024,256]{1,0:T(8,128)(2,1)S(1)}, bf16[8,32,256]{2,1,0:T(8,128)(2,1)}, bf16[80,256]{1,0:T(8,128)(2,1)S(1)}) custom-call(s32[1]{0:T(128)} %get-tuple-element.22.flag_ref, f32[1024,256]{1,0:T(8,128)S(1)} %get-tuple-element.25.part_ref, bf16[1024,256]{1,0:T(8,128)(2,1)S(1)} %get-tuple-element.26.ghost_ref, ...), custom_call_target="tpu_custom_call" | custom-call | tf_op jit(solution)/shard_map/pallas_call | solution.py:510
  18.5 10.6 %all-to-all-start.1 = ((bf16[8,32,256]{2,1,0:T(8,128)(2,1)}), bf16[8,32,256]{2,1,0:T(8,128)(2,1)S(1)}, u32[]{:S(2)}, u32[]{:S(2)}) async-start(bf16[8,32,256]{2,1,0:T(8,128)(2,1)} %get-tuple-element.31), calls=%async_computation.1 | async-start | bytes 262144 | tf_op jit(solution)/shard_map/all_to_all | solution.py:623
  29.0 4.2 %collective-permute-start = (bf16[80,256]{1,0:T(8,128)(2,1)S(1)}, bf16[80,256]{1,0:T(8,128)(2,1)S(1)}, u32[]{:S(2)}, u32[]{:S(2)}) collective-permute-start(bf16[80,256]{1,0:T(8,128)(2,1)S(1)} %get-tuple-element.32.refs_0_), channel_id=1, source_target_pairs={{1,0},{2,1},{3,2},{0,3},{5,4},{6,5},{7,6},{4,7},{9,8},{10,9},{11,1... | collective-permute-start | bytes 122888 | tf_op jit(solution)/shard_map/ppermute | solution.py:641
  33.2 0.0 collective-permute-start.1
  33.2 1.6 %collective-permute-start.2 = (bf16[80,256]{1,0:T(8,128)(2,1)S(1)}, bf16[80,256]{1,0:T(8,128)(2,1)S(1)}, u32[]{:S(2)}, u32[]{:S(2)}) collective-permute-start(bf16[80,256]{1,0:T(8,128)(2,1)S(1)} %get-tuple-element.32.refs_0_), channel_id=1, source_target_pairs={{3,0},{0,1},{1,2},{2,3},{7,4},{4,5},{5,6},{6,7},{11,8},{8,9},{9,10... | collective-permute-start | bytes 122888 | tf_op jit(solution)/shard_map/ppermute | solution.py:641
  34.8 0.1 pad_add_fusion.place_ref
  34.9 3.0 %shard_map.168.part_ref = f32[1024,256]{1,0:T(8,128)S(1)} custom-call(s32[1]{0:T(128)} %get-tuple-element.22.flag_ref, bf16[1024,1024]{1,0:T(8,128)(2,1)} %get-tuple-element.23.own_hbm, bf16[1024,1024]{1,0:T(8,128)(2,1)} %get-tuple-element.24.rest_hbm, bf16[2,1,1,1024,256]{4,3,2,1,0:T(8,128)(2,1)} %noise_hbm.3, bf16[1024,256]{1,0:T(8,128)(2,1)S(1)} %get-tuple-element.30.start_ref), custom_call_target="tpu_custom_call" | custom-call | tf_op jit(solution)/shard_map/pallas_call | solution.py:510
  38.0 0.0 collective-permute-done.refs_1_
  38.0 0.6 collective-permute-done.1.refs_2_
  38.6 0.5 collective-permute-done.2.refs_3_
  39.0 0.0 all-to-all-done.1.table_ref
  39.0 2.3 %shard_map.169 = (bf16[32,32,256]{2,1,0:T(8,128)(2,1)}, bf16[272,256]{1,0:T(8,128)(2,1)S(1)}) custom-call(s32[1]{0:T(128)} %get-tuple-element.22.flag_ref, s32[2]{0:T(128)S(1)} %pad_add_fusion.place_ref, f32[1024,256]{1,0:T(8,128)S(1)} %shard_map.168.part_ref, bf16[1024,256]{1,0:T(8,128)(2,1)S(1)} %get-tuple-element.26.ghost_ref, ...), custom_call_target="tpu_custom_call" | custom-call | tf_op jit(solution)/shard_map/pallas_call | solution.py:510
  41.3 4.2 %all-to-all-start.2 = ((bf16[32,32,256]{2,1,0:T(8,128)(2,1)}), bf16[32,32,256]{2,1,0:T(8,128)(2,1)S(1)}, u32[]{:S(2)}, u32[]{:S(2)}) async-start(bf16[32,32,256]{2,1,0:T(8,128)(2,1)} %get-tuple-element.34), calls=%async_computation.2 | async-start | bytes 1048576 | tf_op jit(solution)/shard_map/all_to_all | solution.py:665
  45.5 1.8 %collective-permute-start.3 = (bf16[272,256]{1,0:T(8,128)(2,1)S(1)}, bf16[272,256]{1,0:T(8,128)(2,1)S(1)}, u32[]{:S(2)}, u32[]{:S(2)}) collective-permute-start(bf16[272,256]{1,0:T(8,128)(2,1)S(1)} %get-tuple-element.33.token_ref.refs_0_), channel_id=1, source_target_pairs={{24,0},{28,4},{0,8},{4,12},{8,16},{12,20},{16,24},{20,28},{25,1},{... | collective-permute-start | bytes 417800 | tf_op jit(solution)/shard_map/ppermute | solution.py:674
  47.4 1.5 %collective-permute-start.4 = (bf16[272,256]{1,0:T(8,128)(2,1)S(1)}, bf16[272,256]{1,0:T(8,128)(2,1)S(1)}, u32[]{:S(2)}, u32[]{:S(2)}) collective-permute-start(bf16[272,256]{1,0:T(8,128)(2,1)S(1)} %get-tuple-element.33.token_ref.refs_0_), channel_id=1, source_target_pairs={{16,0},{20,4},{24,8},{28,12},{0,16},{4,20},{8,24},{12,28},{17,1},{... | collective-permute-start | bytes 417800 | tf_op jit(solution)/shard_map/ppermute | solution.py:674
  48.8 1.5 %collective-permute-start.5 = (bf16[272,256]{1,0:T(8,128)(2,1)S(1)}, bf16[272,256]{1,0:T(8,128)(2,1)S(1)}, u32[]{:S(2)}, u32[]{:S(2)}) collective-permute-start(bf16[272,256]{1,0:T(8,128)(2,1)S(1)} %get-tuple-element.33.token_ref.refs_0_), channel_id=1, source_target_pairs={{8,0},{12,4},{16,8},{20,12},{24,16},{28,20},{0,24},{4,28},{9,1},{1... | collective-permute-start | bytes 417800 | tf_op jit(solution)/shard_map/ppermute | solution.py:674
  50.3 0.0 collective-permute-start.6
  50.3 6.8 %collective-permute-done.3.refs_1_ = bf16[272,256]{1,0:T(8,128)(2,1)S(1)} collective-permute-done((bf16[272,256]{1,0:T(8,128)(2,1)S(1)}, bf16[272,256]{1,0:T(8,128)(2,1)S(1)}, u32[]{:S(2)}, u32[]{:S(2)}) %collective-permute-start.3) | collective-permute-done | bytes 139296 | tf_op jit(solution)/shard_map/ppermute | solution.py:674
  57.1 0.0 collective-permute-start.7
  57.1 2.9 %collective-permute-done.4.refs_2_ = bf16[272,256]{1,0:T(8,128)(2,1)S(1)} collective-permute-done((bf16[272,256]{1,0:T(8,128)(2,1)S(1)}, bf16[272,256]{1,0:T(8,128)(2,1)S(1)}, u32[]{:S(2)}, u32[]{:S(2)}) %collective-permute-start.4) | collective-permute-done | bytes 139296 | tf_op jit(solution)/shard_map/ppermute | solution.py:674
  60.0 0.0 collective-permute-start.8
  60.0 0.0 collective-permute-done.5.refs_3_
  60.0 0.5 collective-permute-start.9
  60.5 2.3 %shard_map.170 = bf16[2,1,1,1024,256]{4,3,2,1,0:T(8,128)(2,1)} custom-call(s32[1]{0:T(128)} %get-tuple-element.22.flag_ref, bf16[272,256]{1,0:T(8,128)(2,1)S(1)} %get-tuple-element.33.token_ref.refs_0_, f32[1024,256]{1,0:T(8,128)S(1)} %shard_map.168.part_ref, bf16[1024,256]{1,0:T(8,128)(2,1)S(1)} %get-tuple-element.26.ghost_ref, ...), custom_call_target="tpu_custom_call" | custom-call | tf_op jit(solution)/shard_map/pallas_call | solution.py:510
  62.8 0.0 collective-permute-done.6.refs_4_
  62.8 0.0 collective-permute-done.7.refs_5_
  62.8 0.0 copy-start
  62.8 0.7 copy-done
  63.5 0.0 collective-permute-done.8.refs_6_
  63.5 0.0 copy-start.2
  63.5 0.7 copy-done.2
  64.2 0.0 collective-permute-done.9.refs_7_
  64.2 0.0 copy-start.4
  64.2 0.7 copy-done.4
  64.8 0.0 all-to-all-done.2.refs_8_
  64.8 0.0 copy-start.1
  64.8 0.9 %copy-done.1 = bf16[272,256]{1,0:T(8,128)(2,1)S(1)} copy-done((bf16[272,256]{1,0:T(8,128)(2,1)S(1)}, bf16[272,256]{1,0:T(8,128)(2,1)}, u32[]{:S(2)}) %copy-start.1) | copy-done | bytes 139288
  65.7 0.0 copy-start.3
  65.7 0.9 %copy-done.3 = bf16[272,256]{1,0:T(8,128)(2,1)S(1)} copy-done((bf16[272,256]{1,0:T(8,128)(2,1)S(1)}, bf16[272,256]{1,0:T(8,128)(2,1)}, u32[]{:S(2)}) %copy-start.3) | copy-done | bytes 139288
  66.6 0.0 copy-start.5
  66.6 0.9 %copy-done.5 = bf16[272,256]{1,0:T(8,128)(2,1)S(1)} copy-done((bf16[272,256]{1,0:T(8,128)(2,1)S(1)}, bf16[272,256]{1,0:T(8,128)(2,1)}, u32[]{:S(2)}) %copy-start.5) | copy-done | bytes 139288
  67.6 16.2 %shard_map.171 = (f32[96,1024]{1,0:T(8,128)}, f32[128,1024]{1,0:T(8,128)}, f32[172,128]{1,0:T(8,128)}) custom-call(s32[2]{0:T(128)S(1)} %pad_add_fusion.place_ref, bf16[272,256]{1,0:T(8,128)(2,1)S(1)} %get-tuple-element.33.token_ref.refs_0_, bf16[272,256]{1,0:T(8,128)(2,1)S(1)} %collective-permute-done.3.refs_1_, ...), custom_call_target="tpu_custom_call" | custom-call | tf_op jit(solution)/shard_map/pallas_call | solution.py:510
Async XLA Ops:
  0.6 15.5 %copy-start.6 = (s32[1,1,8,32]{3,2,1,0:T(8,128)S(1)}, s32[1,1,8,32]{3,2,1,0:T(8,128)}, u32[]{:S(2)}) copy-start(s32[1,1,8,32]{3,2,1,0:T(8,128)} %rows_hbm.1) | copy-start | bytes 3076
  0.6 15.5 %copy-start.8 = (s32[1,1,32]{2,1,0:T(1,128)S(1)}, s32[1,1,32]{2,1,0:T(1,128)}, u32[]{:S(2)}) copy-start(s32[1,1,32]{2,1,0:T(1,128)} %param.21) | copy-start | bytes 388
  3.1 13.0 %all-to-all-start = ((bf16[8,32,256]{2,1,0:T(8,128)(2,1)}), bf16[8,32,256]{2,1,0:T(8,128)(2,1)S(1)}, u32[]{:S(2)}, u32[]{:S(2)}) async-start(bf16[8,32,256]{2,1,0:T(8,128)(2,1)} %get-tuple-element.28), calls=%async_computation | async-start | bytes 262144 | tf_op jit(solution)/shard_map/all_to_all | solution.py:570
  8.9 0.7 copy-start.7
  18.5 20.6 %all-to-all-start.1 = ((bf16[8,32,256]{2,1,0:T(8,128)(2,1)}), bf16[8,32,256]{2,1,0:T(8,128)(2,1)S(1)}, u32[]{:S(2)}, u32[]{:S(2)}) async-start(bf16[8,32,256]{2,1,0:T(8,128)(2,1)} %get-tuple-element.31), calls=%async_computation.1 | async-start | bytes 262144 | tf_op jit(solution)/shard_map/all_to_all | solution.py:623
  29.0 9.0 %collective-permute-start = (bf16[80,256]{1,0:T(8,128)(2,1)S(1)}, bf16[80,256]{1,0:T(8,128)(2,1)S(1)}, u32[]{:S(2)}, u32[]{:S(2)}) collective-permute-start(bf16[80,256]{1,0:T(8,128)(2,1)S(1)} %get-tuple-element.32.refs_0_), channel_id=1, source_target_pairs={{1,0},{2,1},{3,2},{0,3},{5,4},{6,5},{7,6},{4,7},{9,8},{10,9},{11,1... | collective-permute-start | bytes 122888 | tf_op jit(solution)/shard_map/ppermute | solution.py:641
  33.2 5.3 %collective-permute-start.1 = (bf16[80,256]{1,0:T(8,128)(2,1)S(1)}, bf16[80,256]{1,0:T(8,128)(2,1)S(1)}, u32[]{:S(2)}, u32[]{:S(2)}) collective-permute-start(bf16[80,256]{1,0:T(8,128)(2,1)S(1)} %get-tuple-element.32.refs_0_), channel_id=1, source_target_pairs={{2,0},{3,1},{0,2},{1,3},{6,4},{7,5},{4,6},{5,7},{10,8},{11,9},{8,1... | collective-permute-start | bytes 122888 | tf_op jit(solution)/shard_map/ppermute | solution.py:641
  33.2 5.8 %collective-permute-start.2 = (bf16[80,256]{1,0:T(8,128)(2,1)S(1)}, bf16[80,256]{1,0:T(8,128)(2,1)S(1)}, u32[]{:S(2)}, u32[]{:S(2)}) collective-permute-start(bf16[80,256]{1,0:T(8,128)(2,1)S(1)} %get-tuple-element.32.refs_0_), channel_id=1, source_target_pairs={{3,0},{0,1},{1,2},{2,3},{7,4},{4,5},{5,6},{6,7},{11,8},{8,9},{9,10... | collective-permute-start | bytes 122888 | tf_op jit(solution)/shard_map/ppermute | solution.py:641
  41.3 23.5 %all-to-all-start.2 = ((bf16[32,32,256]{2,1,0:T(8,128)(2,1)}), bf16[32,32,256]{2,1,0:T(8,128)(2,1)S(1)}, u32[]{:S(2)}, u32[]{:S(2)}) async-start(bf16[32,32,256]{2,1,0:T(8,128)(2,1)} %get-tuple-element.34), calls=%async_computation.2 | async-start | bytes 1048576 | tf_op jit(solution)/shard_map/all_to_all | solution.py:665
  45.5 11.6 %collective-permute-start.3 = (bf16[272,256]{1,0:T(8,128)(2,1)S(1)}, bf16[272,256]{1,0:T(8,128)(2,1)S(1)}, u32[]{:S(2)}, u32[]{:S(2)}) collective-permute-start(bf16[272,256]{1,0:T(8,128)(2,1)S(1)} %get-tuple-element.33.token_ref.refs_0_), channel_id=1, source_target_pairs={{24,0},{28,4},{0,8},{4,12},{8,16},{12,20},{16,24},{20,28},{25,1},{... | collective-permute-start | bytes 417800 | tf_op jit(solution)/shard_map/ppermute | solution.py:674
  47.4 12.6 %collective-permute-start.4 = (bf16[272,256]{1,0:T(8,128)(2,1)S(1)}, bf16[272,256]{1,0:T(8,128)(2,1)S(1)}, u32[]{:S(2)}, u32[]{:S(2)}) collective-permute-start(bf16[272,256]{1,0:T(8,128)(2,1)S(1)} %get-tuple-element.33.token_ref.refs_0_), channel_id=1, source_target_pairs={{16,0},{20,4},{24,8},{28,12},{0,16},{4,20},{8,24},{12,28},{17,1},{... | collective-permute-start | bytes 417800 | tf_op jit(solution)/shard_map/ppermute | solution.py:674
  48.8 11.2 %collective-permute-start.5 = (bf16[272,256]{1,0:T(8,128)(2,1)S(1)}, bf16[272,256]{1,0:T(8,128)(2,1)S(1)}, u32[]{:S(2)}, u32[]{:S(2)}) collective-permute-start(bf16[272,256]{1,0:T(8,128)(2,1)S(1)} %get-tuple-element.33.token_ref.refs_0_), channel_id=1, source_target_pairs={{8,0},{12,4},{16,8},{20,12},{24,16},{28,20},{0,24},{4,28},{9,1},{1... | collective-permute-start | bytes 417800 | tf_op jit(solution)/shard_map/ppermute | solution.py:674
  50.3 12.6 %collective-permute-start.6 = (bf16[272,256]{1,0:T(8,128)(2,1)S(1)}, bf16[272,256]{1,0:T(8,128)(2,1)S(1)}, u32[]{:S(2)}, u32[]{:S(2)}) collective-permute-start(bf16[272,256]{1,0:T(8,128)(2,1)S(1)} %get-tuple-element.33.token_ref.refs_0_), channel_id=1, source_target_pairs={{0,4},{4,0},{8,12},{12,8},{16,20},{20,16},{24,28},{28,24},{1,5},{5... | collective-permute-start | bytes 417800 | tf_op jit(solution)/shard_map/ppermute | solution.py:676
  57.1 5.7 %collective-permute-start.7 = (bf16[272,256]{1,0:T(8,128)(2,1)S(1)}, bf16[272,256]{1,0:T(8,128)(2,1)S(1)}, u32[]{:S(2)}, u32[]{:S(2)}) collective-permute-start(bf16[272,256]{1,0:T(8,128)(2,1)S(1)} %collective-permute-done.3.refs_1_), channel_id=1, source_target_pairs={{0,4},{4,0},{8,12},{12,8},{16,20},{20,16},{24,28},{28,24},{1,5},{5... | collective-permute-start | bytes 417800 | tf_op jit(solution)/shard_map/ppermute | solution.py:676
  60.0 3.5 %collective-permute-start.8 = (bf16[272,256]{1,0:T(8,128)(2,1)S(1)}, bf16[272,256]{1,0:T(8,128)(2,1)S(1)}, u32[]{:S(2)}, u32[]{:S(2)}) collective-permute-start(bf16[272,256]{1,0:T(8,128)(2,1)S(1)} %collective-permute-done.4.refs_2_), channel_id=1, source_target_pairs={{0,4},{4,0},{8,12},{12,8},{16,20},{20,16},{24,28},{28,24},{1,5},{5... | collective-permute-start | bytes 417800 | tf_op jit(solution)/shard_map/ppermute | solution.py:676
  60.0 4.2 %collective-permute-start.9 = (bf16[272,256]{1,0:T(8,128)(2,1)S(1)}, bf16[272,256]{1,0:T(8,128)(2,1)S(1)}, u32[]{:S(2)}, u32[]{:S(2)}) collective-permute-start(bf16[272,256]{1,0:T(8,128)(2,1)S(1)} %collective-permute-done.5.refs_3_), channel_id=1, source_target_pairs={{0,4},{4,0},{8,12},{12,8},{16,20},{20,16},{24,28},{28,24},{1,5},{5... | collective-permute-start | bytes 417800 | tf_op jit(solution)/shard_map/ppermute | solution.py:676
  62.8 0.7 copy-start
  63.5 0.7 copy-start.2
  64.2 0.7 copy-start.4
  64.8 0.9 %copy-start.1 = (bf16[272,256]{1,0:T(8,128)(2,1)S(1)}, bf16[272,256]{1,0:T(8,128)(2,1)}, u32[]{:S(2)}) copy-start(bf16[272,256]{1,0:T(8,128)(2,1)} %copy-done) | copy-start | bytes 417796
  65.7 0.9 %copy-start.3 = (bf16[272,256]{1,0:T(8,128)(2,1)S(1)}, bf16[272,256]{1,0:T(8,128)(2,1)}, u32[]{:S(2)}) copy-start(bf16[272,256]{1,0:T(8,128)(2,1)} %copy-done.2) | copy-start | bytes 417796
  66.6 0.9 %copy-start.5 = (bf16[272,256]{1,0:T(8,128)(2,1)S(1)}, bf16[272,256]{1,0:T(8,128)(2,1)}, u32[]{:S(2)}) copy-start(bf16[272,256]{1,0:T(8,128)(2,1)} %copy-done.4) | copy-start | bytes 417796

commit v6 on v5

--- a/solution.py
+++ b/solution.py
@@ -8,7 +8,7 @@
 from jax.sharding import PartitionSpec as P
 
 BLOCK = 128
-LOW = 512
+LOW = 256
 GROUP = 4
 clip_bound = 4.0
 noise_mult = 1.0
@@ -94,7 +94,7 @@
 
 
 def build_kernel(
-    blocks_ref,
+    blocks_hbm,
     count_ref,
     src_hbm,
     dst_hbm,
@@ -115,10 +115,12 @@
     sums_ref,
     rest_ref,
     own_ref,
+    blocks_ref,
     sems,
 ):
     copies = fetch(
         (
+            (blocks_hbm, blocks_ref),
             (src_hbm.at[0, 0], src_ref),
             (dst_hbm.at[0, 0], dst_ref),
             (noise_hbm.at[0, 0, 0], noise_ref),
@@ -152,20 +154,23 @@
     one = jnp.ones((), bf16)
     zero = jnp.zeros((), bf16)
 
+    def counts(tile):
+        rows = pl.ds(pl.multiple_of(tile * 16, 16), 16)
+        high, spot = high_ref[rows, :], spot_ref[rows, :]
+        spots = []
+        for piece in range(pieces):
+            wanted = jnp.where(high == piece, spot, -one)
+            tall = jnp.concatenate([wanted] * (BLOCK // 16), 0)
+            spots.append(jnp.where(ids == tall, one, zero))
+        low = low_ref[tile]
+        low_hot = jnp.concatenate([jnp.where(low == ids, one, zero) for ids in lanes], 1)
+        return dot(jnp.concatenate(spots, 0), low_hot)
+
     def turn(add, step, carry):
-        for inner in range(GROUP):
-            tile = step * GROUP + inner
-            rows = pl.ds(pl.multiple_of(tile * 16, 16), 16)
-            high, spot = high_ref[rows, :], spot_ref[rows, :]
-            spots = []
-            for piece in range(pieces):
-                wanted = jnp.where(high == piece, spot, -one)
-                tall = jnp.concatenate([wanted] * (BLOCK // 16), 0)
-                spots.append(jnp.where(ids == tall, one, zero))
-            low = low_ref[tile]
-            low_hot = jnp.concatenate([jnp.where(low == ids, one, zero) for ids in lanes], 1)
-            out = dot(jnp.concatenate(spots, 0), low_hot)
-            base = pl.multiple_of(blocks_ref[0, 0, tile] * BLOCK, BLOCK)
+        first = step * GROUP
+        outs = [counts(first + inner) for inner in range(GROUP)]
+        for inner, out in enumerate(outs):
+            base = pl.multiple_of(blocks_ref[0, 0, first + inner] * BLOCK, BLOCK)
             for piece in range(pieces):
                 add(pl.ds(base, BLOCK), piece * LOW, out[piece * BLOCK : (piece + 1) * BLOCK])
         return carry
@@ -196,7 +201,7 @@
         own_ref[...] = sums_ref[:, :nodes].astype(bf16)
         ghost_ref[...] = sums_ref[:, nodes:].astype(bf16)
 
-    own_copy = pltpu.make_async_copy(own_ref, own_hbm, sems.at[3])
+    own_copy = pltpu.make_async_copy(own_ref, own_hbm, sems.at[4])
     own_copy.start()
     part_ref[...] = dot(own_ref[...], start_ref[...]) + noise_ref[...].astype(f32)
 
@@ -291,9 +296,11 @@
     table_ref,
     start_ref,
     out_ref,
+    again_ref,
     sums_ref,
     rest_ref,
 ):
+    again_ref[...] = token_ref[...]
     table = table_ref[...].reshape(-1, out_ref.shape[-1])
     aggregate(flag_ref, part_ref[...], ghost_ref[...], rest_hbm, table, sums_ref, rest_ref)
     out_ref[0, 0, 0] = start_ref[...]
@@ -324,7 +331,7 @@
     zero_ref,
     one_ref,
     two_ref,
-    side_refs,
+    sides_hbm,
     w_first_hbm,
     w_second_hbm,
     w_third_hbm,
@@ -334,6 +341,7 @@
     g_first_ref,
     g_second_ref,
     g_third_ref,
+    side_refs,
     w_first_ref,
     w_second_ref,
     w_third_ref,
@@ -350,6 +358,7 @@
     slope_two_ref,
     d_one_ref,
     d_two_ref,
+    d_three_ref,
     sems,
 ):
     classes = w_third_ref.shape[0]
@@ -399,8 +408,10 @@
         for hop, ref in enumerate((zero_ref, one_ref)):
             in_ref[:, hop * width : (hop + 1) * width] = ref[...].reshape(-1, width)
     else:
-        copies = fetch(pairs[:1], sems)
         parts = len(side_refs)
+        copies = fetch(tuple(zip(sides_hbm, side_refs)) + pairs[:1], sems)
+        for copy in copies[:parts]:
+            copy.wait()
         groups = two_ref.shape[0] // parts
         rows = groups * train
         chips = parts // 2
@@ -421,29 +432,40 @@
                 column((part * groups + group) * train, turned, part * 16 + group)
     in_ref[:, 2 * width :] = two_ref[...].reshape(-1, width)
     if not many:
-        copies[0].wait()
+        copies[parts].wait()
         copies = fetch(pairs[1:], sems)
 
-    def activate(values, h_ref, slope_ref, cols):
+    def activate(values, h_ref, slope_ref, rows):
         sigma = 0.5 + 0.5 * jnp.tanh(0.5 * values)
         out = values * sigma
-        slope_ref[:, cols] = sigma + out * (1.0 - sigma)
-        rounded = out.astype(bf16)
-        h_ref[:, cols] = rounded
-        return lanes_sum(rounded)
-
-    step = 512
-    cuts = [slice(at, at + step) for at in range(0, hid, step)]
+        slope_ref[rows, :] = sigma + out * (1.0 - sigma)
+        h_ref[rows, :] = out.astype(bf16)
+        return lanes_sum(out)
+
+    def back(values, slope_ref, d_ref, rows):
+        out = values * slope_ref[rows, :]
+        d_ref[rows, :] = out.astype(bf16)
+        return lanes_sum(out)
+
+    def layer(product, finish, *refs):
+        sums = []
+        values = product(cuts[0])
+        for at, cut in enumerate(cuts):
+            ahead = product(cuts[at + 1]) if at + 1 < len(cuts) else None
+            sums.append(finish(values, *refs, cut))
+            values = ahead
+        return jnp.concatenate(sums, 0)
+
+    step = 256
+    cuts = [slice(at, at + step) for at in range(0, in_ref.shape[0], step)]
     sq_in = lanes_sum(in_ref[...])
-    sq_one = sum(
-        activate(dot(in_ref[...], w_first_ref[:, cut]), h_one_ref, slope_one_ref, cut)
-        for cut in cuts
+    sq_one = layer(
+        lambda cut: dot(in_ref[cut, :], w_first_ref[...]), activate, h_one_ref, slope_one_ref
     )
     if not many:
         copies[0].wait()
-    sq_two = sum(
-        activate(dot(h_one_ref[...], w_second_ref[:, cut]), h_two_ref, slope_two_ref, cut)
-        for cut in cuts
+    sq_two = layer(
+        lambda cut: dot(h_one_ref[cut, :], w_second_ref[...]), activate, h_two_ref, slope_two_ref
     )
     if not many:
         copies[1].wait()
@@ -455,19 +477,12 @@
     label = column_ref[:, :1]
     d_three = (probs - jnp.where(ids == label, 1.0, 0.0)).astype(bf16)
     sq_dthree = lanes_sum(d_three)
-
-    def back(values, slope_ref, d_ref, cut):
-        rounded = (values * slope_ref[:, cut]).astype(bf16)
-        d_ref[:, cut] = rounded
-        return lanes_sum(rounded)
-
-    sq_dtwo = sum(
-        back(dot(d_three, w_third_pad_ref[:, cut]), slope_two_ref, d_two_ref, cut)
-        for cut in cuts
-    )
-    sq_done = sum(
-        back(dot_nt(d_two_ref[...], w_second_ref[cut, :]), slope_one_ref, d_one_ref, cut)
-        for cut in cuts
+    d_three_ref[...] = d_three
+    sq_dtwo = layer(
+        lambda cut: dot(d_three_ref[cut, :], w_third_pad_ref[...]), back, slope_two_ref, d_two_ref
+    )
+    sq_done = layer(
+        lambda cut: dot_nt(d_two_ref[cut, :], w_second_ref[...]), back, slope_one_ref, d_one_ref
     )
 
     def total(values):
@@ -580,7 +595,7 @@
             ((nodes, ghosts), bf16, HBM),
         ],
         [
-            (tile_block, SMEM),
+            (tile_block, HBM),
             (tile_count, SMEM),
             (tile_src, HBM),
             (tile_dst, HBM),
@@ -597,7 +612,8 @@
             VMEM((nodes, cols), f32),
             VMEM((nodes, max(nodes, ghosts)), bf16),
             VMEM((nodes, nodes), bf16),
-            DMA((4,)),
+            SMEM(tile_block.shape, jnp.int32),
+            DMA((5,)),
         ],
     )
     start1, out1, side = call(
@@ -672,17 +688,15 @@
                 for core in range(2)
             ]
             sides.append(lax.ppermute(side, "dom", pairs))
-        swap = [(at, at ^ 1) for at in range(parts)]
-        sides += [lax.ppermute(value, "dom", swap) for value in sides]
     else:
         every0, every1, every2 = (
             every(value, axes) for value in (own0[None], start1[None, :train], last)
         )
         every_label = every(labels.reshape(1, train), axes)
-    (hop_feats,) = call(
+    hop_feats, again = call(
         last_kernel,
         12,
-        [((2, 1, 1, nodes, width), bf16, VMEM)],
+        [((2, 1, 1, nodes, width), bf16, VMEM), (side.shape, bf16, None)],
         [
             (flag, SMEM),
             (side, None),
@@ -694,6 +708,9 @@
         ],
         [VMEM((nodes, width), f32), VMEM((nodes, ghosts), bf16)],
     )
+    if few:
+        swap = [(at, at ^ 1) for at in range(parts)]
+        sides += [lax.ppermute(value, "dom", swap) for value in [again] + sides[1:]]
     chunk = train * min(members, 32)
     groups = chunk // train
     wide = (classes + 255) // 256 * 256
@@ -710,23 +727,27 @@
         VMEM((chunk, hid), f32),
         VMEM((chunk, hid), bf16),
         VMEM((chunk, hid), bf16),
-        DMA((6,)),
+        VMEM((chunk, wide), bf16),
+        DMA((16,)),
     ]
     if few:
 
         def classify(place_ref, *refs):
             sides_in, rest = refs[:parts], refs[parts:]
-            classify_kernel(False, place_ref, None, None, None, rest[0], sides_in, *rest[1:])
+            outs, rest, held = rest[:10], rest[10 + parts :], rest[10 : 10 + parts]
+            classify_kernel(
+                False, place_ref, None, None, None, outs[0], sides_in, *outs[1:], held, *rest
+            )
 
         first, second, third = call(
             classify,
             44,
             [(value.shape, f32, VMEM) for value in fixed[3:]],
             [(place, SMEM)]
-            + [(value, None) for value in sides]
+            + [(value, HBM) for value in sides]
             + [(every2, None)]
             + [(value, HBM) for value in fixed],
-            scratch,
+            [VMEM(value.shape, bf16) for value in sides] + scratch,
         )
     else:
 
@@ -734,7 +755,16 @@
 
         def classify(place_ref, label_ref, zero_ref, one_ref, two_ref, *rest):
             classify_kernel(
-                True, place_ref, label_ref, zero_ref, one_ref, two_ref, None, *rest
+                True,
+                place_ref,
+                label_ref,
+                zero_ref,
+                one_ref,
+                two_ref,
+                None,
+                *rest[:9],
+                None,
+                *rest[9:],
             )
 
         def whole(value):

time: 84.2 us -> 77.6 us (0.922)
  local copies, waits for them, and re-layouts: 5.35 us -> 0.64 us
  starting transfers between devices: 31 us -> 29.6 us
    unnamed x18 -> x20, local copies, waits for them, and re-layouts: 5.35 us -> 0.64 us
    ppermute x3, waiting for transfers between devices: 9.71 us -> 7.39 us  [local(): sides.append(lax.ppermute(side, 'dom', pairs))]
    ppermute x4, waiting for transfers between devices: 0.01 us -> 1.02 us  [local(): sides += [lax.ppermute(value, 'dom', swap) for value in [again] + sides[1:]]]
    ppermute x3, starting transfers between devices: 5.82 us -> 4.84 us  [shifted(): lax.ppermute(value, name, [((at + step * shift) % size, at) for at in ran...]
    ppermute x3, waiting for transfers between devices: 1.06 us -> 2.03 us  [shifted(): lax.ppermute(value, name, [((at + step * shift) % size, at) for at in ran...]
  transfers between devices with their start and end apart: 13 -> 13, of which waited for: 4 -> 6; matrix products, arithmetic and copies ran while one was open for 0% -> 0% of each run, Pallas kernels for 14% -> 15%
where the time goes in v6:
time: 77.6 us; the launch traced here: 77.3 us
  Pallas kernels  35 us (45%)
  starting transfers between devices  29.6 us (38%)
  waiting for transfers between devices  10.4 us (13%)
  between operations  1.6 us (2%)
    pallas_call x7, Pallas kernels, call(): pl.pallas_call(kernel, out_shape=[shape_of(*out) for out in outs], in_spe...  35 us
    all_to_all x1, starting transfers between devices, local(): lax.all_to_all(out1, 'dom', split_axis=0, concat_axis=0, tiled=True)  10.4 us
    ppermute x3, waiting for transfers between devices, local(): sides.append(lax.ppermute(side, 'dom', pairs))  7.39 us
    all_to_all x1, starting transfers between devices, local(): lax.all_to_all(out0, 'dom', split_axis=0, concat_axis=0, tiled=True)  5.18 us
    ppermute x3, starting transfers between devices, shifted(): lax.ppermute(value, name, [((at + step * shift) % size, at) for at in ran...  4.84 us
    ppermute x3, starting transfers between devices, local(): sides.append(lax.ppermute(side, 'dom', pairs))  4.75 us
    all_to_all x1, starting transfers between devices, local(): every2 = lax.all_to_all(last, axes, split_axis=0, concat_axis=0, tiled=True)  3.91 us
    ppermute x3, waiting for transfers between devices, shifted(): lax.ppermute(value, name, [((at + step * shift) % size, at) for at in ran...  2.03 us
  transfers between devices with their start and end apart: 13, of which 6 were waited for; matrix products, arithmetic and copies ran while one was open for 0% of the time, Pallas kernels for 15%

profile of v6, /device:TPU:0, one launch (start us, length us, event | category | flops | bytes accessed | tf_op | source)
XLA Modules:
  0.0 77.3 jit_solution(4490965922384224752)
XLA Ops:
  0.6 0.0 copy-start.1
  0.6 0.0 copy-start.2
  0.7 2.4 %shard_map.165 = (bf16[1024,256]{1,0:T(8,128)(2,1)S(1)}, bf16[8,32,256]{2,1,0:T(8,128)(2,1)}, bf16[32,256]{1,0:T(8,128)(2,1)S(1)}) custom-call(bf16[1,1,1024,256]{3,2,1,0:T(8,128)(2,1)} %feats_hbm.1, s32[1,1,8,32]{3,2,1,0:T(8,128)} %rows_hbm.1), custom_call_target="tpu_custom_call" | custom-call | tf_op jit(solution)/shard_map/pallas_call | solution.py:525
  3.1 5.2 %all-to-all-start = ((bf16[8,32,256]{2,1,0:T(8,128)(2,1)}), bf16[8,32,256]{2,1,0:T(8,128)(2,1)S(1)}, u32[]{:S(2)}, u32[]{:S(2)}) async-start(bf16[8,32,256]{2,1,0:T(8,128)(2,1)} %get-tuple-element.30), calls=%async_computation | async-start | bytes 262144 | tf_op jit(solution)/shard_map/all_to_all | solution.py:585
  8.9 6.0 %shard_map.166 = (bf16[1024,1024]{1,0:T(8,128)(2,1)}, bf16[1024,256]{1,0:T(8,128)(2,1)S(1)}, f32[1024,256]{1,0:T(8,128)S(1)}, s32[1]{0:T(128)}, bf16[1024,1024]{1,0:T(8,128)(2,1)}, /*index=5*/bf16[1024,256]{1,0:T(8,128)(2,1)}) custom-call(s32[1,1,64]{2,1,0:T(1,128)} %blocks_hbm.1, s32[1,1]{1,0:T(1,128)S(6)} %copy.18.count_ref, s32[1,1,64,256]{3,2,1,0:T(8,128)} %src_hbm.1, ...), custom_call_target="tpu_custom_call" | custom-call | tf_op jit(solution)/shard_map/pallas_call | solution.py:525
  14.9 0.0 all-to-all-done.table_ref
  14.9 0.0 copy-done.1
  14.9 0.0 copy-done.2
  14.9 2.3 %shard_map.167 = (bf16[1024,256]{1,0:T(8,128)(2,1)S(1)}, bf16[8,32,256]{2,1,0:T(8,128)(2,1)}, bf16[80,256]{1,0:T(8,128)(2,1)S(1)}) custom-call(s32[1]{0:T(128)} %get-tuple-element.24.flag_ref, f32[1024,256]{1,0:T(8,128)S(1)} %get-tuple-element.27.part_ref, bf16[1024,256]{1,0:T(8,128)(2,1)S(1)} %get-tuple-element.28.ghost_ref, ...), custom_call_target="tpu_custom_call" | custom-call | tf_op jit(solution)/shard_map/pallas_call | solution.py:525
  17.2 10.4 %all-to-all-start.1 = ((bf16[8,32,256]{2,1,0:T(8,128)(2,1)}), bf16[8,32,256]{2,1,0:T(8,128)(2,1)S(1)}, u32[]{:S(2)}, u32[]{:S(2)}) async-start(bf16[8,32,256]{2,1,0:T(8,128)(2,1)} %get-tuple-element.33), calls=%async_computation.1 | async-start | bytes 262144 | tf_op jit(solution)/shard_map/all_to_all | solution.py:639
  27.6 4.2 %collective-permute-start = (bf16[80,256]{1,0:T(8,128)(2,1)S(1)}, bf16[80,256]{1,0:T(8,128)(2,1)S(1)}, u32[]{:S(2)}, u32[]{:S(2)}) collective-permute-start(bf16[80,256]{1,0:T(8,128)(2,1)S(1)} %get-tuple-element.34.refs_0_), channel_id=1, source_target_pairs={{1,0},{2,1},{3,2},{0,3},{5,4},{6,5},{7,6},{4,7},{9,8},{10,9},{11,1... | collective-permute-start | bytes 122888 | tf_op jit(solution)/shard_map/ppermute | solution.py:657
  31.8 0.0 collective-permute-start.1
  31.8 0.6 collective-permute-start.2
  32.5 0.1 pad_add_fusion.place_ref
  32.6 3.0 %shard_map.168.part_ref = f32[1024,256]{1,0:T(8,128)S(1)} custom-call(s32[1]{0:T(128)} %get-tuple-element.24.flag_ref, bf16[1024,1024]{1,0:T(8,128)(2,1)} %get-tuple-element.25.own_hbm, bf16[1024,1024]{1,0:T(8,128)(2,1)} %get-tuple-element.26.rest_hbm, bf16[2,1,1,1024,256]{4,3,2,1,0:T(8,128)(2,1)} %noise_hbm.3, bf16[1024,256]{1,0:T(8,128)(2,1)S(1)} %get-tuple-element.32.start_ref), custom_call_target="tpu_custom_call" | custom-call | tf_op jit(solution)/shard_map/pallas_call | solution.py:525
  35.6 0.0 collective-permute-done.refs_1_
  35.6 1.6 %collective-permute-done.1.refs_2_ = bf16[80,256]{1,0:T(8,128)(2,1)S(1)} collective-permute-done((bf16[80,256]{1,0:T(8,128)(2,1)S(1)}, bf16[80,256]{1,0:T(8,128)(2,1)S(1)}, u32[]{:S(2)}, u32[]{:S(2)}) %collective-permute-start.1) | collective-permute-done | bytes 40992 | tf_op jit(solution)/shard_map/ppermute | solution.py:657
  37.2 0.5 collective-permute-done.2.refs_3_
  37.6 0.0 all-to-all-done.1.table_ref
  37.6 2.3 %shard_map.169 = (bf16[32,32,256]{2,1,0:T(8,128)(2,1)}, bf16[272,256]{1,0:T(8,128)(2,1)S(1)}) custom-call(s32[1]{0:T(128)} %get-tuple-element.24.flag_ref, s32[2]{0:T(128)S(1)} %pad_add_fusion.place_ref, f32[1024,256]{1,0:T(8,128)S(1)} %shard_map.168.part_ref, bf16[1024,256]{1,0:T(8,128)(2,1)S(1)} %get-tuple-element.28.ghost_ref, ...), custom_call_target="tpu_custom_call" | custom-call | tf_op jit(solution)/shard_map/pallas_call | solution.py:525
  39.9 0.0 copy-start
  39.9 3.9 %all-to-all-start.2 = ((bf16[32,32,256]{2,1,0:T(8,128)(2,1)}), bf16[32,32,256]{2,1,0:T(8,128)(2,1)S(1)}, u32[]{:S(2)}, u32[]{:S(2)}) async-start(bf16[32,32,256]{2,1,0:T(8,128)(2,1)} %get-tuple-element.38), calls=%async_computation.2 | async-start | bytes 1048576 | tf_op jit(solution)/shard_map/all_to_all | solution.py:681
  43.9 1.8 %collective-permute-start.3 = (bf16[272,256]{1,0:T(8,128)(2,1)S(1)}, bf16[272,256]{1,0:T(8,128)(2,1)S(1)}, u32[]{:S(2)}, u32[]{:S(2)}) collective-permute-start(bf16[272,256]{1,0:T(8,128)(2,1)S(1)} %get-tuple-element.35.token_ref.refs_0_), channel_id=1, source_target_pairs={{24,0},{28,4},{0,8},{4,12},{8,16},{12,20},{16,24},{20,28},{25,1},{... | collective-permute-start | bytes 417800 | tf_op jit(solution)/shard_map/ppermute | solution.py:690
  45.7 1.5 %collective-permute-start.4 = (bf16[272,256]{1,0:T(8,128)(2,1)S(1)}, bf16[272,256]{1,0:T(8,128)(2,1)S(1)}, u32[]{:S(2)}, u32[]{:S(2)}) collective-permute-start(bf16[272,256]{1,0:T(8,128)(2,1)S(1)} %get-tuple-element.35.token_ref.refs_0_), channel_id=1, source_target_pairs={{16,0},{20,4},{24,8},{28,12},{0,16},{4,20},{8,24},{12,28},{17,1},{... | collective-permute-start | bytes 417800 | tf_op jit(solution)/shard_map/ppermute | solution.py:690
  47.1 1.5 %collective-permute-start.5 = (bf16[272,256]{1,0:T(8,128)(2,1)S(1)}, bf16[272,256]{1,0:T(8,128)(2,1)S(1)}, u32[]{:S(2)}, u32[]{:S(2)}) collective-permute-start(bf16[272,256]{1,0:T(8,128)(2,1)S(1)} %get-tuple-element.35.token_ref.refs_0_), channel_id=1, source_target_pairs={{8,0},{12,4},{16,8},{20,12},{24,16},{28,20},{0,24},{4,28},{9,1},{1... | collective-permute-start | bytes 417800 | tf_op jit(solution)/shard_map/ppermute | solution.py:690
  48.6 2.3 %shard_map.170 = (bf16[2,1,1,1024,256]{4,3,2,1,0:T(8,128)(2,1)}, bf16[272,256]{1,0:T(8,128)(2,1)S(1)}) custom-call(s32[1]{0:T(128)} %get-tuple-element.24.flag_ref, bf16[272,256]{1,0:T(8,128)(2,1)S(1)} %get-tuple-element.35.token_ref.refs_0_, f32[1024,256]{1,0:T(8,128)S(1)} %shard_map.168.part_ref, bf16[1024,256]{1,0:T(8,128)(2,1)S(1)} %get-tuple-element.28.ghost_ref, ...), custom_call_target="tpu_custom_call" | custom-call | tf_op jit(solution)/shard_map/pallas_call | solution.py:525
  50.9 0.0 collective-permute-start.6
  50.9 4.5 %collective-permute-done.3.refs_1_ = bf16[272,256]{1,0:T(8,128)(2,1)S(1)} collective-permute-done((bf16[272,256]{1,0:T(8,128)(2,1)S(1)}, bf16[272,256]{1,0:T(8,128)(2,1)S(1)}, u32[]{:S(2)}, u32[]{:S(2)}) %collective-permute-start.3) | collective-permute-done | bytes 139296 | tf_op jit(solution)/shard_map/ppermute | solution.py:690
  55.4 0.0 copy-start.3
  55.4 0.0 collective-permute-start.7
  55.4 2.9 %collective-permute-done.4.refs_2_ = bf16[272,256]{1,0:T(8,128)(2,1)S(1)} collective-permute-done((bf16[272,256]{1,0:T(8,128)(2,1)S(1)}, bf16[272,256]{1,0:T(8,128)(2,1)S(1)}, u32[]{:S(2)}, u32[]{:S(2)}) %collective-permute-start.4) | collective-permute-done | bytes 139296 | tf_op jit(solution)/shard_map/ppermute | solution.py:690
  58.3 0.0 copy-start.4
  58.3 0.0 collective-permute-start.8
  58.3 0.0 collective-permute-done.5.refs_3_
  58.3 0.0 copy-start.5
  58.4 0.5 collective-permute-start.9
  58.8 0.0 collective-permute-done.6.refs_4_
  58.9 0.0 copy-start.6
  58.9 0.0 collective-permute-done.7.refs_5_
  58.9 0.0 copy-start.7
  58.9 0.8 %collective-permute-done.8.refs_6_ = bf16[272,256]{1,0:T(8,128)(2,1)S(1)} collective-permute-done((bf16[272,256]{1,0:T(8,128)(2,1)S(1)}, bf16[272,256]{1,0:T(8,128)(2,1)S(1)}, u32[]{:S(2)}, u32[]{:S(2)}) %collective-permute-start.8) | collective-permute-done | bytes 139296 | tf_op jit(solution)/shard_map/ppermute | solution.py:713
  59.7 0.0 copy-start.8
  59.7 0.2 collective-permute-done.9.refs_7_
  59.9 0.0 copy-start.9
  59.9 0.0 all-to-all-done.2.refs_8_
  59.9 0.0 copy-done
  59.9 0.0 copy-done.3
  59.9 0.0 copy-done.4
  59.9 0.0 copy-done.5
  59.9 0.0 copy-done.6
  59.9 0.0 copy-done.7
  60.0 0.4 copy-done.8
  60.4 0.2 copy-done.9
  60.6 16.6 %shard_map.171 = (f32[96,1024]{1,0:T(8,128)}, f32[128,1024]{1,0:T(8,128)}, f32[172,128]{1,0:T(8,128)}) custom-call(s32[2]{0:T(128)S(1)} %pad_add_fusion.place_ref, bf16[272,256]{1,0:T(8,128)(2,1)} %copy-done, bf16[272,256]{1,0:T(8,128)(2,1)} %copy-done.3, bf16[272,256]{1,0:T(8,128)(2,1)} %copy-done.4, bf16[272,256]{1,0:T(8,128)(2,1)} %copy-done.5, ...), custom_call_target="tpu_custom_call" | custom-call | tf_op jit(solution)/shard_map/pallas_call | solution.py:525
Async XLA Ops:
  0.6 14.3 %copy-start.1 = (s32[1,1,8,32]{3,2,1,0:T(8,128)S(1)}, s32[1,1,8,32]{3,2,1,0:T(8,128)}, u32[]{:S(2)}) copy-start(s32[1,1,8,32]{3,2,1,0:T(8,128)} %rows_hbm.1) | copy-start | bytes 3076
  0.6 14.3 %copy-start.2 = (s32[1,1,32]{2,1,0:T(1,128)S(1)}, s32[1,1,32]{2,1,0:T(1,128)}, u32[]{:S(2)}) copy-start(s32[1,1,32]{2,1,0:T(1,128)} %param.21) | copy-start | bytes 388
  3.1 11.8 %all-to-all-start = ((bf16[8,32,256]{2,1,0:T(8,128)(2,1)}), bf16[8,32,256]{2,1,0:T(8,128)(2,1)S(1)}, u32[]{:S(2)}, u32[]{:S(2)}) async-start(bf16[8,32,256]{2,1,0:T(8,128)(2,1)} %get-tuple-element.30), calls=%async_computation | async-start | bytes 262144 | tf_op jit(solution)/shard_map/all_to_all | solution.py:585
  17.2 20.4 %all-to-all-start.1 = ((bf16[8,32,256]{2,1,0:T(8,128)(2,1)}), bf16[8,32,256]{2,1,0:T(8,128)(2,1)S(1)}, u32[]{:S(2)}, u32[]{:S(2)}) async-start(bf16[8,32,256]{2,1,0:T(8,128)(2,1)} %get-tuple-element.33), calls=%async_computation.1 | async-start | bytes 262144 | tf_op jit(solution)/shard_map/all_to_all | solution.py:639
  27.6 8.0 %collective-permute-start = (bf16[80,256]{1,0:T(8,128)(2,1)S(1)}, bf16[80,256]{1,0:T(8,128)(2,1)S(1)}, u32[]{:S(2)}, u32[]{:S(2)}) collective-permute-start(bf16[80,256]{1,0:T(8,128)(2,1)S(1)} %get-tuple-element.34.refs_0_), channel_id=1, source_target_pairs={{1,0},{2,1},{3,2},{0,3},{5,4},{6,5},{7,6},{4,7},{9,8},{10,9},{11,1... | collective-permute-start | bytes 122888 | tf_op jit(solution)/shard_map/ppermute | solution.py:657
  31.8 5.3 %collective-permute-start.1 = (bf16[80,256]{1,0:T(8,128)(2,1)S(1)}, bf16[80,256]{1,0:T(8,128)(2,1)S(1)}, u32[]{:S(2)}, u32[]{:S(2)}) collective-permute-start(bf16[80,256]{1,0:T(8,128)(2,1)S(1)} %get-tuple-element.34.refs_0_), channel_id=1, source_target_pairs={{2,0},{3,1},{0,2},{1,3},{6,4},{7,5},{4,6},{5,7},{10,8},{11,9},{8,1... | collective-permute-start | bytes 122888 | tf_op jit(solution)/shard_map/ppermute | solution.py:657
  31.8 5.8 %collective-permute-start.2 = (bf16[80,256]{1,0:T(8,128)(2,1)S(1)}, bf16[80,256]{1,0:T(8,128)(2,1)S(1)}, u32[]{:S(2)}, u32[]{:S(2)}) collective-permute-start(bf16[80,256]{1,0:T(8,128)(2,1)S(1)} %get-tuple-element.34.refs_0_), channel_id=1, source_target_pairs={{3,0},{0,1},{1,2},{2,3},{7,4},{4,5},{5,6},{6,7},{11,8},{8,9},{9,10... | collective-permute-start | bytes 122888 | tf_op jit(solution)/shard_map/ppermute | solution.py:657
  39.9 20.0 %copy-start = (bf16[272,256]{1,0:T(8,128)(2,1)}, bf16[272,256]{1,0:T(8,128)(2,1)S(1)}, u32[]{:S(2)}) copy-start(bf16[272,256]{1,0:T(8,128)(2,1)S(1)} %get-tuple-element.35.token_ref.refs_0_) | copy-start | bytes 417796
  39.9 20.0 %all-to-all-start.2 = ((bf16[32,32,256]{2,1,0:T(8,128)(2,1)}), bf16[32,32,256]{2,1,0:T(8,128)(2,1)S(1)}, u32[]{:S(2)}, u32[]{:S(2)}) async-start(bf16[32,32,256]{2,1,0:T(8,128)(2,1)} %get-tuple-element.38), calls=%async_computation.2 | async-start | bytes 1048576 | tf_op jit(solution)/shard_map/all_to_all | solution.py:681
  43.9 11.6 %collective-permute-start.3 = (bf16[272,256]{1,0:T(8,128)(2,1)S(1)}, bf16[272,256]{1,0:T(8,128)(2,1)S(1)}, u32[]{:S(2)}, u32[]{:S(2)}) collective-permute-start(bf16[272,256]{1,0:T(8,128)(2,1)S(1)} %get-tuple-element.35.token_ref.refs_0_), channel_id=1, source_target_pairs={{24,0},{28,4},{0,8},{4,12},{8,16},{12,20},{16,24},{20,28},{25,1},{... | collective-permute-start | bytes 417800 | tf_op jit(solution)/shard_map/ppermute | solution.py:690
  45.7 12.6 %collective-permute-start.4 = (bf16[272,256]{1,0:T(8,128)(2,1)S(1)}, bf16[272,256]{1,0:T(8,128)(2,1)S(1)}, u32[]{:S(2)}, u32[]{:S(2)}) collective-permute-start(bf16[272,256]{1,0:T(8,128)(2,1)S(1)} %get-tuple-element.35.token_ref.refs_0_), channel_id=1, source_target_pairs={{16,0},{20,4},{24,8},{28,12},{0,16},{4,20},{8,24},{12,28},{17,1},{... | collective-permute-start | bytes 417800 | tf_op jit(solution)/shard_map/ppermute | solution.py:690
  47.1 11.2 %collective-permute-start.5 = (bf16[272,256]{1,0:T(8,128)(2,1)S(1)}, bf16[272,256]{1,0:T(8,128)(2,1)S(1)}, u32[]{:S(2)}, u32[]{:S(2)}) collective-permute-start(bf16[272,256]{1,0:T(8,128)(2,1)S(1)} %get-tuple-element.35.token_ref.refs_0_), channel_id=1, source_target_pairs={{8,0},{12,4},{16,8},{20,12},{24,16},{28,20},{0,24},{4,28},{9,1},{1... | collective-permute-start | bytes 417800 | tf_op jit(solution)/shard_map/ppermute | solution.py:690
  50.9 7.9 %collective-permute-start.6 = (bf16[272,256]{1,0:T(8,128)(2,1)S(1)}, bf16[272,256]{1,0:T(8,128)(2,1)S(1)}, u32[]{:S(2)}, u32[]{:S(2)}) collective-permute-start(bf16[272,256]{1,0:T(8,128)(2,1)S(1)} %get-tuple-element.37), channel_id=1, source_target_pairs={{0,4},{4,0},{8,12},{12,8},{16,20},{20,16},{24,28},{28,24},{1,5},{5... | collective-permute-start | bytes 417800 | tf_op jit(solution)/shard_map/ppermute | solution.py:713
  55.4 4.5 %copy-start.3 = (bf16[272,256]{1,0:T(8,128)(2,1)}, bf16[272,256]{1,0:T(8,128)(2,1)S(1)}, u32[]{:S(2)}) copy-start(bf16[272,256]{1,0:T(8,128)(2,1)S(1)} %collective-permute-done.3.refs_1_) | copy-start | bytes 417796
  55.4 3.4 %collective-permute-start.7 = (bf16[272,256]{1,0:T(8,128)(2,1)S(1)}, bf16[272,256]{1,0:T(8,128)(2,1)S(1)}, u32[]{:S(2)}, u32[]{:S(2)}) collective-permute-start(bf16[272,256]{1,0:T(8,128)(2,1)S(1)} %collective-permute-done.3.refs_1_), channel_id=1, source_target_pairs={{0,4},{4,0},{8,12},{12,8},{16,20},{20,16},{24,28},{28,24},{1,5},{5... | collective-permute-start | bytes 417800 | tf_op jit(solution)/shard_map/ppermute | solution.py:713
  58.3 1.6 %copy-start.4 = (bf16[272,256]{1,0:T(8,128)(2,1)}, bf16[272,256]{1,0:T(8,128)(2,1)S(1)}, u32[]{:S(2)}) copy-start(bf16[272,256]{1,0:T(8,128)(2,1)S(1)} %collective-permute-done.4.refs_2_) | copy-start | bytes 417796
  58.3 1.4 %collective-permute-start.8 = (bf16[272,256]{1,0:T(8,128)(2,1)S(1)}, bf16[272,256]{1,0:T(8,128)(2,1)S(1)}, u32[]{:S(2)}, u32[]{:S(2)}) collective-permute-start(bf16[272,256]{1,0:T(8,128)(2,1)S(1)} %collective-permute-done.4.refs_2_), channel_id=1, source_target_pairs={{0,4},{4,0},{8,12},{12,8},{16,20},{20,16},{24,28},{28,24},{1,5},{5... | collective-permute-start | bytes 417800 | tf_op jit(solution)/shard_map/ppermute | solution.py:713
  58.3 1.6 %copy-start.5 = (bf16[272,256]{1,0:T(8,128)(2,1)}, bf16[272,256]{1,0:T(8,128)(2,1)S(1)}, u32[]{:S(2)}) copy-start(bf16[272,256]{1,0:T(8,128)(2,1)S(1)} %collective-permute-done.5.refs_3_) | copy-start | bytes 417796
  58.4 1.5 %collective-permute-start.9 = (bf16[272,256]{1,0:T(8,128)(2,1)S(1)}, bf16[272,256]{1,0:T(8,128)(2,1)S(1)}, u32[]{:S(2)}, u32[]{:S(2)}) collective-permute-start(bf16[272,256]{1,0:T(8,128)(2,1)S(1)} %collective-permute-done.5.refs_3_), channel_id=1, source_target_pairs={{0,4},{4,0},{8,12},{12,8},{16,20},{20,16},{24,28},{28,24},{1,5},{5... | collective-permute-start | bytes 417800 | tf_op jit(solution)/shard_map/ppermute | solution.py:713
  58.9 1.1 %copy-start.6 = (bf16[272,256]{1,0:T(8,128)(2,1)}, bf16[272,256]{1,0:T(8,128)(2,1)S(1)}, u32[]{:S(2)}) copy-start(bf16[272,256]{1,0:T(8,128)(2,1)S(1)} %collective-permute-done.6.refs_4_) | copy-start | bytes 417796
  58.9 1.1 %copy-start.7 = (bf16[272,256]{1,0:T(8,128)(2,1)}, bf16[272,256]{1,0:T(8,128)(2,1)S(1)}, u32[]{:S(2)}) copy-start(bf16[272,256]{1,0:T(8,128)(2,1)S(1)} %collective-permute-done.7.refs_5_) | copy-start | bytes 417796
  59.7 0.7 copy-start.8
  59.9 0.7 copy-start.9

commit v7 on v6

--- a/solution.py
+++ b/solution.py
@@ -164,7 +164,8 @@
             spots.append(jnp.where(ids == tall, one, zero))
         low = low_ref[tile]
         low_hot = jnp.concatenate([jnp.where(low == ids, one, zero) for ids in lanes], 1)
-        return dot(jnp.concatenate(spots, 0), low_hot)
+        spot_hot = jnp.concatenate(spots, 0)
+        return dot(spot_hot.astype(jnp.float8_e4m3fn), low_hot.astype(jnp.float8_e4m3fn))
 
     def turn(add, step, carry):
         first = step * GROUP
@@ -296,11 +297,9 @@
     table_ref,
     start_ref,
     out_ref,
-    again_ref,
     sums_ref,
     rest_ref,
 ):
-    again_ref[...] = token_ref[...]
     table = table_ref[...].reshape(-1, out_ref.shape[-1])
     aggregate(flag_ref, part_ref[...], ghost_ref[...], rest_hbm, table, sums_ref, rest_ref)
     out_ref[0, 0, 0] = start_ref[...]
@@ -341,6 +340,7 @@
     g_first_ref,
     g_second_ref,
     g_third_ref,
+    send_ref,
     side_refs,
     w_first_ref,
     w_second_ref,
@@ -408,16 +408,14 @@
         for hop, ref in enumerate((zero_ref, one_ref)):
             in_ref[:, hop * width : (hop + 1) * width] = ref[...].reshape(-1, width)
     else:
-        parts = len(side_refs)
+        chips = len(side_refs)
         copies = fetch(tuple(zip(sides_hbm, side_refs)) + pairs[:1], sems)
-        for copy in copies[:parts]:
+        for copy in copies[:chips]:
             copy.wait()
-        groups = two_ref.shape[0] // parts
+        groups = two_ref.shape[0] // chips
         rows = groups * train
-        chips = parts // 2
-        for at, ref in enumerate(side_refs):
-            core = place % 2 if at < chips else 1 - place % 2
-            part = 2 * lax.rem(place // 2 - at % chips + chips, chips) + core
+        for shift, ref in enumerate(side_refs):
+            part = lax.rem(place // 2 - shift + chips, chips)
             at = pl.multiple_of(part * rows, rows)
             for group in range(groups):
                 for hop in range(2):
@@ -427,12 +425,12 @@
                     ]
             turn_ref[pl.ds(pl.multiple_of(part * 16, 16), 16), :] = ref[2 * rows :, :128].astype(f32)
         turned = turn_ref[...].T
-        for part in range(parts):
+        for part in range(chips):
             for group in range(groups):
                 column((part * groups + group) * train, turned, part * 16 + group)
     in_ref[:, 2 * width :] = two_ref[...].reshape(-1, width)
     if not many:
-        copies[parts].wait()
+        copies[chips].wait()
         copies = fetch(pairs[1:], sems)
 
     def activate(values, h_ref, slope_ref, rows):
@@ -495,17 +493,43 @@
     )
     factor = clip_bound / jnp.maximum(norm, clip_bound)
 
-    def left(ref, share):
-        return (shares(ref, place * share, share) * factor).astype(bf16)
-
     if not many:
         for copy in copies[2:]:
             copy.wait()
         set_noise()
-    share = g_second_ref.shape[0]
-    g_first_ref[...] += dot_tn(left(in_ref, g_first_ref.shape[0]), d_one_ref[...])
-    g_second_ref[...] += dot_tn(left(h_one_ref, share), d_two_ref[...])
-    g_third_ref[...] += dot_tn(d_three, left(h_two_ref, share))[:classes, :]
+    share_one, share = g_first_ref.shape[0], g_second_ref.shape[0]
+    places = [place] if many else [place, place + 1 - 2 * (place % 2)]
+
+    def left(ref, share):
+        picked = [shares(ref, at * share, share) for at in places]
+        return (jnp.concatenate(picked, 1) * factor).astype(bf16)
+
+    sum_one = dot_tn(left(in_ref, share_one), d_one_ref[...])
+    sum_two = dot_tn(left(h_one_ref, share), d_two_ref[...])
+    sum_three = dot_tn(d_three, left(h_two_ref, share))
+    g_first_ref[...] += sum_one[:share_one]
+    g_second_ref[...] += sum_two[:share]
+    g_third_ref[...] += sum_three[:classes, :share]
+    if not many:
+        send_ref[:share_one, :] = sum_one[share_one:].astype(bf16)
+        send_ref[share_one : share_one + share, :] = sum_two[share:].astype(bf16)
+        first = share_one + share
+        for at in range(0, classes, 32):
+            cols = slice(at // 32 * share, (at // 32 + 1) * share)
+            send_ref[first : first + 32, cols] = sum_three[at : at + 32, share:].astype(bf16)
+
+
+def finish_kernel(got_ref, one_ref, two_ref, three_ref, g_first_ref, g_second_ref, g_third_ref):
+    share_one, share = one_ref.shape[0], two_ref.shape[0]
+    g_first_ref[...] = one_ref[...] + got_ref[:share_one, :].astype(f32)
+    g_second_ref[...] = two_ref[...] + got_ref[share_one : share_one + share, :].astype(f32)
+    first = share_one + share
+    classes = three_ref.shape[0]
+    for at in range(0, classes, 32):
+        size = min(32, classes - at)
+        cols = slice(at // 32 * share, (at // 32 + 1) * share)
+        got = got_ref[first : first + 32, cols].astype(f32)
+        g_third_ref[at : at + size, :] = three_ref[at : at + size, :] + got[:size]
 
 
 def call(kernel, mib, outs, ins, scratch):
@@ -533,6 +557,7 @@
 
 
 def local(
+    axes,
     feats,
     hop_noise,
     send_rows,
@@ -561,10 +586,10 @@
     rows = send_rows.reshape(parts, each)
     turn = VMEM((128, 128), jnp.int32)
     pick = VMEM((ghosts, nodes), bf16)
-    axes = ("dom", "grp")
+    dom = axes[:-1]
     members = lax.axis_size(axes)
-    few = members <= FEW and parts <= 8 and parts % 2 == 0
-    copies = members if few else 1
+    few = len(axes) == 3
+    copies = members // 2 if few else 1
 
     def every(value, *names):
         for name in names:
@@ -582,7 +607,7 @@
         [(feats, HBM), (send_rows, HBM)],
         [VMEM((nodes, width), bf16), VMEM((parts, each), jnp.int32), turn, pick, DMA((2,))],
     )
-    table0 = lax.all_to_all(out0, "dom", split_axis=0, concat_axis=0, tiled=True)
+    table0 = lax.all_to_all(out0, dom, split_axis=0, concat_axis=0, tiled=True)
     own, ghost, part1, flag, own_rest, ghost_rest = call(
         build_kernel,
         28,
@@ -636,7 +661,7 @@
         ],
         [VMEM((nodes, width), f32), VMEM((nodes, ghosts), bf16), turn, pick],
     )
-    table1 = lax.all_to_all(out1, "dom", split_axis=0, concat_axis=0, tiled=True)
+    table1 = lax.all_to_all(out1, dom, split_axis=0, concat_axis=0, tiled=True)
     (part2,) = call(
         own_kernel,
         16,
@@ -649,7 +674,7 @@
             DMA((2,)),
         ],
     )
-    place = jnp.stack([lax.axis_index("dom"), lax.axis_index("grp")]).astype(jnp.int32)
+    place = jnp.stack([lax.axis_index(dom), lax.axis_index("grp")]).astype(jnp.int32)
     grp = lax.axis_size("grp")
 
     def shifted(value, name, size, step):
@@ -678,25 +703,17 @@
         [VMEM((train, width), f32), VMEM((train, ghosts), bf16), VMEM((128, 128), f32)],
     )
     if few:
-        every2 = lax.all_to_all(last, axes, split_axis=0, concat_axis=0, tiled=True)
-        chips = parts // 2
-        sides = [side]
-        for shift in range(1, chips):
-            pairs = [
-                (2 * ((chip - shift) % chips) + core, 2 * chip + core)
-                for chip in range(chips)
-                for core in range(2)
-            ]
-            sides.append(lax.ppermute(side, "dom", pairs))
+        every2 = lax.all_to_all(last, ("chip", "grp"), split_axis=0, concat_axis=0, tiled=True)
+        sides = [side] + shifted(side, "chip", parts // 2, -1)
     else:
         every0, every1, every2 = (
             every(value, axes) for value in (own0[None], start1[None, :train], last)
         )
         every_label = every(labels.reshape(1, train), axes)
-    hop_feats, again = call(
+    (hop_feats,) = call(
         last_kernel,
         12,
-        [((2, 1, 1, nodes, width), bf16, VMEM), (side.shape, bf16, None)],
+        [((2, 1, 1, nodes, width), bf16, VMEM)],
         [
             (flag, SMEM),
             (side, None),
@@ -708,10 +725,7 @@
         ],
         [VMEM((nodes, width), f32), VMEM((nodes, ghosts), bf16)],
     )
-    if few:
-        swap = [(at, at ^ 1) for at in range(parts)]
-        sides += [lax.ppermute(value, "dom", swap) for value in [again] + sides[1:]]
-    chunk = train * min(members, 32)
+    chunk = train * (copies if few else min(members, 32))
     groups = chunk // train
     wide = (classes + 255) // 256 * 256
     fixed = (w_first, w_second, w_third.T, noise_first, noise_second, noise_third.T)
@@ -731,23 +745,33 @@
         DMA((16,)),
     ]
     if few:
+        chips = parts // 2
 
         def classify(place_ref, *refs):
-            sides_in, rest = refs[:parts], refs[parts:]
-            outs, rest, held = rest[:10], rest[10 + parts :], rest[10 : 10 + parts]
+            sides_in, rest = refs[:chips], refs[chips:]
+            outs, held, rest = rest[:11], rest[11 : 11 + chips], rest[11 + chips :]
             classify_kernel(
                 False, place_ref, None, None, None, outs[0], sides_in, *outs[1:], held, *rest
             )
 
-        first, second, third = call(
+        rows = noise_first.shape[0] + noise_second.shape[0] + 32
+        *own_sums, other = call(
             classify,
             44,
-            [(value.shape, f32, VMEM) for value in fixed[3:]],
+            [(value.shape, f32, None) for value in fixed[3:]] + [((rows, hid), bf16, None)],
             [(place, SMEM)]
             + [(value, HBM) for value in sides]
             + [(every2, None)]
             + [(value, HBM) for value in fixed],
             [VMEM(value.shape, bf16) for value in sides] + scratch,
+        )
+        got = lax.ppermute(other, "core", [(0, 1), (1, 0)])
+        first, second, third = call(
+            finish_kernel,
+            16,
+            [(value.shape, f32, VMEM) for value in fixed[3:]],
+            [(got, None)] + [(value, None) for value in own_sums],
+            [],
         )
     else:
 
@@ -763,6 +787,7 @@
                 two_ref,
                 None,
                 *rest[:9],
+                None,
                 None,
                 *rest[9:],
             )
@@ -790,21 +815,33 @@
 
 
 def solution(mesh):
+    dom, grp = mesh.shape["dom"], mesh.shape["grp"]
+    names = ("dom", "grp")
+    if dom * grp <= FEW and dom <= 8 and dom % 2 == 0:
+        names = ("chip", "core", "grp")
+        mesh = jax.sharding.Mesh(mesh.devices.reshape(dom // 2, 2, grp), names)
+    doms, grps = names[:-1], "grp"
     in_specs = (
-        P("dom", "grp", None, None),
-        P(None, "dom", "grp", None, None),
-        P("dom", "grp", None, None),
-        P("dom", "grp", None),
-        P("dom", "grp", None, None),
-        P("dom", "grp", None, None),
-        P("dom", "grp"),
-        P("dom", "grp", None),
+        P(doms, grps, None, None),
+        P(None, doms, grps, None, None),
+        P(doms, grps, None, None),
+        P(doms, grps, None),
+        P(doms, grps, None, None),
+        P(doms, grps, None, None),
+        P(doms, grps),
+        P(doms, grps, None),
         P(),
         P(),
         P(),
-        P("dom", None),
-        P("dom", None),
-        P("dom", None),
-    )
-    out_specs = (P(None, "dom", "grp", None, None), P("dom", None), P("dom", None), P("dom", None))
-    return jax.shard_map(local, mesh=mesh, in_specs=in_specs, out_specs=out_specs, check_vma=False)
+        P(doms, None),
+        P(doms, None),
+        P(doms, None),
+    )
+    out_specs = (P(None, doms, grps, None, None), P(doms, None), P(doms, None), P(doms, None))
+    return jax.shard_map(
+        functools.partial(local, names),
+        mesh=mesh,
+        in_specs=in_specs,
+        out_specs=out_specs,
+        check_vma=False,
+    )

time: 77.6 us -> 69.8 us (0.90); the launches traced: 77.3 us -> 68.8 us
  Pallas kernels: 35 us -> 30.2 us
  starting transfers between devices: 29.6 us -> 26.8 us
  waiting for transfers between devices: 10.4 us -> 8.69 us
  local copies, waits for them, and re-layouts: 0.64 us -> 1.59 us
    ppermute x7 -> x1, waiting for transfers between devices: 8.41 us -> 0.01 us  [local(): got = lax.ppermute(other, 'core', [(0, 1), (1, 0)])]
    ppermute x3 -> x6, starting transfers between devices: 4.84 us -> 12.3 us  [shifted(): lax.ppermute(value, name, [((at + step * shift) % size, at) for at in ran...]
    ppermute x3 -> x6, waiting for transfers between devices: 2.03 us -> 8.68 us  [shifted(): lax.ppermute(value, name, [((at + step * shift) % size, at) for at in ran...]
    ppermute x7 -> x1, starting transfers between devices: 5.25 us -> 0.07 us  [local(): got = lax.ppermute(other, 'core', [(0, 1), (1, 0)])]
    all_to_all x3, starting transfers between devices: 19.5 us -> 14.4 us  [the longest x1 5.18 us: local(): table0 = lax.all_to_all(out0, dom, split_axis=0, concat_axis=0, tiled=True)]
    pallas_call x7 -> x8, Pallas kernels: 35 us -> 30.2 us  [call(): pl.pallas_call(kernel, out_shape=[shape_of(*out) for out in outs], in_spe...]
    unnamed x20 -> x14, local copies, waits for them, and re-layouts: 0.64 us -> 1.59 us
  transfers between devices with their start and end apart: 13 -> 10, of which waited for: 6 -> 4; matrix products, arithmetic and copies ran while one was open for 0% -> 0% of each run, Pallas kernels for 15% -> 18%
where the time goes in v7:
time: 69.8 us; the launch traced here: 68.8 us
  Pallas kernels  30.2 us (43%)
  starting transfers between devices  26.8 us (38%)
  waiting for transfers between devices  8.69 us (12%)
  local copies, waits for them, and re-layouts  1.59 us (2%)
  between operations  1.42 us (2%)
    pallas_call x8, Pallas kernels, call(): pl.pallas_call(kernel, out_shape=[shape_of(*out) for out in outs], in_spe...  30.2 us
    ppermute x6, starting transfers between devices, shifted(): lax.ppermute(value, name, [((at + step * shift) % size, at) for at in ran...  12.3 us
    ppermute x6, waiting for transfers between devices, shifted(): lax.ppermute(value, name, [((at + step * shift) % size, at) for at in ran...  8.68 us
    all_to_all x1, starting transfers between devices, local(): table0 = lax.all_to_all(out0, dom, split_axis=0, concat_axis=0, tiled=True)  5.18 us
    all_to_all x1, starting transfers between devices, local(): lax.all_to_all(last, ('chip', 'grp'), split_axis=0, concat_axis=0, tiled=...  4.93 us
    all_to_all x1, starting transfers between devices, local(): table1 = lax.all_to_all(out1, dom, split_axis=0, concat_axis=0, tiled=True)  4.32 us
    unnamed x14, local copies, waits for them, and re-layouts  1.59 us
  transfers between devices with their start and end apart: 10, of which 4 were waited for; matrix products, arithmetic and copies ran while one was open for 0% of the time, Pallas kernels for 18%

profile of v7, /device:TPU:0, one launch (start us, length us, event | category | flops | bytes accessed | tf_op | source)
XLA Modules:
  0.0 68.8 jit_solution(1962031904898538377)
XLA Ops:
  0.6 0.0 copy-start.2
  0.6 0.0 copy-start.3
  0.7 2.4 %shard_map.165 = (bf16[1024,256]{1,0:T(8,128)(2,1)S(1)}, bf16[8,32,256]{2,1,0:T(8,128)(2,1)}, bf16[32,256]{1,0:T(8,128)(2,1)S(1)}) custom-call(bf16[1,1,1024,256]{3,2,1,0:T(8,128)(2,1)} %feats_hbm.1, s32[1,1,8,32]{3,2,1,0:T(8,128)} %rows_hbm.1), custom_call_target="tpu_custom_call" | custom-call | tf_op jit(solution)/shard_map/pallas_call | solution.py:549
  3.1 5.2 %all-to-all-start = ((bf16[8,32,256]{2,1,0:T(8,128)(2,1)}), bf16[8,32,256]{2,1,0:T(8,128)(2,1)S(1)}, u32[]{:S(2)}, u32[]{:S(2)}) async-start(bf16[8,32,256]{2,1,0:T(8,128)(2,1)} %get-tuple-element.32), calls=%async_computation | async-start | bytes 262144 | tf_op jit(solution)/shard_map/all_to_all | solution.py:610
  8.9 7.3 %shard_map.166 = (bf16[1024,1024]{1,0:T(8,128)(2,1)}, bf16[1024,256]{1,0:T(8,128)(2,1)S(1)}, f32[1024,256]{1,0:T(8,128)S(1)}, s32[1]{0:T(128)}, bf16[1024,1024]{1,0:T(8,128)(2,1)}, /*index=5*/bf16[1024,256]{1,0:T(8,128)(2,1)}) custom-call(s32[1,1,64]{2,1,0:T(1,128)} %blocks_hbm.1, s32[1,1]{1,0:T(1,128)S(6)} %copy.18.count_ref, s32[1,1,64,256]{3,2,1,0:T(8,128)} %src_hbm.1, ...), custom_call_target="tpu_custom_call" | custom-call | tf_op jit(solution)/shard_map/pallas_call | solution.py:549
  16.2 0.0 all-to-all-done.table_ref
  16.2 0.0 copy-done.2
  16.2 0.0 copy-done.3
  16.3 2.3 %shard_map.167 = (bf16[1024,256]{1,0:T(8,128)(2,1)S(1)}, bf16[8,32,256]{2,1,0:T(8,128)(2,1)}, bf16[80,256]{1,0:T(8,128)(2,1)S(1)}) custom-call(s32[1]{0:T(128)} %get-tuple-element.26.flag_ref, f32[1024,256]{1,0:T(8,128)S(1)} %get-tuple-element.29.part_ref, bf16[1024,256]{1,0:T(8,128)(2,1)S(1)} %get-tuple-element.30.ghost_ref, ...), custom_call_target="tpu_custom_call" | custom-call | tf_op jit(solution)/shard_map/pallas_call | solution.py:549
  18.6 4.3 %all-to-all-start.1 = ((bf16[8,32,256]{2,1,0:T(8,128)(2,1)}), bf16[8,32,256]{2,1,0:T(8,128)(2,1)S(1)}, u32[]{:S(2)}, u32[]{:S(2)}) async-start(bf16[8,32,256]{2,1,0:T(8,128)(2,1)} %get-tuple-element.35), calls=%async_computation.1 | async-start | bytes 262144 | tf_op jit(solution)/shard_map/all_to_all | solution.py:664
  22.9 6.8 %collective-permute-start = (bf16[80,256]{1,0:T(8,128)(2,1)S(1)}, bf16[80,256]{1,0:T(8,128)(2,1)S(1)}, u32[]{:S(2)}, u32[]{:S(2)}) collective-permute-start(bf16[80,256]{1,0:T(8,128)(2,1)S(1)} %get-tuple-element.36.refs_0_), channel_id=1, source_target_pairs={{1,0},{2,1},{3,2},{0,3},{5,4},{6,5},{7,6},{4,7},{9,8},{10,9},{11,1... | collective-permute-start | bytes 122888 | tf_op jit(solution)/shard_map/ppermute | solution.py:682
  29.7 0.0 collective-permute-start.1
  29.7 0.6 collective-permute-start.2
  30.3 0.1 pad_add_fusion.place_ref
  30.4 3.0 %shard_map.168.part_ref = f32[1024,256]{1,0:T(8,128)S(1)} custom-call(s32[1]{0:T(128)} %get-tuple-element.26.flag_ref, bf16[1024,1024]{1,0:T(8,128)(2,1)} %get-tuple-element.27.own_hbm, bf16[1024,1024]{1,0:T(8,128)(2,1)} %get-tuple-element.28.rest_hbm, bf16[2,1,1,1024,256]{4,3,2,1,0:T(8,128)(2,1)} %noise_hbm.3, bf16[1024,256]{1,0:T(8,128)(2,1)S(1)} %get-tuple-element.34.start_ref), custom_call_target="tpu_custom_call" | custom-call | tf_op jit(solution)/shard_map/pallas_call | solution.py:549
  33.5 0.0 collective-permute-done.refs_1_
  33.5 1.6 %collective-permute-done.1.refs_2_ = bf16[80,256]{1,0:T(8,128)(2,1)S(1)} collective-permute-done((bf16[80,256]{1,0:T(8,128)(2,1)S(1)}, bf16[80,256]{1,0:T(8,128)(2,1)S(1)}, u32[]{:S(2)}, u32[]{:S(2)}) %collective-permute-start.1) | collective-permute-done | bytes 40992 | tf_op jit(solution)/shard_map/ppermute | solution.py:682
  35.0 0.5 collective-permute-done.2.refs_3_
  35.5 0.0 all-to-all-done.1.table_ref
  35.5 2.2 %shard_map.169 = (bf16[16,32,256]{2,1,0:T(8,128)(2,1)}, bf16[272,256]{1,0:T(8,128)(2,1)S(1)}) custom-call(s32[1]{0:T(128)} %get-tuple-element.26.flag_ref, s32[2]{0:T(128)S(1)} %pad_add_fusion.place_ref, f32[1024,256]{1,0:T(8,128)S(1)} %shard_map.168.part_ref, bf16[1024,256]{1,0:T(8,128)(2,1)S(1)} %get-tuple-element.30.ghost_ref, ...), custom_call_target="tpu_custom_call" | custom-call | tf_op jit(solution)/shard_map/pallas_call | solution.py:549
  37.7 0.0 copy-start
  37.7 4.9 %all-to-all-start.2 = ((bf16[16,32,256]{2,1,0:T(8,128)(2,1)}), bf16[16,32,256]{2,1,0:T(8,128)(2,1)S(1)}, u32[]{:S(2)}, u32[]{:S(2)}) async-start(bf16[16,32,256]{2,1,0:T(8,128)(2,1)} %get-tuple-element.38), calls=%async_computation.2 | async-start | bytes 524288 | tf_op jit(solution)/shard_map/all_to_all | solution.py:706
  42.6 1.9 %collective-permute-start.3 = (bf16[272,256]{1,0:T(8,128)(2,1)S(1)}, bf16[272,256]{1,0:T(8,128)(2,1)S(1)}, u32[]{:S(2)}, u32[]{:S(2)}) collective-permute-start(bf16[272,256]{1,0:T(8,128)(2,1)S(1)} %get-tuple-element.37.token_ref.refs_0_), channel_id=1, source_target_pairs={{24,0},{0,8},{8,16},{16,24},{25,1},{1,9},{9,17},{17,25},{26,2},{2,... | collective-permute-start | bytes 417800 | tf_op jit(solution)/shard_map/ppermute | solution.py:682
  44.5 1.5 %collective-permute-start.4 = (bf16[272,256]{1,0:T(8,128)(2,1)S(1)}, bf16[272,256]{1,0:T(8,128)(2,1)S(1)}, u32[]{:S(2)}, u32[]{:S(2)}) collective-permute-start(bf16[272,256]{1,0:T(8,128)(2,1)S(1)} %get-tuple-element.37.token_ref.refs_0_), channel_id=1, source_target_pairs={{16,0},{24,8},{0,16},{8,24},{17,1},{25,9},{1,17},{9,25},{18,2},{26... | collective-permute-start | bytes 417800 | tf_op jit(solution)/shard_map/ppermute | solution.py:682
  46.0 1.5 %collective-permute-start.5 = (bf16[272,256]{1,0:T(8,128)(2,1)S(1)}, bf16[272,256]{1,0:T(8,128)(2,1)S(1)}, u32[]{:S(2)}, u32[]{:S(2)}) collective-permute-start(bf16[272,256]{1,0:T(8,128)(2,1)S(1)} %get-tuple-element.37.token_ref.refs_0_), channel_id=1, source_target_pairs={{8,0},{16,8},{24,16},{0,24},{9,1},{17,9},{25,17},{1,25},{10,2},{18... | collective-permute-start | bytes 417800 | tf_op jit(solution)/shard_map/ppermute | solution.py:682
  47.5 5.0 %collective-permute-done.3.refs_1_ = bf16[272,256]{1,0:T(8,128)(2,1)S(1)} collective-permute-done((bf16[272,256]{1,0:T(8,128)(2,1)S(1)}, bf16[272,256]{1,0:T(8,128)(2,1)S(1)}, u32[]{:S(2)}, u32[]{:S(2)}) %collective-permute-start.3) | collective-permute-done | bytes 139296 | tf_op jit(solution)/shard_map/ppermute | solution.py:682
  52.5 0.0 copy-start.4
  52.5 1.6 %collective-permute-done.4.refs_2_ = bf16[272,256]{1,0:T(8,128)(2,1)S(1)} collective-permute-done((bf16[272,256]{1,0:T(8,128)(2,1)S(1)}, bf16[272,256]{1,0:T(8,128)(2,1)S(1)}, u32[]{:S(2)}, u32[]{:S(2)}) %collective-permute-start.4) | collective-permute-done | bytes 139296 | tf_op jit(solution)/shard_map/ppermute | solution.py:682
  54.1 0.0 copy-start.5
  54.1 0.0 collective-permute-done.5.refs_3_
  54.1 0.0 copy-start.6
  54.1 0.0 all-to-all-done.2.refs_4_
  54.1 0.0 copy-done
  54.1 0.0 copy-done.4
  54.2 0.6 copy-done.5
  54.8 0.1 copy-done.6
  54.8 9.7 %shard_map.171 = (f32[96,1024]{1,0:T(8,128)S(1)}, f32[128,1024]{1,0:T(8,128)S(1)}, f32[172,128]{1,0:T(8,128)S(1)}, bf16[256,1024]{1,0:T(8,128)(2,1)S(1)}) custom-call(s32[2]{0:T(128)S(1)} %pad_add_fusion.place_ref, bf16[272,256]{1,0:T(8,128)(2,1)} %copy-done, bf16[272,256]{1,0:T(8,128)(2,1)} %copy-done.4, bf16[272,256]{1,0:T(8,128)(2,1)} %copy-done.5, ...), custom_call_target="tpu_custom_call" | custom-call | tf_op jit(solution)/shard_map/pallas_call | solution.py:549
  64.6 0.1 collective-permute-start.6
  64.6 0.0 copy-start.1
  64.7 0.9 %copy-done.1 = bf16[272,256]{1,0:T(8,128)(2,1)S(1)} copy-done((bf16[272,256]{1,0:T(8,128)(2,1)S(1)}, bf16[272,256]{1,0:T(8,128)(2,1)}, u32[]{:S(2)}) %copy-start.1) | copy-done | bytes 139288
  65.6 2.1 %shard_map.170 = bf16[2,1,1,1024,256]{4,3,2,1,0:T(8,128)(2,1)} custom-call(s32[1]{0:T(128)} %get-tuple-element.26.flag_ref, bf16[272,256]{1,0:T(8,128)(2,1)S(1)} %copy-done.1, f32[1024,256]{1,0:T(8,128)S(1)} %shard_map.168.part_ref, bf16[1024,256]{1,0:T(8,128)(2,1)S(1)} %get-tuple-element.30.ghost_ref, bf16[1024,256]{1,0:T(8,128)(2,1)} %get-tuple-element.31.rest_hbm, ...), custom_call_target="tpu_custom_call" | custom-call | tf_op jit(solution)/shard_map/pallas_call | solution.py:549
  67.7 0.0 collective-permute-done.6.got_ref
  67.7 1.1 %shard_map.172 = (f32[96,1024]{1,0:T(8,128)}, f32[128,1024]{1,0:T(8,128)}, f32[172,128]{1,0:T(8,128)}) custom-call(bf16[256,1024]{1,0:T(8,128)(2,1)S(1)} %collective-permute-done.6.got_ref, f32[96,1024]{1,0:T(8,128)S(1)} %get-tuple-element.40.one_ref, f32[128,1024]{1,0:T(8,128)S(1)} %get-tuple-element.41.two_ref, f32[172,128]{1,0:T(8,128)S(1)} %get-tuple-element.42.three_ref), custom_call_target="tpu_custom_call" | custom-call | tf_op jit(solution)/shard_map/pallas_call | solution.py:549
Async XLA Ops:
  0.6 15.6 %copy-start.2 = (s32[1,1,8,32]{3,2,1,0:T(8,128)S(1)}, s32[1,1,8,32]{3,2,1,0:T(8,128)}, u32[]{:S(2)}) copy-start(s32[1,1,8,32]{3,2,1,0:T(8,128)} %rows_hbm.1) | copy-start | bytes 3076
  0.6 15.6 %copy-start.3 = (s32[1,1,32]{2,1,0:T(1,128)S(1)}, s32[1,1,32]{2,1,0:T(1,128)}, u32[]{:S(2)}) copy-start(s32[1,1,32]{2,1,0:T(1,128)} %param.21) | copy-start | bytes 388
  3.1 13.1 %all-to-all-start = ((bf16[8,32,256]{2,1,0:T(8,128)(2,1)}), bf16[8,32,256]{2,1,0:T(8,128)(2,1)S(1)}, u32[]{:S(2)}, u32[]{:S(2)}) async-start(bf16[8,32,256]{2,1,0:T(8,128)(2,1)} %get-tuple-element.32), calls=%async_computation | async-start | bytes 262144 | tf_op jit(solution)/shard_map/all_to_all | solution.py:610
  18.6 17.0 %all-to-all-start.1 = ((bf16[8,32,256]{2,1,0:T(8,128)(2,1)}), bf16[8,32,256]{2,1,0:T(8,128)(2,1)S(1)}, u32[]{:S(2)}, u32[]{:S(2)}) async-start(bf16[8,32,256]{2,1,0:T(8,128)(2,1)} %get-tuple-element.35), calls=%async_computation.1 | async-start | bytes 262144 | tf_op jit(solution)/shard_map/all_to_all | solution.py:664
  22.9 10.6 %collective-permute-start = (bf16[80,256]{1,0:T(8,128)(2,1)S(1)}, bf16[80,256]{1,0:T(8,128)(2,1)S(1)}, u32[]{:S(2)}, u32[]{:S(2)}) collective-permute-start(bf16[80,256]{1,0:T(8,128)(2,1)S(1)} %get-tuple-element.36.refs_0_), channel_id=1, source_target_pairs={{1,0},{2,1},{3,2},{0,3},{5,4},{6,5},{7,6},{4,7},{9,8},{10,9},{11,1... | collective-permute-start | bytes 122888 | tf_op jit(solution)/shard_map/ppermute | solution.py:682
  29.7 5.3 %collective-permute-start.1 = (bf16[80,256]{1,0:T(8,128)(2,1)S(1)}, bf16[80,256]{1,0:T(8,128)(2,1)S(1)}, u32[]{:S(2)}, u32[]{:S(2)}) collective-permute-start(bf16[80,256]{1,0:T(8,128)(2,1)S(1)} %get-tuple-element.36.refs_0_), channel_id=1, source_target_pairs={{2,0},{3,1},{0,2},{1,3},{6,4},{7,5},{4,6},{5,7},{10,8},{11,9},{8,1... | collective-permute-start | bytes 122888 | tf_op jit(solution)/shard_map/ppermute | solution.py:682
  29.7 5.8 %collective-permute-start.2 = (bf16[80,256]{1,0:T(8,128)(2,1)S(1)}, bf16[80,256]{1,0:T(8,128)(2,1)S(1)}, u32[]{:S(2)}, u32[]{:S(2)}) collective-permute-start(bf16[80,256]{1,0:T(8,128)(2,1)S(1)} %get-tuple-element.36.refs_0_), channel_id=1, source_target_pairs={{3,0},{0,1},{1,2},{2,3},{7,4},{4,5},{5,6},{6,7},{11,8},{8,9},{9,10... | collective-permute-start | bytes 122888 | tf_op jit(solution)/shard_map/ppermute | solution.py:682
  37.7 16.5 %copy-start = (bf16[272,256]{1,0:T(8,128)(2,1)}, bf16[272,256]{1,0:T(8,128)(2,1)S(1)}, u32[]{:S(2)}) copy-start(bf16[272,256]{1,0:T(8,128)(2,1)S(1)} %get-tuple-element.37.token_ref.refs_0_) | copy-start | bytes 417796
  37.7 16.5 %all-to-all-start.2 = ((bf16[16,32,256]{2,1,0:T(8,128)(2,1)}), bf16[16,32,256]{2,1,0:T(8,128)(2,1)S(1)}, u32[]{:S(2)}, u32[]{:S(2)}) async-start(bf16[16,32,256]{2,1,0:T(8,128)(2,1)} %get-tuple-element.38), calls=%async_computation.2 | async-start | bytes 524288 | tf_op jit(solution)/shard_map/all_to_all | solution.py:706
  42.6 9.9 %collective-permute-start.3 = (bf16[272,256]{1,0:T(8,128)(2,1)S(1)}, bf16[272,256]{1,0:T(8,128)(2,1)S(1)}, u32[]{:S(2)}, u32[]{:S(2)}) collective-permute-start(bf16[272,256]{1,0:T(8,128)(2,1)S(1)} %get-tuple-element.37.token_ref.refs_0_), channel_id=1, source_target_pairs={{24,0},{0,8},{8,16},{16,24},{25,1},{1,9},{9,17},{17,25},{26,2},{2,... | collective-permute-start | bytes 417800 | tf_op jit(solution)/shard_map/ppermute | solution.py:682
  44.5 9.6 %collective-permute-start.4 = (bf16[272,256]{1,0:T(8,128)(2,1)S(1)}, bf16[272,256]{1,0:T(8,128)(2,1)S(1)}, u32[]{:S(2)}, u32[]{:S(2)}) collective-permute-start(bf16[272,256]{1,0:T(8,128)(2,1)S(1)} %get-tuple-element.37.token_ref.refs_0_), channel_id=1, source_target_pairs={{16,0},{24,8},{0,16},{8,24},{17,1},{25,9},{1,17},{9,25},{18,2},{26... | collective-permute-start | bytes 417800 | tf_op jit(solution)/shard_map/ppermute | solution.py:682
  46.0 8.1 %collective-permute-start.5 = (bf16[272,256]{1,0:T(8,128)(2,1)S(1)}, bf16[272,256]{1,0:T(8,128)(2,1)S(1)}, u32[]{:S(2)}, u32[]{:S(2)}) collective-permute-start(bf16[272,256]{1,0:T(8,128)(2,1)S(1)} %get-tuple-element.37.token_ref.refs_0_), channel_id=1, source_target_pairs={{8,0},{16,8},{24,16},{0,24},{9,1},{17,9},{25,17},{1,25},{10,2},{18... | collective-permute-start | bytes 417800 | tf_op jit(solution)/shard_map/ppermute | solution.py:682
  52.5 1.6 %copy-start.4 = (bf16[272,256]{1,0:T(8,128)(2,1)}, bf16[272,256]{1,0:T(8,128)(2,1)S(1)}, u32[]{:S(2)}) copy-start(bf16[272,256]{1,0:T(8,128)(2,1)S(1)} %collective-permute-done.3.refs_1_) | copy-start | bytes 417796
  54.1 0.7 copy-start.5
  54.1 0.7 %copy-start.6 = (bf16[272,256]{1,0:T(8,128)(2,1)}, bf16[272,256]{1,0:T(8,128)(2,1)S(1)}, u32[]{:S(2)}) copy-start(bf16[272,256]{1,0:T(8,128)(2,1)S(1)} %collective-permute-done.5.refs_3_) | copy-start | bytes 417796
  64.6 3.1 %collective-permute-start.6 = (bf16[256,1024]{1,0:T(8,128)(2,1)S(1)}, bf16[256,1024]{1,0:T(8,128)(2,1)S(1)}, u32[]{:S(2)}, u32[]{:S(2)}) collective-permute-start(bf16[256,1024]{1,0:T(8,128)(2,1)S(1)} %get-tuple-element.39), channel_id=1, source_target_pairs={{0,4},{4,0},{1,5},{5,1},{2,6},{6,2},{3,7},{7,3},{8,12},{12,8},{9,1... | collective-permute-start | bytes 1572872 | tf_op jit(solution)/shard_map/ppermute | solution.py:768
  64.6 0.9 %copy-start.1 = (bf16[272,256]{1,0:T(8,128)(2,1)S(1)}, bf16[272,256]{1,0:T(8,128)(2,1)}, u32[]{:S(2)}) copy-start(bf16[272,256]{1,0:T(8,128)(2,1)} %copy-done) | copy-start | bytes 417796

commit v8 on v7

--- a/solution.py
+++ b/solution.py
@@ -1,4 +1,5 @@
 import functools
+import math
 
 import jax
 import jax.numpy as jnp
@@ -102,6 +103,8 @@
     start_ref,
     own_hbm,
     ghost_ref,
+    own_train_ref,
+    noise_train_ref,
     part_ref,
     flag_ref,
     own_rest_ref,
@@ -118,23 +121,25 @@
     blocks_ref,
     sems,
 ):
+    train = own_train_ref.shape[0]
     copies = fetch(
         (
             (blocks_hbm, blocks_ref),
             (src_hbm.at[0, 0], src_ref),
             (dst_hbm.at[0, 0], dst_ref),
             (noise_hbm.at[0, 0, 0], noise_ref),
+            (noise_hbm.at[1, 0, 0, :train], noise_train_ref),
         ),
         sems,
     )
     nodes, cols = sums_ref.shape
     pieces = -(-cols // LOW)
     tiles, slots = src_ref.shape
-    count = count_ref[0, 0]
     own_ref[...] = jnp.zeros_like(own_ref)
     ghost_ref[...] = jnp.zeros_like(ghost_ref)
     for copy in copies:
         copy.wait()
+    count = count_ref[0, 0]
 
     def sixteen(values):
         wide = jnp.broadcast_to(values.astype(f32)[:, None, :], (tiles, 16, slots))
@@ -202,8 +207,9 @@
         own_ref[...] = sums_ref[:, :nodes].astype(bf16)
         ghost_ref[...] = sums_ref[:, nodes:].astype(bf16)
 
-    own_copy = pltpu.make_async_copy(own_ref, own_hbm, sems.at[4])
+    own_copy = pltpu.make_async_copy(own_ref, own_hbm, sems.at[5])
     own_copy.start()
+    own_train_ref[...] = own_ref[:train, :]
     part_ref[...] = dot(own_ref[...], start_ref[...]) + noise_ref[...].astype(f32)
 
     @pl.when(big)
@@ -218,14 +224,19 @@
     own_copy.wait()
 
 
-def aggregate(flag_ref, part_ref, count_ref, rest_hbm, table, sums_ref, rest_ref):
+def aggregate(flag_ref, start, parts, sums_ref, rest_ref):
     rows = sums_ref.shape[0]
-    sums_ref[...] = part_ref.astype(f32) + dot(count_ref, table)
+    total = start
+    for count, _, table in parts:
+        total += dot(count, table)
+    sums_ref[...] = total
 
     @pl.when(flag_ref[0] > 0)
     def _():
-        pltpu.sync_copy(rest_hbm.at[:rows], rest_ref)
-        sums_ref[...] += dot(rest_ref[...], table)
+        for count, rest_hbm, table in parts:
+            held = rest_ref.at[:, : count.shape[1]]
+            pltpu.sync_copy(rest_hbm.at[:rows], held)
+            sums_ref[...] += dot(held[...], table)
 
 
 def hop_kernel(
@@ -247,7 +258,8 @@
 ):
     width = start_ref.shape[1]
     table = table_ref[...].reshape(-1, width)
-    aggregate(flag_ref, part_ref[...], ghost_ref[...], rest_hbm, table, sums_ref, rest_ref)
+    parts = ((ghost_ref[...], rest_hbm, table),)
+    aggregate(flag_ref, part_ref[...], parts, sums_ref, rest_ref)
     start = normalize(sums_ref[...])
     start_ref[...] = start
     send(start, rows_ref, out_ref, turn_ref, pick_ref)
@@ -258,24 +270,26 @@
     side_ref[2 * train :, :128] = turn_ref[:16, :].astype(f32).astype(bf16)
 
 
-def own_kernel(
-    flag_ref, own_hbm, rest_hbm, noise_hbm, start_ref, part_ref, own_ref, noise_ref, rest_ref, sems
+def train_kernel(
+    flag_ref,
+    place_ref,
+    own_ref,
+    ghost_ref,
+    own_rest_hbm,
+    ghost_rest_hbm,
+    noise_ref,
+    start_ref,
+    table_ref,
+    *refs,
 ):
-    copies = fetch(((own_hbm, own_ref), (noise_hbm.at[1, 0, 0], noise_ref)), sems)
-    for copy in copies:
-        copy.wait()
-    start = start_ref[...]
-    noise = noise_ref[...].astype(f32)
-    aggregate(flag_ref, noise, own_ref[...], rest_hbm, start, part_ref, rest_ref)
-
-
-def train_kernel(flag_ref, place_ref, part_ref, ghost_ref, rest_hbm, table_ref, *refs):
     *piece_refs, out_ref, side_ref, sums_ref, rest_ref, turn_ref = refs
     train, width = sums_ref.shape
     table = table_ref[...].reshape(-1, width)
-    aggregate(
-        flag_ref, part_ref[:train], ghost_ref[:train], rest_hbm, table, sums_ref, rest_ref
-    )
+    parts = (
+        (own_ref[...], own_rest_hbm, start_ref[...]),
+        (ghost_ref[:train], ghost_rest_hbm, table),
+    )
+    aggregate(flag_ref, noise_ref[...].astype(f32), parts, sums_ref, rest_ref)
     spread(normalize(sums_ref[...]), out_ref)
     length = piece_refs[0].shape[0] - 16
     groups = len(piece_refs)
@@ -291,28 +305,40 @@
 def last_kernel(
     flag_ref,
     token_ref,
-    part_ref,
+    own_hbm,
+    own_rest_hbm,
+    ghost_rest_hbm,
+    noise_hbm,
+    weight_hbm,
     ghost_ref,
-    rest_hbm,
     table_ref,
     start_ref,
     out_ref,
+    weight_ref,
+    own_ref,
+    noise_ref,
     sums_ref,
     rest_ref,
+    sems,
 ):
+    copies = fetch(
+        ((own_hbm, own_ref), (noise_hbm.at[1, 0, 0], noise_ref), (weight_hbm, weight_ref)), sems
+    )
     table = table_ref[...].reshape(-1, out_ref.shape[-1])
-    aggregate(flag_ref, part_ref[...], ghost_ref[...], rest_hbm, table, sums_ref, rest_ref)
     out_ref[0, 0, 0] = start_ref[...]
+    copies[0].wait()
+    copies[1].wait()
+    parts = (
+        (own_ref[...], own_rest_hbm, start_ref[...]),
+        (ghost_ref[...], ghost_rest_hbm, table),
+    )
+    aggregate(flag_ref, noise_ref[...].astype(f32), parts, sums_ref, rest_ref)
     out_ref[1, 0, 0] = normalize(sums_ref[...])
+    copies[2].wait()
 
 
 def shares(ref, first, share):
-    if share % 128 == 0:
-        return ref[:, pl.ds(pl.multiple_of(first, 128), share)].astype(f32)
-    length = ref.shape[1]
-    rows = lax.broadcasted_iota(jnp.int32, (length, share), 0)
-    cols = lax.broadcasted_iota(jnp.int32, (length, share), 1)
-    return dot(ref[...], jnp.where(rows == cols + first, 1.0, 0.0).astype(bf16))
+    return ref[:, pl.ds(pl.multiple_of(first, 128), share)].astype(f32)
 
 
 def lanes_sum(values):
@@ -409,7 +435,7 @@
             in_ref[:, hop * width : (hop + 1) * width] = ref[...].reshape(-1, width)
     else:
         chips = len(side_refs)
-        copies = fetch(tuple(zip(sides_hbm, side_refs)) + pairs[:1], sems)
+        copies = fetch(tuple(zip(sides_hbm, side_refs)) + pairs[1:], sems)
         for copy in copies[:chips]:
             copy.wait()
         groups = two_ref.shape[0] // chips
@@ -430,8 +456,7 @@
                 column((part * groups + group) * train, turned, part * 16 + group)
     in_ref[:, 2 * width :] = two_ref[...].reshape(-1, width)
     if not many:
-        copies[chips].wait()
-        copies = fetch(pairs[1:], sems)
+        copies = copies[chips:]
 
     def activate(values, h_ref, slope_ref, rows):
         sigma = 0.5 + 0.5 * jnp.tanh(0.5 * values)
@@ -501,8 +526,23 @@
     places = [place] if many else [place, place + 1 - 2 * (place % 2)]
 
     def left(ref, share):
-        picked = [shares(ref, at * share, share) for at in places]
-        return (jnp.concatenate(picked, 1) * factor).astype(bf16)
+        if share % 128 == 0:
+            picked = [shares(ref, at * share, share) for at in places]
+            return (jnp.concatenate(picked, 1) * factor).astype(bf16)
+        length, count = ref.shape[1], share * len(places)
+        most = 128 - math.gcd(count, 128)
+        size = min(length, -(-(count + most) // 128) * 128)
+        first = [at * share for at in places]
+        least = functools.reduce(jnp.minimum, first)
+        start = jnp.minimum(least // 128 * 128, length - size)
+        rows = lax.broadcasted_iota(jnp.int32, (size, count), 0)
+        cols = lax.broadcasted_iota(jnp.int32, (size, count), 1)
+        wanted = cols + (first[0] - start)
+        for at, other in enumerate(first[1:], 1):
+            wanted = jnp.where(cols >= at * share, cols - at * share + (other - start), wanted)
+        window = ref[:, pl.ds(pl.multiple_of(start, 128), size)]
+        picked = dot(window, jnp.where(rows == wanted, 1.0, 0.0).astype(bf16))
+        return (picked * factor).astype(bf16)
 
     sum_one = dot_tn(left(in_ref, share_one), d_one_ref[...])
     sum_two = dot_tn(left(h_one_ref, share), d_two_ref[...])
@@ -608,12 +648,14 @@
         [VMEM((nodes, width), bf16), VMEM((parts, each), jnp.int32), turn, pick, DMA((2,))],
     )
     table0 = lax.all_to_all(out0, dom, split_axis=0, concat_axis=0, tiled=True)
-    own, ghost, part1, flag, own_rest, ghost_rest = call(
+    own, ghost, own_train, noise_train, part1, flag, own_rest, ghost_rest = call(
         build_kernel,
         28,
         [
             ((nodes, nodes), bf16, HBM),
             ((nodes, ghosts), bf16, None),
+            ((train, nodes), bf16, None),
+            ((train, width), bf16, None),
             ((nodes, width), f32, None),
             ((1,), jnp.int32, SMEM),
             ((nodes, nodes), bf16, HBM),
@@ -638,7 +680,7 @@
             VMEM((nodes, max(nodes, ghosts)), bf16),
             VMEM((nodes, nodes), bf16),
             SMEM(tile_block.shape, jnp.int32),
-            DMA((5,)),
+            DMA((6,)),
         ],
     )
     start1, out1, side = call(
@@ -662,18 +704,6 @@
         [VMEM((nodes, width), f32), VMEM((nodes, ghosts), bf16), turn, pick],
     )
     table1 = lax.all_to_all(out1, dom, split_axis=0, concat_axis=0, tiled=True)
-    (part2,) = call(
-        own_kernel,
-        16,
-        [((nodes, width), f32, None)],
-        [(flag, SMEM), (own, HBM), (own_rest, HBM), (hop_noise, HBM), (start1, None)],
-        [
-            VMEM((nodes, nodes), bf16),
-            VMEM((nodes, width), bf16),
-            VMEM((nodes, nodes), bf16),
-            DMA((2,)),
-        ],
-    )
     place = jnp.stack([lax.axis_index(dom), lax.axis_index("grp")]).astype(jnp.int32)
     grp = lax.axis_size("grp")
 
@@ -694,13 +724,20 @@
         [
             (flag, SMEM),
             (place, SMEM),
-            (part2, None),
+            (own_train, None),
             (ghost, None),
+            (own_rest, HBM),
             (ghost_rest, HBM),
+            (noise_train, None),
+            (start1, None),
             (table1, None),
         ]
         + [(value, None) for value in sides],
-        [VMEM((train, width), f32), VMEM((train, ghosts), bf16), VMEM((128, 128), f32)],
+        [
+            VMEM((train, width), f32),
+            VMEM((train, max(nodes, ghosts)), bf16),
+            VMEM((128, 128), f32),
+        ],
     )
     if few:
         every2 = lax.all_to_all(last, ("chip", "grp"), split_axis=0, concat_axis=0, tiled=True)
@@ -710,20 +747,29 @@
             every(value, axes) for value in (own0[None], start1[None, :train], last)
         )
         every_label = every(labels.reshape(1, train), axes)
-    (hop_feats,) = call(
+    hop_feats, held_first = call(
         last_kernel,
-        12,
-        [((2, 1, 1, nodes, width), bf16, VMEM)],
+        16,
+        [((2, 1, 1, nodes, width), bf16, VMEM), (w_first.shape, bf16, None)],
         [
             (flag, SMEM),
             (side, None),
-            (part2, None),
+            (own, HBM),
+            (own_rest, HBM),
+            (ghost_rest, HBM),
+            (hop_noise, HBM),
+            (w_first, HBM),
             (ghost, None),
-            (ghost_rest, HBM),
             (table1, None),
             (start1, None),
         ],
-        [VMEM((nodes, width), f32), VMEM((nodes, ghosts), bf16)],
+        [
+            VMEM((nodes, nodes), bf16),
+            VMEM((nodes, width), bf16),
+            VMEM((nodes, width), f32),
+            VMEM((nodes, max(nodes, ghosts)), bf16),
+            DMA((3,)),
+        ],
     )
     chunk = train * (copies if few else min(members, 32))
     groups = chunk // train
@@ -749,9 +795,21 @@
 
         def classify(place_ref, *refs):
             sides_in, rest = refs[:chips], refs[chips:]
-            outs, held, rest = rest[:11], rest[11 : 11 + chips], rest[11 + chips :]
+            two_ref, first_ref, *outs = rest[:11]
+            held, rest = rest[11 : 11 + chips], rest[11 + chips :]
             classify_kernel(
-                False, place_ref, None, None, None, outs[0], sides_in, *outs[1:], held, *rest
+                False,
+                place_ref,
+                None,
+                None,
+                None,
+                two_ref,
+                sides_in,
+                first_ref,
+                *outs,
+                held,
+                first_ref,
+                *rest,
             )
 
         rows = noise_first.shape[0] + noise_second.shape[0] + 32
@@ -761,9 +819,9 @@
             [(value.shape, f32, None) for value in fixed[3:]] + [((rows, hid), bf16, None)],
             [(place, SMEM)]
             + [(value, HBM) for value in sides]
-            + [(every2, None)]
-            + [(value, HBM) for value in fixed],
-            [VMEM(value.shape, bf16) for value in sides] + scratch,
+            + [(every2, None), (held_first, None)]
+            + [(value, HBM) for value in fixed[1:]],
+            [VMEM(value.shape, bf16) for value in sides] + scratch[1:],
         )
         got = lax.ppermute(other, "core", [(0, 1), (1, 0)])
         first, second, third = call(

time: 69.8 us -> 67.6 us (0.968); the launches traced: 68.8 us -> 67.4 us
  waiting for transfers between devices: 8.69 us -> 6.32 us
  starting transfers between devices: 26.8 us -> 28 us
  local copies, waits for them, and re-layouts: 1.59 us -> 0.66 us
  Pallas kernels: 30.2 us -> 30.9 us
    ppermute x6, waiting for transfers between devices: 8.68 us -> 4.42 us  [shifted(): lax.ppermute(value, name, [((at + step * shift) % size, at) for at in ran...]
    ppermute x6, starting transfers between devices: 12.3 us -> 9.47 us  [shifted(): lax.ppermute(value, name, [((at + step * shift) % size, at) for at in ran...]
    all_to_all x1, starting transfers between devices: 4.93 us -> 7.42 us  [local(): lax.all_to_all(last, ('chip', 'grp'), split_axis=0, concat_axis=0, tiled=...]
    ppermute x1, waiting for transfers between devices: 0.01 us -> 1.9 us  [local(): got = lax.ppermute(other, 'core', [(0, 1), (1, 0)])]
    all_to_all x1, starting transfers between devices: 4.32 us -> 5.89 us  [local(): table1 = lax.all_to_all(out1, dom, split_axis=0, concat_axis=0, tiled=True)]
    unnamed x14 -> x10, local copies, waits for them, and re-layouts: 1.59 us -> 0.66 us
    pallas_call x8 -> x7, Pallas kernels: 30.2 us -> 30.9 us  [call(): pl.pallas_call(kernel, out_shape=[shape_of(*out) for out in outs], in_spe...]
  transfers between devices with their start and end apart: 10 -> 10, of which waited for: 4 -> 4; matrix products, arithmetic and copies ran while one was open for 0% -> 0% of each run, Pallas kernels for 18% -> 21%
where the time goes in v8:
time: 67.6 us; the launch traced here: 67.4 us
  Pallas kernels  30.9 us (46%)
  starting transfers between devices  28 us (41%)
  waiting for transfers between devices  6.32 us (9%)
  between operations  1.42 us (2%)
    pallas_call x7, Pallas kernels, call(): pl.pallas_call(kernel, out_shape=[shape_of(*out) for out in outs], in_spe...  30.9 us
    ppermute x6, starting transfers between devices, shifted(): lax.ppermute(value, name, [((at + step * shift) % size, at) for at in ran...  9.47 us
    all_to_all x1, starting transfers between devices, local(): lax.all_to_all(last, ('chip', 'grp'), split_axis=0, concat_axis=0, tiled=...  7.42 us
    all_to_all x1, starting transfers between devices, local(): table1 = lax.all_to_all(out1, dom, split_axis=0, concat_axis=0, tiled=True)  5.89 us
    all_to_all x1, starting transfers between devices, local(): table0 = lax.all_to_all(out0, dom, split_axis=0, concat_axis=0, tiled=True)  5.18 us
    ppermute x6, waiting for transfers between devices, shifted(): lax.ppermute(value, name, [((at + step * shift) % size, at) for at in ran...  4.42 us
    ppermute x1, waiting for transfers between devices, local(): got = lax.ppermute(other, 'core', [(0, 1), (1, 0)])  1.9 us
  transfers between devices with their start and end apart: 10, of which 4 were waited for; matrix products, arithmetic and copies ran while one was open for 0% of the time, Pallas kernels for 21%

profile of v8, /device:TPU:0, one launch (start us, length us, event | category | flops | bytes accessed | tf_op | source)
XLA Modules:
  0.0 67.4 jit_solution(15117509585576370400)
XLA Ops:
  0.6 0.0 copy-start.1
  0.6 0.0 copy-start.2
  0.7 2.4 %shard_map.165 = (bf16[1024,256]{1,0:T(8,128)(2,1)S(1)}, bf16[8,32,256]{2,1,0:T(8,128)(2,1)}, bf16[32,256]{1,0:T(8,128)(2,1)S(1)}) custom-call(bf16[1,1,1024,256]{3,2,1,0:T(8,128)(2,1)} %feats_hbm.1, s32[1,1,8,32]{3,2,1,0:T(8,128)} %rows_hbm.1), custom_call_target="tpu_custom_call" | custom-call | tf_op jit(solution)/shard_map/pallas_call | solution.py:589
  3.1 5.2 %all-to-all-start = ((bf16[8,32,256]{2,1,0:T(8,128)(2,1)}), bf16[8,32,256]{2,1,0:T(8,128)(2,1)S(1)}, u32[]{:S(2)}, u32[]{:S(2)}) async-start(bf16[8,32,256]{2,1,0:T(8,128)(2,1)} %get-tuple-element.37), calls=%async_computation | async-start | bytes 262144 | tf_op jit(solution)/shard_map/all_to_all | solution.py:650
  8.9 9.8 %shard_map.166 = (bf16[1024,1024]{1,0:T(8,128)(2,1)}, bf16[1024,256]{1,0:T(8,128)(2,1)S(1)}, bf16[32,1024]{1,0:T(8,128)(2,1)S(1)}, bf16[32,256]{1,0:T(8,128)(2,1...) custom-call(s32[1,1,64]{2,1,0:T(1,128)} %blocks_hbm.1, ...), custom_call_target="tpu_custom_call" | custom-call | tf_op jit(solution)/shard_map/pallas_call | solution.py:589
  18.7 0.0 all-to-all-done.table_ref
  18.7 0.0 copy-done.1
  18.8 0.0 copy-done.2
  18.8 2.3 %shard_map.167 = (bf16[1024,256]{1,0:T(8,128)(2,1)S(1)}, bf16[8,32,256]{2,1,0:T(8,128)(2,1)}, bf16[80,256]{1,0:T(8,128)(2,1)S(1)}) custom-call(s32[1]{0:T(128)} %get-tuple-element.30.flag_ref, f32[1024,256]{1,0:T(8,128)S(1)} %get-tuple-element.36.part_ref, bf16[1024,256]{1,0:T(8,128)(2,1)S(1)} %get-tuple-element.32.ghost_ref, ...), custom_call_target="tpu_custom_call" | custom-call | tf_op jit(solution)/shard_map/pallas_call | solution.py:589
  21.1 5.9 %all-to-all-start.1 = ((bf16[8,32,256]{2,1,0:T(8,128)(2,1)}), bf16[8,32,256]{2,1,0:T(8,128)(2,1)S(1)}, u32[]{:S(2)}, u32[]{:S(2)}) async-start(bf16[8,32,256]{2,1,0:T(8,128)(2,1)} %get-tuple-element.40), calls=%async_computation.1 | async-start | bytes 262144 | tf_op jit(solution)/shard_map/all_to_all | solution.py:706
  27.0 1.1 %collective-permute-start.2 = (bf16[80,256]{1,0:T(8,128)(2,1)S(1)}, bf16[80,256]{1,0:T(8,128)(2,1)S(1)}, u32[]{:S(2)}, u32[]{:S(2)}) collective-permute-start(bf16[80,256]{1,0:T(8,128)(2,1)S(1)} %get-tuple-element.41.refs_0_), channel_id=1, source_target_pairs={{3,0},{0,1},{1,2},{2,3},{7,4},{4,5},{5,6},{6,7},{11,8},{8,9},{9,10... | collective-permute-start | bytes 122888 | tf_op jit(solution)/shard_map/ppermute | solution.py:712
  28.1 1.9 %collective-permute-start.1 = (bf16[80,256]{1,0:T(8,128)(2,1)S(1)}, bf16[80,256]{1,0:T(8,128)(2,1)S(1)}, u32[]{:S(2)}, u32[]{:S(2)}) collective-permute-start(bf16[80,256]{1,0:T(8,128)(2,1)S(1)} %get-tuple-element.41.refs_0_), channel_id=1, source_target_pairs={{2,0},{3,1},{0,2},{1,3},{6,4},{7,5},{4,6},{5,7},{10,8},{11,9},{8,1... | collective-permute-start | bytes 122888 | tf_op jit(solution)/shard_map/ppermute | solution.py:712
  30.0 2.5 %collective-permute-start = (bf16[80,256]{1,0:T(8,128)(2,1)S(1)}, bf16[80,256]{1,0:T(8,128)(2,1)S(1)}, u32[]{:S(2)}, u32[]{:S(2)}) collective-permute-start(bf16[80,256]{1,0:T(8,128)(2,1)S(1)} %get-tuple-element.41.refs_0_), channel_id=1, source_target_pairs={{1,0},{2,1},{3,2},{0,3},{5,4},{6,5},{7,6},{4,7},{9,8},{10,9},{11,1... | collective-permute-start | bytes 122888 | tf_op jit(solution)/shard_map/ppermute | solution.py:712
  32.5 0.1 pad_add_fusion.place_ref
  32.6 0.3 collective-permute-done.2.refs_3_
  32.9 1.7 %collective-permute-done.1.refs_2_ = bf16[80,256]{1,0:T(8,128)(2,1)S(1)} collective-permute-done((bf16[80,256]{1,0:T(8,128)(2,1)S(1)}, bf16[80,256]{1,0:T(8,128)(2,1)S(1)}, u32[]{:S(2)}, u32[]{:S(2)}) %collective-permute-start.1) | collective-permute-done | bytes 40992 | tf_op jit(solution)/shard_map/ppermute | solution.py:712
  34.6 0.0 collective-permute-done.refs_1_
  34.6 0.0 all-to-all-done.1.table_ref
  34.6 2.2 %shard_map.168 = (bf16[16,32,256]{2,1,0:T(8,128)(2,1)}, bf16[272,256]{1,0:T(8,128)(2,1)S(1)}) custom-call(s32[1]{0:T(128)} %get-tuple-element.30.flag_ref, s32[2]{0:T(128)S(1)} %pad_add_fusion.place_ref, bf16[32,1024]{1,0:T(8,128)(2,1)S(1)} %get-tuple-element.31.own_ref, bf16[1024,256]{1,0:T(8,128)(2,1)S(1)} %get-tuple-element.32.ghost_ref, ...), custom_call_target="tpu_custom_call" | custom-call | tf_op jit(solution)/shard_map/pallas_call | solution.py:589
  36.8 0.0 copy-start
  36.8 7.4 %all-to-all-start.2 = ((bf16[16,32,256]{2,1,0:T(8,128)(2,1)}), bf16[16,32,256]{2,1,0:T(8,128)(2,1)S(1)}, u32[]{:S(2)}, u32[]{:S(2)}) async-start(bf16[16,32,256]{2,1,0:T(8,128)(2,1)} %get-tuple-element.45), calls=%async_computation.2 | async-start | bytes 524288 | tf_op jit(solution)/shard_map/all_to_all | solution.py:743
  44.3 2.8 %collective-permute-start.5 = (bf16[272,256]{1,0:T(8,128)(2,1)S(1)}, bf16[272,256]{1,0:T(8,128)(2,1)S(1)}, u32[]{:S(2)}, u32[]{:S(2)}) collective-permute-start(bf16[272,256]{1,0:T(8,128)(2,1)S(1)} %get-tuple-element.42.token_ref.refs_0_), channel_id=1, source_target_pairs={{8,0},{16,8},{24,16},{0,24},{9,1},{17,9},{25,17},{1,25},{10,2},{18... | collective-permute-start | bytes 417800 | tf_op jit(solution)/shard_map/ppermute | solution.py:712
  47.1 0.6 collective-permute-start.4
  47.7 0.6 collective-permute-start.3
  48.2 4.6 %shard_map.169 = (bf16[2,1,1,1024,256]{4,3,2,1,0:T(8,128)(2,1)}, bf16[768,1024]{1,0:T(8,128)(2,1)S(1)}) custom-call(s32[1]{0:T(128)} %get-tuple-element.30.flag_ref, bf16[272,256]{1,0:T(8,128)(2,1)S(1)} %get-tuple-element.42.token_ref.refs_0_, bf16[1024,1024]{1,0:T(8,128)(2,1)} %get-tuple-element.43.own_hbm, ...), custom_call_target="tpu_custom_call" | custom-call | tf_op jit(solution)/shard_map/pallas_call | solution.py:589
  52.8 0.0 copy-done
  52.8 0.0 collective-permute-done.5.refs_3_
  52.8 0.0 copy-start.3
  52.8 2.4 %collective-permute-done.4.refs_2_ = bf16[272,256]{1,0:T(8,128)(2,1)S(1)} collective-permute-done((bf16[272,256]{1,0:T(8,128)(2,1)S(1)}, bf16[272,256]{1,0:T(8,128)(2,1)S(1)}, u32[]{:S(2)}, u32[]{:S(2)}) %collective-permute-start.4) | collective-permute-done | bytes 139296 | tf_op jit(solution)/shard_map/ppermute | solution.py:712
  55.2 0.0 copy-start.4
  55.2 0.0 collective-permute-done.3.refs_1_
  55.2 0.0 all-to-all-done.2.refs_4_
  55.2 0.0 copy-done.3
  55.2 0.6 copy-done.4
  55.9 8.5 %shard_map.170 = (f32[96,1024]{1,0:T(8,128)S(1)}, f32[128,1024]{1,0:T(8,128)S(1)}, f32[172,128]{1,0:T(8,128)S(1)}, bf16[256,1024]{1,0:T(8,128)(2,1)S(1)}) custom-call(s32[2]{0:T(128)S(1)} %pad_add_fusion.place_ref, bf16[272,256]{1,0:T(8,128)(2,1)} %copy-done, bf16[272,256]{1,0:T(8,128)(2,1)} %collective-permute-done.3.refs_1_, bf16[272,256]{1,0:T(8,128)(2,1)} %copy-done.4, ...), custom_call_target="tpu_custom_call" | custom-call | tf_op jit(solution)/shard_map/pallas_call | solution.py:589
  64.4 0.1 collective-permute-start.6
  64.4 1.9 %collective-permute-done.6.got_ref = bf16[256,1024]{1,0:T(8,128)(2,1)S(1)} collective-permute-done((bf16[256,1024]{1,0:T(8,128)(2,1)S(1)}, bf16[256,1024]{1,0:T(8,128)(2,1)S(1)}, u32[]{:S(2)}, u32[]{:S(2)}) %collective-permute-start.6) | collective-permute-done | bytes 524320 | tf_op jit(solution)/shard_map/ppermute | solution.py:826
  66.3 1.1 %shard_map.171 = (f32[96,1024]{1,0:T(8,128)}, f32[128,1024]{1,0:T(8,128)}, f32[172,128]{1,0:T(8,128)}) custom-call(bf16[256,1024]{1,0:T(8,128)(2,1)S(1)} %collective-permute-done.6.got_ref, f32[96,1024]{1,0:T(8,128)S(1)} %get-tuple-element.48.one_ref, f32[128,1024]{1,0:T(8,128)S(1)} %get-tuple-element.49.two_ref, f32[172,128]{1,0:T(8,128)S(1)} %get-tuple-element.50.three_ref), custom_call_target="tpu_custom_call" | custom-call | tf_op jit(solution)/shard_map/pallas_call | solution.py:589
Async XLA Ops:
  0.6 18.1 %copy-start.1 = (s32[1,1,8,32]{3,2,1,0:T(8,128)S(1)}, s32[1,1,8,32]{3,2,1,0:T(8,128)}, u32[]{:S(2)}) copy-start(s32[1,1,8,32]{3,2,1,0:T(8,128)} %rows_hbm.1) | copy-start | bytes 3076
  0.6 18.1 %copy-start.2 = (s32[1,1,32]{2,1,0:T(1,128)S(1)}, s32[1,1,32]{2,1,0:T(1,128)}, u32[]{:S(2)}) copy-start(s32[1,1,32]{2,1,0:T(1,128)} %param.21) | copy-start | bytes 388
  3.1 15.6 %all-to-all-start = ((bf16[8,32,256]{2,1,0:T(8,128)(2,1)}), bf16[8,32,256]{2,1,0:T(8,128)(2,1)S(1)}, u32[]{:S(2)}, u32[]{:S(2)}) async-start(bf16[8,32,256]{2,1,0:T(8,128)(2,1)} %get-tuple-element.37), calls=%async_computation | async-start | bytes 262144 | tf_op jit(solution)/shard_map/all_to_all | solution.py:650
  21.1 13.5 %all-to-all-start.1 = ((bf16[8,32,256]{2,1,0:T(8,128)(2,1)}), bf16[8,32,256]{2,1,0:T(8,128)(2,1)S(1)}, u32[]{:S(2)}, u32[]{:S(2)}) async-start(bf16[8,32,256]{2,1,0:T(8,128)(2,1)} %get-tuple-element.40), calls=%async_computation.1 | async-start | bytes 262144 | tf_op jit(solution)/shard_map/all_to_all | solution.py:706
  27.0 5.9 %collective-permute-start.2 = (bf16[80,256]{1,0:T(8,128)(2,1)S(1)}, bf16[80,256]{1,0:T(8,128)(2,1)S(1)}, u32[]{:S(2)}, u32[]{:S(2)}) collective-permute-start(bf16[80,256]{1,0:T(8,128)(2,1)S(1)} %get-tuple-element.41.refs_0_), channel_id=1, source_target_pairs={{3,0},{0,1},{1,2},{2,3},{7,4},{4,5},{5,6},{6,7},{11,8},{8,9},{9,10... | collective-permute-start | bytes 122888 | tf_op jit(solution)/shard_map/ppermute | solution.py:712
  28.1 6.5 %collective-permute-start.1 = (bf16[80,256]{1,0:T(8,128)(2,1)S(1)}, bf16[80,256]{1,0:T(8,128)(2,1)S(1)}, u32[]{:S(2)}, u32[]{:S(2)}) collective-permute-start(bf16[80,256]{1,0:T(8,128)(2,1)S(1)} %get-tuple-element.41.refs_0_), channel_id=1, source_target_pairs={{2,0},{3,1},{0,2},{1,3},{6,4},{7,5},{4,6},{5,7},{10,8},{11,9},{8,1... | collective-permute-start | bytes 122888 | tf_op jit(solution)/shard_map/ppermute | solution.py:712
  30.0 4.6 %collective-permute-start = (bf16[80,256]{1,0:T(8,128)(2,1)S(1)}, bf16[80,256]{1,0:T(8,128)(2,1)S(1)}, u32[]{:S(2)}, u32[]{:S(2)}) collective-permute-start(bf16[80,256]{1,0:T(8,128)(2,1)S(1)} %get-tuple-element.41.refs_0_), channel_id=1, source_target_pairs={{1,0},{2,1},{3,2},{0,3},{5,4},{6,5},{7,6},{4,7},{9,8},{10,9},{11,1... | collective-permute-start | bytes 122888 | tf_op jit(solution)/shard_map/ppermute | solution.py:712
  36.8 16.0 %copy-start = (bf16[272,256]{1,0:T(8,128)(2,1)}, bf16[272,256]{1,0:T(8,128)(2,1)S(1)}, u32[]{:S(2)}) copy-start(bf16[272,256]{1,0:T(8,128)(2,1)S(1)} %get-tuple-element.42.token_ref.refs_0_) | copy-start | bytes 417796
  36.8 18.4 %all-to-all-start.2 = ((bf16[16,32,256]{2,1,0:T(8,128)(2,1)}), bf16[16,32,256]{2,1,0:T(8,128)(2,1)S(1)}, u32[]{:S(2)}, u32[]{:S(2)}) async-start(bf16[16,32,256]{2,1,0:T(8,128)(2,1)} %get-tuple-element.45), calls=%async_computation.2 | async-start | bytes 524288 | tf_op jit(solution)/shard_map/all_to_all | solution.py:743
  44.3 8.5 %collective-permute-start.5 = (bf16[272,256]{1,0:T(8,128)(2,1)S(1)}, bf16[272,256]{1,0:T(8,128)(2,1)S(1)}, u32[]{:S(2)}, u32[]{:S(2)}) collective-permute-start(bf16[272,256]{1,0:T(8,128)(2,1)S(1)} %get-tuple-element.42.token_ref.refs_0_), channel_id=1, source_target_pairs={{8,0},{16,8},{24,16},{0,24},{9,1},{17,9},{25,17},{1,25},{10,2},{18... | collective-permute-start | bytes 417800 | tf_op jit(solution)/shard_map/ppermute | solution.py:712
  47.1 8.1 %collective-permute-start.4 = (bf16[272,256]{1,0:T(8,128)(2,1)S(1)}, bf16[272,256]{1,0:T(8,128)(2,1)S(1)}, u32[]{:S(2)}, u32[]{:S(2)}) collective-permute-start(bf16[272,256]{1,0:T(8,128)(2,1)S(1)} %get-tuple-element.42.token_ref.refs_0_), channel_id=1, source_target_pairs={{16,0},{24,8},{0,16},{8,24},{17,1},{25,9},{1,17},{9,25},{18,2},{26... | collective-permute-start | bytes 417800 | tf_op jit(solution)/shard_map/ppermute | solution.py:712
  47.7 7.5 %collective-permute-start.3 = (bf16[272,256]{1,0:T(8,128)(2,1)S(1)}, bf16[272,256]{1,0:T(8,128)(2,1)}, u32[]{:S(2)}, u32[]{:S(2)}) collective-permute-start(bf16[272,256]{1,0:T(8,128)(2,1)S(1)} %get-tuple-element.42.token_ref.refs_0_), channel_id=1, source_target_pairs={{24,0},{0,8},{8,16},{16,24},{25,1},{1,9},{9,17},{17,25},{26,2},{2,... | collective-permute-start | bytes 417800 | tf_op jit(solution)/shard_map/ppermute | solution.py:712
  52.8 2.4 %copy-start.3 = (bf16[272,256]{1,0:T(8,128)(2,1)}, bf16[272,256]{1,0:T(8,128)(2,1)S(1)}, u32[]{:S(2)}) copy-start(bf16[272,256]{1,0:T(8,128)(2,1)S(1)} %collective-permute-done.5.refs_3_) | copy-start | bytes 417796
  55.2 0.7 copy-start.4
  64.4 2.0 %collective-permute-start.6 = (bf16[256,1024]{1,0:T(8,128)(2,1)S(1)}, bf16[256,1024]{1,0:T(8,128)(2,1)S(1)}, u32[]{:S(2)}, u32[]{:S(2)}) collective-permute-start(bf16[256,1024]{1,0:T(8,128)(2,1)S(1)} %get-tuple-element.47), channel_id=1, source_target_pairs={{0,4},{4,0},{1,5},{5,1},{2,6},{6,2},{3,7},{7,3},{8,12},{12,8},{9,1... | collective-permute-start | bytes 1572872 | tf_op jit(solution)/shard_map/ppermute | solution.py:826

commit v9 on v8

--- a/solution.py
+++ b/solution.py
@@ -10,7 +10,7 @@
 
 BLOCK = 128
 LOW = 256
-GROUP = 4
+GROUP = 8
 clip_bound = 4.0
 noise_mult = 1.0
 
@@ -52,53 +52,69 @@
     return lax.dot_general(left, right, (((0,), (0,)), ((), ())), preferred_element_type=f32)
 
 
-def send(start, rows_ref, out_ref, turn_ref, pick_ref):
+def choose(rows_ref, turn_ref, pick_ref):
     parts, each = rows_ref.shape
-    nodes = start.shape[0]
     turn_ref[:parts, :each] = rows_ref[...]
     columns = turn_ref[...].T
-    spots = lax.broadcasted_iota(jnp.int32, (each, nodes), 1)
+    spots = lax.broadcasted_iota(jnp.int32, (each, pick_ref.shape[1]), 1)
     for part in range(parts):
         wanted = columns[:each, part : part + 1]
         pick_ref[part * each : (part + 1) * each, :] = jnp.where(wanted == spots, 1.0, 0.0).astype(
             bf16
         )
-    out = dot(pick_ref[...], start).astype(bf16)
-    out_ref[...] = out.reshape(out_ref.shape)
-
-
-def spread(rows, out_ref):
-    out_ref[...] = jnp.broadcast_to(rows[None], out_ref.shape)
+
+
+def post(rows, staged_ref, out_hbm, sem):
+    staged_ref[...] = rows.reshape(staged_ref.shape)
+    copy = pltpu.make_async_copy(staged_ref, out_hbm, sem)
+    copy.start()
+    return copy
 
 
 def first_kernel(
     feats_hbm,
     rows_hbm,
+    src_hbm,
+    dst_hbm,
     start_ref,
-    out_ref,
+    out_hbm,
     own_ref,
+    src_ref,
+    dst_ref,
     feats_ref,
     rows_ref,
     turn_ref,
     pick_ref,
+    staged_ref,
     sems,
 ):
     copies = fetch(
-        ((feats_hbm.at[0, 0], feats_ref), (rows_hbm.at[0, 0], rows_ref)), sems
-    )
-    for copy in copies:
-        copy.wait()
+        (
+            (rows_hbm.at[0, 0], rows_ref),
+            (feats_hbm.at[0, 0], feats_ref),
+            (src_hbm.at[0, 0], src_ref),
+            (dst_hbm.at[0, 0], dst_ref),
+        ),
+        sems,
+    )
+    copies[0].wait()
+    choose(rows_ref, turn_ref, pick_ref)
+    copies[1].wait()
+    sent = normalize(dot(pick_ref[...], feats_ref[...]))
+    out_copy = post(sent, staged_ref, out_hbm, sems.at[4])
     start = normalize(feats_ref[...].astype(f32))
     start_ref[...] = start
     own_ref[...] = start[: own_ref.shape[0]]
-    send(start, rows_ref, out_ref, turn_ref, pick_ref)
+    copies[2].wait()
+    copies[3].wait()
+    out_copy.wait()
 
 
 def build_kernel(
     blocks_hbm,
     count_ref,
-    src_hbm,
-    dst_hbm,
+    src_ref,
+    dst_ref,
     noise_hbm,
     start_ref,
     own_hbm,
@@ -109,8 +125,6 @@
     flag_ref,
     own_rest_ref,
     ghost_rest_ref,
-    src_ref,
-    dst_ref,
     noise_ref,
     low_ref,
     high_ref,
@@ -125,8 +139,6 @@
     copies = fetch(
         (
             (blocks_hbm, blocks_ref),
-            (src_hbm.at[0, 0], src_ref),
-            (dst_hbm.at[0, 0], dst_ref),
             (noise_hbm.at[0, 0, 0], noise_ref),
             (noise_hbm.at[1, 0, 0, :train], noise_train_ref),
         ),
@@ -137,8 +149,7 @@
     tiles, slots = src_ref.shape
     own_ref[...] = jnp.zeros_like(own_ref)
     ghost_ref[...] = jnp.zeros_like(ghost_ref)
-    for copy in copies:
-        copy.wait()
+    copies[0].wait()
     count = count_ref[0, 0]
 
     def sixteen(values):
@@ -207,9 +218,11 @@
         own_ref[...] = sums_ref[:, :nodes].astype(bf16)
         ghost_ref[...] = sums_ref[:, nodes:].astype(bf16)
 
-    own_copy = pltpu.make_async_copy(own_ref, own_hbm, sems.at[5])
+    own_copy = pltpu.make_async_copy(own_ref, own_hbm, sems.at[3])
     own_copy.start()
     own_train_ref[...] = own_ref[:train, :]
+    for copy in copies[1:]:
+        copy.wait()
     part_ref[...] = dot(own_ref[...], start_ref[...]) + noise_ref[...].astype(f32)
 
     @pl.when(big)
@@ -249,25 +262,29 @@
     old_ref,
     labels_ref,
     start_ref,
-    out_ref,
+    out_hbm,
     side_ref,
     sums_ref,
     rest_ref,
     turn_ref,
     pick_ref,
+    staged_ref,
+    sem,
 ):
     width = start_ref.shape[1]
     table = table_ref[...].reshape(-1, width)
     parts = ((ghost_ref[...], rest_hbm, table),)
     aggregate(flag_ref, part_ref[...], parts, sums_ref, rest_ref)
+    choose(rows_ref, turn_ref, pick_ref)
     start = normalize(sums_ref[...])
     start_ref[...] = start
-    send(start, rows_ref, out_ref, turn_ref, pick_ref)
+    out_copy = post(dot(pick_ref[...], start).astype(bf16), staged_ref, out_hbm, sem)
     train = labels_ref.shape[1]
     side_ref[:train, :] = old_ref[...]
     side_ref[train : 2 * train, :] = start[:train]
     turn_ref[:1, :train] = labels_ref[...]
     side_ref[2 * train :, :128] = turn_ref[:16, :].astype(f32).astype(bf16)
+    out_copy.wait()
 
 
 def train_kernel(
@@ -282,7 +299,7 @@
     table_ref,
     *refs,
 ):
-    *piece_refs, out_ref, side_ref, sums_ref, rest_ref, turn_ref = refs
+    *piece_refs, out_hbm, side_ref, sums_ref, rest_ref, turn_ref, staged_ref, sem = refs
     train, width = sums_ref.shape
     table = table_ref[...].reshape(-1, width)
     parts = (
@@ -290,7 +307,8 @@
         (ghost_ref[:train], ghost_rest_hbm, table),
     )
     aggregate(flag_ref, noise_ref[...].astype(f32), parts, sums_ref, rest_ref)
-    spread(normalize(sums_ref[...]), out_ref)
+    last = jnp.broadcast_to(normalize(sums_ref[...])[None], staged_ref.shape)
+    out_copy = post(last, staged_ref, out_hbm, sem)
     length = piece_refs[0].shape[0] - 16
     groups = len(piece_refs)
     if groups > 1:
@@ -300,6 +318,7 @@
             side_ref[pl.ds(at, length), :] = ref[:length, :]
             turn_ref[pl.ds(group, 1), :] = ref[length:, :128].astype(f32)[:1]
         side_ref[groups * length :, :128] = turn_ref[:16, :].astype(bf16)
+    out_copy.wait()
 
 
 def last_kernel(
@@ -356,7 +375,7 @@
     zero_ref,
     one_ref,
     two_ref,
-    sides_hbm,
+    side_refs,
     w_first_hbm,
     w_second_hbm,
     w_third_hbm,
@@ -367,7 +386,6 @@
     g_second_ref,
     g_third_ref,
     send_ref,
-    side_refs,
     w_first_ref,
     w_second_ref,
     w_third_ref,
@@ -435,9 +453,7 @@
             in_ref[:, hop * width : (hop + 1) * width] = ref[...].reshape(-1, width)
     else:
         chips = len(side_refs)
-        copies = fetch(tuple(zip(sides_hbm, side_refs)) + pairs[1:], sems)
-        for copy in copies[:chips]:
-            copy.wait()
+        copies = fetch(pairs[1:], sems)
         groups = two_ref.shape[0] // chips
         rows = groups * train
         for shift, ref in enumerate(side_refs):
@@ -455,8 +471,6 @@
             for group in range(groups):
                 column((part * groups + group) * train, turned, part * 16 + group)
     in_ref[:, 2 * width :] = two_ref[...].reshape(-1, width)
-    if not many:
-        copies = copies[chips:]
 
     def activate(values, h_ref, slope_ref, rows):
         sigma = 0.5 + 0.5 * jnp.tanh(0.5 * values)
@@ -479,7 +493,7 @@
             values = ahead
         return jnp.concatenate(sums, 0)
 
-    step = 256
+    step = min(512, in_ref.shape[0])
     cuts = [slice(at, at + step) for at in range(0, in_ref.shape[0], step)]
     sq_in = lanes_sum(in_ref[...])
     sq_one = layer(
@@ -636,16 +650,26 @@
             value = lax.all_gather(value, name, axis=0, tiled=True)
         return value
 
-    start0, out0, own0 = call(
+    staged = VMEM((parts, each, width), bf16)
+    start0, out0, own0, src, dst = call(
         first_kernel,
         16,
         [
             ((nodes, width), bf16, None),
-            ((parts, each, width), bf16, None),
+            ((parts, each, width), bf16, HBM),
             ((train, width), bf16, None),
-        ],
-        [(feats, HBM), (send_rows, HBM)],
-        [VMEM((nodes, width), bf16), VMEM((parts, each), jnp.int32), turn, pick, DMA((2,))],
+            ((tiles, slots), jnp.int32, None),
+            ((tiles, slots), jnp.int32, None),
+        ],
+        [(feats, HBM), (send_rows, HBM), (tile_src, HBM), (tile_dst, HBM)],
+        [
+            VMEM((nodes, width), bf16),
+            VMEM((parts, each), jnp.int32),
+            turn,
+            pick,
+            staged,
+            DMA((5,)),
+        ],
     )
     table0 = lax.all_to_all(out0, dom, split_axis=0, concat_axis=0, tiled=True)
     own, ghost, own_train, noise_train, part1, flag, own_rest, ghost_rest = call(
@@ -664,14 +688,12 @@
         [
             (tile_block, HBM),
             (tile_count, SMEM),
-            (tile_src, HBM),
-            (tile_dst, HBM),
+            (src, None),
+            (dst, None),
             (hop_noise, HBM),
             (start0, None),
         ],
         [
-            VMEM((tiles, slots), jnp.int32),
-            VMEM((tiles, slots), jnp.int32),
             VMEM((nodes, width), bf16),
             VMEM((tiles, slots, 128), bf16),
             VMEM((tiles * 16, slots), bf16),
@@ -680,7 +702,7 @@
             VMEM((nodes, max(nodes, ghosts)), bf16),
             VMEM((nodes, nodes), bf16),
             SMEM(tile_block.shape, jnp.int32),
-            DMA((6,)),
+            DMA((4,)),
         ],
     )
     start1, out1, side = call(
@@ -688,7 +710,7 @@
         16,
         [
             ((nodes, width), bf16, None),
-            ((parts, each, width), bf16, None),
+            ((parts, each, width), bf16, HBM),
             ((2 * train + 16, width), bf16, None),
         ],
         [
@@ -701,7 +723,7 @@
             (own0, None),
             (labels.reshape(1, train), VMEM),
         ],
-        [VMEM((nodes, width), f32), VMEM((nodes, ghosts), bf16), turn, pick],
+        [VMEM((nodes, width), f32), VMEM((nodes, ghosts), bf16), turn, pick, staged, DMA(())],
     )
     table1 = lax.all_to_all(out1, dom, split_axis=0, concat_axis=0, tiled=True)
     place = jnp.stack([lax.axis_index(dom), lax.axis_index("grp")]).astype(jnp.int32)
@@ -718,7 +740,7 @@
         train_kernel,
         12,
         [
-            ((copies, train, width), bf16, None),
+            ((copies, train, width), bf16, HBM),
             ((len(sides) * 2 * train + 16, width), bf16, None),
         ],
         [
@@ -737,6 +759,8 @@
             VMEM((train, width), f32),
             VMEM((train, max(nodes, ghosts)), bf16),
             VMEM((128, 128), f32),
+            VMEM((copies, train, width), bf16),
+            DMA(()),
         ],
     )
     if few:
@@ -796,7 +820,7 @@
         def classify(place_ref, *refs):
             sides_in, rest = refs[:chips], refs[chips:]
             two_ref, first_ref, *outs = rest[:11]
-            held, rest = rest[11 : 11 + chips], rest[11 + chips :]
+            rest = rest[11:]
             classify_kernel(
                 False,
                 place_ref,
@@ -807,7 +831,6 @@
                 sides_in,
                 first_ref,
                 *outs,
-                held,
                 first_ref,
                 *rest,
             )
@@ -818,10 +841,10 @@
             44,
             [(value.shape, f32, None) for value in fixed[3:]] + [((rows, hid), bf16, None)],
             [(place, SMEM)]
-            + [(value, HBM) for value in sides]
+            + [(value, None) for value in sides]
             + [(every2, None), (held_first, None)]
             + [(value, HBM) for value in fixed[1:]],
-            [VMEM(value.shape, bf16) for value in sides] + scratch[1:],
+            scratch[1:],
         )
         got = lax.ppermute(other, "core", [(0, 1), (1, 0)])
         first, second, third = call(
@@ -845,7 +868,6 @@
                 two_ref,
                 None,
                 *rest[:9],
-                None,
                 None,
                 *rest[9:],
             )

time: 67.6 us -> 67.6 us (level)
  Pallas kernels: 30.9 us -> 29.4 us
  waiting for transfers between devices: 6.32 us -> 7.28 us
  local copies, waits for them, and re-layouts: 0.66 us -> 1.57 us
    pallas_call x7, Pallas kernels: 30.9 us -> 29.4 us  [call(): pl.pallas_call(kernel, out_shape=[shape_of(*out) for out in outs], in_spe...]
    ppermute x6, waiting for transfers between devices: 4.42 us -> 5.38 us  [shifted(): lax.ppermute(value, name, [((at + step * shift) % size, at) for at in ran...]
    unnamed x10 -> x8, local copies, waits for them, and re-layouts: 0.66 us -> 1.57 us
  transfers between devices with their start and end apart: 10 -> 10, of which waited for: 4 -> 5; matrix products, arithmetic and copies ran while one was open for 0% -> 0% of each run, Pallas kernels for 21% -> 19%
where the time goes in v9:
time: 67.6 us; the launch traced here: 67.1 us
  Pallas kernels  29.4 us (43%)
  starting transfers between devices  27.4 us (41%)
  waiting for transfers between devices  7.28 us (11%)
  local copies, waits for them, and re-layouts  1.57 us (2%)
  between operations  1.41 us (2%)
    pallas_call x7, Pallas kernels, call(): pl.pallas_call(kernel, out_shape=[shape_of(*out) for out in outs], in_spe...  29.4 us
    ppermute x6, starting transfers between devices, shifted(): lax.ppermute(value, name, [((at + step * shift) % size, at) for at in ran...  9.46 us
    all_to_all x1, starting transfers between devices, local(): lax.all_to_all(last, ('chip', 'grp'), split_axis=0, concat_axis=0, tiled=...  6.89 us
    all_to_all x1, starting transfers between devices, local(): table1 = lax.all_to_all(out1, dom, split_axis=0, concat_axis=0, tiled=True)  5.8 us
    ppermute x6, waiting for transfers between devices, shifted(): lax.ppermute(value, name, [((at + step * shift) % size, at) for at in ran...  5.38 us
    all_to_all x1, starting transfers between devices, local(): table0 = lax.all_to_all(out0, dom, split_axis=0, concat_axis=0, tiled=True)  5.18 us
    ppermute x1, waiting for transfers between devices, local(): got = lax.ppermute(other, 'core', [(0, 1), (1, 0)])  1.9 us
    unnamed x8, local copies, waits for them, and re-layouts  1.57 us
  transfers between devices with their start and end apart: 10, of which 5 were waited for; matrix products, arithmetic and copies ran while one was open for 0% of the time, Pallas kernels for 19%

profile of v9, /device:TPU:0, one launch (start us, length us, event | category | flops | bytes accessed | tf_op | source)
XLA Modules:
  0.0 67.1 jit_solution(7909571668187728540)
XLA Ops:
  0.6 0.0 copy-start.2
  0.6 0.0 copy-start.3
  0.7 2.2 %shard_map.165 = (bf16[1024,256]{1,0:T(8,128)(2,1)S(1)}, bf16[8,32,256]{2,1,0:T(8,128)(2,1)}, bf16[32,256]{1,0:T(8,128)(2,1)S(1)}, s32[64,256]{1,0:T(8,128)S(1)}, s32[64,256]{1,0:T(8,128)S(1)}) custom-call(bf16[1,1,1024,256]{3,2,1,0:T(8,128)(2,1)} %feats_hbm.1, s32[1,1,8,32]{3,2,1,0:T(8,128)} %rows_hbm.1, s32[1,1,64,256]{3,2,1,0:T(8,128)} %src_hbm.1, ...), custom_call_target="tpu_custom_call" | custom-call | tf_op jit(solution)/shard_map/pallas_call | solution.py:603
  2.8 5.2 %all-to-all-start = ((bf16[8,32,256]{2,1,0:T(8,128)(2,1)}), bf16[8,32,256]{2,1,0:T(8,128)(2,1)S(1)}, u32[]{:S(2)}, u32[]{:S(2)}) async-start(bf16[8,32,256]{2,1,0:T(8,128)(2,1)} %get-tuple-element.41), calls=%async_computation | async-start | bytes 262144 | tf_op jit(solution)/shard_map/all_to_all | solution.py:674
  8.7 8.4 %shard_map.166 = (bf16[1024,1024]{1,0:T(8,128)(2,1)}, bf16[1024,256]{1,0:T(8,128)(2,1)S(1)}, bf16[32,1024]{1,0:T(8,128)(2,1)S(1)}, bf16[32,256]{1,0:T(8,128)(2,1...) custom-call(s32[1,1,64]{2,1,0:T(1,128)} %blocks_hbm.1, ...), custom_call_target="tpu_custom_call" | custom-call | tf_op jit(solution)/shard_map/pallas_call | solution.py:603
  17.1 0.0 all-to-all-done.table_ref
  17.1 0.0 copy-done.2
  17.1 0.0 copy-done.3
  17.1 2.3 %shard_map.167 = (bf16[1024,256]{1,0:T(8,128)(2,1)S(1)}, bf16[8,32,256]{2,1,0:T(8,128)(2,1)}, bf16[80,256]{1,0:T(8,128)(2,1)S(1)}) custom-call(s32[1]{0:T(128)} %get-tuple-element.34.flag_ref, f32[1024,256]{1,0:T(8,128)S(1)} %get-tuple-element.40.part_ref, bf16[1024,256]{1,0:T(8,128)(2,1)S(1)} %get-tuple-element.36.ghost_ref, ...), custom_call_target="tpu_custom_call" | custom-call | tf_op jit(solution)/shard_map/pallas_call | solution.py:603
  19.4 5.8 %all-to-all-start.1 = ((bf16[8,32,256]{2,1,0:T(8,128)(2,1)}), bf16[8,32,256]{2,1,0:T(8,128)(2,1)S(1)}, u32[]{:S(2)}, u32[]{:S(2)}) async-start(bf16[8,32,256]{2,1,0:T(8,128)(2,1)} %get-tuple-element.44), calls=%async_computation.1 | async-start | bytes 262144 | tf_op jit(solution)/shard_map/all_to_all | solution.py:728
  25.2 0.1 collective-permute-start.2
  25.3 4.1 %collective-permute-start.1 = (bf16[80,256]{1,0:T(8,128)(2,1)S(1)}, bf16[80,256]{1,0:T(8,128)(2,1)S(1)}, u32[]{:S(2)}, u32[]{:S(2)}) collective-permute-start(bf16[80,256]{1,0:T(8,128)(2,1)S(1)} %get-tuple-element.45.refs_0_), channel_id=1, source_target_pairs={{2,0},{3,1},{0,2},{1,3},{6,4},{7,5},{4,6},{5,7},{10,8},{11,9},{8,1... | collective-permute-start | bytes 122888 | tf_op jit(solution)/shard_map/ppermute | solution.py:734
  29.4 1.3 %collective-permute-start = (bf16[80,256]{1,0:T(8,128)(2,1)S(1)}, bf16[80,256]{1,0:T(8,128)(2,1)S(1)}, u32[]{:S(2)}, u32[]{:S(2)}) collective-permute-start(bf16[80,256]{1,0:T(8,128)(2,1)S(1)} %get-tuple-element.45.refs_0_), channel_id=1, source_target_pairs={{1,0},{2,1},{3,2},{0,3},{5,4},{6,5},{7,6},{4,7},{9,8},{10,9},{11,1... | collective-permute-start | bytes 122888 | tf_op jit(solution)/shard_map/ppermute | solution.py:734
  30.7 0.1 pad_add_fusion.place_ref
  30.8 0.3 collective-permute-done.2.refs_3_
  31.1 1.5 %collective-permute-done.1.refs_2_ = bf16[80,256]{1,0:T(8,128)(2,1)S(1)} collective-permute-done((bf16[80,256]{1,0:T(8,128)(2,1)S(1)}, bf16[80,256]{1,0:T(8,128)(2,1)S(1)}, u32[]{:S(2)}, u32[]{:S(2)}) %collective-permute-start.1) | collective-permute-done | bytes 40992 | tf_op jit(solution)/shard_map/ppermute | solution.py:734
  32.6 0.8 %collective-permute-done.refs_1_ = bf16[80,256]{1,0:T(8,128)(2,1)S(1)} collective-permute-done((bf16[80,256]{1,0:T(8,128)(2,1)S(1)}, bf16[80,256]{1,0:T(8,128)(2,1)S(1)}, u32[]{:S(2)}, u32[]{:S(2)}) %collective-permute-start) | collective-permute-done | bytes 40992 | tf_op jit(solution)/shard_map/ppermute | solution.py:734
  33.4 0.0 all-to-all-done.1.table_ref
  33.4 2.2 %shard_map.168 = (bf16[16,32,256]{2,1,0:T(8,128)(2,1)}, bf16[272,256]{1,0:T(8,128)(2,1)S(1)}) custom-call(s32[1]{0:T(128)} %get-tuple-element.34.flag_ref, s32[2]{0:T(128)S(1)} %pad_add_fusion.place_ref, bf16[32,1024]{1,0:T(8,128)(2,1)S(1)} %get-tuple-element.35.own_ref, bf16[1024,256]{1,0:T(8,128)(2,1)S(1)} %get-tuple-element.36.ghost_ref, ...), custom_call_target="tpu_custom_call" | custom-call | tf_op jit(solution)/shard_map/pallas_call | solution.py:603
  35.7 6.9 %all-to-all-start.2 = ((bf16[16,32,256]{2,1,0:T(8,128)(2,1)}), bf16[16,32,256]{2,1,0:T(8,128)(2,1)S(1)}, u32[]{:S(2)}, u32[]{:S(2)}) async-start(bf16[16,32,256]{2,1,0:T(8,128)(2,1)} %get-tuple-element.49), calls=%async_computation.2 | async-start | bytes 524288 | tf_op jit(solution)/shard_map/all_to_all | solution.py:767
  42.6 2.8 %collective-permute-start.5 = (bf16[272,256]{1,0:T(8,128)(2,1)S(1)}, bf16[272,256]{1,0:T(8,128)(2,1)S(1)}, u32[]{:S(2)}, u32[]{:S(2)}) collective-permute-start(bf16[272,256]{1,0:T(8,128)(2,1)S(1)} %get-tuple-element.46.token_ref.refs_0_), channel_id=1, source_target_pairs={{8,0},{16,8},{24,16},{0,24},{9,1},{17,9},{25,17},{1,25},{10,2},{18... | collective-permute-start | bytes 417800 | tf_op jit(solution)/shard_map/ppermute | solution.py:734
  45.4 0.6 collective-permute-start.4
  46.0 0.6 collective-permute-start.3
  46.5 4.6 %shard_map.169 = (bf16[2,1,1,1024,256]{4,3,2,1,0:T(8,128)(2,1)}, bf16[768,1024]{1,0:T(8,128)(2,1)S(1)}) custom-call(s32[1]{0:T(128)} %get-tuple-element.34.flag_ref, bf16[272,256]{1,0:T(8,128)(2,1)S(1)} %get-tuple-element.46.token_ref.refs_0_, bf16[1024,1024]{1,0:T(8,128)(2,1)} %get-tuple-element.47.own_hbm, ...), custom_call_target="tpu_custom_call" | custom-call | tf_op jit(solution)/shard_map/pallas_call | solution.py:603
  51.1 0.0 collective-permute-done.5.refs_3_
  51.1 2.8 %collective-permute-done.4.refs_2_ = bf16[272,256]{1,0:T(8,128)(2,1)S(1)} collective-permute-done((bf16[272,256]{1,0:T(8,128)(2,1)S(1)}, bf16[272,256]{1,0:T(8,128)(2,1)S(1)}, u32[]{:S(2)}, u32[]{:S(2)}) %collective-permute-start.4) | collective-permute-done | bytes 139296 | tf_op jit(solution)/shard_map/ppermute | solution.py:734
  53.9 0.0 collective-permute-done.3.refs_1_
  53.9 0.0 copy-start
  53.9 0.7 copy-done
  54.6 0.0 all-to-all-done.2.refs_4_
  54.6 0.0 copy-start.1
  54.6 0.9 %copy-done.1 = bf16[272,256]{1,0:T(8,128)(2,1)S(1)} copy-done((bf16[272,256]{1,0:T(8,128)(2,1)S(1)}, bf16[272,256]{1,0:T(8,128)(2,1)}, u32[]{:S(2)}) %copy-start.1) | copy-done | bytes 139288
  55.5 8.6 %shard_map.170 = (f32[96,1024]{1,0:T(8,128)S(1)}, f32[128,1024]{1,0:T(8,128)S(1)}, f32[172,128]{1,0:T(8,128)S(1)}, bf16[256,1024]{1,0:T(8,128)(2,1)S(1)}) custom-call(s32[2]{0:T(128)S(1)} %pad_add_fusion.place_ref, bf16[272,256]{1,0:T(8,128)(2,1)S(1)} %get-tuple-element.46.token_ref.refs_0_, bf16[272,256]{1,0:T(8,128)(2,1)S(1)} %copy-done.1, ...), custom_call_target="tpu_custom_call" | custom-call | tf_op jit(solution)/shard_map/pallas_call | solution.py:603
  64.1 0.1 collective-permute-start.6
  64.1 1.9 %collective-permute-done.6.got_ref = bf16[256,1024]{1,0:T(8,128)(2,1)S(1)} collective-permute-done((bf16[256,1024]{1,0:T(8,128)(2,1)S(1)}, bf16[256,1024]{1,0:T(8,128)(2,1)S(1)}, u32[]{:S(2)}, u32[]{:S(2)}) %collective-permute-start.6) | collective-permute-done | bytes 524320 | tf_op jit(solution)/shard_map/ppermute | solution.py:849
  66.0 1.1 %shard_map.171 = (f32[96,1024]{1,0:T(8,128)}, f32[128,1024]{1,0:T(8,128)}, f32[172,128]{1,0:T(8,128)}) custom-call(bf16[256,1024]{1,0:T(8,128)(2,1)S(1)} %collective-permute-done.6.got_ref, f32[96,1024]{1,0:T(8,128)S(1)} %get-tuple-element.52.one_ref, f32[128,1024]{1,0:T(8,128)S(1)} %get-tuple-element.53.two_ref, f32[172,128]{1,0:T(8,128)S(1)} %get-tuple-element.54.three_ref), custom_call_target="tpu_custom_call" | custom-call | tf_op jit(solution)/shard_map/pallas_call | solution.py:603
Async XLA Ops:
  0.6 16.5 %copy-start.2 = (s32[1,1,8,32]{3,2,1,0:T(8,128)S(1)}, s32[1,1,8,32]{3,2,1,0:T(8,128)}, u32[]{:S(2)}) copy-start(s32[1,1,8,32]{3,2,1,0:T(8,128)} %rows_hbm.1) | copy-start | bytes 3076
  0.6 16.5 %copy-start.3 = (s32[1,1,32]{2,1,0:T(1,128)S(1)}, s32[1,1,32]{2,1,0:T(1,128)}, u32[]{:S(2)}) copy-start(s32[1,1,32]{2,1,0:T(1,128)} %param.21) | copy-start | bytes 388
  2.8 14.2 %all-to-all-start = ((bf16[8,32,256]{2,1,0:T(8,128)(2,1)}), bf16[8,32,256]{2,1,0:T(8,128)(2,1)S(1)}, u32[]{:S(2)}, u32[]{:S(2)}) async-start(bf16[8,32,256]{2,1,0:T(8,128)(2,1)} %get-tuple-element.41), calls=%async_computation | async-start | bytes 262144 | tf_op jit(solution)/shard_map/all_to_all | solution.py:674
  19.4 14.0 %all-to-all-start.1 = ((bf16[8,32,256]{2,1,0:T(8,128)(2,1)}), bf16[8,32,256]{2,1,0:T(8,128)(2,1)S(1)}, u32[]{:S(2)}, u32[]{:S(2)}) async-start(bf16[8,32,256]{2,1,0:T(8,128)(2,1)} %get-tuple-element.44), calls=%async_computation.1 | async-start | bytes 262144 | tf_op jit(solution)/shard_map/all_to_all | solution.py:728
  25.2 5.9 %collective-permute-start.2 = (bf16[80,256]{1,0:T(8,128)(2,1)S(1)}, bf16[80,256]{1,0:T(8,128)(2,1)S(1)}, u32[]{:S(2)}, u32[]{:S(2)}) collective-permute-start(bf16[80,256]{1,0:T(8,128)(2,1)S(1)} %get-tuple-element.45.refs_0_), channel_id=1, source_target_pairs={{3,0},{0,1},{1,2},{2,3},{7,4},{4,5},{5,6},{6,7},{11,8},{8,9},{9,10... | collective-permute-start | bytes 122888 | tf_op jit(solution)/shard_map/ppermute | solution.py:734
  25.3 7.3 %collective-permute-start.1 = (bf16[80,256]{1,0:T(8,128)(2,1)S(1)}, bf16[80,256]{1,0:T(8,128)(2,1)S(1)}, u32[]{:S(2)}, u32[]{:S(2)}) collective-permute-start(bf16[80,256]{1,0:T(8,128)(2,1)S(1)} %get-tuple-element.45.refs_0_), channel_id=1, source_target_pairs={{2,0},{3,1},{0,2},{1,3},{6,4},{7,5},{4,6},{5,7},{10,8},{11,9},{8,1... | collective-permute-start | bytes 122888 | tf_op jit(solution)/shard_map/ppermute | solution.py:734
  29.4 4.0 %collective-permute-start = (bf16[80,256]{1,0:T(8,128)(2,1)S(1)}, bf16[80,256]{1,0:T(8,128)(2,1)S(1)}, u32[]{:S(2)}, u32[]{:S(2)}) collective-permute-start(bf16[80,256]{1,0:T(8,128)(2,1)S(1)} %get-tuple-element.45.refs_0_), channel_id=1, source_target_pairs={{1,0},{2,1},{3,2},{0,3},{5,4},{6,5},{7,6},{4,7},{9,8},{10,9},{11,1... | collective-permute-start | bytes 122888 | tf_op jit(solution)/shard_map/ppermute | solution.py:734
  35.7 18.9 %all-to-all-start.2 = ((bf16[16,32,256]{2,1,0:T(8,128)(2,1)}), bf16[16,32,256]{2,1,0:T(8,128)(2,1)S(1)}, u32[]{:S(2)}, u32[]{:S(2)}) async-start(bf16[16,32,256]{2,1,0:T(8,128)(2,1)} %get-tuple-element.49), calls=%async_computation.2 | async-start | bytes 524288 | tf_op jit(solution)/shard_map/all_to_all | solution.py:767
  42.6 8.5 %collective-permute-start.5 = (bf16[272,256]{1,0:T(8,128)(2,1)S(1)}, bf16[272,256]{1,0:T(8,128)(2,1)S(1)}, u32[]{:S(2)}, u32[]{:S(2)}) collective-permute-start(bf16[272,256]{1,0:T(8,128)(2,1)S(1)} %get-tuple-element.46.token_ref.refs_0_), channel_id=1, source_target_pairs={{8,0},{16,8},{24,16},{0,24},{9,1},{17,9},{25,17},{1,25},{10,2},{18... | collective-permute-start | bytes 417800 | tf_op jit(solution)/shard_map/ppermute | solution.py:734
  45.4 8.5 %collective-permute-start.4 = (bf16[272,256]{1,0:T(8,128)(2,1)S(1)}, bf16[272,256]{1,0:T(8,128)(2,1)S(1)}, u32[]{:S(2)}, u32[]{:S(2)}) collective-permute-start(bf16[272,256]{1,0:T(8,128)(2,1)S(1)} %get-tuple-element.46.token_ref.refs_0_), channel_id=1, source_target_pairs={{16,0},{24,8},{0,16},{8,24},{17,1},{25,9},{1,17},{9,25},{18,2},{26... | collective-permute-start | bytes 417800 | tf_op jit(solution)/shard_map/ppermute | solution.py:734
  46.0 7.9 %collective-permute-start.3 = (bf16[272,256]{1,0:T(8,128)(2,1)S(1)}, bf16[272,256]{1,0:T(8,128)(2,1)S(1)}, u32[]{:S(2)}, u32[]{:S(2)}) collective-permute-start(bf16[272,256]{1,0:T(8,128)(2,1)S(1)} %get-tuple-element.46.token_ref.refs_0_), channel_id=1, source_target_pairs={{24,0},{0,8},{8,16},{16,24},{25,1},{1,9},{9,17},{17,25},{26,2},{2,... | collective-permute-start | bytes 417800 | tf_op jit(solution)/shard_map/ppermute | solution.py:734
  53.9 0.7 copy-start
  54.6 0.9 %copy-start.1 = (bf16[272,256]{1,0:T(8,128)(2,1)S(1)}, bf16[272,256]{1,0:T(8,128)(2,1)}, u32[]{:S(2)}) copy-start(bf16[272,256]{1,0:T(8,128)(2,1)} %copy-done) | copy-start | bytes 417796
  64.1 2.0 %collective-permute-start.6 = (bf16[256,1024]{1,0:T(8,128)(2,1)S(1)}, bf16[256,1024]{1,0:T(8,128)(2,1)S(1)}, u32[]{:S(2)}, u32[]{:S(2)}) collective-permute-start(bf16[256,1024]{1,0:T(8,128)(2,1)S(1)} %get-tuple-element.51), channel_id=1, source_target_pairs={{0,4},{4,0},{1,5},{5,1},{2,6},{6,2},{3,7},{7,3},{8,12},{12,8},{9,1... | collective-permute-start | bytes 1572872 | tf_op jit(solution)/shard_map/ppermute | solution.py:849

commit v10 on v9

--- a/solution.py
+++ b/solution.py
@@ -9,7 +9,7 @@
 from jax.sharding import PartitionSpec as P
 
 BLOCK = 128
-LOW = 256
+LOW = 512
 GROUP = 8
 clip_bound = 4.0
 noise_mult = 1.0
@@ -299,7 +299,7 @@
     table_ref,
     *refs,
 ):
-    *piece_refs, out_hbm, side_ref, sums_ref, rest_ref, turn_ref, staged_ref, sem = refs
+    *piece_refs, out_hbm, side_hbm, sums_ref, rest_ref, turn_ref, staged_ref, side_ref, sems = refs
     train, width = sums_ref.shape
     table = table_ref[...].reshape(-1, width)
     parts = (
@@ -308,7 +308,7 @@
     )
     aggregate(flag_ref, noise_ref[...].astype(f32), parts, sums_ref, rest_ref)
     last = jnp.broadcast_to(normalize(sums_ref[...])[None], staged_ref.shape)
-    out_copy = post(last, staged_ref, out_hbm, sem)
+    out_copy = post(last, staged_ref, out_hbm, sems.at[0])
     length = piece_refs[0].shape[0] - 16
     groups = len(piece_refs)
     if groups > 1:
@@ -318,6 +318,9 @@
             side_ref[pl.ds(at, length), :] = ref[:length, :]
             turn_ref[pl.ds(group, 1), :] = ref[length:, :128].astype(f32)[:1]
         side_ref[groups * length :, :128] = turn_ref[:16, :].astype(bf16)
+        side_copy = pltpu.make_async_copy(side_ref, side_hbm, sems.at[1])
+        side_copy.start()
+        side_copy.wait()
     out_copy.wait()
 
 
@@ -386,6 +389,7 @@
     g_second_ref,
     g_third_ref,
     send_ref,
+    side_hbm,
     w_first_ref,
     w_second_ref,
     w_third_ref,
@@ -453,10 +457,12 @@
             in_ref[:, hop * width : (hop + 1) * width] = ref[...].reshape(-1, width)
     else:
         chips = len(side_refs)
-        copies = fetch(pairs[1:], sems)
+        copies = fetch(((side_hbm, side_refs[0]),) + pairs[1:], sems)
         groups = two_ref.shape[0] // chips
         rows = groups * train
-        for shift, ref in enumerate(side_refs):
+        for shift, ref in [*enumerate(side_refs)][::-1]:
+            if shift == 0:
+                copies[0].wait()
             part = lax.rem(place // 2 - shift + chips, chips)
             at = pl.multiple_of(part * rows, rows)
             for group in range(groups):
@@ -500,12 +506,12 @@
         lambda cut: dot(in_ref[cut, :], w_first_ref[...]), activate, h_one_ref, slope_one_ref
     )
     if not many:
-        copies[0].wait()
+        copies[1].wait()
     sq_two = layer(
         lambda cut: dot(h_one_ref[cut, :], w_second_ref[...]), activate, h_two_ref, slope_two_ref
     )
     if not many:
-        copies[1].wait()
+        copies[2].wait()
         pad()
     logits = dot_nt(h_two_ref[...], w_third_pad_ref[...])
     ids = lax.broadcasted_iota(jnp.int32, (logits.shape[0], wide), 1)
@@ -533,7 +539,7 @@
     factor = clip_bound / jnp.maximum(norm, clip_bound)
 
     if not many:
-        for copy in copies[2:]:
+        for copy in copies[3:]:
             copy.wait()
         set_noise()
     share_one, share = g_first_ref.shape[0], g_second_ref.shape[0]
@@ -736,12 +742,13 @@
         ]
 
     sides = [side] + (shifted(side, "grp", grp, 1) if few else [])
+    side_shape = (len(sides) * 2 * train + 16, width)
     last, side = call(
         train_kernel,
         12,
         [
             ((copies, train, width), bf16, HBM),
-            ((len(sides) * 2 * train + 16, width), bf16, None),
+            (side_shape, bf16, HBM),
         ],
         [
             (flag, SMEM),
@@ -760,7 +767,8 @@
             VMEM((train, max(nodes, ghosts)), bf16),
             VMEM((128, 128), f32),
             VMEM((copies, train, width), bf16),
-            DMA(()),
+            VMEM(side_shape, bf16),
+            DMA((2,)),
         ],
     )
     if few:
@@ -777,7 +785,7 @@
         [((2, 1, 1, nodes, width), bf16, VMEM), (w_first.shape, bf16, None)],
         [
             (flag, SMEM),
-            (side, None),
+            (side, HBM),
             (own, HBM),
             (own_rest, HBM),
             (ghost_rest, HBM),
@@ -820,7 +828,7 @@
         def classify(place_ref, *refs):
             sides_in, rest = refs[:chips], refs[chips:]
             two_ref, first_ref, *outs = rest[:11]
-            rest = rest[11:]
+            held, *rest = rest[11:]
             classify_kernel(
                 False,
                 place_ref,
@@ -828,9 +836,10 @@
                 None,
                 None,
                 two_ref,
-                sides_in,
+                (held,) + sides_in[1:],
                 first_ref,
                 *outs,
+                sides_in[0],
                 first_ref,
                 *rest,
             )
@@ -841,10 +850,11 @@
             44,
             [(value.shape, f32, None) for value in fixed[3:]] + [((rows, hid), bf16, None)],
             [(place, SMEM)]
-            + [(value, None) for value in sides]
+            + [(side, HBM)]
+            + [(value, None) for value in sides[1:]]
             + [(every2, None), (held_first, None)]
             + [(value, HBM) for value in fixed[1:]],
-            scratch[1:],
+            [VMEM(side_shape, bf16)] + scratch[1:],
         )
         got = lax.ppermute(other, "core", [(0, 1), (1, 0)])
         first, second, third = call(
@@ -868,6 +878,7 @@
                 two_ref,
                 None,
                 *rest[:9],
+                None,
                 None,
                 *rest[9:],
             )

time: 67.6 us -> 65.4 us (0.967)
  Pallas kernels: 29.4 us -> 25.8 us
  starting transfers between devices: 27.4 us -> 29.2 us
  local copies, waits for them, and re-layouts: 1.57 us -> 0.01 us
    all_to_all x1, starting transfers between devices: 5.8 us -> 9.71 us  [local(): table1 = lax.all_to_all(out1, dom, split_axis=0, concat_axis=0, tiled=True)]
    pallas_call x7, Pallas kernels: 29.4 us -> 25.8 us  [call(): pl.pallas_call(kernel, out_shape=[shape_of(*out) for out in outs], in_spe...]
    unnamed x8 -> x4, local copies, waits for them, and re-layouts: 1.57 us -> 0.01 us
    ppermute x6, starting transfers between devices: 9.46 us -> 8.13 us  [shifted(): lax.ppermute(value, name, [((at + step * shift) % size, at) for at in ran...]
    all_to_all x1, starting transfers between devices: 6.89 us -> 6.08 us  [local(): lax.all_to_all(last, ('chip', 'grp'), split_axis=0, concat_axis=0, tiled=...]
  transfers between devices with their start and end apart: 10 -> 10, of which waited for: 5 -> 5; matrix products, arithmetic and copies ran while one was open for 0% -> 0% of each run, Pallas kernels for 19% -> 15%
where the time goes in v10:
time: 65.4 us; the launch traced here: 64.3 us
  starting transfers between devices  29.2 us (45%)
  Pallas kernels  25.8 us (39%)
  waiting for transfers between devices  7.83 us (12%)
  between operations  1.4 us (2%)
    pallas_call x7, Pallas kernels, call(): pl.pallas_call(kernel, out_shape=[shape_of(*out) for out in outs], in_spe...  25.8 us
    all_to_all x1, starting transfers between devices, local(): table1 = lax.all_to_all(out1, dom, split_axis=0, concat_axis=0, tiled=True)  9.71 us
    ppermute x6, starting transfers between devices, shifted(): lax.ppermute(value, name, [((at + step * shift) % size, at) for at in ran...  8.13 us
    all_to_all x1, starting transfers between devices, local(): lax.all_to_all(last, ('chip', 'grp'), split_axis=0, concat_axis=0, tiled=...  6.08 us
    ppermute x6, waiting for transfers between devices, shifted(): lax.ppermute(value, name, [((at + step * shift) % size, at) for at in ran...  5.93 us
    all_to_all x1, starting transfers between devices, local(): table0 = lax.all_to_all(out0, dom, split_axis=0, concat_axis=0, tiled=True)  5.18 us
    ppermute x1, waiting for transfers between devices, local(): got = lax.ppermute(other, 'core', [(0, 1), (1, 0)])  1.9 us
  transfers between devices with their start and end apart: 10, of which 5 were waited for; matrix products, arithmetic and copies ran while one was open for 0% of the time, Pallas kernels for 15%

profile of v10, /device:TPU:0, one launch (start us, length us, event | category | flops | bytes accessed | tf_op | source)
XLA Modules:
  0.0 64.3 jit_solution(7866499853733954143)
XLA Ops:
  0.6 0.0 copy-start
  0.6 0.0 copy-start.1
  0.7 2.2 %shard_map.165 = (bf16[1024,256]{1,0:T(8,128)(2,1)S(1)}, bf16[8,32,256]{2,1,0:T(8,128)(2,1)}, bf16[32,256]{1,0:T(8,128)(2,1)S(1)}, s32[64,256]{1,0:T(8,128)S(1)}, s32[64,256]{1,0:T(8,128)S(1)}) custom-call(bf16[1,1,1024,256]{3,2,1,0:T(8,128)(2,1)} %feats_hbm.1, s32[1,1,8,32]{3,2,1,0:T(8,128)} %rows_hbm.1, s32[1,1,64,256]{3,2,1,0:T(8,128)} %src_hbm.1, ...), custom_call_target="tpu_custom_call" | custom-call | tf_op jit(solution)/shard_map/pallas_call | solution.py:609
  2.8 5.2 %all-to-all-start = ((bf16[8,32,256]{2,1,0:T(8,128)(2,1)}), bf16[8,32,256]{2,1,0:T(8,128)(2,1)S(1)}, u32[]{:S(2)}, u32[]{:S(2)}) async-start(bf16[8,32,256]{2,1,0:T(8,128)(2,1)} %get-tuple-element.41), calls=%async_computation | async-start | bytes 262144 | tf_op jit(solution)/shard_map/all_to_all | solution.py:680
  8.7 5.1 %shard_map.166 = (bf16[1024,1024]{1,0:T(8,128)(2,1)}, bf16[1024,256]{1,0:T(8,128)(2,1)S(1)}, bf16[32,1024]{1,0:T(8,128)(2,1)S(1)}, bf16[32,256]{1,0:T(8,128)(2,1...) custom-call(s32[1,1,64]{2,1,0:T(1,128)} %blocks_hbm.1, ...), custom_call_target="tpu_custom_call" | custom-call | tf_op jit(solution)/shard_map/pallas_call | solution.py:609
  13.8 0.0 all-to-all-done.table_ref
  13.8 0.0 copy-done
  13.8 0.0 copy-done.1
  13.8 2.3 %shard_map.167 = (bf16[1024,256]{1,0:T(8,128)(2,1)S(1)}, bf16[8,32,256]{2,1,0:T(8,128)(2,1)}, bf16[80,256]{1,0:T(8,128)(2,1)S(1)}) custom-call(s32[1]{0:T(128)} %get-tuple-element.34.flag_ref, f32[1024,256]{1,0:T(8,128)S(1)} %get-tuple-element.40.part_ref, bf16[1024,256]{1,0:T(8,128)(2,1)S(1)} %get-tuple-element.36.ghost_ref, ...), custom_call_target="tpu_custom_call" | custom-call | tf_op jit(solution)/shard_map/pallas_call | solution.py:609
  16.1 9.7 %all-to-all-start.1 = ((bf16[8,32,256]{2,1,0:T(8,128)(2,1)}), bf16[8,32,256]{2,1,0:T(8,128)(2,1)S(1)}, u32[]{:S(2)}, u32[]{:S(2)}) async-start(bf16[8,32,256]{2,1,0:T(8,128)(2,1)} %get-tuple-element.44), calls=%async_computation.1 | async-start | bytes 262144 | tf_op jit(solution)/shard_map/all_to_all | solution.py:734
  25.8 0.7 %collective-permute-start.2 = (bf16[80,256]{1,0:T(8,128)(2,1)S(1)}, bf16[80,256]{1,0:T(8,128)(2,1)S(1)}, u32[]{:S(2)}, u32[]{:S(2)}) collective-permute-start(bf16[80,256]{1,0:T(8,128)(2,1)S(1)} %get-tuple-element.45.refs_0_), channel_id=1, source_target_pairs={{3,0},{0,1},{1,2},{2,3},{7,4},{4,5},{5,6},{6,7},{11,8},{8,9},{9,10... | collective-permute-start | bytes 122888 | tf_op jit(solution)/shard_map/ppermute | solution.py:740
  26.5 2.6 %collective-permute-start.1 = (bf16[80,256]{1,0:T(8,128)(2,1)S(1)}, bf16[80,256]{1,0:T(8,128)(2,1)S(1)}, u32[]{:S(2)}, u32[]{:S(2)}) collective-permute-start(bf16[80,256]{1,0:T(8,128)(2,1)S(1)} %get-tuple-element.45.refs_0_), channel_id=1, source_target_pairs={{2,0},{3,1},{0,2},{1,3},{6,4},{7,5},{4,6},{5,7},{10,8},{11,9},{8,1... | collective-permute-start | bytes 122888 | tf_op jit(solution)/shard_map/ppermute | solution.py:740
  29.1 0.9 %collective-permute-start = (bf16[80,256]{1,0:T(8,128)(2,1)S(1)}, bf16[80,256]{1,0:T(8,128)(2,1)S(1)}, u32[]{:S(2)}, u32[]{:S(2)}) collective-permute-start(bf16[80,256]{1,0:T(8,128)(2,1)S(1)} %get-tuple-element.45.refs_0_), channel_id=1, source_target_pairs={{1,0},{2,1},{3,2},{0,3},{5,4},{6,5},{7,6},{4,7},{9,8},{10,9},{11,1... | collective-permute-start | bytes 122888 | tf_op jit(solution)/shard_map/ppermute | solution.py:740
  30.0 0.1 pad_add_fusion.place_ref
  30.1 2.0 %collective-permute-done.2.refs_3_ = bf16[80,256]{1,0:T(8,128)(2,1)S(1)} collective-permute-done((bf16[80,256]{1,0:T(8,128)(2,1)S(1)}, bf16[80,256]{1,0:T(8,128)(2,1)S(1)}, u32[]{:S(2)}, u32[]{:S(2)}) %collective-permute-start.2) | collective-permute-done | bytes 40992 | tf_op jit(solution)/shard_map/ppermute | solution.py:740
  32.1 1.2 %collective-permute-done.1.refs_2_ = bf16[80,256]{1,0:T(8,128)(2,1)S(1)} collective-permute-done((bf16[80,256]{1,0:T(8,128)(2,1)S(1)}, bf16[80,256]{1,0:T(8,128)(2,1)S(1)}, u32[]{:S(2)}, u32[]{:S(2)}) %collective-permute-start.1) | collective-permute-done | bytes 40992 | tf_op jit(solution)/shard_map/ppermute | solution.py:740
  33.3 0.1 collective-permute-done.refs_1_
  33.4 0.0 all-to-all-done.1.table_ref
  33.4 2.3 %shard_map.168 = (bf16[16,32,256]{2,1,0:T(8,128)(2,1)}, bf16[272,256]{1,0:T(8,128)(2,1)}) custom-call(s32[1]{0:T(128)} %get-tuple-element.34.flag_ref, s32[2]{0:T(128)S(1)} %pad_add_fusion.place_ref, bf16[32,1024]{1,0:T(8,128)(2,1)S(1)} %get-tuple-element.35.own_ref, bf16[1024,256]{1,0:T(8,128)(2,1)S(1)} %get-tuple-element.36.ghost_ref, ...), custom_call_target="tpu_custom_call" | custom-call | tf_op jit(solution)/shard_map/pallas_call | solution.py:609
  35.7 6.1 %all-to-all-start.2 = ((bf16[16,32,256]{2,1,0:T(8,128)(2,1)}), bf16[16,32,256]{2,1,0:T(8,128)(2,1)S(1)}, u32[]{:S(2)}, u32[]{:S(2)}) async-start(bf16[16,32,256]{2,1,0:T(8,128)(2,1)} %get-tuple-element.49), calls=%async_computation.2 | async-start | bytes 524288 | tf_op jit(solution)/shard_map/all_to_all | solution.py:775
  41.8 2.8 %collective-permute-start.5 = (bf16[272,256]{1,0:T(8,128)(2,1)}, bf16[272,256]{1,0:T(8,128)(2,1)S(1)}, u32[]{:S(2)}, u32[]{:S(2)}) collective-permute-start(bf16[272,256]{1,0:T(8,128)(2,1)} %get-tuple-element.46.token_ref.refs_0_), channel_id=1, source_target_pairs={{8,0},{16,8},{24,16},{0,24},{9,1},{17,9},{25,17},{1,25},{10,2},{18... | collective-permute-start | bytes 417800 | tf_op jit(solution)/shard_map/ppermute | solution.py:740
  44.6 0.6 collective-permute-start.4
  45.1 0.6 collective-permute-start.3
  45.7 4.6 %shard_map.169 = (bf16[2,1,1,1024,256]{4,3,2,1,0:T(8,128)(2,1)}, bf16[768,1024]{1,0:T(8,128)(2,1)S(1)}) custom-call(s32[1]{0:T(128)} %get-tuple-element.34.flag_ref, bf16[272,256]{1,0:T(8,128)(2,1)} %get-tuple-element.46.token_ref.refs_0_, bf16[1024,1024]{1,0:T(8,128)(2,1)} %get-tuple-element.47.own_hbm, bf16[1024,1024]{1,0:T(8,128)(2,1)} %get-tuple-element.37.own_rest_hbm, ...), custom_call_target="tpu_custom_call" | custom-call | tf_op jit(solution)/shard_map/pallas_call | solution.py:609
  50.3 0.0 collective-permute-done.5.refs_3_
  50.3 2.7 %collective-permute-done.4.refs_2_ = bf16[272,256]{1,0:T(8,128)(2,1)S(1)} collective-permute-done((bf16[272,256]{1,0:T(8,128)(2,1)}, bf16[272,256]{1,0:T(8,128)(2,1)S(1)}, u32[]{:S(2)}, u32[]{:S(2)}) %collective-permute-start.4) | collective-permute-done | bytes 139296 | tf_op jit(solution)/shard_map/ppermute | solution.py:740
  52.9 0.0 collective-permute-done.3.refs_1_
  52.9 0.0 all-to-all-done.2.refs_4_
  53.0 8.4 %shard_map.170 = (f32[96,1024]{1,0:T(8,128)S(1)}, f32[128,1024]{1,0:T(8,128)S(1)}, f32[172,128]{1,0:T(8,128)S(1)}, bf16[256,1024]{1,0:T(8,128)(2,1)S(1)}) custom-call(s32[2]{0:T(128)S(1)} %pad_add_fusion.place_ref, bf16[272,256]{1,0:T(8,128)(2,1)} %get-tuple-element.46.token_ref.refs_0_, bf16[272,256]{1,0:T(8,128)(2,1)S(1)} %collective-permute-done.3.refs_1_, ...), custom_call_target="tpu_custom_call" | custom-call | tf_op jit(solution)/shard_map/pallas_call | solution.py:609
  61.3 0.1 collective-permute-start.6
  61.4 1.9 %collective-permute-done.6.got_ref = bf16[256,1024]{1,0:T(8,128)(2,1)S(1)} collective-permute-done((bf16[256,1024]{1,0:T(8,128)(2,1)S(1)}, bf16[256,1024]{1,0:T(8,128)(2,1)S(1)}, u32[]{:S(2)}, u32[]{:S(2)}) %collective-permute-start.6) | collective-permute-done | bytes 524320 | tf_op jit(solution)/shard_map/ppermute | solution.py:859
  63.3 1.0 %shard_map.171 = (f32[96,1024]{1,0:T(8,128)}, f32[128,1024]{1,0:T(8,128)}, f32[172,128]{1,0:T(8,128)}) custom-call(bf16[256,1024]{1,0:T(8,128)(2,1)S(1)} %collective-permute-done.6.got_ref, f32[96,1024]{1,0:T(8,128)S(1)} %get-tuple-element.52.one_ref, f32[128,1024]{1,0:T(8,128)S(1)} %get-tuple-element.53.two_ref, f32[172,128]{1,0:T(8,128)S(1)} %get-tuple-element.54.three_ref), custom_call_target="tpu_custom_call" | custom-call | tf_op jit(solution)/shard_map/pallas_call | solution.py:609
Async XLA Ops:
  0.6 13.1 %copy-start = (s32[1,1,8,32]{3,2,1,0:T(8,128)S(1)}, s32[1,1,8,32]{3,2,1,0:T(8,128)}, u32[]{:S(2)}) copy-start(s32[1,1,8,32]{3,2,1,0:T(8,128)} %rows_hbm.1) | copy-start | bytes 3076
  0.6 13.1 %copy-start.1 = (s32[1,1,32]{2,1,0:T(1,128)S(1)}, s32[1,1,32]{2,1,0:T(1,128)}, u32[]{:S(2)}) copy-start(s32[1,1,32]{2,1,0:T(1,128)} %param.21) | copy-start | bytes 388
  2.8 10.9 %all-to-all-start = ((bf16[8,32,256]{2,1,0:T(8,128)(2,1)}), bf16[8,32,256]{2,1,0:T(8,128)(2,1)S(1)}, u32[]{:S(2)}, u32[]{:S(2)}) async-start(bf16[8,32,256]{2,1,0:T(8,128)(2,1)} %get-tuple-element.41), calls=%async_computation | async-start | bytes 262144 | tf_op jit(solution)/shard_map/all_to_all | solution.py:680
  16.1 17.2 %all-to-all-start.1 = ((bf16[8,32,256]{2,1,0:T(8,128)(2,1)}), bf16[8,32,256]{2,1,0:T(8,128)(2,1)S(1)}, u32[]{:S(2)}, u32[]{:S(2)}) async-start(bf16[8,32,256]{2,1,0:T(8,128)(2,1)} %get-tuple-element.44), calls=%async_computation.1 | async-start | bytes 262144 | tf_op jit(solution)/shard_map/all_to_all | solution.py:734
  25.8 6.3 %collective-permute-start.2 = (bf16[80,256]{1,0:T(8,128)(2,1)S(1)}, bf16[80,256]{1,0:T(8,128)(2,1)S(1)}, u32[]{:S(2)}, u32[]{:S(2)}) collective-permute-start(bf16[80,256]{1,0:T(8,128)(2,1)S(1)} %get-tuple-element.45.refs_0_), channel_id=1, source_target_pairs={{3,0},{0,1},{1,2},{2,3},{7,4},{4,5},{5,6},{6,7},{11,8},{8,9},{9,10... | collective-permute-start | bytes 122888 | tf_op jit(solution)/shard_map/ppermute | solution.py:740
  26.5 6.8 %collective-permute-start.1 = (bf16[80,256]{1,0:T(8,128)(2,1)S(1)}, bf16[80,256]{1,0:T(8,128)(2,1)S(1)}, u32[]{:S(2)}, u32[]{:S(2)}) collective-permute-start(bf16[80,256]{1,0:T(8,128)(2,1)S(1)} %get-tuple-element.45.refs_0_), channel_id=1, source_target_pairs={{2,0},{3,1},{0,2},{1,3},{6,4},{7,5},{4,6},{5,7},{10,8},{11,9},{8,1... | collective-permute-start | bytes 122888 | tf_op jit(solution)/shard_map/ppermute | solution.py:740
  29.1 4.3 %collective-permute-start = (bf16[80,256]{1,0:T(8,128)(2,1)S(1)}, bf16[80,256]{1,0:T(8,128)(2,1)S(1)}, u32[]{:S(2)}, u32[]{:S(2)}) collective-permute-start(bf16[80,256]{1,0:T(8,128)(2,1)S(1)} %get-tuple-element.45.refs_0_), channel_id=1, source_target_pairs={{1,0},{2,1},{3,2},{0,3},{5,4},{6,5},{7,6},{4,7},{9,8},{10,9},{11,1... | collective-permute-start | bytes 122888 | tf_op jit(solution)/shard_map/ppermute | solution.py:740
  35.7 17.3 %all-to-all-start.2 = ((bf16[16,32,256]{2,1,0:T(8,128)(2,1)}), bf16[16,32,256]{2,1,0:T(8,128)(2,1)S(1)}, u32[]{:S(2)}, u32[]{:S(2)}) async-start(bf16[16,32,256]{2,1,0:T(8,128)(2,1)} %get-tuple-element.49), calls=%async_computation.2 | async-start | bytes 524288 | tf_op jit(solution)/shard_map/all_to_all | solution.py:775
  41.8 8.5 %collective-permute-start.5 = (bf16[272,256]{1,0:T(8,128)(2,1)}, bf16[272,256]{1,0:T(8,128)(2,1)S(1)}, u32[]{:S(2)}, u32[]{:S(2)}) collective-permute-start(bf16[272,256]{1,0:T(8,128)(2,1)} %get-tuple-element.46.token_ref.refs_0_), channel_id=1, source_target_pairs={{8,0},{16,8},{24,16},{0,24},{9,1},{17,9},{25,17},{1,25},{10,2},{18... | collective-permute-start | bytes 417800 | tf_op jit(solution)/shard_map/ppermute | solution.py:740
  44.6 8.4 %collective-permute-start.4 = (bf16[272,256]{1,0:T(8,128)(2,1)}, bf16[272,256]{1,0:T(8,128)(2,1)S(1)}, u32[]{:S(2)}, u32[]{:S(2)}) collective-permute-start(bf16[272,256]{1,0:T(8,128)(2,1)} %get-tuple-element.46.token_ref.refs_0_), channel_id=1, source_target_pairs={{16,0},{24,8},{0,16},{8,24},{17,1},{25,9},{1,17},{9,25},{18,2},{26... | collective-permute-start | bytes 417800 | tf_op jit(solution)/shard_map/ppermute | solution.py:740
  45.1 7.8 %collective-permute-start.3 = (bf16[272,256]{1,0:T(8,128)(2,1)}, bf16[272,256]{1,0:T(8,128)(2,1)S(1)}, u32[]{:S(2)}, u32[]{:S(2)}) collective-permute-start(bf16[272,256]{1,0:T(8,128)(2,1)} %get-tuple-element.46.token_ref.refs_0_), channel_id=1, source_target_pairs={{24,0},{0,8},{8,16},{16,24},{25,1},{1,9},{9,17},{17,25},{26,2},{2,... | collective-permute-start | bytes 417800 | tf_op jit(solution)/shard_map/ppermute | solution.py:740
  61.3 2.0 %collective-permute-start.6 = (bf16[256,1024]{1,0:T(8,128)(2,1)S(1)}, bf16[256,1024]{1,0:T(8,128)(2,1)S(1)}, u32[]{:S(2)}, u32[]{:S(2)}) collective-permute-start(bf16[256,1024]{1,0:T(8,128)(2,1)S(1)} %get-tuple-element.51), channel_id=1, source_target_pairs={{0,4},{4,0},{1,5},{5,1},{2,6},{6,2},{3,7},{7,3},{8,12},{12,8},{9,1... | collective-permute-start | bytes 1572872 | tf_op jit(solution)/shard_map/ppermute | solution.py:859

commit v11 on v10

--- a/solution.py
+++ b/solution.py
@@ -9,7 +9,7 @@
 from jax.sharding import PartitionSpec as P
 
 BLOCK = 128
-LOW = 512
+LOW = 256
 GROUP = 8
 clip_bound = 4.0
 noise_mult = 1.0
@@ -112,7 +112,7 @@
 
 def build_kernel(
     blocks_hbm,
-    count_ref,
+    count_any,
     src_ref,
     dst_ref,
     noise_hbm,
@@ -133,11 +133,13 @@
     rest_ref,
     own_ref,
     blocks_ref,
+    count_ref,
     sems,
 ):
     train = own_train_ref.shape[0]
     copies = fetch(
         (
+            (count_any, count_ref),
             (blocks_hbm, blocks_ref),
             (noise_hbm.at[0, 0, 0], noise_ref),
             (noise_hbm.at[1, 0, 0, :train], noise_train_ref),
@@ -185,8 +187,8 @@
 
     def turn(add, step, carry):
         first = step * GROUP
-        outs = [counts(first + inner) for inner in range(GROUP)]
-        for inner, out in enumerate(outs):
+        for inner in range(GROUP):
+            out = counts(first + inner)
             base = pl.multiple_of(blocks_ref[0, 0, first + inner] * BLOCK, BLOCK)
             for piece in range(pieces):
                 add(pl.ds(base, BLOCK), piece * LOW, out[piece * BLOCK : (piece + 1) * BLOCK])
@@ -202,6 +204,7 @@
         sums_ref[rows, at : at + size] += values[:, :size]
 
     steps = (count + GROUP - 1) // GROUP
+    copies[1].wait()
     lax.fori_loop(0, steps, functools.partial(turn, add_short), 0)
     top = ghost_ref[:BLOCK, :256]
     for first in range(0, nodes, BLOCK):
@@ -218,10 +221,10 @@
         own_ref[...] = sums_ref[:, :nodes].astype(bf16)
         ghost_ref[...] = sums_ref[:, nodes:].astype(bf16)
 
-    own_copy = pltpu.make_async_copy(own_ref, own_hbm, sems.at[3])
+    own_copy = pltpu.make_async_copy(own_ref, own_hbm, sems.at[4])
     own_copy.start()
     own_train_ref[...] = own_ref[:train, :]
-    for copy in copies[1:]:
+    for copy in copies[2:]:
         copy.wait()
     part_ref[...] = dot(own_ref[...], start_ref[...]) + noise_ref[...].astype(f32)
 
@@ -693,7 +696,7 @@
         ],
         [
             (tile_block, HBM),
-            (tile_count, SMEM),
+            (tile_count, pl.ANY),
             (src, None),
             (dst, None),
             (hop_noise, HBM),
@@ -708,7 +711,8 @@
             VMEM((nodes, max(nodes, ghosts)), bf16),
             VMEM((nodes, nodes), bf16),
             SMEM(tile_block.shape, jnp.int32),
-            DMA((4,)),
+            SMEM(tile_count.shape, jnp.int32),
+            DMA((5,)),
         ],
     )
     start1, out1, side = call(

time: 65.4 us -> 65.3 us (level)
  starting transfers between devices: 29.2 us -> 27.7 us
  waiting for transfers between devices: 7.83 us -> 8.7 us
  Pallas kernels: 25.8 us -> 26.6 us
    all_to_all x1, starting transfers between devices: 9.71 us -> 8.23 us  [local(): table1 = lax.all_to_all(out1, dom, split_axis=0, concat_axis=0, tiled=True)]
    ppermute x6, waiting for transfers between devices: 5.93 us -> 6.8 us  [shifted(): lax.ppermute(value, name, [((at + step * shift) % size, at) for at in ran...]
    pallas_call x7, Pallas kernels: 25.8 us -> 26.6 us  [call(): pl.pallas_call(kernel, out_shape=[shape_of(*out) for out in outs], in_spe...]
  transfers between devices with their start and end apart: 10 -> 10, of which waited for: 5 -> 5; matrix products, arithmetic and copies ran while one was open for 0% -> 0% of each run, Pallas kernels for 15% -> 16%
where the time goes in v11:
time: 65.3 us; the launch traced here: 64.5 us
  starting transfers between devices  27.7 us (42%)
  Pallas kernels  26.6 us (41%)
  waiting for transfers between devices  8.7 us (13%)
  between operations  1.4 us (2%)
    pallas_call x7, Pallas kernels, call(): pl.pallas_call(kernel, out_shape=[shape_of(*out) for out in outs], in_spe...  26.6 us
    ppermute x6, starting transfers between devices, shifted(): lax.ppermute(value, name, [((at + step * shift) % size, at) for at in ran...  8.35 us
    all_to_all x1, starting transfers between devices, local(): table1 = lax.all_to_all(out1, dom, split_axis=0, concat_axis=0, tiled=True)  8.23 us
    ppermute x6, waiting for transfers between devices, shifted(): lax.ppermute(value, name, [((at + step * shift) % size, at) for at in ran...  6.8 us
    all_to_all x1, starting transfers between devices, local(): lax.all_to_all(last, ('chip', 'grp'), split_axis=0, concat_axis=0, tiled=...  5.87 us
    all_to_all x1, starting transfers between devices, local(): table0 = lax.all_to_all(out0, dom, split_axis=0, concat_axis=0, tiled=True)  5.18 us
    ppermute x1, waiting for transfers between devices, local(): got = lax.ppermute(other, 'core', [(0, 1), (1, 0)])  1.9 us
  transfers between devices with their start and end apart: 10, of which 5 were waited for; matrix products, arithmetic and copies ran while one was open for 0% of the time, Pallas kernels for 16%

profile of v11, /device:TPU:0, one launch (start us, length us, event | category | flops | bytes accessed | tf_op | source)
XLA Modules:
  0.0 64.5 jit_solution(14513724800480345652)
XLA Ops:
  0.6 0.0 copy-start
  0.6 0.0 copy-start.1
  0.7 2.2 %shard_map.165 = (bf16[1024,256]{1,0:T(8,128)(2,1)S(1)}, bf16[8,32,256]{2,1,0:T(8,128)(2,1)}, bf16[32,256]{1,0:T(8,128)(2,1)S(1)}, s32[64,256]{1,0:T(8,128)S(1)}, s32[64,256]{1,0:T(8,128)S(1)}) custom-call(bf16[1,1,1024,256]{3,2,1,0:T(8,128)(2,1)} %feats_hbm.1, s32[1,1,8,32]{3,2,1,0:T(8,128)} %rows_hbm.1, s32[1,1,64,256]{3,2,1,0:T(8,128)} %src_hbm.1, ...), custom_call_target="tpu_custom_call" | custom-call | tf_op jit(solution)/shard_map/pallas_call | solution.py:612
  2.8 5.2 %all-to-all-start = ((bf16[8,32,256]{2,1,0:T(8,128)(2,1)}), bf16[8,32,256]{2,1,0:T(8,128)(2,1)S(1)}, u32[]{:S(2)}, u32[]{:S(2)}) async-start(bf16[8,32,256]{2,1,0:T(8,128)(2,1)} %get-tuple-element.41), calls=%async_computation | async-start | bytes 262144 | tf_op jit(solution)/shard_map/all_to_all | solution.py:683
  8.7 5.9 %shard_map.166 = (bf16[1024,1024]{1,0:T(8,128)(2,1)}, bf16[1024,256]{1,0:T(8,128)(2,1)S(1)}, bf16[32,1024]{1,0:T(8,128)(2,1)S(1)}, bf16[32,256]{1,0:T(8,128)(2,1...) custom-call(s32[1,1,64]{2,1,0:T(1,128)} %blocks_hbm.1, ...), custom_call_target="tpu_custom_call" | custom-call | tf_op jit(solution)/shard_map/pallas_call | solution.py:612
  14.6 0.0 all-to-all-done.table_ref
  14.6 0.0 copy-done
  14.6 0.0 copy-done.1
  14.6 2.3 %shard_map.167 = (bf16[1024,256]{1,0:T(8,128)(2,1)S(1)}, bf16[8,32,256]{2,1,0:T(8,128)(2,1)}, bf16[80,256]{1,0:T(8,128)(2,1)S(1)}) custom-call(s32[1]{0:T(128)} %get-tuple-element.34.flag_ref, f32[1024,256]{1,0:T(8,128)S(1)} %get-tuple-element.40.part_ref, bf16[1024,256]{1,0:T(8,128)(2,1)S(1)} %get-tuple-element.36.ghost_ref, ...), custom_call_target="tpu_custom_call" | custom-call | tf_op jit(solution)/shard_map/pallas_call | solution.py:612
  16.9 8.2 %all-to-all-start.1 = ((bf16[8,32,256]{2,1,0:T(8,128)(2,1)}), bf16[8,32,256]{2,1,0:T(8,128)(2,1)S(1)}, u32[]{:S(2)}, u32[]{:S(2)}) async-start(bf16[8,32,256]{2,1,0:T(8,128)(2,1)} %get-tuple-element.44), calls=%async_computation.1 | async-start | bytes 262144 | tf_op jit(solution)/shard_map/all_to_all | solution.py:738
  25.2 2.0 %collective-permute-start.2 = (bf16[80,256]{1,0:T(8,128)(2,1)S(1)}, bf16[80,256]{1,0:T(8,128)(2,1)S(1)}, u32[]{:S(2)}, u32[]{:S(2)}) collective-permute-start(bf16[80,256]{1,0:T(8,128)(2,1)S(1)} %get-tuple-element.45.refs_0_), channel_id=1, source_target_pairs={{3,0},{0,1},{1,2},{2,3},{7,4},{4,5},{5,6},{6,7},{11,8},{8,9},{9,10... | collective-permute-start | bytes 122888 | tf_op jit(solution)/shard_map/ppermute | solution.py:744
  27.1 2.2 %collective-permute-start.1 = (bf16[80,256]{1,0:T(8,128)(2,1)S(1)}, bf16[80,256]{1,0:T(8,128)(2,1)S(1)}, u32[]{:S(2)}, u32[]{:S(2)}) collective-permute-start(bf16[80,256]{1,0:T(8,128)(2,1)S(1)} %get-tuple-element.45.refs_0_), channel_id=1, source_target_pairs={{2,0},{3,1},{0,2},{1,3},{6,4},{7,5},{4,6},{5,7},{10,8},{11,9},{8,1... | collective-permute-start | bytes 122888 | tf_op jit(solution)/shard_map/ppermute | solution.py:744
  29.3 0.2 collective-permute-start
  29.6 0.1 pad_add_fusion.place_ref
  29.6 1.7 %collective-permute-done.2.refs_3_ = bf16[80,256]{1,0:T(8,128)(2,1)S(1)} collective-permute-done((bf16[80,256]{1,0:T(8,128)(2,1)S(1)}, bf16[80,256]{1,0:T(8,128)(2,1)S(1)}, u32[]{:S(2)}, u32[]{:S(2)}) %collective-permute-start.2) | collective-permute-done | bytes 40992 | tf_op jit(solution)/shard_map/ppermute | solution.py:744
  31.4 1.5 %collective-permute-done.1.refs_2_ = bf16[80,256]{1,0:T(8,128)(2,1)S(1)} collective-permute-done((bf16[80,256]{1,0:T(8,128)(2,1)S(1)}, bf16[80,256]{1,0:T(8,128)(2,1)S(1)}, u32[]{:S(2)}, u32[]{:S(2)}) %collective-permute-start.1) | collective-permute-done | bytes 40992 | tf_op jit(solution)/shard_map/ppermute | solution.py:744
  32.9 0.7 %collective-permute-done.refs_1_ = bf16[80,256]{1,0:T(8,128)(2,1)S(1)} collective-permute-done((bf16[80,256]{1,0:T(8,128)(2,1)S(1)}, bf16[80,256]{1,0:T(8,128)(2,1)S(1)}, u32[]{:S(2)}, u32[]{:S(2)}) %collective-permute-start) | collective-permute-done | bytes 40992 | tf_op jit(solution)/shard_map/ppermute | solution.py:744
  33.5 0.0 all-to-all-done.1.table_ref
  33.5 2.3 %shard_map.168 = (bf16[16,32,256]{2,1,0:T(8,128)(2,1)}, bf16[272,256]{1,0:T(8,128)(2,1)}) custom-call(s32[1]{0:T(128)} %get-tuple-element.34.flag_ref, s32[2]{0:T(128)S(1)} %pad_add_fusion.place_ref, bf16[32,1024]{1,0:T(8,128)(2,1)S(1)} %get-tuple-element.35.own_ref, bf16[1024,256]{1,0:T(8,128)(2,1)S(1)} %get-tuple-element.36.ghost_ref, ...), custom_call_target="tpu_custom_call" | custom-call | tf_op jit(solution)/shard_map/pallas_call | solution.py:612
  35.8 5.9 %all-to-all-start.2 = ((bf16[16,32,256]{2,1,0:T(8,128)(2,1)}), bf16[16,32,256]{2,1,0:T(8,128)(2,1)S(1)}, u32[]{:S(2)}, u32[]{:S(2)}) async-start(bf16[16,32,256]{2,1,0:T(8,128)(2,1)} %get-tuple-element.49), calls=%async_computation.2 | async-start | bytes 524288 | tf_op jit(solution)/shard_map/all_to_all | solution.py:779
  41.7 2.8 %collective-permute-start.5 = (bf16[272,256]{1,0:T(8,128)(2,1)}, bf16[272,256]{1,0:T(8,128)(2,1)S(1)}, u32[]{:S(2)}, u32[]{:S(2)}) collective-permute-start(bf16[272,256]{1,0:T(8,128)(2,1)} %get-tuple-element.46.token_ref.refs_0_), channel_id=1, source_target_pairs={{8,0},{16,8},{24,16},{0,24},{9,1},{17,9},{25,17},{1,25},{10,2},{18... | collective-permute-start | bytes 417800 | tf_op jit(solution)/shard_map/ppermute | solution.py:744
  44.5 0.6 collective-permute-start.4
  45.1 0.6 collective-permute-start.3
  45.7 4.6 %shard_map.169 = (bf16[2,1,1,1024,256]{4,3,2,1,0:T(8,128)(2,1)}, bf16[768,1024]{1,0:T(8,128)(2,1)S(1)}) custom-call(s32[1]{0:T(128)} %get-tuple-element.34.flag_ref, bf16[272,256]{1,0:T(8,128)(2,1)} %get-tuple-element.46.token_ref.refs_0_, bf16[1024,1024]{1,0:T(8,128)(2,1)} %get-tuple-element.47.own_hbm, bf16[1024,1024]{1,0:T(8,128)(2,1)} %get-tuple-element.37.own_rest_hbm, ...), custom_call_target="tpu_custom_call" | custom-call | tf_op jit(solution)/shard_map/pallas_call | solution.py:612
  50.2 0.0 collective-permute-done.5.refs_3_
  50.2 2.9 %collective-permute-done.4.refs_2_ = bf16[272,256]{1,0:T(8,128)(2,1)S(1)} collective-permute-done((bf16[272,256]{1,0:T(8,128)(2,1)}, bf16[272,256]{1,0:T(8,128)(2,1)S(1)}, u32[]{:S(2)}, u32[]{:S(2)}) %collective-permute-start.4) | collective-permute-done | bytes 139296 | tf_op jit(solution)/shard_map/ppermute | solution.py:744
  53.1 0.0 collective-permute-done.3.refs_1_
  53.2 0.0 all-to-all-done.2.refs_4_
  53.2 8.4 %shard_map.170 = (f32[96,1024]{1,0:T(8,128)S(1)}, f32[128,1024]{1,0:T(8,128)S(1)}, f32[172,128]{1,0:T(8,128)S(1)}, bf16[256,1024]{1,0:T(8,128)(2,1)S(1)}) custom-call(s32[2]{0:T(128)S(1)} %pad_add_fusion.place_ref, bf16[272,256]{1,0:T(8,128)(2,1)} %get-tuple-element.46.token_ref.refs_0_, bf16[272,256]{1,0:T(8,128)(2,1)S(1)} %collective-permute-done.3.refs_1_, ...), custom_call_target="tpu_custom_call" | custom-call | tf_op jit(solution)/shard_map/pallas_call | solution.py:612
  61.5 0.1 collective-permute-start.6
  61.6 1.9 %collective-permute-done.6.got_ref = bf16[256,1024]{1,0:T(8,128)(2,1)S(1)} collective-permute-done((bf16[256,1024]{1,0:T(8,128)(2,1)S(1)}, bf16[256,1024]{1,0:T(8,128)(2,1)S(1)}, u32[]{:S(2)}, u32[]{:S(2)}) %collective-permute-start.6) | collective-permute-done | bytes 524320 | tf_op jit(solution)/shard_map/ppermute | solution.py:863
  63.5 1.0 %shard_map.171 = (f32[96,1024]{1,0:T(8,128)}, f32[128,1024]{1,0:T(8,128)}, f32[172,128]{1,0:T(8,128)}) custom-call(bf16[256,1024]{1,0:T(8,128)(2,1)S(1)} %collective-permute-done.6.got_ref, f32[96,1024]{1,0:T(8,128)S(1)} %get-tuple-element.52.one_ref, f32[128,1024]{1,0:T(8,128)S(1)} %get-tuple-element.53.two_ref, f32[172,128]{1,0:T(8,128)S(1)} %get-tuple-element.54.three_ref), custom_call_target="tpu_custom_call" | custom-call | tf_op jit(solution)/shard_map/pallas_call | solution.py:612
Async XLA Ops:
  0.6 13.9 %copy-start = (s32[1,1,8,32]{3,2,1,0:T(8,128)S(1)}, s32[1,1,8,32]{3,2,1,0:T(8,128)}, u32[]{:S(2)}) copy-start(s32[1,1,8,32]{3,2,1,0:T(8,128)} %rows_hbm.1) | copy-start | bytes 3076
  0.6 13.9 %copy-start.1 = (s32[1,1,32]{2,1,0:T(1,128)S(1)}, s32[1,1,32]{2,1,0:T(1,128)}, u32[]{:S(2)}) copy-start(s32[1,1,32]{2,1,0:T(1,128)} %param.21) | copy-start | bytes 388
  2.8 11.7 %all-to-all-start = ((bf16[8,32,256]{2,1,0:T(8,128)(2,1)}), bf16[8,32,256]{2,1,0:T(8,128)(2,1)S(1)}, u32[]{:S(2)}, u32[]{:S(2)}) async-start(bf16[8,32,256]{2,1,0:T(8,128)(2,1)} %get-tuple-element.41), calls=%async_computation | async-start | bytes 262144 | tf_op jit(solution)/shard_map/all_to_all | solution.py:683
  16.9 16.6 %all-to-all-start.1 = ((bf16[8,32,256]{2,1,0:T(8,128)(2,1)}), bf16[8,32,256]{2,1,0:T(8,128)(2,1)S(1)}, u32[]{:S(2)}, u32[]{:S(2)}) async-start(bf16[8,32,256]{2,1,0:T(8,128)(2,1)} %get-tuple-element.44), calls=%async_computation.1 | async-start | bytes 262144 | tf_op jit(solution)/shard_map/all_to_all | solution.py:738
  25.2 6.2 %collective-permute-start.2 = (bf16[80,256]{1,0:T(8,128)(2,1)S(1)}, bf16[80,256]{1,0:T(8,128)(2,1)S(1)}, u32[]{:S(2)}, u32[]{:S(2)}) collective-permute-start(bf16[80,256]{1,0:T(8,128)(2,1)S(1)} %get-tuple-element.45.refs_0_), channel_id=1, source_target_pairs={{3,0},{0,1},{1,2},{2,3},{7,4},{4,5},{5,6},{6,7},{11,8},{8,9},{9,10... | collective-permute-start | bytes 122888 | tf_op jit(solution)/shard_map/ppermute | solution.py:744
  27.1 5.7 %collective-permute-start.1 = (bf16[80,256]{1,0:T(8,128)(2,1)S(1)}, bf16[80,256]{1,0:T(8,128)(2,1)S(1)}, u32[]{:S(2)}, u32[]{:S(2)}) collective-permute-start(bf16[80,256]{1,0:T(8,128)(2,1)S(1)} %get-tuple-element.45.refs_0_), channel_id=1, source_target_pairs={{2,0},{3,1},{0,2},{1,3},{6,4},{7,5},{4,6},{5,7},{10,8},{11,9},{8,1... | collective-permute-start | bytes 122888 | tf_op jit(solution)/shard_map/ppermute | solution.py:744
  29.3 4.2 %collective-permute-start = (bf16[80,256]{1,0:T(8,128)(2,1)S(1)}, bf16[80,256]{1,0:T(8,128)(2,1)S(1)}, u32[]{:S(2)}, u32[]{:S(2)}) collective-permute-start(bf16[80,256]{1,0:T(8,128)(2,1)S(1)} %get-tuple-element.45.refs_0_), channel_id=1, source_target_pairs={{1,0},{2,1},{3,2},{0,3},{5,4},{6,5},{7,6},{4,7},{9,8},{10,9},{11,1... | collective-permute-start | bytes 122888 | tf_op jit(solution)/shard_map/ppermute | solution.py:744
  35.8 17.3 %all-to-all-start.2 = ((bf16[16,32,256]{2,1,0:T(8,128)(2,1)}), bf16[16,32,256]{2,1,0:T(8,128)(2,1)S(1)}, u32[]{:S(2)}, u32[]{:S(2)}) async-start(bf16[16,32,256]{2,1,0:T(8,128)(2,1)} %get-tuple-element.49), calls=%async_computation.2 | async-start | bytes 524288 | tf_op jit(solution)/shard_map/all_to_all | solution.py:779
  41.7 8.5 %collective-permute-start.5 = (bf16[272,256]{1,0:T(8,128)(2,1)}, bf16[272,256]{1,0:T(8,128)(2,1)S(1)}, u32[]{:S(2)}, u32[]{:S(2)}) collective-permute-start(bf16[272,256]{1,0:T(8,128)(2,1)} %get-tuple-element.46.token_ref.refs_0_), channel_id=1, source_target_pairs={{8,0},{16,8},{24,16},{0,24},{9,1},{17,9},{25,17},{1,25},{10,2},{18... | collective-permute-start | bytes 417800 | tf_op jit(solution)/shard_map/ppermute | solution.py:744
  44.5 8.6 %collective-permute-start.4 = (bf16[272,256]{1,0:T(8,128)(2,1)}, bf16[272,256]{1,0:T(8,128)(2,1)S(1)}, u32[]{:S(2)}, u32[]{:S(2)}) collective-permute-start(bf16[272,256]{1,0:T(8,128)(2,1)} %get-tuple-element.46.token_ref.refs_0_), channel_id=1, source_target_pairs={{16,0},{24,8},{0,16},{8,24},{17,1},{25,9},{1,17},{9,25},{18,2},{26... | collective-permute-start | bytes 417800 | tf_op jit(solution)/shard_map/ppermute | solution.py:744
  45.1 8.0 %collective-permute-start.3 = (bf16[272,256]{1,0:T(8,128)(2,1)}, bf16[272,256]{1,0:T(8,128)(2,1)S(1)}, u32[]{:S(2)}, u32[]{:S(2)}) collective-permute-start(bf16[272,256]{1,0:T(8,128)(2,1)} %get-tuple-element.46.token_ref.refs_0_), channel_id=1, source_target_pairs={{24,0},{0,8},{8,16},{16,24},{25,1},{1,9},{9,17},{17,25},{26,2},{2,... | collective-permute-start | bytes 417800 | tf_op jit(solution)/shard_map/ppermute | solution.py:744
  61.5 2.0 %collective-permute-start.6 = (bf16[256,1024]{1,0:T(8,128)(2,1)S(1)}, bf16[256,1024]{1,0:T(8,128)(2,1)S(1)}, u32[]{:S(2)}, u32[]{:S(2)}) collective-permute-start(bf16[256,1024]{1,0:T(8,128)(2,1)S(1)} %get-tuple-element.51), channel_id=1, source_target_pairs={{0,4},{4,0},{1,5},{5,1},{2,6},{6,2},{3,7},{7,3},{8,12},{12,8},{9,1... | collective-permute-start | bytes 1572872 | tf_op jit(solution)/shard_map/ppermute | solution.py:863

commit v12 on v10

--- a/solution.py
+++ b/solution.py
@@ -9,7 +9,7 @@
 from jax.sharding import PartitionSpec as P
 
 BLOCK = 128
-LOW = 512
+LOW = 256
 GROUP = 8
 clip_bound = 4.0
 noise_mult = 1.0
@@ -42,10 +42,6 @@
 
 def dot(left, right):
     return jnp.dot(left, right, preferred_element_type=f32)
-
-
-def dot_nt(left, right):
-    return lax.dot_general(left, right, (((1,), (1,)), ((), ())), preferred_element_type=f32)
 
 
 def dot_tn(left, right):
@@ -149,7 +145,6 @@
     tiles, slots = src_ref.shape
     own_ref[...] = jnp.zeros_like(own_ref)
     ghost_ref[...] = jnp.zeros_like(ghost_ref)
-    copies[0].wait()
     count = count_ref[0, 0]
 
     def sixteen(values):
@@ -173,11 +168,12 @@
     def counts(tile):
         rows = pl.ds(pl.multiple_of(tile * 16, 16), 16)
         high, spot = high_ref[rows, :], spot_ref[rows, :]
+        tall = jnp.concatenate([spot] * (BLOCK // 16), 0)
+        spot_one = jnp.where(ids == tall, one, zero)
         spots = []
         for piece in range(pieces):
-            wanted = jnp.where(high == piece, spot, -one)
-            tall = jnp.concatenate([wanted] * (BLOCK // 16), 0)
-            spots.append(jnp.where(ids == tall, one, zero))
+            here = jnp.where(high == piece, one, zero)
+            spots.append(spot_one * jnp.concatenate([here] * (BLOCK // 16), 0))
         low = low_ref[tile]
         low_hot = jnp.concatenate([jnp.where(low == ids, one, zero) for ids in lanes], 1)
         spot_hot = jnp.concatenate(spots, 0)
@@ -202,6 +198,7 @@
         sums_ref[rows, at : at + size] += values[:, :size]
 
     steps = (count + GROUP - 1) // GROUP
+    copies[0].wait()
     lax.fori_loop(0, steps, functools.partial(turn, add_short), 0)
     top = ghost_ref[:BLOCK, :256]
     for first in range(0, nodes, BLOCK):
@@ -332,19 +329,35 @@
     ghost_rest_hbm,
     noise_hbm,
     weight_hbm,
+    second_hbm,
+    third_hbm,
     ghost_ref,
     table_ref,
     start_ref,
-    out_ref,
+    out_hbm,
     weight_ref,
+    second_t_hbm,
+    third_t_hbm,
     own_ref,
     noise_ref,
     sums_ref,
     rest_ref,
+    out_ref,
+    second_ref,
+    third_ref,
+    second_t_ref,
+    third_t_ref,
     sems,
 ):
     copies = fetch(
-        ((own_hbm, own_ref), (noise_hbm.at[1, 0, 0], noise_ref), (weight_hbm, weight_ref)), sems
+        (
+            (own_hbm, own_ref),
+            (noise_hbm.at[1, 0, 0], noise_ref),
+            (second_hbm, second_ref),
+            (third_hbm, third_ref),
+            (weight_hbm, weight_ref),
+        ),
+        sems,
     )
     table = table_ref[...].reshape(-1, out_ref.shape[-1])
     out_ref[0, 0, 0] = start_ref[...]
@@ -356,7 +369,23 @@
     )
     aggregate(flag_ref, noise_ref[...].astype(f32), parts, sums_ref, rest_ref)
     out_ref[1, 0, 0] = normalize(sums_ref[...])
+    out_copy = pltpu.make_async_copy(out_ref, out_hbm, sems.at[5])
+    out_copy.start()
+    copies[3].wait()
+    classes = third_ref.shape[0]
+    third_t_ref[:, 128:] = jnp.zeros((third_t_ref.shape[0], third_t_ref.shape[1] - 128), bf16)
+    third_t_ref[:, :128] = third_ref[:128, :].T
+    third_t_ref[:, 128:classes] = third_ref[128:, :].T
+    third_copy = pltpu.make_async_copy(third_t_ref, third_t_hbm, sems.at[6])
+    third_copy.start()
     copies[2].wait()
+    hid = second_ref.shape[0]
+    for at in range(0, hid, 256):
+        second_t_ref[at : at + 256, :] = second_ref[:, at : at + 256].T
+    second_copy = pltpu.make_async_copy(second_t_ref, second_t_hbm, sems.at[7])
+    second_copy.start()
+    for copy in (copies[4], out_copy, third_copy, second_copy):
+        copy.wait()
 
 
 def shares(ref, first, share):
@@ -381,7 +410,9 @@
     side_refs,
     w_first_hbm,
     w_second_hbm,
+    w_third_t_hbm,
     w_third_hbm,
+    w_second_t_hbm,
     n_first_hbm,
     n_second_hbm,
     n_third_hbm,
@@ -392,7 +423,9 @@
     side_hbm,
     w_first_ref,
     w_second_ref,
+    w_third_t_ref,
     w_third_ref,
+    w_second_t_ref,
     n_first_ref,
     n_second_ref,
     n_third_ref,
@@ -419,7 +452,9 @@
     pairs = (
         (w_first_hbm, w_first_ref),
         (w_second_hbm, w_second_ref),
+        (w_third_t_hbm, w_third_t_ref),
         (w_third_hbm, w_third_ref),
+        (w_second_t_hbm, w_second_t_ref),
         (n_first_hbm, n_first_ref),
         (n_second_hbm, n_second_ref),
         (n_third_hbm, n_third_ref),
@@ -512,8 +547,7 @@
     )
     if not many:
         copies[2].wait()
-        pad()
-    logits = dot_nt(h_two_ref[...], w_third_pad_ref[...])
+    logits = dot(h_two_ref[...], w_third_t_ref[...])
     ids = lax.broadcasted_iota(jnp.int32, (logits.shape[0], wide), 1)
     expo = jnp.where(ids < classes, jnp.exp(logits), 0.0)
     probs = expo / jnp.sum(expo, -1, keepdims=True)
@@ -521,11 +555,15 @@
     d_three = (probs - jnp.where(ids == label, 1.0, 0.0)).astype(bf16)
     sq_dthree = lanes_sum(d_three)
     d_three_ref[...] = d_three
+    if not many:
+        copies[3].wait()
+        copies[4].wait()
+        pad()
     sq_dtwo = layer(
         lambda cut: dot(d_three_ref[cut, :], w_third_pad_ref[...]), back, slope_two_ref, d_two_ref
     )
     sq_done = layer(
-        lambda cut: dot_nt(d_two_ref[cut, :], w_second_ref[...]), back, slope_one_ref, d_one_ref
+        lambda cut: dot(d_two_ref[cut, :], w_second_t_ref[...]), back, slope_one_ref, d_one_ref
     )
 
     def total(values):
@@ -539,7 +577,7 @@
     factor = clip_bound / jnp.maximum(norm, clip_bound)
 
     if not many:
-        for copy in copies[3:]:
+        for copy in copies[5:]:
             copy.wait()
         set_noise()
     share_one, share = g_first_ref.shape[0], g_second_ref.shape[0]
@@ -779,10 +817,16 @@
             every(value, axes) for value in (own0[None], start1[None, :train], last)
         )
         every_label = every(labels.reshape(1, train), axes)
-    hop_feats, held_first = call(
+    wide = (classes + 255) // 256 * 256
+    hop_feats, held_first, second_t, third_t = call(
         last_kernel,
-        16,
-        [((2, 1, 1, nodes, width), bf16, VMEM), (w_first.shape, bf16, None)],
+        28,
+        [
+            ((2, 1, 1, nodes, width), bf16, HBM),
+            (w_first.shape, bf16, None),
+            ((hid, hid), bf16, HBM),
+            ((hid, wide), bf16, HBM),
+        ],
         [
             (flag, SMEM),
             (side, HBM),
@@ -791,6 +835,8 @@
             (ghost_rest, HBM),
             (hop_noise, HBM),
             (w_first, HBM),
+            (w_second, HBM),
+            (w_third.T, HBM),
             (ghost, None),
             (table1, None),
             (start1, None),
@@ -800,13 +846,18 @@
             VMEM((nodes, width), bf16),
             VMEM((nodes, width), f32),
             VMEM((nodes, max(nodes, ghosts)), bf16),
-            DMA((3,)),
+            VMEM((2, 1, 1, nodes, width), bf16),
+            VMEM((hid, hid), bf16),
+            VMEM((classes, hid), bf16),
+            VMEM((hid, hid), bf16),
+            VMEM((hid, wide), bf16),
+            DMA((8,)),
         ],
     )
     chunk = train * (copies if few else min(members, 32))
     groups = chunk // train
-    wide = (classes + 255) // 256 * 256
-    fixed = (w_first, w_second, w_third.T, noise_first, noise_second, noise_third.T)
+    noises = (noise_first, noise_second, noise_third.T)
+    fixed = (w_first, w_second, third_t, w_third.T, second_t) + noises
     scratch = [VMEM(value.shape, value.dtype) for value in fixed]
     scratch += [
         VMEM((chunk, d_in), bf16),
@@ -827,8 +878,8 @@
 
         def classify(place_ref, *refs):
             sides_in, rest = refs[:chips], refs[chips:]
-            two_ref, first_ref, *outs = rest[:11]
-            held, *rest = rest[11:]
+            two_ref, first_ref, *outs = rest[:13]
+            held, *rest = rest[13:]
             classify_kernel(
                 False,
                 place_ref,
@@ -848,7 +899,7 @@
         *own_sums, other = call(
             classify,
             44,
-            [(value.shape, f32, None) for value in fixed[3:]] + [((rows, hid), bf16, None)],
+            [(value.shape, f32, None) for value in noises] + [((rows, hid), bf16, None)],
             [(place, SMEM)]
             + [(side, HBM)]
             + [(value, None) for value in sides[1:]]
@@ -860,7 +911,7 @@
         first, second, third = call(
             finish_kernel,
             16,
-            [(value.shape, f32, VMEM) for value in fixed[3:]],
+            [(value.shape, f32, VMEM) for value in noises],
             [(got, None)] + [(value, None) for value in own_sums],
             [],
         )
@@ -877,10 +928,10 @@
                 one_ref,
                 two_ref,
                 None,
-                *rest[:9],
+                *rest[:11],
                 None,
                 None,
-                *rest[9:],
+                *rest[11:],
             )
 
         def whole(value):
@@ -894,11 +945,11 @@
         first, second, third = pl.pallas_call(
             classify,
             grid=(members // groups,),
-            out_shape=[jax.ShapeDtypeStruct(value.shape, f32) for value in fixed[3:]],
+            out_shape=[jax.ShapeDtypeStruct(value.shape, f32) for value in noises],
             in_specs=[pl.BlockSpec(memory_space=SMEM)]
             + [piece(value) for value in ins]
             + [pl.BlockSpec(memory_space=HBM) for value in fixed],
-            out_specs=[whole(value) for value in fixed[3:]],
+            out_specs=[whole(value) for value in noises],
             scratch_shapes=scratch,
             compiler_params=params(56),
         )(place, *ins, *fixed)

time: 65.4 us -> 65.4 us (level)
  Pallas kernels: 25.8 us -> 32.4 us
  starting transfers between devices: 29.2 us -> 23.5 us
  waiting for transfers between devices: 7.83 us -> 6.89 us
    pallas_call x7, Pallas kernels: 25.8 us -> 32.4 us  [call(): pl.pallas_call(kernel, out_shape=[shape_of(*out) for out in outs], in_spe...]
    all_to_all x1, starting transfers between devices: 9.71 us -> 3.38 us  [local(): table1 = lax.all_to_all(out1, dom, split_axis=0, concat_axis=0, tiled=True)]
    ppermute x6, waiting for transfers between devices: 5.93 us -> 4.99 us  [shifted(): lax.ppermute(value, name, [((at + step * shift) % size, at) for at in ran...]
  transfers between devices with their start and end apart: 10 -> 10, of which waited for: 5 -> 5; matrix products, arithmetic and copies ran while one was open for 0% -> 0% of each run, Pallas kernels for 15% -> 25%
where the time goes in v12:
time: 65.4 us; the launch traced here: 64.2 us
  Pallas kernels  32.4 us (50%)
  starting transfers between devices  23.5 us (36%)
  waiting for transfers between devices  6.89 us (11%)
  between operations  1.42 us (2%)
    pallas_call x7, Pallas kernels, call(): pl.pallas_call(kernel, out_shape=[shape_of(*out) for out in outs], in_spe...  32.4 us
    ppermute x6, starting transfers between devices, shifted(): lax.ppermute(value, name, [((at + step * shift) % size, at) for at in ran...  8.78 us
    all_to_all x1, starting transfers between devices, local(): lax.all_to_all(last, ('chip', 'grp'), split_axis=0, concat_axis=0, tiled=...  6.05 us
    all_to_all x1, starting transfers between devices, local(): table0 = lax.all_to_all(out0, dom, split_axis=0, concat_axis=0, tiled=True)  5.18 us
    ppermute x6, waiting for transfers between devices, shifted(): lax.ppermute(value, name, [((at + step * shift) % size, at) for at in ran...  4.99 us
    all_to_all x1, starting transfers between devices, local(): table1 = lax.all_to_all(out1, dom, split_axis=0, concat_axis=0, tiled=True)  3.38 us
    ppermute x1, waiting for transfers between devices, local(): got = lax.ppermute(other, 'core', [(0, 1), (1, 0)])  1.9 us
  transfers between devices with their start and end apart: 10, of which 5 were waited for; matrix products, arithmetic and copies ran while one was open for 0% of the time, Pallas kernels for 25%

profile of v12, /device:TPU:0, one launch (start us, length us, event | category | flops | bytes accessed | tf_op | source)
XLA Modules:
  0.0 64.2 jit_solution(12506306524298633755)
XLA Ops:
  0.6 0.0 copy-start
  0.6 0.0 copy-start.1
  0.7 2.2 %shard_map.165 = (bf16[1024,256]{1,0:T(8,128)(2,1)S(1)}, bf16[8,32,256]{2,1,0:T(8,128)(2,1)}, bf16[32,256]{1,0:T(8,128)(2,1)S(1)}, s32[64,256]{1,0:T(8,128)S(1)}, s32[64,256]{1,0:T(8,128)S(1)}) custom-call(bf16[1,1,1024,256]{3,2,1,0:T(8,128)(2,1)} %feats_hbm.1, s32[1,1,8,32]{3,2,1,0:T(8,128)} %rows_hbm.1, s32[1,1,64,256]{3,2,1,0:T(8,128)} %src_hbm.1, ...), custom_call_target="tpu_custom_call" | custom-call | tf_op jit(solution)/shard_map/pallas_call | solution.py:647
  2.8 5.2 %all-to-all-start = ((bf16[8,32,256]{2,1,0:T(8,128)(2,1)}), bf16[8,32,256]{2,1,0:T(8,128)(2,1)S(1)}, u32[]{:S(2)}, u32[]{:S(2)}) async-start(bf16[8,32,256]{2,1,0:T(8,128)(2,1)} %get-tuple-element.43), calls=%async_computation | async-start | bytes 262144 | tf_op jit(solution)/shard_map/all_to_all | solution.py:718
  8.7 10.2 %shard_map.166 = (bf16[1024,1024]{1,0:T(8,128)(2,1)}, bf16[1024,256]{1,0:T(8,128)(2,1)S(1)}, bf16[32,1024]{1,0:T(8,128)(2,1)S(1)}, bf16[32,256]{1,0:T(8,128)(2,1...) custom-call(s32[1,1,64]{2,1,0:T(1,128)} %blocks_hbm.1, ...), custom_call_target="tpu_custom_call" | custom-call | tf_op jit(solution)/shard_map/pallas_call | solution.py:647
  18.9 0.0 all-to-all-done.table_ref
  18.9 0.0 copy-done
  18.9 0.0 copy-done.1
  18.9 2.3 %shard_map.167 = (bf16[1024,256]{1,0:T(8,128)(2,1)S(1)}, bf16[8,32,256]{2,1,0:T(8,128)(2,1)}, bf16[80,256]{1,0:T(8,128)(2,1)S(1)}) custom-call(s32[1]{0:T(128)} %get-tuple-element.36.flag_ref, f32[1024,256]{1,0:T(8,128)S(1)} %get-tuple-element.42.part_ref, bf16[1024,256]{1,0:T(8,128)(2,1)S(1)} %get-tuple-element.38.ghost_ref, ...), custom_call_target="tpu_custom_call" | custom-call | tf_op jit(solution)/shard_map/pallas_call | solution.py:647
  21.3 3.4 %all-to-all-start.1 = ((bf16[8,32,256]{2,1,0:T(8,128)(2,1)}), bf16[8,32,256]{2,1,0:T(8,128)(2,1)S(1)}, u32[]{:S(2)}, u32[]{:S(2)}) async-start(bf16[8,32,256]{2,1,0:T(8,128)(2,1)} %get-tuple-element.46), calls=%async_computation.1 | async-start | bytes 262144 | tf_op jit(solution)/shard_map/all_to_all | solution.py:772
  24.7 2.4 %collective-permute-start.2 = (bf16[80,256]{1,0:T(8,128)(2,1)S(1)}, bf16[80,256]{1,0:T(8,128)(2,1)S(1)}, u32[]{:S(2)}, u32[]{:S(2)}) collective-permute-start(bf16[80,256]{1,0:T(8,128)(2,1)S(1)} %get-tuple-element.47.refs_0_), channel_id=1, source_target_pairs={{3,0},{0,1},{1,2},{2,3},{7,4},{4,5},{5,6},{6,7},{11,8},{8,9},{9,10... | collective-permute-start | bytes 122888 | tf_op jit(solution)/shard_map/ppermute | solution.py:778
  27.1 1.8 %collective-permute-start.1 = (bf16[80,256]{1,0:T(8,128)(2,1)S(1)}, bf16[80,256]{1,0:T(8,128)(2,1)S(1)}, u32[]{:S(2)}, u32[]{:S(2)}) collective-permute-start(bf16[80,256]{1,0:T(8,128)(2,1)S(1)} %get-tuple-element.47.refs_0_), channel_id=1, source_target_pairs={{2,0},{3,1},{0,2},{1,3},{6,4},{7,5},{4,6},{5,7},{10,8},{11,9},{8,1... | collective-permute-start | bytes 122888 | tf_op jit(solution)/shard_map/ppermute | solution.py:778
  28.9 0.6 collective-permute-start
  29.5 0.1 pad_add_fusion.place_ref
  29.6 1.0 %collective-permute-done.2.refs_3_ = bf16[80,256]{1,0:T(8,128)(2,1)S(1)} collective-permute-done((bf16[80,256]{1,0:T(8,128)(2,1)S(1)}, bf16[80,256]{1,0:T(8,128)(2,1)S(1)}, u32[]{:S(2)}, u32[]{:S(2)}) %collective-permute-start.2) | collective-permute-done | bytes 40992 | tf_op jit(solution)/shard_map/ppermute | solution.py:778
  30.6 1.8 %collective-permute-done.1.refs_2_ = bf16[80,256]{1,0:T(8,128)(2,1)S(1)} collective-permute-done((bf16[80,256]{1,0:T(8,128)(2,1)S(1)}, bf16[80,256]{1,0:T(8,128)(2,1)S(1)}, u32[]{:S(2)}, u32[]{:S(2)}) %collective-permute-start.1) | collective-permute-done | bytes 40992 | tf_op jit(solution)/shard_map/ppermute | solution.py:778
  32.4 0.5 collective-permute-done.refs_1_
  32.9 0.0 all-to-all-done.1.table_ref
  32.9 2.3 %shard_map.168 = (bf16[16,32,256]{2,1,0:T(8,128)(2,1)}, bf16[272,256]{1,0:T(8,128)(2,1)}) custom-call(s32[1]{0:T(128)} %get-tuple-element.36.flag_ref, s32[2]{0:T(128)S(1)} %pad_add_fusion.place_ref, bf16[32,1024]{1,0:T(8,128)(2,1)S(1)} %get-tuple-element.37.own_ref, bf16[1024,256]{1,0:T(8,128)(2,1)S(1)} %get-tuple-element.38.ghost_ref, ...), custom_call_target="tpu_custom_call" | custom-call | tf_op jit(solution)/shard_map/pallas_call | solution.py:647
  35.3 6.1 %all-to-all-start.2 = ((bf16[16,32,256]{2,1,0:T(8,128)(2,1)}), bf16[16,32,256]{2,1,0:T(8,128)(2,1)S(1)}, u32[]{:S(2)}, u32[]{:S(2)}) async-start(bf16[16,32,256]{2,1,0:T(8,128)(2,1)} %get-tuple-element.51), calls=%async_computation.2 | async-start | bytes 524288 | tf_op jit(solution)/shard_map/all_to_all | solution.py:813
  41.3 2.8 %collective-permute-start.5 = (bf16[272,256]{1,0:T(8,128)(2,1)}, bf16[272,256]{1,0:T(8,128)(2,1)S(1)}, u32[]{:S(2)}, u32[]{:S(2)}) collective-permute-start(bf16[272,256]{1,0:T(8,128)(2,1)} %get-tuple-element.48.token_ref.refs_0_), channel_id=1, source_target_pairs={{8,0},{16,8},{24,16},{0,24},{9,1},{17,9},{25,17},{1,25},{10,2},{18... | collective-permute-start | bytes 417800 | tf_op jit(solution)/shard_map/ppermute | solution.py:778
  44.1 0.6 collective-permute-start.4
  44.7 0.6 collective-permute-start.3
  45.3 5.8 %shard_map.169 = (bf16[2,1,1,1024,256]{4,3,2,1,0:T(8,128)(2,1)}, bf16[768,1024]{1,0:T(8,128)(2,1)S(1)}, bf16[1024,1024]{1,0:T(8,128)(2,1)}, bf16[1024,256]{1,0:T(8,128)(2,1)}) custom-call(s32[1]{0:T(128)} %get-tuple-element.36.flag_ref, bf16[272,256]{1,0:T(8,128)(2,1)} %get-tuple-element.48.token_ref.refs_0_, bf16[1024,1024]{1,0:T(8,128)(2,1)} %get-tuple-element.49.own_hbm, ...), custom_call_target="tpu_custom_call" | custom-call | tf_op jit(solution)/shard_map/pallas_call | solution.py:647
  51.1 0.0 collective-permute-done.5.refs_3_
  51.1 1.6 %collective-permute-done.4.refs_2_ = bf16[272,256]{1,0:T(8,128)(2,1)S(1)} collective-permute-done((bf16[272,256]{1,0:T(8,128)(2,1)}, bf16[272,256]{1,0:T(8,128)(2,1)S(1)}, u32[]{:S(2)}, u32[]{:S(2)}) %collective-permute-start.4) | collective-permute-done | bytes 139296 | tf_op jit(solution)/shard_map/ppermute | solution.py:778
  52.7 0.0 collective-permute-done.3.refs_1_
  52.7 0.0 all-to-all-done.2.refs_4_
  52.7 8.5 %shard_map.170 = (f32[96,1024]{1,0:T(8,128)S(1)}, f32[128,1024]{1,0:T(8,128)S(1)}, f32[172,128]{1,0:T(8,128)S(1)}, bf16[256,1024]{1,0:T(8,128)(2,1)S(1)}) custom-call(s32[2]{0:T(128)S(1)} %pad_add_fusion.place_ref, bf16[272,256]{1,0:T(8,128)(2,1)} %get-tuple-element.48.token_ref.refs_0_, bf16[272,256]{1,0:T(8,128)(2,1)S(1)} %collective-permute-done.3.refs_1_, ...), custom_call_target="tpu_custom_call" | custom-call | tf_op jit(solution)/shard_map/pallas_call | solution.py:647
  61.2 0.1 collective-permute-start.6
  61.3 1.9 %collective-permute-done.6.got_ref = bf16[256,1024]{1,0:T(8,128)(2,1)S(1)} collective-permute-done((bf16[256,1024]{1,0:T(8,128)(2,1)S(1)}, bf16[256,1024]{1,0:T(8,128)(2,1)S(1)}, u32[]{:S(2)}, u32[]{:S(2)}) %collective-permute-start.6) | collective-permute-done | bytes 524320 | tf_op jit(solution)/shard_map/ppermute | solution.py:910
  63.2 1.0 %shard_map.171 = (f32[96,1024]{1,0:T(8,128)}, f32[128,1024]{1,0:T(8,128)}, f32[172,128]{1,0:T(8,128)}) custom-call(bf16[256,1024]{1,0:T(8,128)(2,1)S(1)} %collective-permute-done.6.got_ref, f32[96,1024]{1,0:T(8,128)S(1)} %get-tuple-element.56.one_ref, f32[128,1024]{1,0:T(8,128)S(1)} %get-tuple-element.57.two_ref, f32[172,128]{1,0:T(8,128)S(1)} %get-tuple-element.58.three_ref), custom_call_target="tpu_custom_call" | custom-call | tf_op jit(solution)/shard_map/pallas_call | solution.py:647
Async XLA Ops:
  0.6 18.3 %copy-start = (s32[1,1,8,32]{3,2,1,0:T(8,128)S(1)}, s32[1,1,8,32]{3,2,1,0:T(8,128)}, u32[]{:S(2)}) copy-start(s32[1,1,8,32]{3,2,1,0:T(8,128)} %rows_hbm.1) | copy-start | bytes 3076
  0.6 18.3 %copy-start.1 = (s32[1,1,32]{2,1,0:T(1,128)S(1)}, s32[1,1,32]{2,1,0:T(1,128)}, u32[]{:S(2)}) copy-start(s32[1,1,32]{2,1,0:T(1,128)} %param.21) | copy-start | bytes 388
  2.8 16.1 %all-to-all-start = ((bf16[8,32,256]{2,1,0:T(8,128)(2,1)}), bf16[8,32,256]{2,1,0:T(8,128)(2,1)S(1)}, u32[]{:S(2)}, u32[]{:S(2)}) async-start(bf16[8,32,256]{2,1,0:T(8,128)(2,1)} %get-tuple-element.43), calls=%async_computation | async-start | bytes 262144 | tf_op jit(solution)/shard_map/all_to_all | solution.py:718
  21.3 11.7 %all-to-all-start.1 = ((bf16[8,32,256]{2,1,0:T(8,128)(2,1)}), bf16[8,32,256]{2,1,0:T(8,128)(2,1)S(1)}, u32[]{:S(2)}, u32[]{:S(2)}) async-start(bf16[8,32,256]{2,1,0:T(8,128)(2,1)} %get-tuple-element.46), calls=%async_computation.1 | async-start | bytes 262144 | tf_op jit(solution)/shard_map/all_to_all | solution.py:772
  24.7 5.9 %collective-permute-start.2 = (bf16[80,256]{1,0:T(8,128)(2,1)S(1)}, bf16[80,256]{1,0:T(8,128)(2,1)S(1)}, u32[]{:S(2)}, u32[]{:S(2)}) collective-permute-start(bf16[80,256]{1,0:T(8,128)(2,1)S(1)} %get-tuple-element.47.refs_0_), channel_id=1, source_target_pairs={{3,0},{0,1},{1,2},{2,3},{7,4},{4,5},{5,6},{6,7},{11,8},{8,9},{9,10... | collective-permute-start | bytes 122888 | tf_op jit(solution)/shard_map/ppermute | solution.py:778
  27.1 5.3 %collective-permute-start.1 = (bf16[80,256]{1,0:T(8,128)(2,1)S(1)}, bf16[80,256]{1,0:T(8,128)(2,1)S(1)}, u32[]{:S(2)}, u32[]{:S(2)}) collective-permute-start(bf16[80,256]{1,0:T(8,128)(2,1)S(1)} %get-tuple-element.47.refs_0_), channel_id=1, source_target_pairs={{2,0},{3,1},{0,2},{1,3},{6,4},{7,5},{4,6},{5,7},{10,8},{11,9},{8,1... | collective-permute-start | bytes 122888 | tf_op jit(solution)/shard_map/ppermute | solution.py:778
  28.9 4.0 %collective-permute-start = (bf16[80,256]{1,0:T(8,128)(2,1)S(1)}, bf16[80,256]{1,0:T(8,128)(2,1)S(1)}, u32[]{:S(2)}, u32[]{:S(2)}) collective-permute-start(bf16[80,256]{1,0:T(8,128)(2,1)S(1)} %get-tuple-element.47.refs_0_), channel_id=1, source_target_pairs={{1,0},{2,1},{3,2},{0,3},{5,4},{6,5},{7,6},{4,7},{9,8},{10,9},{11,1... | collective-permute-start | bytes 122888 | tf_op jit(solution)/shard_map/ppermute | solution.py:778
  35.3 17.5 %all-to-all-start.2 = ((bf16[16,32,256]{2,1,0:T(8,128)(2,1)}), bf16[16,32,256]{2,1,0:T(8,128)(2,1)S(1)}, u32[]{:S(2)}, u32[]{:S(2)}) async-start(bf16[16,32,256]{2,1,0:T(8,128)(2,1)} %get-tuple-element.51), calls=%async_computation.2 | async-start | bytes 524288 | tf_op jit(solution)/shard_map/all_to_all | solution.py:813
  41.3 9.8 %collective-permute-start.5 = (bf16[272,256]{1,0:T(8,128)(2,1)}, bf16[272,256]{1,0:T(8,128)(2,1)S(1)}, u32[]{:S(2)}, u32[]{:S(2)}) collective-permute-start(bf16[272,256]{1,0:T(8,128)(2,1)} %get-tuple-element.48.token_ref.refs_0_), channel_id=1, source_target_pairs={{8,0},{16,8},{24,16},{0,24},{9,1},{17,9},{25,17},{1,25},{10,2},{18... | collective-permute-start | bytes 417800 | tf_op jit(solution)/shard_map/ppermute | solution.py:778
  44.1 8.6 %collective-permute-start.4 = (bf16[272,256]{1,0:T(8,128)(2,1)}, bf16[272,256]{1,0:T(8,128)(2,1)S(1)}, u32[]{:S(2)}, u32[]{:S(2)}) collective-permute-start(bf16[272,256]{1,0:T(8,128)(2,1)} %get-tuple-element.48.token_ref.refs_0_), channel_id=1, source_target_pairs={{16,0},{24,8},{0,16},{8,24},{17,1},{25,9},{1,17},{9,25},{18,2},{26... | collective-permute-start | bytes 417800 | tf_op jit(solution)/shard_map/ppermute | solution.py:778
  44.7 8.0 %collective-permute-start.3 = (bf16[272,256]{1,0:T(8,128)(2,1)}, bf16[272,256]{1,0:T(8,128)(2,1)S(1)}, u32[]{:S(2)}, u32[]{:S(2)}) collective-permute-start(bf16[272,256]{1,0:T(8,128)(2,1)} %get-tuple-element.48.token_ref.refs_0_), channel_id=1, source_target_pairs={{24,0},{0,8},{8,16},{16,24},{25,1},{1,9},{9,17},{17,25},{26,2},{2,... | collective-permute-start | bytes 417800 | tf_op jit(solution)/shard_map/ppermute | solution.py:778
  61.2 2.0 %collective-permute-start.6 = (bf16[256,1024]{1,0:T(8,128)(2,1)S(1)}, bf16[256,1024]{1,0:T(8,128)(2,1)S(1)}, u32[]{:S(2)}, u32[]{:S(2)}) collective-permute-start(bf16[256,1024]{1,0:T(8,128)(2,1)S(1)} %get-tuple-element.55), channel_id=1, source_target_pairs={{0,4},{4,0},{1,5},{5,1},{2,6},{6,2},{3,7},{7,3},{8,12},{12,8},{9,1... | collective-permute-start | bytes 1572872 | tf_op jit(solution)/shard_map/ppermute | solution.py:910

commit v13 on v12

--- a/solution.py
+++ b/solution.py
@@ -16,6 +16,7 @@
 
 f32 = jnp.float32
 bf16 = jnp.bfloat16
+f8 = jnp.float8_e4m3fn
 VMEM = pltpu.VMEM
 SMEM = pltpu.SMEM
 HBM = pltpu.HBM
@@ -38,6 +39,10 @@
 
 def normalize(values):
     return (values * lax.rsqrt(jnp.sum(values * values, -1, keepdims=True) + 1e-06)).astype(bf16)
+
+
+def blocks_of(length, step):
+    return [slice(at, min(at + step, length)) for at in range(0, length, step)]
 
 
 def dot(left, right):
@@ -96,11 +101,15 @@
     copies[0].wait()
     choose(rows_ref, turn_ref, pick_ref)
     copies[1].wait()
-    sent = normalize(dot(pick_ref[...], feats_ref[...]))
-    out_copy = post(sent, staged_ref, out_hbm, sems.at[4])
-    start = normalize(feats_ref[...].astype(f32))
-    start_ref[...] = start
-    own_ref[...] = start[: own_ref.shape[0]]
+    picked = dot(pick_ref[...], feats_ref[...])
+    each = staged_ref.shape[1]
+    for part in range(staged_ref.shape[0]):
+        staged_ref[part] = normalize(picked[part * each : (part + 1) * each])
+    out_copy = pltpu.make_async_copy(staged_ref, out_hbm, sems.at[4])
+    out_copy.start()
+    for cut in blocks_of(start_ref.shape[0], 32):
+        start_ref[cut, :] = normalize(feats_ref[cut, :].astype(f32))
+    own_ref[...] = start_ref[: own_ref.shape[0], :]
     copies[2].wait()
     copies[3].wait()
     out_copy.wait()
@@ -173,11 +182,11 @@
         spots = []
         for piece in range(pieces):
             here = jnp.where(high == piece, one, zero)
-            spots.append(spot_one * jnp.concatenate([here] * (BLOCK // 16), 0))
+            hot = spot_one * jnp.concatenate([here] * (BLOCK // 16), 0)
+            spots.append(hot.astype(f8))
         low = low_ref[tile]
-        low_hot = jnp.concatenate([jnp.where(low == ids, one, zero) for ids in lanes], 1)
-        spot_hot = jnp.concatenate(spots, 0)
-        return dot(spot_hot.astype(jnp.float8_e4m3fn), low_hot.astype(jnp.float8_e4m3fn))
+        low_hot = [jnp.where(low == ids, one, zero).astype(f8) for ids in lanes]
+        return dot(jnp.concatenate(spots, 0), jnp.concatenate(low_hot, 1))
 
     def turn(add, step, carry):
         first = step * GROUP
@@ -234,17 +243,18 @@
     own_copy.wait()
 
 
-def aggregate(flag_ref, start, parts, sums_ref, rest_ref):
+def aggregate(flag_ref, first_ref, parts, sums_ref, rest_ref):
     rows = sums_ref.shape[0]
-    total = start
-    for count, _, table in parts:
-        total += dot(count, table)
-    sums_ref[...] = total
+    for cut in blocks_of(rows, 256):
+        total = sum(dot(count_ref[cut, :], table) for count_ref, _, table in parts)
+        for inner in blocks_of(total.shape[0], 32):
+            at = slice(cut.start + inner.start, cut.start + inner.stop)
+            sums_ref[at, :] = first_ref[at, :].astype(f32) + total[inner]
 
     @pl.when(flag_ref[0] > 0)
     def _():
-        for count, rest_hbm, table in parts:
-            held = rest_ref.at[:, : count.shape[1]]
+        for count_ref, rest_hbm, table in parts:
+            held = rest_ref.at[:, : count_ref.shape[1]]
             pltpu.sync_copy(rest_hbm.at[:rows], held)
             sums_ref[...] += dot(held[...], table)
 
@@ -270,15 +280,15 @@
 ):
     width = start_ref.shape[1]
     table = table_ref[...].reshape(-1, width)
-    parts = ((ghost_ref[...], rest_hbm, table),)
-    aggregate(flag_ref, part_ref[...], parts, sums_ref, rest_ref)
+    parts = ((ghost_ref, rest_hbm, table),)
     choose(rows_ref, turn_ref, pick_ref)
-    start = normalize(sums_ref[...])
-    start_ref[...] = start
-    out_copy = post(dot(pick_ref[...], start).astype(bf16), staged_ref, out_hbm, sem)
+    aggregate(flag_ref, part_ref, parts, sums_ref, rest_ref)
+    for cut in blocks_of(start_ref.shape[0], 32):
+        start_ref[cut, :] = normalize(sums_ref[cut, :])
+    out_copy = post(dot(pick_ref[...], start_ref[...]).astype(bf16), staged_ref, out_hbm, sem)
     train = labels_ref.shape[1]
     side_ref[:train, :] = old_ref[...]
-    side_ref[train : 2 * train, :] = start[:train]
+    side_ref[train : 2 * train, :] = start_ref[:train, :]
     turn_ref[:1, :train] = labels_ref[...]
     side_ref[2 * train :, :128] = turn_ref[:16, :].astype(f32).astype(bf16)
     out_copy.wait()
@@ -300,10 +310,10 @@
     train, width = sums_ref.shape
     table = table_ref[...].reshape(-1, width)
     parts = (
-        (own_ref[...], own_rest_hbm, start_ref[...]),
-        (ghost_ref[:train], ghost_rest_hbm, table),
-    )
-    aggregate(flag_ref, noise_ref[...].astype(f32), parts, sums_ref, rest_ref)
+        (own_ref, own_rest_hbm, start_ref[...]),
+        (ghost_ref, ghost_rest_hbm, table),
+    )
+    aggregate(flag_ref, noise_ref, parts, sums_ref, rest_ref)
     last = jnp.broadcast_to(normalize(sums_ref[...])[None], staged_ref.shape)
     out_copy = post(last, staged_ref, out_hbm, sems.at[0])
     length = piece_refs[0].shape[0] - 16
@@ -364,11 +374,12 @@
     copies[0].wait()
     copies[1].wait()
     parts = (
-        (own_ref[...], own_rest_hbm, start_ref[...]),
-        (ghost_ref[...], ghost_rest_hbm, table),
-    )
-    aggregate(flag_ref, noise_ref[...].astype(f32), parts, sums_ref, rest_ref)
-    out_ref[1, 0, 0] = normalize(sums_ref[...])
+        (own_ref, own_rest_hbm, start_ref[...]),
+        (ghost_ref, ghost_rest_hbm, table),
+    )
+    aggregate(flag_ref, noise_ref, parts, sums_ref, rest_ref)
+    for cut in blocks_of(sums_ref.shape[0], 32):
+        out_ref[1, 0, 0, cut, :] = normalize(sums_ref[cut, :])
     out_copy = pltpu.make_async_copy(out_ref, out_hbm, sems.at[5])
     out_copy.start()
     copies[3].wait()
@@ -513,16 +524,16 @@
                 column((part * groups + group) * train, turned, part * 16 + group)
     in_ref[:, 2 * width :] = two_ref[...].reshape(-1, width)
 
-    def activate(values, h_ref, slope_ref, rows):
+    def activate(values, at, cols, h_ref, slope_ref):
         sigma = 0.5 + 0.5 * jnp.tanh(0.5 * values)
         out = values * sigma
-        slope_ref[rows, :] = sigma + out * (1.0 - sigma)
-        h_ref[rows, :] = out.astype(bf16)
+        slope_ref[at, cols] = sigma + out * (1.0 - sigma)
+        h_ref[at, cols] = out.astype(bf16)
         return lanes_sum(out)
 
-    def back(values, slope_ref, d_ref, rows):
-        out = values * slope_ref[rows, :]
-        d_ref[rows, :] = out.astype(bf16)
+    def back(values, at, cols, slope_ref, d_ref):
+        out = values * slope_ref[at, cols]
+        d_ref[at, cols] = out.astype(bf16)
         return lanes_sum(out)
 
     def layer(product, finish, *refs):
@@ -530,13 +541,20 @@
         values = product(cuts[0])
         for at, cut in enumerate(cuts):
             ahead = product(cuts[at + 1]) if at + 1 < len(cuts) else None
-            sums.append(finish(values, *refs, cut))
+            for rows in blocks_of(values.shape[0], 32):
+                here = slice(cut.start + rows.start, cut.start + rows.stop)
+                sums.append(
+                    sum(
+                        finish(values[rows, cols], here, cols, *refs)
+                        for cols in blocks_of(values.shape[1], 256)
+                    )
+                )
             values = ahead
         return jnp.concatenate(sums, 0)
 
     step = min(512, in_ref.shape[0])
     cuts = [slice(at, at + step) for at in range(0, in_ref.shape[0], step)]
-    sq_in = lanes_sum(in_ref[...])
+    sq_in = jnp.concatenate([lanes_sum(in_ref[at, :]) for at in blocks_of(in_ref.shape[0], 32)], 0)
     sq_one = layer(
         lambda cut: dot(in_ref[cut, :], w_first_ref[...]), activate, h_one_ref, slope_one_ref
     )
@@ -548,13 +566,16 @@
     if not many:
         copies[2].wait()
     logits = dot(h_two_ref[...], w_third_t_ref[...])
-    ids = lax.broadcasted_iota(jnp.int32, (logits.shape[0], wide), 1)
-    expo = jnp.where(ids < classes, jnp.exp(logits), 0.0)
-    probs = expo / jnp.sum(expo, -1, keepdims=True)
-    label = column_ref[:, :1]
-    d_three = (probs - jnp.where(ids == label, 1.0, 0.0)).astype(bf16)
-    sq_dthree = lanes_sum(d_three)
-    d_three_ref[...] = d_three
+    sums = []
+    for at in blocks_of(logits.shape[0], 32):
+        ids = lax.broadcasted_iota(jnp.int32, (at.stop - at.start, wide), 1)
+        expo = jnp.where(ids < classes, jnp.exp(logits[at]), 0.0)
+        probs = expo / jnp.sum(expo, -1, keepdims=True)
+        label = column_ref[at, :1]
+        d_three = (probs - jnp.where(ids == label, 1.0, 0.0)).astype(bf16)
+        d_three_ref[at, :] = d_three
+        sums.append(lanes_sum(d_three))
+    sq_dthree = jnp.concatenate(sums, 0)
     if not many:
         copies[3].wait()
         copies[4].wait()
@@ -604,7 +625,7 @@
 
     sum_one = dot_tn(left(in_ref, share_one), d_one_ref[...])
     sum_two = dot_tn(left(h_one_ref, share), d_two_ref[...])
-    sum_three = dot_tn(d_three, left(h_two_ref, share))
+    sum_three = dot_tn(d_three_ref[...], left(h_two_ref, share))
     g_first_ref[...] += sum_one[:share_one]
     g_second_ref[...] += sum_two[:share]
     g_third_ref[...] += sum_three[:classes, :share]

time: 65.4 us -> 65.3 us (level)
  Pallas kernels: 32.4 us -> 28.9 us
  starting transfers between devices: 23.5 us -> 27 us
    pallas_call x7, Pallas kernels: 32.4 us -> 28.9 us  [call(): pl.pallas_call(kernel, out_shape=[shape_of(*out) for out in outs], in_spe...]
    all_to_all x1, starting transfers between devices: 3.38 us -> 6.31 us  [local(): table1 = lax.all_to_all(out1, dom, split_axis=0, concat_axis=0, tiled=True)]
    ppermute x6, starting transfers between devices: 8.78 us -> 9.55 us  [shifted(): lax.ppermute(value, name, [((at + step * shift) % size, at) for at in ran...]
  transfers between devices with their start and end apart: 10 -> 10, of which waited for: 5 -> 5; matrix products, arithmetic and copies ran while one was open for 0% -> 0% of each run, Pallas kernels for 25% -> 20%
where the time goes in v13:
time: 65.3 us; the launch traced here: 64.5 us
  Pallas kernels  28.9 us (44%)
  starting transfers between devices  27 us (41%)
  waiting for transfers between devices  7.07 us (11%)
  between operations  1.4 us (2%)
    pallas_call x7, Pallas kernels, call(): pl.pallas_call(kernel, out_shape=[shape_of(*out) for out in outs], in_spe...  28.9 us
    ppermute x6, starting transfers between devices, shifted(): lax.ppermute(value, name, [((at + step * shift) % size, at) for at in ran...  9.55 us
    all_to_all x1, starting transfers between devices, local(): table1 = lax.all_to_all(out1, dom, split_axis=0, concat_axis=0, tiled=True)  6.31 us
    all_to_all x1, starting transfers between devices, local(): lax.all_to_all(last, ('chip', 'grp'), split_axis=0, concat_axis=0, tiled=...  5.93 us
    all_to_all x1, starting transfers between devices, local(): table0 = lax.all_to_all(out0, dom, split_axis=0, concat_axis=0, tiled=True)  5.18 us
    ppermute x6, waiting for transfers between devices, shifted(): lax.ppermute(value, name, [((at + step * shift) % size, at) for at in ran...  5.17 us
    ppermute x1, waiting for transfers between devices, local(): got = lax.ppermute(other, 'core', [(0, 1), (1, 0)])  1.9 us
  transfers between devices with their start and end apart: 10, of which 5 were waited for; matrix products, arithmetic and copies ran while one was open for 0% of the time, Pallas kernels for 20%

profile of v13, /device:TPU:0, one launch (start us, length us, event | category | flops | bytes accessed | tf_op | source)
XLA Modules:
  0.0 64.5 jit_solution(14172227480238916564)
XLA Ops:
  0.6 0.0 copy-start
  0.6 0.0 copy-start.1
  0.7 2.2 %shard_map.165 = (bf16[1024,256]{1,0:T(8,128)(2,1)S(1)}, bf16[8,32,256]{2,1,0:T(8,128)(2,1)}, bf16[32,256]{1,0:T(8,128)(2,1)S(1)}, s32[64,256]{1,0:T(8,128)S(1)}, s32[64,256]{1,0:T(8,128)S(1)}) custom-call(bf16[1,1,1024,256]{3,2,1,0:T(8,128)(2,1)} %feats_hbm.1, s32[1,1,8,32]{3,2,1,0:T(8,128)} %rows_hbm.1, s32[1,1,64,256]{3,2,1,0:T(8,128)} %src_hbm.1, ...), custom_call_target="tpu_custom_call" | custom-call | tf_op jit(solution)/shard_map/pallas_call | solution.py:668
  2.8 5.2 %all-to-all-start = ((bf16[8,32,256]{2,1,0:T(8,128)(2,1)}), bf16[8,32,256]{2,1,0:T(8,128)(2,1)S(1)}, u32[]{:S(2)}, u32[]{:S(2)}) async-start(bf16[8,32,256]{2,1,0:T(8,128)(2,1)} %get-tuple-element.43), calls=%async_computation | async-start | bytes 262144 | tf_op jit(solution)/shard_map/all_to_all | solution.py:739
  8.7 7.0 %shard_map.166 = (bf16[1024,1024]{1,0:T(8,128)(2,1)}, bf16[1024,256]{1,0:T(8,128)(2,1)S(1)}, bf16[32,1024]{1,0:T(8,128)(2,1)S(1)}, bf16[32,256]{1,0:T(8,128)(2,1...) custom-call(s32[1,1,64]{2,1,0:T(1,128)} %blocks_hbm.1, ...), custom_call_target="tpu_custom_call" | custom-call | tf_op jit(solution)/shard_map/pallas_call | solution.py:668
  15.7 0.0 all-to-all-done.table_ref
  15.7 0.0 copy-done
  15.7 0.0 copy-done.1
  15.7 2.1 %shard_map.167 = (bf16[1024,256]{1,0:T(8,128)(2,1)S(1)}, bf16[8,32,256]{2,1,0:T(8,128)(2,1)}, bf16[80,256]{1,0:T(8,128)(2,1)S(1)}) custom-call(s32[1]{0:T(128)} %get-tuple-element.36.flag_ref, f32[1024,256]{1,0:T(8,128)S(1)} %get-tuple-element.42.part_ref, bf16[1024,256]{1,0:T(8,128)(2,1)S(1)} %get-tuple-element.38.ghost_ref, ...), custom_call_target="tpu_custom_call" | custom-call | tf_op jit(solution)/shard_map/pallas_call | solution.py:668
  17.8 6.3 %all-to-all-start.1 = ((bf16[8,32,256]{2,1,0:T(8,128)(2,1)}), bf16[8,32,256]{2,1,0:T(8,128)(2,1)S(1)}, u32[]{:S(2)}, u32[]{:S(2)}) async-start(bf16[8,32,256]{2,1,0:T(8,128)(2,1)} %get-tuple-element.46), calls=%async_computation.1 | async-start | bytes 262144 | tf_op jit(solution)/shard_map/all_to_all | solution.py:793
  24.1 1.6 %collective-permute-start.2 = (bf16[80,256]{1,0:T(8,128)(2,1)S(1)}, bf16[80,256]{1,0:T(8,128)(2,1)S(1)}, u32[]{:S(2)}, u32[]{:S(2)}) collective-permute-start(bf16[80,256]{1,0:T(8,128)(2,1)S(1)} %get-tuple-element.47.refs_0_), channel_id=1, source_target_pairs={{3,0},{0,1},{1,2},{2,3},{7,4},{4,5},{5,6},{6,7},{11,8},{8,9},{9,10... | collective-permute-start | bytes 122888 | tf_op jit(solution)/shard_map/ppermute | solution.py:799
  25.7 3.5 %collective-permute-start.1 = (bf16[80,256]{1,0:T(8,128)(2,1)S(1)}, bf16[80,256]{1,0:T(8,128)(2,1)S(1)}, u32[]{:S(2)}, u32[]{:S(2)}) collective-permute-start(bf16[80,256]{1,0:T(8,128)(2,1)S(1)} %get-tuple-element.47.refs_0_), channel_id=1, source_target_pairs={{2,0},{3,1},{0,2},{1,3},{6,4},{7,5},{4,6},{5,7},{10,8},{11,9},{8,1... | collective-permute-start | bytes 122888 | tf_op jit(solution)/shard_map/ppermute | solution.py:799
  29.2 0.5 collective-permute-start
  29.7 0.1 pad_add_fusion.place_ref
  29.8 1.3 %collective-permute-done.2.refs_3_ = bf16[80,256]{1,0:T(8,128)(2,1)S(1)} collective-permute-done((bf16[80,256]{1,0:T(8,128)(2,1)S(1)}, bf16[80,256]{1,0:T(8,128)(2,1)S(1)}, u32[]{:S(2)}, u32[]{:S(2)}) %collective-permute-start.2) | collective-permute-done | bytes 40992 | tf_op jit(solution)/shard_map/ppermute | solution.py:799
  31.1 1.6 %collective-permute-done.1.refs_2_ = bf16[80,256]{1,0:T(8,128)(2,1)S(1)} collective-permute-done((bf16[80,256]{1,0:T(8,128)(2,1)S(1)}, bf16[80,256]{1,0:T(8,128)(2,1)S(1)}, u32[]{:S(2)}, u32[]{:S(2)}) %collective-permute-start.1) | collective-permute-done | bytes 40992 | tf_op jit(solution)/shard_map/ppermute | solution.py:799
  32.7 0.6 collective-permute-done.refs_1_
  33.3 0.0 all-to-all-done.1.table_ref
  33.3 2.3 %shard_map.168 = (bf16[16,32,256]{2,1,0:T(8,128)(2,1)}, bf16[272,256]{1,0:T(8,128)(2,1)}) custom-call(s32[1]{0:T(128)} %get-tuple-element.36.flag_ref, s32[2]{0:T(128)S(1)} %pad_add_fusion.place_ref, bf16[32,1024]{1,0:T(8,128)(2,1)S(1)} %get-tuple-element.37.own_ref, bf16[1024,256]{1,0:T(8,128)(2,1)S(1)} %get-tuple-element.38.ghost_ref, ...), custom_call_target="tpu_custom_call" | custom-call | tf_op jit(solution)/shard_map/pallas_call | solution.py:668
  35.7 5.9 %all-to-all-start.2 = ((bf16[16,32,256]{2,1,0:T(8,128)(2,1)}), bf16[16,32,256]{2,1,0:T(8,128)(2,1)S(1)}, u32[]{:S(2)}, u32[]{:S(2)}) async-start(bf16[16,32,256]{2,1,0:T(8,128)(2,1)} %get-tuple-element.51), calls=%async_computation.2 | async-start | bytes 524288 | tf_op jit(solution)/shard_map/all_to_all | solution.py:834
  41.6 2.8 %collective-permute-start.5 = (bf16[272,256]{1,0:T(8,128)(2,1)}, bf16[272,256]{1,0:T(8,128)(2,1)S(1)}, u32[]{:S(2)}, u32[]{:S(2)}) collective-permute-start(bf16[272,256]{1,0:T(8,128)(2,1)} %get-tuple-element.48.token_ref.refs_0_), channel_id=1, source_target_pairs={{8,0},{16,8},{24,16},{0,24},{9,1},{17,9},{25,17},{1,25},{10,2},{18... | collective-permute-start | bytes 417800 | tf_op jit(solution)/shard_map/ppermute | solution.py:799
  44.4 0.6 collective-permute-start.4
  45.0 0.6 collective-permute-start.3
  45.6 5.8 %shard_map.169 = (bf16[2,1,1,1024,256]{4,3,2,1,0:T(8,128)(2,1)}, bf16[768,1024]{1,0:T(8,128)(2,1)S(1)}, bf16[1024,1024]{1,0:T(8,128)(2,1)}, bf16[1024,256]{1,0:T(8,128)(2,1)}) custom-call(s32[1]{0:T(128)} %get-tuple-element.36.flag_ref, bf16[272,256]{1,0:T(8,128)(2,1)} %get-tuple-element.48.token_ref.refs_0_, bf16[1024,1024]{1,0:T(8,128)(2,1)} %get-tuple-element.49.own_hbm, ...), custom_call_target="tpu_custom_call" | custom-call | tf_op jit(solution)/shard_map/pallas_call | solution.py:668
  51.4 0.0 collective-permute-done.5.refs_3_
  51.4 1.6 %collective-permute-done.4.refs_2_ = bf16[272,256]{1,0:T(8,128)(2,1)S(1)} collective-permute-done((bf16[272,256]{1,0:T(8,128)(2,1)}, bf16[272,256]{1,0:T(8,128)(2,1)S(1)}, u32[]{:S(2)}, u32[]{:S(2)}) %collective-permute-start.4) | collective-permute-done | bytes 139296 | tf_op jit(solution)/shard_map/ppermute | solution.py:799
  53.0 0.0 collective-permute-done.3.refs_1_
  53.0 0.0 all-to-all-done.2.refs_4_
  53.0 8.5 %shard_map.170 = (f32[96,1024]{1,0:T(8,128)S(1)}, f32[128,1024]{1,0:T(8,128)S(1)}, f32[172,128]{1,0:T(8,128)S(1)}, bf16[256,1024]{1,0:T(8,128)(2,1)S(1)}) custom-call(s32[2]{0:T(128)S(1)} %pad_add_fusion.place_ref, bf16[272,256]{1,0:T(8,128)(2,1)} %get-tuple-element.48.token_ref.refs_0_, bf16[272,256]{1,0:T(8,128)(2,1)S(1)} %collective-permute-done.3.refs_1_, ...), custom_call_target="tpu_custom_call" | custom-call | tf_op jit(solution)/shard_map/pallas_call | solution.py:668
  61.5 0.1 collective-permute-start.6
  61.6 1.9 %collective-permute-done.6.got_ref = bf16[256,1024]{1,0:T(8,128)(2,1)S(1)} collective-permute-done((bf16[256,1024]{1,0:T(8,128)(2,1)S(1)}, bf16[256,1024]{1,0:T(8,128)(2,1)S(1)}, u32[]{:S(2)}, u32[]{:S(2)}) %collective-permute-start.6) | collective-permute-done | bytes 524320 | tf_op jit(solution)/shard_map/ppermute | solution.py:931
  63.5 1.0 %shard_map.171 = (f32[96,1024]{1,0:T(8,128)}, f32[128,1024]{1,0:T(8,128)}, f32[172,128]{1,0:T(8,128)}) custom-call(bf16[256,1024]{1,0:T(8,128)(2,1)S(1)} %collective-permute-done.6.got_ref, f32[96,1024]{1,0:T(8,128)S(1)} %get-tuple-element.56.one_ref, f32[128,1024]{1,0:T(8,128)S(1)} %get-tuple-element.57.two_ref, f32[172,128]{1,0:T(8,128)S(1)} %get-tuple-element.58.three_ref), custom_call_target="tpu_custom_call" | custom-call | tf_op jit(solution)/shard_map/pallas_call | solution.py:668
Async XLA Ops:
  0.6 15.1 %copy-start = (s32[1,1,8,32]{3,2,1,0:T(8,128)S(1)}, s32[1,1,8,32]{3,2,1,0:T(8,128)}, u32[]{:S(2)}) copy-start(s32[1,1,8,32]{3,2,1,0:T(8,128)} %rows_hbm.1) | copy-start | bytes 3076
  0.6 15.1 %copy-start.1 = (s32[1,1,32]{2,1,0:T(1,128)S(1)}, s32[1,1,32]{2,1,0:T(1,128)}, u32[]{:S(2)}) copy-start(s32[1,1,32]{2,1,0:T(1,128)} %param.21) | copy-start | bytes 388
  2.8 12.8 %all-to-all-start = ((bf16[8,32,256]{2,1,0:T(8,128)(2,1)}), bf16[8,32,256]{2,1,0:T(8,128)(2,1)S(1)}, u32[]{:S(2)}, u32[]{:S(2)}) async-start(bf16[8,32,256]{2,1,0:T(8,128)(2,1)} %get-tuple-element.43), calls=%async_computation | async-start | bytes 262144 | tf_op jit(solution)/shard_map/all_to_all | solution.py:739
  17.8 15.5 %all-to-all-start.1 = ((bf16[8,32,256]{2,1,0:T(8,128)(2,1)}), bf16[8,32,256]{2,1,0:T(8,128)(2,1)S(1)}, u32[]{:S(2)}, u32[]{:S(2)}) async-start(bf16[8,32,256]{2,1,0:T(8,128)(2,1)} %get-tuple-element.46), calls=%async_computation.1 | async-start | bytes 262144 | tf_op jit(solution)/shard_map/all_to_all | solution.py:793
  24.1 7.0 %collective-permute-start.2 = (bf16[80,256]{1,0:T(8,128)(2,1)S(1)}, bf16[80,256]{1,0:T(8,128)(2,1)S(1)}, u32[]{:S(2)}, u32[]{:S(2)}) collective-permute-start(bf16[80,256]{1,0:T(8,128)(2,1)S(1)} %get-tuple-element.47.refs_0_), channel_id=1, source_target_pairs={{3,0},{0,1},{1,2},{2,3},{7,4},{4,5},{5,6},{6,7},{11,8},{8,9},{9,10... | collective-permute-start | bytes 122888 | tf_op jit(solution)/shard_map/ppermute | solution.py:799
  25.7 7.0 %collective-permute-start.1 = (bf16[80,256]{1,0:T(8,128)(2,1)S(1)}, bf16[80,256]{1,0:T(8,128)(2,1)S(1)}, u32[]{:S(2)}, u32[]{:S(2)}) collective-permute-start(bf16[80,256]{1,0:T(8,128)(2,1)S(1)} %get-tuple-element.47.refs_0_), channel_id=1, source_target_pairs={{2,0},{3,1},{0,2},{1,3},{6,4},{7,5},{4,6},{5,7},{10,8},{11,9},{8,1... | collective-permute-start | bytes 122888 | tf_op jit(solution)/shard_map/ppermute | solution.py:799
  29.2 4.2 %collective-permute-start = (bf16[80,256]{1,0:T(8,128)(2,1)S(1)}, bf16[80,256]{1,0:T(8,128)(2,1)S(1)}, u32[]{:S(2)}, u32[]{:S(2)}) collective-permute-start(bf16[80,256]{1,0:T(8,128)(2,1)S(1)} %get-tuple-element.47.refs_0_), channel_id=1, source_target_pairs={{1,0},{2,1},{3,2},{0,3},{5,4},{6,5},{7,6},{4,7},{9,8},{10,9},{11,1... | collective-permute-start | bytes 122888 | tf_op jit(solution)/shard_map/ppermute | solution.py:799
  35.7 17.3 %all-to-all-start.2 = ((bf16[16,32,256]{2,1,0:T(8,128)(2,1)}), bf16[16,32,256]{2,1,0:T(8,128)(2,1)S(1)}, u32[]{:S(2)}, u32[]{:S(2)}) async-start(bf16[16,32,256]{2,1,0:T(8,128)(2,1)} %get-tuple-element.51), calls=%async_computation.2 | async-start | bytes 524288 | tf_op jit(solution)/shard_map/all_to_all | solution.py:834
  41.6 9.8 %collective-permute-start.5 = (bf16[272,256]{1,0:T(8,128)(2,1)}, bf16[272,256]{1,0:T(8,128)(2,1)S(1)}, u32[]{:S(2)}, u32[]{:S(2)}) collective-permute-start(bf16[272,256]{1,0:T(8,128)(2,1)} %get-tuple-element.48.token_ref.refs_0_), channel_id=1, source_target_pairs={{8,0},{16,8},{24,16},{0,24},{9,1},{17,9},{25,17},{1,25},{10,2},{18... | collective-permute-start | bytes 417800 | tf_op jit(solution)/shard_map/ppermute | solution.py:799
  44.4 8.6 %collective-permute-start.4 = (bf16[272,256]{1,0:T(8,128)(2,1)}, bf16[272,256]{1,0:T(8,128)(2,1)S(1)}, u32[]{:S(2)}, u32[]{:S(2)}) collective-permute-start(bf16[272,256]{1,0:T(8,128)(2,1)} %get-tuple-element.48.token_ref.refs_0_), channel_id=1, source_target_pairs={{16,0},{24,8},{0,16},{8,24},{17,1},{25,9},{1,17},{9,25},{18,2},{26... | collective-permute-start | bytes 417800 | tf_op jit(solution)/shard_map/ppermute | solution.py:799
  45.0 8.0 %collective-permute-start.3 = (bf16[272,256]{1,0:T(8,128)(2,1)}, bf16[272,256]{1,0:T(8,128)(2,1)S(1)}, u32[]{:S(2)}, u32[]{:S(2)}) collective-permute-start(bf16[272,256]{1,0:T(8,128)(2,1)} %get-tuple-element.48.token_ref.refs_0_), channel_id=1, source_target_pairs={{24,0},{0,8},{8,16},{16,24},{25,1},{1,9},{9,17},{17,25},{26,2},{2,... | collective-permute-start | bytes 417800 | tf_op jit(solution)/shard_map/ppermute | solution.py:799
  61.5 2.0 %collective-permute-start.6 = (bf16[256,1024]{1,0:T(8,128)(2,1)S(1)}, bf16[256,1024]{1,0:T(8,128)(2,1)S(1)}, u32[]{:S(2)}, u32[]{:S(2)}) collective-permute-start(bf16[256,1024]{1,0:T(8,128)(2,1)S(1)} %get-tuple-element.55), channel_id=1, source_target_pairs={{0,4},{4,0},{1,5},{5,1},{2,6},{6,2},{3,7},{7,3},{8,12},{12,8},{9,1... | collective-permute-start | bytes 1572872 | tf_op jit(solution)/shard_map/ppermute | solution.py:931

commit v14 on v13

--- a/solution.py
+++ b/solution.py
@@ -47,6 +47,10 @@
 
 def dot(left, right):
     return jnp.dot(left, right, preferred_element_type=f32)
+
+
+def dot_nt(left, right):
+    return lax.dot_general(left, right, (((1,), (1,)), ((), ())), preferred_element_type=f32)
 
 
 def dot_tn(left, right):
@@ -103,13 +107,16 @@
     copies[1].wait()
     picked = dot(pick_ref[...], feats_ref[...])
     each = staged_ref.shape[1]
+    train = own_ref.shape[0]
+    each -= train
+    own_ref[...] = normalize(feats_ref[:train, :].astype(f32))
     for part in range(staged_ref.shape[0]):
-        staged_ref[part] = normalize(picked[part * each : (part + 1) * each])
+        staged_ref[part, :each] = normalize(picked[part * each : (part + 1) * each])
+        staged_ref[part, each:] = own_ref[...]
     out_copy = pltpu.make_async_copy(staged_ref, out_hbm, sems.at[4])
     out_copy.start()
     for cut in blocks_of(start_ref.shape[0], 32):
         start_ref[cut, :] = normalize(feats_ref[cut, :].astype(f32))
-    own_ref[...] = start_ref[: own_ref.shape[0], :]
     copies[2].wait()
     copies[3].wait()
     out_copy.wait()
@@ -259,8 +266,19 @@
             sums_ref[...] += dot(held[...], table)
 
 
+def near_rows(place_ref, table_ref, each, near_ref, first):
+    chips, _, width = near_ref.shape
+    size = table_ref.shape[1] - each
+    for chip in range(chips):
+        member = 2 * chip + place_ref[0] % 2
+        near_ref[chip, first : first + size, :] = table_ref[pl.ds(member, 1), each:, :].reshape(
+            size, width
+        )
+
+
 def hop_kernel(
     flag_ref,
+    place_ref,
     part_ref,
     ghost_ref,
     rest_hbm,
@@ -271,6 +289,7 @@
     start_ref,
     out_hbm,
     side_ref,
+    near_ref,
     sums_ref,
     rest_ref,
     turn_ref,
@@ -279,14 +298,20 @@
     sem,
 ):
     width = start_ref.shape[1]
-    table = table_ref[...].reshape(-1, width)
-    parts = ((ghost_ref, rest_hbm, table),)
+    parts, each = rows_ref.shape
+    table = table_ref[:, :each, :].reshape(-1, width)
     choose(rows_ref, turn_ref, pick_ref)
-    aggregate(flag_ref, part_ref, parts, sums_ref, rest_ref)
+    aggregate(flag_ref, part_ref, ((ghost_ref, rest_hbm, table),), sums_ref, rest_ref)
     for cut in blocks_of(start_ref.shape[0], 32):
         start_ref[cut, :] = normalize(sums_ref[cut, :])
-    out_copy = post(dot(pick_ref[...], start_ref[...]).astype(bf16), staged_ref, out_hbm, sem)
+    sent = dot(pick_ref[...], start_ref[...]).astype(bf16)
     train = labels_ref.shape[1]
+    for part in range(parts):
+        staged_ref[part, :each] = sent[part * each : (part + 1) * each]
+        staged_ref[part, each:] = start_ref[:train, :]
+    out_copy = pltpu.make_async_copy(staged_ref, out_hbm, sem)
+    out_copy.start()
+    near_rows(place_ref, table_ref, each, near_ref, 0)
     side_ref[:train, :] = old_ref[...]
     side_ref[train : 2 * train, :] = start_ref[:train, :]
     turn_ref[:1, :train] = labels_ref[...]
@@ -306,9 +331,12 @@
     table_ref,
     *refs,
 ):
-    *piece_refs, out_hbm, side_hbm, sums_ref, rest_ref, turn_ref, staged_ref, side_ref, sems = refs
+    near0_ref, *piece_refs = refs[: -10]
+    out_hbm, side_hbm, near_hbm, sums_ref, rest_ref, turn_ref, staged_ref = refs[-10:-3]
+    side_ref, near_ref, sems = refs[-3:]
     train, width = sums_ref.shape
-    table = table_ref[...].reshape(-1, width)
+    each = table_ref.shape[1] - train
+    table = table_ref[:, :each, :].reshape(-1, width)
     parts = (
         (own_ref, own_rest_hbm, start_ref[...]),
         (ghost_ref, ghost_rest_hbm, table),
@@ -319,15 +347,20 @@
     length = piece_refs[0].shape[0] - 16
     groups = len(piece_refs)
     if groups > 1:
+        near_ref[:, :train, :] = near0_ref[...]
+        near_rows(place_ref, table_ref, each, near_ref, train)
+        near_copy = pltpu.make_async_copy(near_ref, near_hbm, sems.at[2])
+        near_copy.start()
         for shift, ref in enumerate(piece_refs):
+            if shift:
+                side_ref[(shift - 1) * length : shift * length, :] = ref[:length, :]
             group = lax.rem(place_ref[1] + shift, groups)
-            at = pl.multiple_of(group * length, length)
-            side_ref[pl.ds(at, length), :] = ref[:length, :]
             turn_ref[pl.ds(group, 1), :] = ref[length:, :128].astype(f32)[:1]
-        side_ref[groups * length :, :128] = turn_ref[:16, :].astype(bf16)
+        side_ref[(groups - 1) * length :, :128] = turn_ref[:16, :].astype(bf16)
         side_copy = pltpu.make_async_copy(side_ref, side_hbm, sems.at[1])
         side_copy.start()
         side_copy.wait()
+        near_copy.wait()
     out_copy.wait()
 
 
@@ -339,37 +372,29 @@
     ghost_rest_hbm,
     noise_hbm,
     weight_hbm,
-    second_hbm,
-    third_hbm,
     ghost_ref,
     table_ref,
     start_ref,
     out_hbm,
     weight_ref,
-    second_t_hbm,
-    third_t_hbm,
     own_ref,
     noise_ref,
     sums_ref,
     rest_ref,
     out_ref,
-    second_ref,
-    third_ref,
-    second_t_ref,
-    third_t_ref,
     sems,
 ):
     copies = fetch(
         (
             (own_hbm, own_ref),
             (noise_hbm.at[1, 0, 0], noise_ref),
-            (second_hbm, second_ref),
-            (third_hbm, third_ref),
             (weight_hbm, weight_ref),
         ),
         sems,
     )
-    table = table_ref[...].reshape(-1, out_ref.shape[-1])
+    width = out_ref.shape[-1]
+    ghosts = ghost_ref.shape[1]
+    table = table_ref[:, : ghosts // table_ref.shape[0], :].reshape(ghosts, width)
     out_ref[0, 0, 0] = start_ref[...]
     copies[0].wait()
     copies[1].wait()
@@ -380,23 +405,10 @@
     aggregate(flag_ref, noise_ref, parts, sums_ref, rest_ref)
     for cut in blocks_of(sums_ref.shape[0], 32):
         out_ref[1, 0, 0, cut, :] = normalize(sums_ref[cut, :])
-    out_copy = pltpu.make_async_copy(out_ref, out_hbm, sems.at[5])
+    out_copy = pltpu.make_async_copy(out_ref, out_hbm, sems.at[3])
     out_copy.start()
-    copies[3].wait()
-    classes = third_ref.shape[0]
-    third_t_ref[:, 128:] = jnp.zeros((third_t_ref.shape[0], third_t_ref.shape[1] - 128), bf16)
-    third_t_ref[:, :128] = third_ref[:128, :].T
-    third_t_ref[:, 128:classes] = third_ref[128:, :].T
-    third_copy = pltpu.make_async_copy(third_t_ref, third_t_hbm, sems.at[6])
-    third_copy.start()
     copies[2].wait()
-    hid = second_ref.shape[0]
-    for at in range(0, hid, 256):
-        second_t_ref[at : at + 256, :] = second_ref[:, at : at + 256].T
-    second_copy = pltpu.make_async_copy(second_t_ref, second_t_hbm, sems.at[7])
-    second_copy.start()
-    for copy in (copies[4], out_copy, third_copy, second_copy):
-        copy.wait()
+    out_copy.wait()
 
 
 def shares(ref, first, share):
@@ -421,9 +433,7 @@
     side_refs,
     w_first_hbm,
     w_second_hbm,
-    w_third_t_hbm,
     w_third_hbm,
-    w_second_t_hbm,
     n_first_hbm,
     n_second_hbm,
     n_third_hbm,
@@ -432,11 +442,11 @@
     g_third_ref,
     send_ref,
     side_hbm,
+    near_hbm,
+    near_ref,
     w_first_ref,
     w_second_ref,
-    w_third_t_ref,
     w_third_ref,
-    w_second_t_ref,
     n_first_ref,
     n_second_ref,
     n_third_ref,
@@ -463,9 +473,7 @@
     pairs = (
         (w_first_hbm, w_first_ref),
         (w_second_hbm, w_second_ref),
-        (w_third_t_hbm, w_third_t_ref),
         (w_third_hbm, w_third_ref),
-        (w_second_t_hbm, w_second_t_ref),
         (n_first_hbm, n_first_ref),
         (n_second_hbm, n_second_ref),
         (n_third_hbm, n_third_ref),
@@ -503,7 +511,7 @@
             in_ref[:, hop * width : (hop + 1) * width] = ref[...].reshape(-1, width)
     else:
         chips = len(side_refs)
-        copies = fetch(((side_hbm, side_refs[0]),) + pairs[1:], sems)
+        copies = fetch(((side_hbm, side_refs[0]), (near_hbm, near_ref)) + pairs[1:], sems)
         groups = two_ref.shape[0] // chips
         rows = groups * train
         for shift, ref in [*enumerate(side_refs)][::-1]:
@@ -511,13 +519,21 @@
                 copies[0].wait()
             part = lax.rem(place // 2 - shift + chips, chips)
             at = pl.multiple_of(part * rows, rows)
-            for group in range(groups):
+            for after in range(1, groups):
+                row = at + lax.rem(place_ref[1] + after, groups) * train
                 for hop in range(2):
-                    first = (2 * group + hop) * train
-                    in_ref[pl.ds(at + group * train, train), hop * width : (hop + 1) * width] = ref[
-                        first : first + train, :
-                    ]
-            turn_ref[pl.ds(pl.multiple_of(part * 16, 16), 16), :] = ref[2 * rows :, :128].astype(f32)
+                    first = (2 * (after - 1) + hop) * train
+                    in_ref[
+                        pl.ds(pl.multiple_of(row, train), train), hop * width : (hop + 1) * width
+                    ] = ref[first : first + train, :]
+            turn_ref[pl.ds(pl.multiple_of(part * 16, 16), 16), :] = ref[2 * (rows - train) :, :128].astype(f32)
+        copies[1].wait()
+        for chip in range(chips):
+            row = pl.multiple_of(chip * rows + place_ref[1] * train, train)
+            for hop in range(2):
+                in_ref[pl.ds(row, train), hop * width : (hop + 1) * width] = near_ref[
+                    chip, hop * train : (hop + 1) * train, :
+                ]
         turned = turn_ref[...].T
         for part in range(chips):
             for group in range(groups):
@@ -559,13 +575,14 @@
         lambda cut: dot(in_ref[cut, :], w_first_ref[...]), activate, h_one_ref, slope_one_ref
     )
     if not many:
-        copies[1].wait()
+        copies[2].wait()
     sq_two = layer(
         lambda cut: dot(h_one_ref[cut, :], w_second_ref[...]), activate, h_two_ref, slope_two_ref
     )
     if not many:
-        copies[2].wait()
-    logits = dot(h_two_ref[...], w_third_t_ref[...])
+        copies[3].wait()
+        pad()
+    logits = dot_nt(h_two_ref[...], w_third_pad_ref[...])
     sums = []
     for at in blocks_of(logits.shape[0], 32):
         ids = lax.broadcasted_iota(jnp.int32, (at.stop - at.start, wide), 1)
@@ -576,15 +593,11 @@
         d_three_ref[at, :] = d_three
         sums.append(lanes_sum(d_three))
     sq_dthree = jnp.concatenate(sums, 0)
-    if not many:
-        copies[3].wait()
-        copies[4].wait()
-        pad()
     sq_dtwo = layer(
         lambda cut: dot(d_three_ref[cut, :], w_third_pad_ref[...]), back, slope_two_ref, d_two_ref
     )
     sq_done = layer(
-        lambda cut: dot(d_two_ref[cut, :], w_second_t_ref[...]), back, slope_one_ref, d_one_ref
+        lambda cut: dot_nt(d_two_ref[cut, :], w_second_ref[...]), back, slope_one_ref, d_one_ref
     )
 
     def total(values):
@@ -598,7 +611,7 @@
     factor = clip_bound / jnp.maximum(norm, clip_bound)
 
     if not many:
-        for copy in copies[5:]:
+        for copy in copies[4:]:
             copy.wait()
         set_noise()
     share_one, share = g_first_ref.shape[0], g_second_ref.shape[0]
@@ -715,13 +728,13 @@
             value = lax.all_gather(value, name, axis=0, tiled=True)
         return value
 
-    staged = VMEM((parts, each, width), bf16)
+    staged = VMEM((parts, each + train, width), bf16)
     start0, out0, own0, src, dst = call(
         first_kernel,
         16,
         [
             ((nodes, width), bf16, None),
-            ((parts, each, width), bf16, HBM),
+            ((parts, each + train, width), bf16, HBM),
             ((train, width), bf16, None),
             ((tiles, slots), jnp.int32, None),
             ((tiles, slots), jnp.int32, None),
@@ -770,16 +783,19 @@
             DMA((4,)),
         ],
     )
-    start1, out1, side = call(
+    place = jnp.stack([lax.axis_index(dom), lax.axis_index("grp")]).astype(jnp.int32)
+    start1, out1, side, near0 = call(
         hop_kernel,
         16,
         [
             ((nodes, width), bf16, None),
-            ((parts, each, width), bf16, HBM),
+            ((parts, each + train, width), bf16, HBM),
             ((2 * train + 16, width), bf16, None),
+            ((parts // 2, train, width), bf16, None),
         ],
         [
             (flag, SMEM),
+            (place, SMEM),
             (part1, None),
             (ghost, None),
             (ghost_rest, HBM),
@@ -791,7 +807,6 @@
         [VMEM((nodes, width), f32), VMEM((nodes, ghosts), bf16), turn, pick, staged, DMA(())],
     )
     table1 = lax.all_to_all(out1, dom, split_axis=0, concat_axis=0, tiled=True)
-    place = jnp.stack([lax.axis_index(dom), lax.axis_index("grp")]).astype(jnp.int32)
     grp = lax.axis_size("grp")
 
     def shifted(value, name, size, step):
@@ -801,13 +816,15 @@
         ]
 
     sides = [side] + (shifted(side, "grp", grp, 1) if few else [])
-    side_shape = (len(sides) * 2 * train + 16, width)
-    last, side = call(
+    side_shape = ((len(sides) - 1) * 2 * train + 16, width)
+    near_shape = (parts // 2, 2 * train, width)
+    last, side, near = call(
         train_kernel,
         12,
         [
             ((copies, train, width), bf16, HBM),
             (side_shape, bf16, HBM),
+            (near_shape, bf16, HBM),
         ],
         [
             (flag, SMEM),
@@ -819,6 +836,7 @@
             (noise_train, None),
             (start1, None),
             (table1, None),
+            (near0, None),
         ]
         + [(value, None) for value in sides],
         [
@@ -827,7 +845,8 @@
             VMEM((128, 128), f32),
             VMEM((copies, train, width), bf16),
             VMEM(side_shape, bf16),
-            DMA((2,)),
+            VMEM(near_shape, bf16),
+            DMA((3,)),
         ],
     )
     if few:
@@ -839,14 +858,12 @@
         )
         every_label = every(labels.reshape(1, train), axes)
     wide = (classes + 255) // 256 * 256
-    hop_feats, held_first, second_t, third_t = call(
+    hop_feats, held_first = call(
         last_kernel,
         28,
         [
             ((2, 1, 1, nodes, width), bf16, HBM),
             (w_first.shape, bf16, None),
-            ((hid, hid), bf16, HBM),
-            ((hid, wide), bf16, HBM),
         ],
         [
             (flag, SMEM),
@@ -856,8 +873,6 @@
             (ghost_rest, HBM),
             (hop_noise, HBM),
             (w_first, HBM),
-            (w_second, HBM),
-            (w_third.T, HBM),
             (ghost, None),
             (table1, None),
             (start1, None),
@@ -868,17 +883,13 @@
             VMEM((nodes, width), f32),
             VMEM((nodes, max(nodes, ghosts)), bf16),
             VMEM((2, 1, 1, nodes, width), bf16),
-            VMEM((hid, hid), bf16),
-            VMEM((classes, hid), bf16),
-            VMEM((hid, hid), bf16),
-            VMEM((hid, wide), bf16),
-            DMA((8,)),
+            DMA((4,)),
         ],
     )
     chunk = train * (copies if few else min(members, 32))
     groups = chunk // train
     noises = (noise_first, noise_second, noise_third.T)
-    fixed = (w_first, w_second, third_t, w_third.T, second_t) + noises
+    fixed = (w_first, w_second, w_third.T) + noises
     scratch = [VMEM(value.shape, value.dtype) for value in fixed]
     scratch += [
         VMEM((chunk, d_in), bf16),
@@ -899,8 +910,8 @@
 
         def classify(place_ref, *refs):
             sides_in, rest = refs[:chips], refs[chips:]
-            two_ref, first_ref, *outs = rest[:13]
-            held, *rest = rest[13:]
+            near_hbm, two_ref, first_ref, *outs = rest[:12]
+            held, near_ref, *rest = rest[12:]
             classify_kernel(
                 False,
                 place_ref,
@@ -912,6 +923,8 @@
                 first_ref,
                 *outs,
                 sides_in[0],
+                near_hbm,
+                near_ref,
                 first_ref,
                 *rest,
             )
@@ -924,9 +937,9 @@
             [(place, SMEM)]
             + [(side, HBM)]
             + [(value, None) for value in sides[1:]]
-            + [(every2, None), (held_first, None)]
+            + [(near, HBM), (every2, None), (held_first, None)]
             + [(value, HBM) for value in fixed[1:]],
-            [VMEM(side_shape, bf16)] + scratch[1:],
+            [VMEM(side_shape, bf16), VMEM(near_shape, bf16)] + scratch[1:],
         )
         got = lax.ppermute(other, "core", [(0, 1), (1, 0)])
         first, second, third = call(
@@ -949,10 +962,12 @@
                 one_ref,
                 two_ref,
                 None,
-                *rest[:11],
+                *rest[:9],
                 None,
                 None,
-                *rest[11:],
+                None,
+                None,
+                *rest[9:],
             )
 
         def whole(value):

time: 65.3 us -> 63.7 us (0.975)
  Pallas kernels: 28.9 us -> 27.5 us
  starting transfers between devices: 27 us -> 27.7 us
    all_to_all x1, starting transfers between devices: 6.31 us -> 8.25 us  [local(): table1 = lax.all_to_all(out1, dom, split_axis=0, concat_axis=0, tiled=True)]
    ppermute x6, starting transfers between devices: 9.55 us -> 7.78 us  [shifted(): lax.ppermute(value, name, [((at + step * shift) % size, at) for at in ran...]
    pallas_call x7, Pallas kernels: 28.9 us -> 27.5 us  [call(): pl.pallas_call(kernel, out_shape=[shape_of(*out) for out in outs], in_spe...]
    ppermute x6, waiting for transfers between devices: 5.17 us -> 4.4 us  [shifted(): lax.ppermute(value, name, [((at + step * shift) % size, at) for at in ran...]
  transfers between devices with their start and end apart: 10 -> 10, of which waited for: 5 -> 5; matrix products, arithmetic and copies ran while one was open for 0% -> 0% of each run, Pallas kernels for 20% -> 17%
where the time goes in v14:
time: 63.7 us; the launch traced here: 63.2 us
  starting transfers between devices  27.7 us (43%)
  Pallas kernels  27.5 us (43%)
  waiting for transfers between devices  6.5 us (10%)
  between operations  1.39 us (2%)
    pallas_call x7, Pallas kernels, call(): pl.pallas_call(kernel, out_shape=[shape_of(*out) for out in outs], in_spe...  27.5 us
    all_to_all x1, starting transfers between devices, local(): table1 = lax.all_to_all(out1, dom, split_axis=0, concat_axis=0, tiled=True)  8.25 us
    ppermute x6, starting transfers between devices, shifted(): lax.ppermute(value, name, [((at + step * shift) % size, at) for at in ran...  7.78 us
    all_to_all x1, starting transfers between devices, local(): lax.all_to_all(last, ('chip', 'grp'), split_axis=0, concat_axis=0, tiled=...  6.45 us
    all_to_all x1, starting transfers between devices, local(): table0 = lax.all_to_all(out0, dom, split_axis=0, concat_axis=0, tiled=True)  5.18 us
    ppermute x6, waiting for transfers between devices, shifted(): lax.ppermute(value, name, [((at + step * shift) % size, at) for at in ran...  4.4 us
    ppermute x1, waiting for transfers between devices, local(): got = lax.ppermute(other, 'core', [(0, 1), (1, 0)])  1.9 us
  transfers between devices with their start and end apart: 10, of which 5 were waited for; matrix products, arithmetic and copies ran while one was open for 0% of the time, Pallas kernels for 17%

profile of v14, /device:TPU:0, one launch (start us, length us, event | category | flops | bytes accessed | tf_op | source)
XLA Modules:
  0.0 63.2 jit_solution(4262709572279809156)
XLA Ops:
  0.6 0.0 copy-start
  0.6 0.0 copy-start.1
  0.7 2.2 %shard_map.165 = (bf16[1024,256]{1,0:T(8,128)(2,1)S(1)}, bf16[8,64,256]{2,1,0:T(8,128)(2,1)}, bf16[32,256]{1,0:T(8,128)(2,1)S(1)}, s32[64,256]{1,0:T(8,128)S(1)}, s32[64,256]{1,0:T(8,128)S(1)}) custom-call(bf16[1,1,1024,256]{3,2,1,0:T(8,128)(2,1)} %feats_hbm.1, s32[1,1,8,32]{3,2,1,0:T(8,128)} %rows_hbm.1, s32[1,1,64,256]{3,2,1,0:T(8,128)} %src_hbm.1, ...), custom_call_target="tpu_custom_call" | custom-call | tf_op jit(solution)/shard_map/pallas_call | solution.py:681
  2.9 5.2 %all-to-all-start = ((bf16[8,64,256]{2,1,0:T(8,128)(2,1)}), bf16[8,64,256]{2,1,0:T(8,128)(2,1)S(1)}, u32[]{:S(2)}, u32[]{:S(2)}) async-start(bf16[8,64,256]{2,1,0:T(8,128)(2,1)} %get-tuple-element.43), calls=%async_computation | async-start | bytes 524288 | tf_op jit(solution)/shard_map/all_to_all | solution.py:752
  8.7 6.2 %shard_map.166 = (bf16[1024,1024]{1,0:T(8,128)(2,1)}, bf16[1024,256]{1,0:T(8,128)(2,1)S(1)}, bf16[32,1024]{1,0:T(8,128)(2,1)S(1)}, bf16[32,256]{1,0:T(8,128)(2,1...) custom-call(s32[1,1,64]{2,1,0:T(1,128)} %blocks_hbm.1, ...), custom_call_target="tpu_custom_call" | custom-call | tf_op jit(solution)/shard_map/pallas_call | solution.py:681
  14.9 0.1 pad_add_fusion.place_ref
  15.0 0.0 all-to-all-done.table_ref
  15.0 0.0 copy-done
  15.0 0.0 copy-done.1
  15.0 2.7 %shard_map.167 = (bf16[1024,256]{1,0:T(8,128)(2,1)S(1)}, bf16[8,64,256]{2,1,0:T(8,128)(2,1)}, bf16[80,256]{1,0:T(8,128)(2,1)S(1)}, bf16[4,32,256]{2,1,0:T(8,128)(2,1)S(1)}) custom-call(s32[1]{0:T(128)} %get-tuple-element.36.flag_ref, s32[2]{0:T(128)S(1)} %pad_add_fusion.place_ref, f32[1024,256]{1,0:T(8,128)S(1)} %get-tuple-element.42.part_ref, ...), custom_call_target="tpu_custom_call" | custom-call | tf_op jit(solution)/shard_map/pallas_call | solution.py:681
  17.7 8.3 %all-to-all-start.1 = ((bf16[8,64,256]{2,1,0:T(8,128)(2,1)}), bf16[8,64,256]{2,1,0:T(8,128)(2,1)S(1)}, u32[]{:S(2)}, u32[]{:S(2)}) async-start(bf16[8,64,256]{2,1,0:T(8,128)(2,1)} %get-tuple-element.46), calls=%async_computation.1 | async-start | bytes 524288 | tf_op jit(solution)/shard_map/all_to_all | solution.py:809
  26.0 0.0 collective-permute-start.2
  26.0 0.8 %collective-permute-start.1 = (bf16[80,256]{1,0:T(8,128)(2,1)S(1)}, bf16[80,256]{1,0:T(8,128)(2,1)S(1)}, u32[]{:S(2)}, u32[]{:S(2)}) collective-permute-start(bf16[80,256]{1,0:T(8,128)(2,1)S(1)} %get-tuple-element.48.refs_1_), channel_id=1, source_target_pairs={{2,0},{3,1},{0,2},{1,3},{6,4},{7,5},{4,6},{5,7},{10,8},{11,9},{8,1... | collective-permute-start | bytes 122888 | tf_op jit(solution)/shard_map/ppermute | solution.py:814
  26.8 3.0 %collective-permute-start = (bf16[80,256]{1,0:T(8,128)(2,1)S(1)}, bf16[80,256]{1,0:T(8,128)(2,1)S(1)}, u32[]{:S(2)}, u32[]{:S(2)}) collective-permute-start(bf16[80,256]{1,0:T(8,128)(2,1)S(1)} %get-tuple-element.48.refs_1_), channel_id=1, source_target_pairs={{1,0},{2,1},{3,2},{0,3},{5,4},{6,5},{7,6},{4,7},{9,8},{10,9},{11,1... | collective-permute-start | bytes 122888 | tf_op jit(solution)/shard_map/ppermute | solution.py:814
  29.8 2.3 %collective-permute-done.2.refs_4_ = bf16[80,256]{1,0:T(8,128)(2,1)S(1)} collective-permute-done((bf16[80,256]{1,0:T(8,128)(2,1)S(1)}, bf16[80,256]{1,0:T(8,128)(2,1)S(1)}, u32[]{:S(2)}, u32[]{:S(2)}) %collective-permute-start.2) | collective-permute-done | bytes 40992 | tf_op jit(solution)/shard_map/ppermute | solution.py:814
  32.1 0.0 collective-permute-done.1.refs_3_
  32.1 0.6 collective-permute-done.refs_2_
  32.7 0.2 all-to-all-done.1.table_ref
  32.9 2.4 %shard_map.168 = (bf16[16,32,256]{2,1,0:T(8,128)(2,1)}, bf16[208,256]{1,0:T(8,128)(2,1)}, bf16[4,64,256]{2,1,0:T(8,128)(2,1)}) custom-call(s32[1]{0:T(128)} %get-tuple-element.36.flag_ref, s32[2]{0:T(128)S(1)} %pad_add_fusion.place_ref, bf16[32,1024]{1,0:T(8,128)(2,1)S(1)} %get-tuple-element.37.own_ref, bf16[1024,256]{1,0:T(8,128)(2,1)S(1)} %get-tuple-element.38.ghost_ref, ...), custom_call_target="tpu_custom_call" | custom-call | tf_op jit(solution)/shard_map/pallas_call | solution.py:681
  35.2 6.4 %all-to-all-start.2 = ((bf16[16,32,256]{2,1,0:T(8,128)(2,1)}), bf16[16,32,256]{2,1,0:T(8,128)(2,1)S(1)}, u32[]{:S(2)}, u32[]{:S(2)}) async-start(bf16[16,32,256]{2,1,0:T(8,128)(2,1)} %get-tuple-element.53), calls=%async_computation.2 | async-start | bytes 524288 | tf_op jit(solution)/shard_map/all_to_all | solution.py:853
  41.7 2.8 %collective-permute-start.5 = (bf16[208,256]{1,0:T(8,128)(2,1)}, bf16[208,256]{1,0:T(8,128)(2,1)S(1)}, u32[]{:S(2)}, u32[]{:S(2)}) collective-permute-start(bf16[208,256]{1,0:T(8,128)(2,1)} %get-tuple-element.49.token_ref.refs_0_), channel_id=1, source_target_pairs={{8,0},{16,8},{24,16},{0,24},{9,1},{17,9},{25,17},{1,25},{10,2},{18... | collective-permute-start | bytes 319496 | tf_op jit(solution)/shard_map/ppermute | solution.py:814
  44.5 0.6 collective-permute-start.4
  45.1 0.6 collective-permute-start.3
  45.7 4.6 %shard_map.169 = (bf16[2,1,1,1024,256]{4,3,2,1,0:T(8,128)(2,1)}, bf16[768,1024]{1,0:T(8,128)(2,1)S(1)}) custom-call(s32[1]{0:T(128)} %get-tuple-element.36.flag_ref, bf16[208,256]{1,0:T(8,128)(2,1)} %get-tuple-element.49.token_ref.refs_0_, bf16[1024,1024]{1,0:T(8,128)(2,1)} %get-tuple-element.50.own_hbm, bf16[1024,1024]{1,0:T(8,128)(2,1)} %get-tuple-element.39.own_rest_hbm, ...), custom_call_target="tpu_custom_call" | custom-call | tf_op jit(solution)/shard_map/pallas_call | solution.py:681
  50.2 0.0 collective-permute-done.5.refs_3_
  50.2 1.5 %collective-permute-done.4.refs_2_ = bf16[208,256]{1,0:T(8,128)(2,1)S(1)} collective-permute-done((bf16[208,256]{1,0:T(8,128)(2,1)}, bf16[208,256]{1,0:T(8,128)(2,1)S(1)}, u32[]{:S(2)}, u32[]{:S(2)}) %collective-permute-start.4) | collective-permute-done | bytes 106528 | tf_op jit(solution)/shard_map/ppermute | solution.py:814
  51.7 0.0 collective-permute-done.3.refs_1_
  51.7 0.0 all-to-all-done.2.refs_5_
  51.7 8.4 %shard_map.170 = (f32[96,1024]{1,0:T(8,128)S(1)}, f32[128,1024]{1,0:T(8,128)S(1)}, f32[172,128]{1,0:T(8,128)S(1)}, bf16[256,1024]{1,0:T(8,128)(2,1)S(1)}) custom-call(s32[2]{0:T(128)S(1)} %pad_add_fusion.place_ref, bf16[208,256]{1,0:T(8,128)(2,1)} %get-tuple-element.49.token_ref.refs_0_, bf16[208,256]{1,0:T(8,128)(2,1)S(1)} %collective-permute-done.3.refs_1_, ...), custom_call_target="tpu_custom_call" | custom-call | tf_op jit(solution)/shard_map/pallas_call | solution.py:681
  60.2 0.1 collective-permute-start.6
  60.3 1.9 %collective-permute-done.6.got_ref = bf16[256,1024]{1,0:T(8,128)(2,1)S(1)} collective-permute-done((bf16[256,1024]{1,0:T(8,128)(2,1)S(1)}, bf16[256,1024]{1,0:T(8,128)(2,1)S(1)}, u32[]{:S(2)}, u32[]{:S(2)}) %collective-permute-start.6) | collective-permute-done | bytes 524320 | tf_op jit(solution)/shard_map/ppermute | solution.py:944
  62.2 1.0 %shard_map.171 = (f32[96,1024]{1,0:T(8,128)}, f32[128,1024]{1,0:T(8,128)}, f32[172,128]{1,0:T(8,128)}) custom-call(bf16[256,1024]{1,0:T(8,128)(2,1)S(1)} %collective-permute-done.6.got_ref, f32[96,1024]{1,0:T(8,128)S(1)} %get-tuple-element.56.one_ref, f32[128,1024]{1,0:T(8,128)S(1)} %get-tuple-element.57.two_ref, f32[172,128]{1,0:T(8,128)S(1)} %get-tuple-element.58.three_ref), custom_call_target="tpu_custom_call" | custom-call | tf_op jit(solution)/shard_map/pallas_call | solution.py:681
Async XLA Ops:
  0.6 14.4 %copy-start = (s32[1,1,8,32]{3,2,1,0:T(8,128)S(1)}, s32[1,1,8,32]{3,2,1,0:T(8,128)}, u32[]{:S(2)}) copy-start(s32[1,1,8,32]{3,2,1,0:T(8,128)} %rows_hbm.1) | copy-start | bytes 3076
  0.6 14.4 %copy-start.1 = (s32[1,1,32]{2,1,0:T(1,128)S(1)}, s32[1,1,32]{2,1,0:T(1,128)}, u32[]{:S(2)}) copy-start(s32[1,1,32]{2,1,0:T(1,128)} %param.21) | copy-start | bytes 388
  2.9 12.1 %all-to-all-start = ((bf16[8,64,256]{2,1,0:T(8,128)(2,1)}), bf16[8,64,256]{2,1,0:T(8,128)(2,1)S(1)}, u32[]{:S(2)}, u32[]{:S(2)}) async-start(bf16[8,64,256]{2,1,0:T(8,128)(2,1)} %get-tuple-element.43), calls=%async_computation | async-start | bytes 524288 | tf_op jit(solution)/shard_map/all_to_all | solution.py:752
  17.7 15.2 %all-to-all-start.1 = ((bf16[8,64,256]{2,1,0:T(8,128)(2,1)}), bf16[8,64,256]{2,1,0:T(8,128)(2,1)S(1)}, u32[]{:S(2)}, u32[]{:S(2)}) async-start(bf16[8,64,256]{2,1,0:T(8,128)(2,1)} %get-tuple-element.46), calls=%async_computation.1 | async-start | bytes 524288 | tf_op jit(solution)/shard_map/all_to_all | solution.py:809
  26.0 6.1 %collective-permute-start.2 = (bf16[80,256]{1,0:T(8,128)(2,1)S(1)}, bf16[80,256]{1,0:T(8,128)(2,1)S(1)}, u32[]{:S(2)}, u32[]{:S(2)}) collective-permute-start(bf16[80,256]{1,0:T(8,128)(2,1)S(1)} %get-tuple-element.48.refs_1_), channel_id=1, source_target_pairs={{3,0},{0,1},{1,2},{2,3},{7,4},{4,5},{5,6},{6,7},{11,8},{8,9},{9,10... | collective-permute-start | bytes 122888 | tf_op jit(solution)/shard_map/ppermute | solution.py:814
  26.0 6.1 %collective-permute-start.1 = (bf16[80,256]{1,0:T(8,128)(2,1)S(1)}, bf16[80,256]{1,0:T(8,128)(2,1)S(1)}, u32[]{:S(2)}, u32[]{:S(2)}) collective-permute-start(bf16[80,256]{1,0:T(8,128)(2,1)S(1)} %get-tuple-element.48.refs_1_), channel_id=1, source_target_pairs={{2,0},{3,1},{0,2},{1,3},{6,4},{7,5},{4,6},{5,7},{10,8},{11,9},{8,1... | collective-permute-start | bytes 122888 | tf_op jit(solution)/shard_map/ppermute | solution.py:814
  26.8 5.9 %collective-permute-start = (bf16[80,256]{1,0:T(8,128)(2,1)S(1)}, bf16[80,256]{1,0:T(8,128)(2,1)S(1)}, u32[]{:S(2)}, u32[]{:S(2)}) collective-permute-start(bf16[80,256]{1,0:T(8,128)(2,1)S(1)} %get-tuple-element.48.refs_1_), channel_id=1, source_target_pairs={{1,0},{2,1},{3,2},{0,3},{5,4},{6,5},{7,6},{4,7},{9,8},{10,9},{11,1... | collective-permute-start | bytes 122888 | tf_op jit(solution)/shard_map/ppermute | solution.py:814
  35.2 16.5 %all-to-all-start.2 = ((bf16[16,32,256]{2,1,0:T(8,128)(2,1)}), bf16[16,32,256]{2,1,0:T(8,128)(2,1)S(1)}, u32[]{:S(2)}, u32[]{:S(2)}) async-start(bf16[16,32,256]{2,1,0:T(8,128)(2,1)} %get-tuple-element.53), calls=%async_computation.2 | async-start | bytes 524288 | tf_op jit(solution)/shard_map/all_to_all | solution.py:853
  41.7 8.5 %collective-permute-start.5 = (bf16[208,256]{1,0:T(8,128)(2,1)}, bf16[208,256]{1,0:T(8,128)(2,1)S(1)}, u32[]{:S(2)}, u32[]{:S(2)}) collective-permute-start(bf16[208,256]{1,0:T(8,128)(2,1)} %get-tuple-element.49.token_ref.refs_0_), channel_id=1, source_target_pairs={{8,0},{16,8},{24,16},{0,24},{9,1},{17,9},{25,17},{1,25},{10,2},{18... | collective-permute-start | bytes 319496 | tf_op jit(solution)/shard_map/ppermute | solution.py:814
  44.5 7.2 %collective-permute-start.4 = (bf16[208,256]{1,0:T(8,128)(2,1)}, bf16[208,256]{1,0:T(8,128)(2,1)S(1)}, u32[]{:S(2)}, u32[]{:S(2)}) collective-permute-start(bf16[208,256]{1,0:T(8,128)(2,1)} %get-tuple-element.49.token_ref.refs_0_), channel_id=1, source_target_pairs={{16,0},{24,8},{0,16},{8,24},{17,1},{25,9},{1,17},{9,25},{18,2},{26... | collective-permute-start | bytes 319496 | tf_op jit(solution)/shard_map/ppermute | solution.py:814
  45.1 6.6 %collective-permute-start.3 = (bf16[208,256]{1,0:T(8,128)(2,1)}, bf16[208,256]{1,0:T(8,128)(2,1)S(1)}, u32[]{:S(2)}, u32[]{:S(2)}) collective-permute-start(bf16[208,256]{1,0:T(8,128)(2,1)} %get-tuple-element.49.token_ref.refs_0_), channel_id=1, source_target_pairs={{24,0},{0,8},{8,16},{16,24},{25,1},{1,9},{9,17},{17,25},{26,2},{2,... | collective-permute-start | bytes 319496 | tf_op jit(solution)/shard_map/ppermute | solution.py:814
  60.2 2.0 %collective-permute-start.6 = (bf16[256,1024]{1,0:T(8,128)(2,1)S(1)}, bf16[256,1024]{1,0:T(8,128)(2,1)S(1)}, u32[]{:S(2)}, u32[]{:S(2)}) collective-permute-start(bf16[256,1024]{1,0:T(8,128)(2,1)S(1)} %get-tuple-element.55), channel_id=1, source_target_pairs={{0,4},{4,0},{1,5},{5,1},{2,6},{6,2},{3,7},{7,3},{8,12},{12,8},{9,1... | collective-permute-start | bytes 1572872 | tf_op jit(solution)/shard_map/ppermute | solution.py:944

commit v15 on v14

--- a/solution.py
+++ b/solution.py
@@ -236,7 +236,8 @@
     own_train_ref[...] = own_ref[:train, :]
     for copy in copies[1:]:
         copy.wait()
-    part_ref[...] = dot(own_ref[...], start_ref[...]) + noise_ref[...].astype(f32)
+    for cut in blocks_of(nodes, 256):
+        part_ref[cut, :] = dot(own_ref[cut, :], start_ref[...]) + noise_ref[cut, :].astype(f32)
 
     @pl.when(big)
     def _():
@@ -295,7 +296,7 @@
     turn_ref,
     pick_ref,
     staged_ref,
-    sem,
+    sems,
 ):
     width = start_ref.shape[1]
     parts, each = rows_ref.shape
@@ -304,18 +305,21 @@
     aggregate(flag_ref, part_ref, ((ghost_ref, rest_hbm, table),), sums_ref, rest_ref)
     for cut in blocks_of(start_ref.shape[0], 32):
         start_ref[cut, :] = normalize(sums_ref[cut, :])
+    train = labels_ref.shape[1]
+    copies = fetch(
+        [(start_ref.at[:train], out_hbm.at[part, each:]) for part in range(parts)], sems
+    )
     sent = dot(pick_ref[...], start_ref[...]).astype(bf16)
-    train = labels_ref.shape[1]
-    for part in range(parts):
-        staged_ref[part, :each] = sent[part * each : (part + 1) * each]
-        staged_ref[part, each:] = start_ref[:train, :]
-    out_copy = pltpu.make_async_copy(staged_ref, out_hbm, sem)
+    staged_ref[...] = sent.reshape(staged_ref.shape)
+    out_copy = pltpu.make_async_copy(staged_ref, out_hbm.at[:, :each], sems.at[parts])
     out_copy.start()
     near_rows(place_ref, table_ref, each, near_ref, 0)
     side_ref[:train, :] = old_ref[...]
     side_ref[train : 2 * train, :] = start_ref[:train, :]
     turn_ref[:1, :train] = labels_ref[...]
     side_ref[2 * train :, :128] = turn_ref[:16, :].astype(f32).astype(bf16)
+    for copy in copies:
+        copy.wait()
     out_copy.wait()
 
 
@@ -384,31 +388,42 @@
     out_ref,
     sems,
 ):
-    copies = fetch(
-        (
-            (own_hbm, own_ref),
-            (noise_hbm.at[1, 0, 0], noise_ref),
-            (weight_hbm, weight_ref),
-        ),
-        sems,
-    )
+    cuts = blocks_of(sums_ref.shape[0], 256)
+    pairs = []
+    for cut in cuts:
+        pairs.append((own_hbm.at[cut], own_ref.at[cut]))
+        pairs.append((noise_hbm.at[1, 0, 0, cut], noise_ref.at[cut]))
+    pairs.append((weight_hbm, weight_ref))
+    pairs.append((start_ref, out_hbm.at[0, 0, 0]))
+    copies = fetch(pairs, sems)
     width = out_ref.shape[-1]
     ghosts = ghost_ref.shape[1]
     table = table_ref[:, : ghosts // table_ref.shape[0], :].reshape(ghosts, width)
-    out_ref[0, 0, 0] = start_ref[...]
-    copies[0].wait()
-    copies[1].wait()
-    parts = (
-        (own_ref, own_rest_hbm, start_ref[...]),
-        (ghost_ref, ghost_rest_hbm, table),
-    )
-    aggregate(flag_ref, noise_ref, parts, sums_ref, rest_ref)
-    for cut in blocks_of(sums_ref.shape[0], 32):
-        out_ref[1, 0, 0, cut, :] = normalize(sums_ref[cut, :])
-    out_copy = pltpu.make_async_copy(out_ref, out_hbm, sems.at[3])
-    out_copy.start()
-    copies[2].wait()
-    out_copy.wait()
+    tables = ((own_ref, own_rest_hbm, start_ref[...]), (ghost_ref, ghost_rest_hbm, table))
+    outs = []
+    for at, cut in enumerate(cuts):
+        copies[2 * at].wait()
+        copies[2 * at + 1].wait()
+        rows = cut.stop - cut.start
+        sums = sums_ref.at[cut]
+        aggregate(
+            flag_ref,
+            noise_ref.at[cut],
+            [(ref.at[cut], rest.at[cut], table) for ref, rest, table in tables],
+            sums,
+            rest_ref.at[:rows],
+        )
+        for inner in blocks_of(rows, 32):
+            row = slice(cut.start + inner.start, cut.start + inner.stop)
+            out_ref[row, :] = normalize(sums_ref[row, :])
+        outs.append(
+            pltpu.make_async_copy(
+                out_ref.at[cut], out_hbm.at[1, 0, 0, cut], sems.at[len(pairs) + at]
+            )
+        )
+        outs[-1].start()
+    for copy in copies[-2:] + outs:
+        copy.wait()
 
 
 def shares(ref, first, share):
@@ -804,7 +819,14 @@
             (own0, None),
             (labels.reshape(1, train), VMEM),
         ],
-        [VMEM((nodes, width), f32), VMEM((nodes, ghosts), bf16), turn, pick, staged, DMA(())],
+        [
+            VMEM((nodes, width), f32),
+            VMEM((nodes, ghosts), bf16),
+            turn,
+            pick,
+            VMEM((parts, each, width), bf16),
+            DMA((parts + 1,)),
+        ],
     )
     table1 = lax.all_to_all(out1, dom, split_axis=0, concat_axis=0, tiled=True)
     grp = lax.axis_size("grp")
@@ -882,8 +904,8 @@
             VMEM((nodes, width), bf16),
             VMEM((nodes, width), f32),
             VMEM((nodes, max(nodes, ghosts)), bf16),
-            VMEM((2, 1, 1, nodes, width), bf16),
-            DMA((4,)),
+            VMEM((nodes, width), bf16),
+            DMA((3 * -(-nodes // 256) + 2,)),
         ],
     )
     chunk = train * (copies if few else min(members, 32))

time: 63.7 us -> 64.3 us (level)
  Pallas kernels: 27.5 us -> 26.1 us
  waiting for transfers between devices: 6.5 us -> 7.77 us
  starting transfers between devices: 27.7 us -> 28.5 us
    ppermute x6, starting transfers between devices: 7.78 us -> 12.3 us  [shifted(): lax.ppermute(value, name, [((at + step * shift) % size, at) for at in ran...]
    all_to_all x1, starting transfers between devices: 8.25 us -> 4.68 us  [local(): table1 = lax.all_to_all(out1, dom, split_axis=0, concat_axis=0, tiled=True)]
    all_to_all x1, waiting for transfers between devices: 0.01 us -> 1.62 us  [local(): table0 = lax.all_to_all(out0, dom, split_axis=0, concat_axis=0, tiled=True)]
    pallas_call x7, Pallas kernels: 27.5 us -> 26.1 us  [call(): pl.pallas_call(kernel, out_shape=[shape_of(*out) for out in outs], in_spe...]
  transfers between devices with their start and end apart: 10 -> 10, of which waited for: 5 -> 6; matrix products, arithmetic and copies ran while one was open for 0% -> 0% of each run, Pallas kernels for 17% -> 15%
where the time goes in v15:
time: 64.3 us; the launch traced here: 63.8 us
  starting transfers between devices  28.5 us (44%)
  Pallas kernels  26.1 us (41%)
  waiting for transfers between devices  7.77 us (12%)
  between operations  1.39 us (2%)
    pallas_call x7, Pallas kernels, call(): pl.pallas_call(kernel, out_shape=[shape_of(*out) for out in outs], in_spe...  26.1 us
    ppermute x6, starting transfers between devices, shifted(): lax.ppermute(value, name, [((at + step * shift) % size, at) for at in ran...  12.3 us
    all_to_all x1, starting transfers between devices, local(): lax.all_to_all(last, ('chip', 'grp'), split_axis=0, concat_axis=0, tiled=...  6.29 us
    all_to_all x1, starting transfers between devices, local(): table0 = lax.all_to_all(out0, dom, split_axis=0, concat_axis=0, tiled=True)  5.18 us
    all_to_all x1, starting transfers between devices, local(): table1 = lax.all_to_all(out1, dom, split_axis=0, concat_axis=0, tiled=True)  4.68 us
    ppermute x6, waiting for transfers between devices, shifted(): lax.ppermute(value, name, [((at + step * shift) % size, at) for at in ran...  4.25 us
    ppermute x1, waiting for transfers between devices, local(): got = lax.ppermute(other, 'core', [(0, 1), (1, 0)])  1.9 us
    all_to_all x1, waiting for transfers between devices, local(): table0 = lax.all_to_all(out0, dom, split_axis=0, concat_axis=0, tiled=True)  1.62 us
  transfers between devices with their start and end apart: 10, of which 6 were waited for; matrix products, arithmetic and copies ran while one was open for 0% of the time, Pallas kernels for 15%

profile of v15, /device:TPU:0, one launch (start us, length us, event | category | flops | bytes accessed | tf_op | source)
XLA Modules:
  0.0 63.8 jit_solution(1474867283591510565)
XLA Ops:
  0.6 0.0 copy-start
  0.6 0.0 copy-start.1
  0.7 2.2 %shard_map.165 = (bf16[1024,256]{1,0:T(8,128)(2,1)S(1)}, bf16[8,64,256]{2,1,0:T(8,128)(2,1)}, bf16[32,256]{1,0:T(8,128)(2,1)S(1)}, s32[64,256]{1,0:T(8,128)S(1)}, s32[64,256]{1,0:T(8,128)S(1)}) custom-call(bf16[1,1,1024,256]{3,2,1,0:T(8,128)(2,1)} %feats_hbm.1, s32[1,1,8,32]{3,2,1,0:T(8,128)} %rows_hbm.1, s32[1,1,64,256]{3,2,1,0:T(8,128)} %src_hbm.1, ...), custom_call_target="tpu_custom_call" | custom-call | tf_op jit(solution)/shard_map/pallas_call | solution.py:696
  2.9 5.2 %all-to-all-start = ((bf16[8,64,256]{2,1,0:T(8,128)(2,1)}), bf16[8,64,256]{2,1,0:T(8,128)(2,1)S(1)}, u32[]{:S(2)}, u32[]{:S(2)}) async-start(bf16[8,64,256]{2,1,0:T(8,128)(2,1)} %get-tuple-element.43), calls=%async_computation | async-start | bytes 524288 | tf_op jit(solution)/shard_map/all_to_all | solution.py:767
  8.7 4.6 %shard_map.166 = (bf16[1024,1024]{1,0:T(8,128)(2,1)}, bf16[1024,256]{1,0:T(8,128)(2,1)S(1)}, bf16[32,1024]{1,0:T(8,128)(2,1)S(1)}, bf16[32,256]{1,0:T(8,128)(2,1...) custom-call(s32[1,1,64]{2,1,0:T(1,128)} %blocks_hbm.1, ...), custom_call_target="tpu_custom_call" | custom-call | tf_op jit(solution)/shard_map/pallas_call | solution.py:696
  13.3 0.1 pad_add_fusion.place_ref
  13.4 1.6 %all-to-all-done.table_ref = bf16[8,64,256]{2,1,0:T(8,128)(2,1)S(1)} async-done(((bf16[8,64,256]{2,1,0:T(8,128)(2,1)}), bf16[8,64,256]{2,1,0:T(8,128)(2,1)S(1)}, u32[]{:S(2)}, u32[]{:S(2)}) %all-to-all-start) | async-done | bytes 262176 | tf_op jit(solution)/shard_map/all_to_all | solution.py:767
  15.0 0.0 copy-done
  15.0 0.0 copy-done.1
  15.0 2.7 %shard_map.167 = (bf16[1024,256]{1,0:T(8,128)(2,1)S(1)}, bf16[8,64,256]{2,1,0:T(8,128)(2,1)}, bf16[80,256]{1,0:T(8,128)(2,1)S(1)}, bf16[4,32,256]{2,1,0:T(8,128)(2,1)S(1)}) custom-call(s32[1]{0:T(128)} %get-tuple-element.36.flag_ref, s32[2]{0:T(128)S(1)} %pad_add_fusion.place_ref, f32[1024,256]{1,0:T(8,128)S(1)} %get-tuple-element.42.part_ref, ...), custom_call_target="tpu_custom_call" | custom-call | tf_op jit(solution)/shard_map/pallas_call | solution.py:696
  17.7 4.7 %all-to-all-start.1 = ((bf16[8,64,256]{2,1,0:T(8,128)(2,1)}), bf16[8,64,256]{2,1,0:T(8,128)(2,1)S(1)}, u32[]{:S(2)}, u32[]{:S(2)}) async-start(bf16[8,64,256]{2,1,0:T(8,128)(2,1)} %get-tuple-element.46), calls=%async_computation.1 | async-start | bytes 524288 | tf_op jit(solution)/shard_map/all_to_all | solution.py:831
  22.4 2.6 %collective-permute-start.2 = (bf16[80,256]{1,0:T(8,128)(2,1)S(1)}, bf16[80,256]{1,0:T(8,128)(2,1)S(1)}, u32[]{:S(2)}, u32[]{:S(2)}) collective-permute-start(bf16[80,256]{1,0:T(8,128)(2,1)S(1)} %get-tuple-element.48.refs_1_), channel_id=1, source_target_pairs={{3,0},{0,1},{1,2},{2,3},{7,4},{4,5},{5,6},{6,7},{11,8},{8,9},{9,10... | collective-permute-start | bytes 122888 | tf_op jit(solution)/shard_map/ppermute | solution.py:836
  25.0 4.9 %collective-permute-start.1 = (bf16[80,256]{1,0:T(8,128)(2,1)S(1)}, bf16[80,256]{1,0:T(8,128)(2,1)S(1)}, u32[]{:S(2)}, u32[]{:S(2)}) collective-permute-start(bf16[80,256]{1,0:T(8,128)(2,1)S(1)} %get-tuple-element.48.refs_1_), channel_id=1, source_target_pairs={{2,0},{3,1},{0,2},{1,3},{6,4},{7,5},{4,6},{5,7},{10,8},{11,9},{8,1... | collective-permute-start | bytes 122888 | tf_op jit(solution)/shard_map/ppermute | solution.py:836
  29.9 0.9 %collective-permute-start = (bf16[80,256]{1,0:T(8,128)(2,1)S(1)}, bf16[80,256]{1,0:T(8,128)(2,1)S(1)}, u32[]{:S(2)}, u32[]{:S(2)}) collective-permute-start(bf16[80,256]{1,0:T(8,128)(2,1)S(1)} %get-tuple-element.48.refs_1_), channel_id=1, source_target_pairs={{1,0},{2,1},{3,2},{0,3},{5,4},{6,5},{7,6},{4,7},{9,8},{10,9},{11,1... | collective-permute-start | bytes 122888 | tf_op jit(solution)/shard_map/ppermute | solution.py:836
  30.8 1.1 %collective-permute-done.2.refs_4_ = bf16[80,256]{1,0:T(8,128)(2,1)S(1)} collective-permute-done((bf16[80,256]{1,0:T(8,128)(2,1)S(1)}, bf16[80,256]{1,0:T(8,128)(2,1)S(1)}, u32[]{:S(2)}, u32[]{:S(2)}) %collective-permute-start.2) | collective-permute-done | bytes 40992 | tf_op jit(solution)/shard_map/ppermute | solution.py:836
  31.8 1.6 %collective-permute-done.1.refs_3_ = bf16[80,256]{1,0:T(8,128)(2,1)S(1)} collective-permute-done((bf16[80,256]{1,0:T(8,128)(2,1)S(1)}, bf16[80,256]{1,0:T(8,128)(2,1)S(1)}, u32[]{:S(2)}, u32[]{:S(2)}) %collective-permute-start.1) | collective-permute-done | bytes 40992 | tf_op jit(solution)/shard_map/ppermute | solution.py:836
  33.4 0.5 collective-permute-done.refs_2_
  33.9 0.0 all-to-all-done.1.table_ref
  33.9 2.4 %shard_map.168 = (bf16[16,32,256]{2,1,0:T(8,128)(2,1)}, bf16[208,256]{1,0:T(8,128)(2,1)}, bf16[4,64,256]{2,1,0:T(8,128)(2,1)}) custom-call(s32[1]{0:T(128)} %get-tuple-element.36.flag_ref, s32[2]{0:T(128)S(1)} %pad_add_fusion.place_ref, bf16[32,1024]{1,0:T(8,128)(2,1)S(1)} %get-tuple-element.37.own_ref, bf16[1024,256]{1,0:T(8,128)(2,1)S(1)} %get-tuple-element.38.ghost_ref, ...), custom_call_target="tpu_custom_call" | custom-call | tf_op jit(solution)/shard_map/pallas_call | solution.py:696
  36.3 6.3 %all-to-all-start.2 = ((bf16[16,32,256]{2,1,0:T(8,128)(2,1)}), bf16[16,32,256]{2,1,0:T(8,128)(2,1)S(1)}, u32[]{:S(2)}, u32[]{:S(2)}) async-start(bf16[16,32,256]{2,1,0:T(8,128)(2,1)} %get-tuple-element.53), calls=%async_computation.2 | async-start | bytes 524288 | tf_op jit(solution)/shard_map/all_to_all | solution.py:875
  42.6 2.8 %collective-permute-start.5 = (bf16[208,256]{1,0:T(8,128)(2,1)}, bf16[208,256]{1,0:T(8,128)(2,1)S(1)}, u32[]{:S(2)}, u32[]{:S(2)}) collective-permute-start(bf16[208,256]{1,0:T(8,128)(2,1)} %get-tuple-element.49.token_ref.refs_0_), channel_id=1, source_target_pairs={{8,0},{16,8},{24,16},{0,24},{9,1},{17,9},{25,17},{1,25},{10,2},{18... | collective-permute-start | bytes 319496 | tf_op jit(solution)/shard_map/ppermute | solution.py:836
  45.4 0.6 collective-permute-start.4
  46.0 0.6 collective-permute-start.3
  46.5 4.7 %shard_map.169 = (bf16[2,1,1,1024,256]{4,3,2,1,0:T(8,128)(2,1)}, bf16[768,1024]{1,0:T(8,128)(2,1)S(1)}) custom-call(s32[1]{0:T(128)} %get-tuple-element.36.flag_ref, bf16[208,256]{1,0:T(8,128)(2,1)} %get-tuple-element.49.token_ref.refs_0_, bf16[1024,1024]{1,0:T(8,128)(2,1)} %get-tuple-element.50.own_hbm, bf16[1024,1024]{1,0:T(8,128)(2,1)} %get-tuple-element.39.own_rest_hbm, ...), custom_call_target="tpu_custom_call" | custom-call | tf_op jit(solution)/shard_map/pallas_call | solution.py:696
  51.3 0.0 collective-permute-done.5.refs_3_
  51.3 0.0 collective-permute-done.4.refs_2_
  51.3 1.1 %collective-permute-done.3.refs_1_ = bf16[208,256]{1,0:T(8,128)(2,1)S(1)} collective-permute-done((bf16[208,256]{1,0:T(8,128)(2,1)}, bf16[208,256]{1,0:T(8,128)(2,1)S(1)}, u32[]{:S(2)}, u32[]{:S(2)}) %collective-permute-start.3) | collective-permute-done | bytes 106528 | tf_op jit(solution)/shard_map/ppermute | solution.py:836
  52.4 0.0 all-to-all-done.2.refs_5_
  52.4 8.4 %shard_map.170 = (f32[96,1024]{1,0:T(8,128)S(1)}, f32[128,1024]{1,0:T(8,128)S(1)}, f32[172,128]{1,0:T(8,128)S(1)}, bf16[256,1024]{1,0:T(8,128)(2,1)S(1)}) custom-call(s32[2]{0:T(128)S(1)} %pad_add_fusion.place_ref, bf16[208,256]{1,0:T(8,128)(2,1)} %get-tuple-element.49.token_ref.refs_0_, bf16[208,256]{1,0:T(8,128)(2,1)S(1)} %collective-permute-done.3.refs_1_, ...), custom_call_target="tpu_custom_call" | custom-call | tf_op jit(solution)/shard_map/pallas_call | solution.py:696
  60.8 0.1 collective-permute-start.6
  60.9 1.9 %collective-permute-done.6.got_ref = bf16[256,1024]{1,0:T(8,128)(2,1)S(1)} collective-permute-done((bf16[256,1024]{1,0:T(8,128)(2,1)S(1)}, bf16[256,1024]{1,0:T(8,128)(2,1)S(1)}, u32[]{:S(2)}, u32[]{:S(2)}) %collective-permute-start.6) | collective-permute-done | bytes 524320 | tf_op jit(solution)/shard_map/ppermute | solution.py:966
  62.8 1.0 %shard_map.171 = (f32[96,1024]{1,0:T(8,128)}, f32[128,1024]{1,0:T(8,128)}, f32[172,128]{1,0:T(8,128)}) custom-call(bf16[256,1024]{1,0:T(8,128)(2,1)S(1)} %collective-permute-done.6.got_ref, f32[96,1024]{1,0:T(8,128)S(1)} %get-tuple-element.56.one_ref, f32[128,1024]{1,0:T(8,128)S(1)} %get-tuple-element.57.two_ref, f32[172,128]{1,0:T(8,128)S(1)} %get-tuple-element.58.three_ref), custom_call_target="tpu_custom_call" | custom-call | tf_op jit(solution)/shard_map/pallas_call | solution.py:696
Async XLA Ops:
  0.6 14.4 %copy-start = (s32[1,1,8,32]{3,2,1,0:T(8,128)S(1)}, s32[1,1,8,32]{3,2,1,0:T(8,128)}, u32[]{:S(2)}) copy-start(s32[1,1,8,32]{3,2,1,0:T(8,128)} %rows_hbm.1) | copy-start | bytes 3076
  0.6 14.4 %copy-start.1 = (s32[1,1,32]{2,1,0:T(1,128)S(1)}, s32[1,1,32]{2,1,0:T(1,128)}, u32[]{:S(2)}) copy-start(s32[1,1,32]{2,1,0:T(1,128)} %param.21) | copy-start | bytes 388
  2.9 12.1 %all-to-all-start = ((bf16[8,64,256]{2,1,0:T(8,128)(2,1)}), bf16[8,64,256]{2,1,0:T(8,128)(2,1)S(1)}, u32[]{:S(2)}, u32[]{:S(2)}) async-start(bf16[8,64,256]{2,1,0:T(8,128)(2,1)} %get-tuple-element.43), calls=%async_computation | async-start | bytes 524288 | tf_op jit(solution)/shard_map/all_to_all | solution.py:767
  17.7 16.2 %all-to-all-start.1 = ((bf16[8,64,256]{2,1,0:T(8,128)(2,1)}), bf16[8,64,256]{2,1,0:T(8,128)(2,1)S(1)}, u32[]{:S(2)}, u32[]{:S(2)}) async-start(bf16[8,64,256]{2,1,0:T(8,128)(2,1)} %get-tuple-element.46), calls=%async_computation.1 | async-start | bytes 524288 | tf_op jit(solution)/shard_map/all_to_all | solution.py:831
  22.4 9.4 %collective-permute-start.2 = (bf16[80,256]{1,0:T(8,128)(2,1)S(1)}, bf16[80,256]{1,0:T(8,128)(2,1)S(1)}, u32[]{:S(2)}, u32[]{:S(2)}) collective-permute-start(bf16[80,256]{1,0:T(8,128)(2,1)S(1)} %get-tuple-element.48.refs_1_), channel_id=1, source_target_pairs={{3,0},{0,1},{1,2},{2,3},{7,4},{4,5},{5,6},{6,7},{11,8},{8,9},{9,10... | collective-permute-start | bytes 122888 | tf_op jit(solution)/shard_map/ppermute | solution.py:836
  25.0 8.4 %collective-permute-start.1 = (bf16[80,256]{1,0:T(8,128)(2,1)S(1)}, bf16[80,256]{1,0:T(8,128)(2,1)S(1)}, u32[]{:S(2)}, u32[]{:S(2)}) collective-permute-start(bf16[80,256]{1,0:T(8,128)(2,1)S(1)} %get-tuple-element.48.refs_1_), channel_id=1, source_target_pairs={{2,0},{3,1},{0,2},{1,3},{6,4},{7,5},{4,6},{5,7},{10,8},{11,9},{8,1... | collective-permute-start | bytes 122888 | tf_op jit(solution)/shard_map/ppermute | solution.py:836
  29.9 4.0 %collective-permute-start = (bf16[80,256]{1,0:T(8,128)(2,1)S(1)}, bf16[80,256]{1,0:T(8,128)(2,1)S(1)}, u32[]{:S(2)}, u32[]{:S(2)}) collective-permute-start(bf16[80,256]{1,0:T(8,128)(2,1)S(1)} %get-tuple-element.48.refs_1_), channel_id=1, source_target_pairs={{1,0},{2,1},{3,2},{0,3},{5,4},{6,5},{7,6},{4,7},{9,8},{10,9},{11,1... | collective-permute-start | bytes 122888 | tf_op jit(solution)/shard_map/ppermute | solution.py:836
  36.3 16.1 %all-to-all-start.2 = ((bf16[16,32,256]{2,1,0:T(8,128)(2,1)}), bf16[16,32,256]{2,1,0:T(8,128)(2,1)S(1)}, u32[]{:S(2)}, u32[]{:S(2)}) async-start(bf16[16,32,256]{2,1,0:T(8,128)(2,1)} %get-tuple-element.53), calls=%async_computation.2 | async-start | bytes 524288 | tf_op jit(solution)/shard_map/all_to_all | solution.py:875
  42.6 8.7 %collective-permute-start.5 = (bf16[208,256]{1,0:T(8,128)(2,1)}, bf16[208,256]{1,0:T(8,128)(2,1)S(1)}, u32[]{:S(2)}, u32[]{:S(2)}) collective-permute-start(bf16[208,256]{1,0:T(8,128)(2,1)} %get-tuple-element.49.token_ref.refs_0_), channel_id=1, source_target_pairs={{8,0},{16,8},{24,16},{0,24},{9,1},{17,9},{25,17},{1,25},{10,2},{18... | collective-permute-start | bytes 319496 | tf_op jit(solution)/shard_map/ppermute | solution.py:836
  45.4 5.9 %collective-permute-start.4 = (bf16[208,256]{1,0:T(8,128)(2,1)}, bf16[208,256]{1,0:T(8,128)(2,1)S(1)}, u32[]{:S(2)}, u32[]{:S(2)}) collective-permute-start(bf16[208,256]{1,0:T(8,128)(2,1)} %get-tuple-element.49.token_ref.refs_0_), channel_id=1, source_target_pairs={{16,0},{24,8},{0,16},{8,24},{17,1},{25,9},{1,17},{9,25},{18,2},{26... | collective-permute-start | bytes 319496 | tf_op jit(solution)/shard_map/ppermute | solution.py:836
  46.0 6.4 %collective-permute-start.3 = (bf16[208,256]{1,0:T(8,128)(2,1)}, bf16[208,256]{1,0:T(8,128)(2,1)S(1)}, u32[]{:S(2)}, u32[]{:S(2)}) collective-permute-start(bf16[208,256]{1,0:T(8,128)(2,1)} %get-tuple-element.49.token_ref.refs_0_), channel_id=1, source_target_pairs={{24,0},{0,8},{8,16},{16,24},{25,1},{1,9},{9,17},{17,25},{26,2},{2,... | collective-permute-start | bytes 319496 | tf_op jit(solution)/shard_map/ppermute | solution.py:836
  60.8 2.0 %collective-permute-start.6 = (bf16[256,1024]{1,0:T(8,128)(2,1)S(1)}, bf16[256,1024]{1,0:T(8,128)(2,1)S(1)}, u32[]{:S(2)}, u32[]{:S(2)}) collective-permute-start(bf16[256,1024]{1,0:T(8,128)(2,1)S(1)} %get-tuple-element.55), channel_id=1, source_target_pairs={{0,4},{4,0},{1,5},{5,1},{2,6},{6,2},{3,7},{7,3},{8,12},{12,8},{9,1... | collective-permute-start | bytes 1572872 | tf_op jit(solution)/shard_map/ppermute | solution.py:966

commit v16 on v14

--- a/solution.py
+++ b/solution.py
@@ -278,7 +278,6 @@
 
 def hop_kernel(
     flag_ref,
-    place_ref,
     part_ref,
     ghost_ref,
     rest_hbm,
@@ -311,7 +310,7 @@
         staged_ref[part, each:] = start_ref[:train, :]
     out_copy = pltpu.make_async_copy(staged_ref, out_hbm, sem)
     out_copy.start()
-    near_rows(place_ref, table_ref, each, near_ref, 0)
+    near_ref[...] = table_ref[:, each:, :]
     side_ref[:train, :] = old_ref[...]
     side_ref[train : 2 * train, :] = start_ref[:train, :]
     turn_ref[:1, :train] = labels_ref[...]
@@ -347,7 +346,7 @@
     length = piece_refs[0].shape[0] - 16
     groups = len(piece_refs)
     if groups > 1:
-        near_ref[:, :train, :] = near0_ref[...]
+        near_rows(place_ref, near0_ref, 0, near_ref, 0)
         near_rows(place_ref, table_ref, each, near_ref, train)
         near_copy = pltpu.make_async_copy(near_ref, near_hbm, sems.at[2])
         near_copy.start()
@@ -791,11 +790,10 @@
             ((nodes, width), bf16, None),
             ((parts, each + train, width), bf16, HBM),
             ((2 * train + 16, width), bf16, None),
-            ((parts // 2, train, width), bf16, None),
+            ((parts, train, width), bf16, None),
         ],
         [
             (flag, SMEM),
-            (place, SMEM),
             (part1, None),
             (ghost, None),
             (ghost_rest, HBM),

time: 63.7 us -> 63.2 us (level)
  waiting for transfers between devices: 6.5 us -> 9.39 us
  Pallas kernels: 27.5 us -> 25.3 us
  starting transfers between devices: 27.7 us -> 26.4 us
    all_to_all x1, starting transfers between devices: 8.25 us -> 5.44 us  [local(): table1 = lax.all_to_all(out1, dom, split_axis=0, concat_axis=0, tiled=True)]
    ppermute x6, starting transfers between devices: 7.78 us -> 9.99 us  [shifted(): lax.ppermute(value, name, [((at + step * shift) % size, at) for at in ran...]
    pallas_call x7, Pallas kernels: 27.5 us -> 25.3 us  [call(): pl.pallas_call(kernel, out_shape=[shape_of(*out) for out in outs], in_spe...]
    all_to_all x1, waiting for transfers between devices: 0.01 us -> 1.7 us  [local(): table0 = lax.all_to_all(out0, dom, split_axis=0, concat_axis=0, tiled=True)]
    ppermute x6, waiting for transfers between devices: 4.4 us -> 5.79 us  [shifted(): lax.ppermute(value, name, [((at + step * shift) % size, at) for at in ran...]
    all_to_all x1, starting transfers between devices: 6.45 us -> 5.68 us  [local(): lax.all_to_all(last, ('chip', 'grp'), split_axis=0, concat_axis=0, tiled=...]
  transfers between devices with their start and end apart: 10 -> 10, of which waited for: 5 -> 6; matrix products, arithmetic and copies ran while one was open for 0% -> 0% of each run, Pallas kernels for 17% -> 15%
where the time goes in v16:
time: 63.2 us; the launch traced here: 62.5 us
  starting transfers between devices  26.4 us (42%)
  Pallas kernels  25.3 us (40%)
  waiting for transfers between devices  9.39 us (15%)
  between operations  1.38 us (2%)
    pallas_call x7, Pallas kernels, call(): pl.pallas_call(kernel, out_shape=[shape_of(*out) for out in outs], in_spe...  25.3 us
    ppermute x6, starting transfers between devices, shifted(): lax.ppermute(value, name, [((at + step * shift) % size, at) for at in ran...  9.99 us
    ppermute x6, waiting for transfers between devices, shifted(): lax.ppermute(value, name, [((at + step * shift) % size, at) for at in ran...  5.79 us
    all_to_all x1, starting transfers between devices, local(): lax.all_to_all(last, ('chip', 'grp'), split_axis=0, concat_axis=0, tiled=...  5.68 us
    all_to_all x1, starting transfers between devices, local(): table1 = lax.all_to_all(out1, dom, split_axis=0, concat_axis=0, tiled=True)  5.44 us
    all_to_all x1, starting transfers between devices, local(): table0 = lax.all_to_all(out0, dom, split_axis=0, concat_axis=0, tiled=True)  5.18 us
    ppermute x1, waiting for transfers between devices, local(): got = lax.ppermute(other, 'core', [(0, 1), (1, 0)])  1.9 us
    all_to_all x1, waiting for transfers between devices, local(): table0 = lax.all_to_all(out0, dom, split_axis=0, concat_axis=0, tiled=True)  1.7 us
  transfers between devices with their start and end apart: 10, of which 6 were waited for; matrix products, arithmetic and copies ran while one was open for 0% of the time, Pallas kernels for 15%

profile of v16, /device:TPU:0, one launch (start us, length us, event | category | flops | bytes accessed | tf_op | source)
XLA Modules:
  0.0 62.5 jit_solution(6637359905326144033)
XLA Ops:
  0.6 0.0 copy-start
  0.6 0.0 copy-start.1
  0.7 2.2 %shard_map.165 = (bf16[1024,256]{1,0:T(8,128)(2,1)S(1)}, bf16[8,64,256]{2,1,0:T(8,128)(2,1)}, bf16[32,256]{1,0:T(8,128)(2,1)S(1)}, s32[64,256]{1,0:T(8,128)S(1)}, s32[64,256]{1,0:T(8,128)S(1)}) custom-call(bf16[1,1,1024,256]{3,2,1,0:T(8,128)(2,1)} %feats_hbm.1, s32[1,1,8,32]{3,2,1,0:T(8,128)} %rows_hbm.1, s32[1,1,64,256]{3,2,1,0:T(8,128)} %src_hbm.1, ...), custom_call_target="tpu_custom_call" | custom-call | tf_op jit(solution)/shard_map/pallas_call | solution.py:680
  2.9 5.2 %all-to-all-start = ((bf16[8,64,256]{2,1,0:T(8,128)(2,1)}), bf16[8,64,256]{2,1,0:T(8,128)(2,1)S(1)}, u32[]{:S(2)}, u32[]{:S(2)}) async-start(bf16[8,64,256]{2,1,0:T(8,128)(2,1)} %get-tuple-element.43), calls=%async_computation | async-start | bytes 524288 | tf_op jit(solution)/shard_map/all_to_all | solution.py:751
  8.7 4.6 %shard_map.166 = (bf16[1024,1024]{1,0:T(8,128)(2,1)}, bf16[1024,256]{1,0:T(8,128)(2,1)S(1)}, bf16[32,1024]{1,0:T(8,128)(2,1)S(1)}, bf16[32,256]{1,0:T(8,128)(2,1...) custom-call(s32[1,1,64]{2,1,0:T(1,128)} %blocks_hbm.1, ...), custom_call_target="tpu_custom_call" | custom-call | tf_op jit(solution)/shard_map/pallas_call | solution.py:680
  13.3 1.7 %all-to-all-done.table_ref = bf16[8,64,256]{2,1,0:T(8,128)(2,1)S(1)} async-done(((bf16[8,64,256]{2,1,0:T(8,128)(2,1)}), bf16[8,64,256]{2,1,0:T(8,128)(2,1)S(1)}, u32[]{:S(2)}, u32[]{:S(2)}) %all-to-all-start) | async-done | bytes 262176 | tf_op jit(solution)/shard_map/all_to_all | solution.py:751
  15.0 0.0 copy-done
  15.0 0.0 copy-done.1
  15.0 2.1 %shard_map.167 = (bf16[1024,256]{1,0:T(8,128)(2,1)S(1)}, bf16[8,64,256]{2,1,0:T(8,128)(2,1)}, bf16[80,256]{1,0:T(8,128)(2,1)S(1)}, bf16[8,32,256]{2,1,0:T(8,128)(2,1)S(1)}) custom-call(s32[1]{0:T(128)} %get-tuple-element.36.flag_ref, f32[1024,256]{1,0:T(8,128)S(1)} %get-tuple-element.42.part_ref, bf16[1024,256]{1,0:T(8,128)(2,1)S(1)} %get-tuple-element.38.ghost_ref, ...), custom_call_target="tpu_custom_call" | custom-call | tf_op jit(solution)/shard_map/pallas_call | solution.py:680
  17.2 5.4 %all-to-all-start.1 = ((bf16[8,64,256]{2,1,0:T(8,128)(2,1)}), bf16[8,64,256]{2,1,0:T(8,128)(2,1)S(1)}, u32[]{:S(2)}, u32[]{:S(2)}) async-start(bf16[8,64,256]{2,1,0:T(8,128)(2,1)} %get-tuple-element.46), calls=%async_computation.1 | async-start | bytes 524288 | tf_op jit(solution)/shard_map/all_to_all | solution.py:807
  22.6 2.7 %collective-permute-start.2 = (bf16[80,256]{1,0:T(8,128)(2,1)S(1)}, bf16[80,256]{1,0:T(8,128)(2,1)S(1)}, u32[]{:S(2)}, u32[]{:S(2)}) collective-permute-start(bf16[80,256]{1,0:T(8,128)(2,1)S(1)} %get-tuple-element.48.refs_1_), channel_id=1, source_target_pairs={{3,0},{0,1},{1,2},{2,3},{7,4},{4,5},{5,6},{6,7},{11,8},{8,9},{9,10... | collective-permute-start | bytes 122888 | tf_op jit(solution)/shard_map/ppermute | solution.py:812
  25.3 3.3 %collective-permute-start.1 = (bf16[80,256]{1,0:T(8,128)(2,1)S(1)}, bf16[80,256]{1,0:T(8,128)(2,1)S(1)}, u32[]{:S(2)}, u32[]{:S(2)}) collective-permute-start(bf16[80,256]{1,0:T(8,128)(2,1)S(1)} %get-tuple-element.48.refs_1_), channel_id=1, source_target_pairs={{2,0},{3,1},{0,2},{1,3},{6,4},{7,5},{4,6},{5,7},{10,8},{11,9},{8,1... | collective-permute-start | bytes 122888 | tf_op jit(solution)/shard_map/ppermute | solution.py:812
  28.6 0.0 collective-permute-start
  28.6 0.1 pad_add_fusion.place_ref
  28.7 1.8 %collective-permute-done.2.refs_4_ = bf16[80,256]{1,0:T(8,128)(2,1)S(1)} collective-permute-done((bf16[80,256]{1,0:T(8,128)(2,1)S(1)}, bf16[80,256]{1,0:T(8,128)(2,1)S(1)}, u32[]{:S(2)}, u32[]{:S(2)}) %collective-permute-start.2) | collective-permute-done | bytes 40992 | tf_op jit(solution)/shard_map/ppermute | solution.py:812
  30.6 1.7 %collective-permute-done.1.refs_3_ = bf16[80,256]{1,0:T(8,128)(2,1)S(1)} collective-permute-done((bf16[80,256]{1,0:T(8,128)(2,1)S(1)}, bf16[80,256]{1,0:T(8,128)(2,1)S(1)}, u32[]{:S(2)}, u32[]{:S(2)}) %collective-permute-start.1) | collective-permute-done | bytes 40992 | tf_op jit(solution)/shard_map/ppermute | solution.py:812
  32.3 0.7 %collective-permute-done.refs_2_ = bf16[80,256]{1,0:T(8,128)(2,1)S(1)} collective-permute-done((bf16[80,256]{1,0:T(8,128)(2,1)S(1)}, bf16[80,256]{1,0:T(8,128)(2,1)S(1)}, u32[]{:S(2)}, u32[]{:S(2)}) %collective-permute-start) | collective-permute-done | bytes 40992 | tf_op jit(solution)/shard_map/ppermute | solution.py:812
  32.9 0.0 all-to-all-done.1.table_ref
  32.9 2.4 %shard_map.168 = (bf16[16,32,256]{2,1,0:T(8,128)(2,1)}, bf16[208,256]{1,0:T(8,128)(2,1)}, bf16[4,64,256]{2,1,0:T(8,128)(2,1)}) custom-call(s32[1]{0:T(128)} %get-tuple-element.36.flag_ref, s32[2]{0:T(128)S(1)} %pad_add_fusion.place_ref, bf16[32,1024]{1,0:T(8,128)(2,1)S(1)} %get-tuple-element.37.own_ref, bf16[1024,256]{1,0:T(8,128)(2,1)S(1)} %get-tuple-element.38.ghost_ref, ...), custom_call_target="tpu_custom_call" | custom-call | tf_op jit(solution)/shard_map/pallas_call | solution.py:680
  35.3 5.7 %all-to-all-start.2 = ((bf16[16,32,256]{2,1,0:T(8,128)(2,1)}), bf16[16,32,256]{2,1,0:T(8,128)(2,1)S(1)}, u32[]{:S(2)}, u32[]{:S(2)}) async-start(bf16[16,32,256]{2,1,0:T(8,128)(2,1)} %get-tuple-element.53), calls=%async_computation.2 | async-start | bytes 524288 | tf_op jit(solution)/shard_map/all_to_all | solution.py:851
  41.0 2.8 %collective-permute-start.5 = (bf16[208,256]{1,0:T(8,128)(2,1)}, bf16[208,256]{1,0:T(8,128)(2,1)S(1)}, u32[]{:S(2)}, u32[]{:S(2)}) collective-permute-start(bf16[208,256]{1,0:T(8,128)(2,1)} %get-tuple-element.49.token_ref.refs_0_), channel_id=1, source_target_pairs={{8,0},{16,8},{24,16},{0,24},{9,1},{17,9},{25,17},{1,25},{10,2},{18... | collective-permute-start | bytes 319496 | tf_op jit(solution)/shard_map/ppermute | solution.py:812
  43.8 0.6 collective-permute-start.4
  44.4 0.6 collective-permute-start.3
  45.0 4.6 %shard_map.169 = (bf16[2,1,1,1024,256]{4,3,2,1,0:T(8,128)(2,1)}, bf16[768,1024]{1,0:T(8,128)(2,1)S(1)}) custom-call(s32[1]{0:T(128)} %get-tuple-element.36.flag_ref, bf16[208,256]{1,0:T(8,128)(2,1)} %get-tuple-element.49.token_ref.refs_0_, bf16[1024,1024]{1,0:T(8,128)(2,1)} %get-tuple-element.50.own_hbm, bf16[1024,1024]{1,0:T(8,128)(2,1)} %get-tuple-element.39.own_rest_hbm, ...), custom_call_target="tpu_custom_call" | custom-call | tf_op jit(solution)/shard_map/pallas_call | solution.py:680
  49.5 0.0 collective-permute-done.5.refs_3_
  49.5 1.6 %collective-permute-done.4.refs_2_ = bf16[208,256]{1,0:T(8,128)(2,1)S(1)} collective-permute-done((bf16[208,256]{1,0:T(8,128)(2,1)}, bf16[208,256]{1,0:T(8,128)(2,1)S(1)}, u32[]{:S(2)}, u32[]{:S(2)}) %collective-permute-start.4) | collective-permute-done | bytes 106528 | tf_op jit(solution)/shard_map/ppermute | solution.py:812
  51.1 0.0 collective-permute-done.3.refs_1_
  51.1 0.0 all-to-all-done.2.refs_5_
  51.1 8.4 %shard_map.170 = (f32[96,1024]{1,0:T(8,128)S(1)}, f32[128,1024]{1,0:T(8,128)S(1)}, f32[172,128]{1,0:T(8,128)S(1)}, bf16[256,1024]{1,0:T(8,128)(2,1)S(1)}) custom-call(s32[2]{0:T(128)S(1)} %pad_add_fusion.place_ref, bf16[208,256]{1,0:T(8,128)(2,1)} %get-tuple-element.49.token_ref.refs_0_, bf16[208,256]{1,0:T(8,128)(2,1)S(1)} %collective-permute-done.3.refs_1_, ...), custom_call_target="tpu_custom_call" | custom-call | tf_op jit(solution)/shard_map/pallas_call | solution.py:680
  59.5 0.1 collective-permute-start.6
  59.6 1.9 %collective-permute-done.6.got_ref = bf16[256,1024]{1,0:T(8,128)(2,1)S(1)} collective-permute-done((bf16[256,1024]{1,0:T(8,128)(2,1)S(1)}, bf16[256,1024]{1,0:T(8,128)(2,1)S(1)}, u32[]{:S(2)}, u32[]{:S(2)}) %collective-permute-start.6) | collective-permute-done | bytes 524320 | tf_op jit(solution)/shard_map/ppermute | solution.py:942
  61.5 1.0 %shard_map.171 = (f32[96,1024]{1,0:T(8,128)}, f32[128,1024]{1,0:T(8,128)}, f32[172,128]{1,0:T(8,128)}) custom-call(bf16[256,1024]{1,0:T(8,128)(2,1)S(1)} %collective-permute-done.6.got_ref, f32[96,1024]{1,0:T(8,128)S(1)} %get-tuple-element.56.one_ref, f32[128,1024]{1,0:T(8,128)S(1)} %get-tuple-element.57.two_ref, f32[172,128]{1,0:T(8,128)S(1)} %get-tuple-element.58.three_ref), custom_call_target="tpu_custom_call" | custom-call | tf_op jit(solution)/shard_map/pallas_call | solution.py:680
Async XLA Ops:
  0.6 14.4 %copy-start = (s32[1,1,8,32]{3,2,1,0:T(8,128)S(1)}, s32[1,1,8,32]{3,2,1,0:T(8,128)}, u32[]{:S(2)}) copy-start(s32[1,1,8,32]{3,2,1,0:T(8,128)} %rows_hbm.1) | copy-start | bytes 3076
  0.6 14.4 %copy-start.1 = (s32[1,1,32]{2,1,0:T(1,128)S(1)}, s32[1,1,32]{2,1,0:T(1,128)}, u32[]{:S(2)}) copy-start(s32[1,1,32]{2,1,0:T(1,128)} %param.21) | copy-start | bytes 388
  2.9 12.1 %all-to-all-start = ((bf16[8,64,256]{2,1,0:T(8,128)(2,1)}), bf16[8,64,256]{2,1,0:T(8,128)(2,1)S(1)}, u32[]{:S(2)}, u32[]{:S(2)}) async-start(bf16[8,64,256]{2,1,0:T(8,128)(2,1)} %get-tuple-element.43), calls=%async_computation | async-start | bytes 524288 | tf_op jit(solution)/shard_map/all_to_all | solution.py:751
  17.2 15.8 %all-to-all-start.1 = ((bf16[8,64,256]{2,1,0:T(8,128)(2,1)}), bf16[8,64,256]{2,1,0:T(8,128)(2,1)S(1)}, u32[]{:S(2)}, u32[]{:S(2)}) async-start(bf16[8,64,256]{2,1,0:T(8,128)(2,1)} %get-tuple-element.46), calls=%async_computation.1 | async-start | bytes 524288 | tf_op jit(solution)/shard_map/all_to_all | solution.py:807
  22.6 8.0 %collective-permute-start.2 = (bf16[80,256]{1,0:T(8,128)(2,1)S(1)}, bf16[80,256]{1,0:T(8,128)(2,1)S(1)}, u32[]{:S(2)}, u32[]{:S(2)}) collective-permute-start(bf16[80,256]{1,0:T(8,128)(2,1)S(1)} %get-tuple-element.48.refs_1_), channel_id=1, source_target_pairs={{3,0},{0,1},{1,2},{2,3},{7,4},{4,5},{5,6},{6,7},{11,8},{8,9},{9,10... | collective-permute-start | bytes 122888 | tf_op jit(solution)/shard_map/ppermute | solution.py:812
  25.3 7.0 %collective-permute-start.1 = (bf16[80,256]{1,0:T(8,128)(2,1)S(1)}, bf16[80,256]{1,0:T(8,128)(2,1)S(1)}, u32[]{:S(2)}, u32[]{:S(2)}) collective-permute-start(bf16[80,256]{1,0:T(8,128)(2,1)S(1)} %get-tuple-element.48.refs_1_), channel_id=1, source_target_pairs={{2,0},{3,1},{0,2},{1,3},{6,4},{7,5},{4,6},{5,7},{10,8},{11,9},{8,1... | collective-permute-start | bytes 122888 | tf_op jit(solution)/shard_map/ppermute | solution.py:812
  28.6 4.3 %collective-permute-start = (bf16[80,256]{1,0:T(8,128)(2,1)S(1)}, bf16[80,256]{1,0:T(8,128)(2,1)S(1)}, u32[]{:S(2)}, u32[]{:S(2)}) collective-permute-start(bf16[80,256]{1,0:T(8,128)(2,1)S(1)} %get-tuple-element.48.refs_1_), channel_id=1, source_target_pairs={{1,0},{2,1},{3,2},{0,3},{5,4},{6,5},{7,6},{4,7},{9,8},{10,9},{11,1... | collective-permute-start | bytes 122888 | tf_op jit(solution)/shard_map/ppermute | solution.py:812
  35.3 15.8 %all-to-all-start.2 = ((bf16[16,32,256]{2,1,0:T(8,128)(2,1)}), bf16[16,32,256]{2,1,0:T(8,128)(2,1)S(1)}, u32[]{:S(2)}, u32[]{:S(2)}) async-start(bf16[16,32,256]{2,1,0:T(8,128)(2,1)} %get-tuple-element.53), calls=%async_computation.2 | async-start | bytes 524288 | tf_op jit(solution)/shard_map/all_to_all | solution.py:851
  41.0 8.5 %collective-permute-start.5 = (bf16[208,256]{1,0:T(8,128)(2,1)}, bf16[208,256]{1,0:T(8,128)(2,1)S(1)}, u32[]{:S(2)}, u32[]{:S(2)}) collective-permute-start(bf16[208,256]{1,0:T(8,128)(2,1)} %get-tuple-element.49.token_ref.refs_0_), channel_id=1, source_target_pairs={{8,0},{16,8},{24,16},{0,24},{9,1},{17,9},{25,17},{1,25},{10,2},{18... | collective-permute-start | bytes 319496 | tf_op jit(solution)/shard_map/ppermute | solution.py:812
  43.8 7.3 %collective-permute-start.4 = (bf16[208,256]{1,0:T(8,128)(2,1)}, bf16[208,256]{1,0:T(8,128)(2,1)S(1)}, u32[]{:S(2)}, u32[]{:S(2)}) collective-permute-start(bf16[208,256]{1,0:T(8,128)(2,1)} %get-tuple-element.49.token_ref.refs_0_), channel_id=1, source_target_pairs={{16,0},{24,8},{0,16},{8,24},{17,1},{25,9},{1,17},{9,25},{18,2},{26... | collective-permute-start | bytes 319496 | tf_op jit(solution)/shard_map/ppermute | solution.py:812
  44.4 6.7 %collective-permute-start.3 = (bf16[208,256]{1,0:T(8,128)(2,1)}, bf16[208,256]{1,0:T(8,128)(2,1)S(1)}, u32[]{:S(2)}, u32[]{:S(2)}) collective-permute-start(bf16[208,256]{1,0:T(8,128)(2,1)} %get-tuple-element.49.token_ref.refs_0_), channel_id=1, source_target_pairs={{24,0},{0,8},{8,16},{16,24},{25,1},{1,9},{9,17},{17,25},{26,2},{2,... | collective-permute-start | bytes 319496 | tf_op jit(solution)/shard_map/ppermute | solution.py:812
  59.5 2.0 %collective-permute-start.6 = (bf16[256,1024]{1,0:T(8,128)(2,1)S(1)}, bf16[256,1024]{1,0:T(8,128)(2,1)S(1)}, u32[]{:S(2)}, u32[]{:S(2)}) collective-permute-start(bf16[256,1024]{1,0:T(8,128)(2,1)S(1)} %get-tuple-element.55), channel_id=1, source_target_pairs={{0,4},{4,0},{1,5},{5,1},{2,6},{6,2},{3,7},{7,3},{8,12},{12,8},{9,1... | collective-permute-start | bytes 1572872 | tf_op jit(solution)/shard_map/ppermute | solution.py:942

commit v17 on v16

--- a/solution.py
+++ b/solution.py
@@ -222,7 +222,7 @@
             for at in range(0, ref.shape[1], 256):
                 top = jnp.maximum(top, ref[first : first + BLOCK, at : at + 256])
     big = jnp.max(top.astype(f32)) >= 256.0
-    flag_ref[0] = big.astype(jnp.int32)
+    flag_ref[...] = jnp.where(big, 1.0, 0.0) + jnp.zeros_like(flag_ref)
 
     @pl.when(big)
     def _():
@@ -258,7 +258,7 @@
             at = slice(cut.start + inner.start, cut.start + inner.stop)
             sums_ref[at, :] = first_ref[at, :].astype(f32) + total[inner]
 
-    @pl.when(flag_ref[0] > 0)
+    @pl.when(jnp.max(flag_ref[...]) > 0.0)
     def _():
         for count_ref, rest_hbm, table in parts:
             held = rest_ref.at[:, : count_ref.shape[1]]
@@ -758,7 +758,7 @@
             ((train, nodes), bf16, None),
             ((train, width), bf16, None),
             ((nodes, width), f32, None),
-            ((1,), jnp.int32, SMEM),
+            ((8, 128), f32, None),
             ((nodes, nodes), bf16, HBM),
             ((nodes, ghosts), bf16, HBM),
         ],
@@ -782,7 +782,17 @@
             DMA((4,)),
         ],
     )
-    place = jnp.stack([lax.axis_index(dom), lax.axis_index("grp")]).astype(jnp.int32)
+    place = lax.axis_index(dom).reshape(1).astype(jnp.int32)
+
+    def here():
+        along = 0
+        for name in dom:
+            along = along * lax.axis_size(name) + lax.axis_index(name)
+        return along, lax.axis_index("grp")
+
+    def train_here(flag_ref, *refs):
+        train_kernel(flag_ref, here(), *refs)
+
     start1, out1, side, near0 = call(
         hop_kernel,
         16,
@@ -793,7 +803,7 @@
             ((parts, train, width), bf16, None),
         ],
         [
-            (flag, SMEM),
+            (flag, None),
             (part1, None),
             (ghost, None),
             (ghost_rest, HBM),
@@ -817,7 +827,7 @@
     side_shape = ((len(sides) - 1) * 2 * train + 16, width)
     near_shape = (parts // 2, 2 * train, width)
     last, side, near = call(
-        train_kernel,
+        train_here,
         12,
         [
             ((copies, train, width), bf16, HBM),
@@ -825,8 +835,7 @@
             (near_shape, bf16, HBM),
         ],
         [
-            (flag, SMEM),
-            (place, SMEM),
+            (flag, None),
             (own_train, None),
             (ghost, None),
             (own_rest, HBM),
@@ -864,7 +873,7 @@
             (w_first.shape, bf16, None),
         ],
         [
-            (flag, SMEM),
+            (flag, None),
             (side, HBM),
             (own, HBM),
             (own_rest, HBM),
@@ -906,13 +915,13 @@
     if few:
         chips = parts // 2
 
-        def classify(place_ref, *refs):
+        def classify(*refs):
             sides_in, rest = refs[:chips], refs[chips:]
             near_hbm, two_ref, first_ref, *outs = rest[:12]
             held, near_ref, *rest = rest[12:]
             classify_kernel(
                 False,
-                place_ref,
+                here(),
                 None,
                 None,
                 None,
@@ -932,8 +941,7 @@
             classify,
             44,
             [(value.shape, f32, None) for value in noises] + [((rows, hid), bf16, None)],
-            [(place, SMEM)]
-            + [(side, HBM)]
+            [(side, HBM)]
             + [(value, None) for value in sides[1:]]
             + [(near, HBM), (every2, None), (held_first, None)]
             + [(value, HBM) for value in fixed[1:]],

time: 63.2 us -> 61.6 us (0.975)
  waiting for transfers between devices: 9.39 us -> 5.48 us
  starting transfers between devices: 26.4 us -> 29.4 us
  Pallas kernels: 25.3 us -> 24.5 us
    ppermute x6, waiting for transfers between devices: 5.79 us -> 3.57 us  [shifted(): lax.ppermute(value, name, [((at + step * shift) % size, at) for at in ran...]
    all_to_all x1, starting transfers between devices: 5.68 us -> 7.75 us  [local(): lax.all_to_all(last, ('chip', 'grp'), split_axis=0, concat_axis=0, tiled=...]
    all_to_all x1, waiting for transfers between devices: 1.7 us -> 0.01 us  [local(): table0 = lax.all_to_all(out0, dom, split_axis=0, concat_axis=0, tiled=True)]
    ppermute x6, starting transfers between devices: 9.99 us -> 11.4 us  [shifted(): lax.ppermute(value, name, [((at + step * shift) % size, at) for at in ran...]
    pallas_call x7, Pallas kernels: 25.3 us -> 24.5 us  [call(): pl.pallas_call(kernel, out_shape=[shape_of(*out) for out in outs], in_spe...]
  transfers between devices with their start and end apart: 10 -> 10, of which waited for: 6 -> 4; matrix products, arithmetic and copies ran while one was open for 0% -> 0% of each run, Pallas kernels for 15% -> 17%
where the time goes in v17:
time: 61.6 us; the launch traced here: 60.8 us
  starting transfers between devices  29.4 us (48%)
  Pallas kernels  24.5 us (40%)
  waiting for transfers between devices  5.48 us (9%)
  between operations  1.4 us (2%)
    pallas_call x7, Pallas kernels, call(): pl.pallas_call(kernel, out_shape=[shape_of(*out) for out in outs], in_spe...  24.5 us
    ppermute x6, starting transfers between devices, shifted(): lax.ppermute(value, name, [((at + step * shift) % size, at) for at in ran...  11.4 us
    all_to_all x1, starting transfers between devices, local(): lax.all_to_all(last, ('chip', 'grp'), split_axis=0, concat_axis=0, tiled=...  7.75 us
    all_to_all x1, starting transfers between devices, local(): table0 = lax.all_to_all(out0, dom, split_axis=0, concat_axis=0, tiled=True)  5.18 us
    all_to_all x1, starting transfers between devices, local(): table1 = lax.all_to_all(out1, dom, split_axis=0, concat_axis=0, tiled=True)  5.08 us
    ppermute x6, waiting for transfers between devices, shifted(): lax.ppermute(value, name, [((at + step * shift) % size, at) for at in ran...  3.57 us
    ppermute x1, waiting for transfers between devices, local(): got = lax.ppermute(other, 'core', [(0, 1), (1, 0)])  1.9 us
  transfers between devices with their start and end apart: 10, of which 4 were waited for; matrix products, arithmetic and copies ran while one was open for 0% of the time, Pallas kernels for 17%

profile of v17, /device:TPU:0, one launch (start us, length us, event | category | flops | bytes accessed | tf_op | source)
XLA Modules:
  0.0 60.8 jit_solution(1768491316239472297)
XLA Ops:
  0.6 0.0 copy-start
  0.6 0.0 copy-start.1
  0.7 2.2 %shard_map.165 = (bf16[1024,256]{1,0:T(8,128)(2,1)S(1)}, bf16[8,64,256]{2,1,0:T(8,128)(2,1)}, bf16[32,256]{1,0:T(8,128)(2,1)S(1)}, s32[64,256]{1,0:T(8,128)S(1)}, s32[64,256]{1,0:T(8,128)S(1)}) custom-call(bf16[1,1,1024,256]{3,2,1,0:T(8,128)(2,1)} %feats_hbm.1, s32[1,1,8,32]{3,2,1,0:T(8,128)} %rows_hbm.1, s32[1,1,64,256]{3,2,1,0:T(8,128)} %src_hbm.1, ...), custom_call_target="tpu_custom_call" | custom-call | tf_op jit(solution)/shard_map/pallas_call | solution.py:680
  2.9 5.2 %all-to-all-start = ((bf16[8,64,256]{2,1,0:T(8,128)(2,1)}), bf16[8,64,256]{2,1,0:T(8,128)(2,1)S(1)}, u32[]{:S(2)}, u32[]{:S(2)}) async-start(bf16[8,64,256]{2,1,0:T(8,128)(2,1)} %get-tuple-element.43), calls=%async_computation | async-start | bytes 524288 | tf_op jit(solution)/shard_map/all_to_all | solution.py:751
  8.7 6.7 %shard_map.166 = (bf16[1024,1024]{1,0:T(8,128)(2,1)}, bf16[1024,256]{1,0:T(8,128)(2,1)S(1)}, bf16[32,1024]{1,0:T(8,128)(2,1)S(1)}, bf16[32,256]{1,0:T(8,128)(2,1...) custom-call(s32[1,1,64]{2,1,0:T(1,128)} %blocks_hbm.1, ...), custom_call_target="tpu_custom_call" | custom-call | tf_op jit(solution)/shard_map/pallas_call | solution.py:680
  15.4 0.0 all-to-all-done.table_ref
  15.4 0.0 copy-done
  15.4 0.0 copy-done.1
  15.5 1.5 %shard_map.167 = (bf16[1024,256]{1,0:T(8,128)(2,1)S(1)}, bf16[8,64,256]{2,1,0:T(8,128)(2,1)}, bf16[80,256]{1,0:T(8,128)(2,1)S(1)}, bf16[8,32,256]{2,1,0:T(8,128)(2,1)S(1)}) custom-call(f32[8,128]{1,0:T(8,128)S(1)} %get-tuple-element.36.flag_ref, f32[1024,256]{1,0:T(8,128)S(1)} %get-tuple-element.42.part_ref, ...), custom_call_target="tpu_custom_call" | custom-call | tf_op jit(solution)/shard_map/pallas_call | solution.py:680
  17.0 5.1 %all-to-all-start.1 = ((bf16[8,64,256]{2,1,0:T(8,128)(2,1)}), bf16[8,64,256]{2,1,0:T(8,128)(2,1)S(1)}, u32[]{:S(2)}, u32[]{:S(2)}) async-start(bf16[8,64,256]{2,1,0:T(8,128)(2,1)} %get-tuple-element.46), calls=%async_computation.1 | async-start | bytes 524288 | tf_op jit(solution)/shard_map/all_to_all | solution.py:817
  22.0 2.4 %collective-permute-start.2 = (bf16[80,256]{1,0:T(8,128)(2,1)S(1)}, bf16[80,256]{1,0:T(8,128)(2,1)S(1)}, u32[]{:S(2)}, u32[]{:S(2)}) collective-permute-start(bf16[80,256]{1,0:T(8,128)(2,1)S(1)} %get-tuple-element.48.refs_8_), channel_id=1, source_target_pairs={{3,0},{0,1},{1,2},{2,3},{7,4},{4,5},{5,6},{6,7},{11,8},{8,9},{9,10... | collective-permute-start | bytes 122888 | tf_op jit(solution)/shard_map/ppermute | solution.py:822
  24.5 2.1 %collective-permute-start.1 = (bf16[80,256]{1,0:T(8,128)(2,1)S(1)}, bf16[80,256]{1,0:T(8,128)(2,1)S(1)}, u32[]{:S(2)}, u32[]{:S(2)}) collective-permute-start(bf16[80,256]{1,0:T(8,128)(2,1)S(1)} %get-tuple-element.48.refs_8_), channel_id=1, source_target_pairs={{2,0},{3,1},{0,2},{1,3},{6,4},{7,5},{4,6},{5,7},{10,8},{11,9},{8,1... | collective-permute-start | bytes 122888 | tf_op jit(solution)/shard_map/ppermute | solution.py:822
  26.6 2.8 %collective-permute-start = (bf16[80,256]{1,0:T(8,128)(2,1)S(1)}, bf16[80,256]{1,0:T(8,128)(2,1)S(1)}, u32[]{:S(2)}, u32[]{:S(2)}) collective-permute-start(bf16[80,256]{1,0:T(8,128)(2,1)S(1)} %get-tuple-element.48.refs_8_), channel_id=1, source_target_pairs={{1,0},{2,1},{3,2},{0,3},{5,4},{6,5},{7,6},{4,7},{9,8},{10,9},{11,1... | collective-permute-start | bytes 122888 | tf_op jit(solution)/shard_map/ppermute | solution.py:822
  29.4 0.0 collective-permute-done.2.refs_11_
  29.5 0.0 collective-permute-done.1.refs_10_
  29.5 1.6 %collective-permute-done.refs_9_ = bf16[80,256]{1,0:T(8,128)(2,1)S(1)} collective-permute-done((bf16[80,256]{1,0:T(8,128)(2,1)S(1)}, bf16[80,256]{1,0:T(8,128)(2,1)S(1)}, u32[]{:S(2)}, u32[]{:S(2)}) %collective-permute-start) | collective-permute-done | bytes 40992 | tf_op jit(solution)/shard_map/ppermute | solution.py:822
  31.1 0.0 all-to-all-done.1.refs_6_.table_ref
  31.1 1.2 %shard_map.168 = (bf16[16,32,256]{2,1,0:T(8,128)(2,1)}, bf16[208,256]{1,0:T(8,128)(2,1)}, bf16[4,64,256]{2,1,0:T(8,128)(2,1)}) custom-call(f32[8,128]{1,0:T(8,128)S(1)} %get-tuple-element.36.flag_ref, bf16[32,1024]{1,0:T(8,128)(2,1)S(1)} %get-tuple-element.37.refs_0_, bf16[1024,256]{1,0:T(8,128)(2,1)S(1)} %get-tuple-element.38.ghost_ref.refs_1_, ...), custom_call_target="tpu_custom_call" | custom-call | tf_op jit(solution)/shard_map/pallas_call | solution.py:680
  32.3 7.8 %all-to-all-start.2 = ((bf16[16,32,256]{2,1,0:T(8,128)(2,1)}), bf16[16,32,256]{2,1,0:T(8,128)(2,1)S(1)}, u32[]{:S(2)}, u32[]{:S(2)}) async-start(bf16[16,32,256]{2,1,0:T(8,128)(2,1)} %get-tuple-element.53), calls=%async_computation.2 | async-start | bytes 524288 | tf_op jit(solution)/shard_map/all_to_all | solution.py:860
  40.1 2.8 %collective-permute-start.5 = (bf16[208,256]{1,0:T(8,128)(2,1)}, bf16[208,256]{1,0:T(8,128)(2,1)S(1)}, u32[]{:S(2)}, u32[]{:S(2)}) collective-permute-start(bf16[208,256]{1,0:T(8,128)(2,1)} %get-tuple-element.49.token_ref.refs_0_), channel_id=1, source_target_pairs={{8,0},{16,8},{24,16},{0,24},{9,1},{17,9},{25,17},{1,25},{10,2},{18... | collective-permute-start | bytes 319496 | tf_op jit(solution)/shard_map/ppermute | solution.py:822
  42.9 0.6 collective-permute-start.4
  43.5 0.6 collective-permute-start.3
  44.0 3.9 %shard_map.169 = (bf16[2,1,1,1024,256]{4,3,2,1,0:T(8,128)(2,1)}, bf16[768,1024]{1,0:T(8,128)(2,1)S(1)}) custom-call(f32[8,128]{1,0:T(8,128)S(1)} %get-tuple-element.36.flag_ref, bf16[208,256]{1,0:T(8,128)(2,1)} %get-tuple-element.49.token_ref.refs_0_, bf16[1024,1024]{1,0:T(8,128)(2,1)} %get-tuple-element.50.own_hbm, ...), custom_call_target="tpu_custom_call" | custom-call | tf_op jit(solution)/shard_map/pallas_call | solution.py:680
  48.0 0.0 collective-permute-done.5.refs_3_
  48.0 1.2 %collective-permute-done.4.refs_2_ = bf16[208,256]{1,0:T(8,128)(2,1)S(1)} collective-permute-done((bf16[208,256]{1,0:T(8,128)(2,1)}, bf16[208,256]{1,0:T(8,128)(2,1)S(1)}, u32[]{:S(2)}, u32[]{:S(2)}) %collective-permute-start.4) | collective-permute-done | bytes 106528 | tf_op jit(solution)/shard_map/ppermute | solution.py:822
  49.1 0.7 %collective-permute-done.3.refs_1_ = bf16[208,256]{1,0:T(8,128)(2,1)S(1)} collective-permute-done((bf16[208,256]{1,0:T(8,128)(2,1)}, bf16[208,256]{1,0:T(8,128)(2,1)S(1)}, u32[]{:S(2)}, u32[]{:S(2)}) %collective-permute-start.3) | collective-permute-done | bytes 106528 | tf_op jit(solution)/shard_map/ppermute | solution.py:822
  49.9 0.0 all-to-all-done.2.refs_5_
  49.9 7.9 %shard_map.170 = (f32[96,1024]{1,0:T(8,128)S(1)}, f32[128,1024]{1,0:T(8,128)S(1)}, f32[172,128]{1,0:T(8,128)S(1)}, bf16[256,1024]{1,0:T(8,128)(2,1)S(1)}) custom-call(bf16[208,256]{1,0:T(8,128)(2,1)} %get-tuple-element.49.token_ref.refs_0_, bf16[208,256]{1,0:T(8,128)(2,1)S(1)} %collective-permute-done.3.refs_1_, ...), custom_call_target="tpu_custom_call" | custom-call | tf_op jit(solution)/shard_map/pallas_call | solution.py:680
  57.8 0.1 collective-permute-start.6
  57.9 1.9 %collective-permute-done.6.got_ref = bf16[256,1024]{1,0:T(8,128)(2,1)S(1)} collective-permute-done((bf16[256,1024]{1,0:T(8,128)(2,1)S(1)}, bf16[256,1024]{1,0:T(8,128)(2,1)S(1)}, u32[]{:S(2)}, u32[]{:S(2)}) %collective-permute-start.6) | collective-permute-done | bytes 524320 | tf_op jit(solution)/shard_map/ppermute | solution.py:950
  59.8 1.0 %shard_map.171 = (f32[96,1024]{1,0:T(8,128)}, f32[128,1024]{1,0:T(8,128)}, f32[172,128]{1,0:T(8,128)}) custom-call(bf16[256,1024]{1,0:T(8,128)(2,1)S(1)} %collective-permute-done.6.got_ref, f32[96,1024]{1,0:T(8,128)S(1)} %get-tuple-element.56.one_ref, f32[128,1024]{1,0:T(8,128)S(1)} %get-tuple-element.57.two_ref, f32[172,128]{1,0:T(8,128)S(1)} %get-tuple-element.58.three_ref), custom_call_target="tpu_custom_call" | custom-call | tf_op jit(solution)/shard_map/pallas_call | solution.py:680
Async XLA Ops:
  0.6 14.8 %copy-start = (s32[1,1,8,32]{3,2,1,0:T(8,128)S(1)}, s32[1,1,8,32]{3,2,1,0:T(8,128)}, u32[]{:S(2)}) copy-start(s32[1,1,8,32]{3,2,1,0:T(8,128)} %rows_hbm.1) | copy-start | bytes 3076
  0.6 14.8 %copy-start.1 = (s32[1,1,32]{2,1,0:T(1,128)S(1)}, s32[1,1,32]{2,1,0:T(1,128)}, u32[]{:S(2)}) copy-start(s32[1,1,32]{2,1,0:T(1,128)} %param.21) | copy-start | bytes 388
  2.9 12.5 %all-to-all-start = ((bf16[8,64,256]{2,1,0:T(8,128)(2,1)}), bf16[8,64,256]{2,1,0:T(8,128)(2,1)S(1)}, u32[]{:S(2)}, u32[]{:S(2)}) async-start(bf16[8,64,256]{2,1,0:T(8,128)(2,1)} %get-tuple-element.43), calls=%async_computation | async-start | bytes 524288 | tf_op jit(solution)/shard_map/all_to_all | solution.py:751
  17.0 14.2 %all-to-all-start.1 = ((bf16[8,64,256]{2,1,0:T(8,128)(2,1)}), bf16[8,64,256]{2,1,0:T(8,128)(2,1)S(1)}, u32[]{:S(2)}, u32[]{:S(2)}) async-start(bf16[8,64,256]{2,1,0:T(8,128)(2,1)} %get-tuple-element.46), calls=%async_computation.1 | async-start | bytes 524288 | tf_op jit(solution)/shard_map/all_to_all | solution.py:817
  22.0 7.4 %collective-permute-start.2 = (bf16[80,256]{1,0:T(8,128)(2,1)S(1)}, bf16[80,256]{1,0:T(8,128)(2,1)S(1)}, u32[]{:S(2)}, u32[]{:S(2)}) collective-permute-start(bf16[80,256]{1,0:T(8,128)(2,1)S(1)} %get-tuple-element.48.refs_8_), channel_id=1, source_target_pairs={{3,0},{0,1},{1,2},{2,3},{7,4},{4,5},{5,6},{6,7},{11,8},{8,9},{9,10... | collective-permute-start | bytes 122888 | tf_op jit(solution)/shard_map/ppermute | solution.py:822
  24.5 5.0 %collective-permute-start.1 = (bf16[80,256]{1,0:T(8,128)(2,1)S(1)}, bf16[80,256]{1,0:T(8,128)(2,1)S(1)}, u32[]{:S(2)}, u32[]{:S(2)}) collective-permute-start(bf16[80,256]{1,0:T(8,128)(2,1)S(1)} %get-tuple-element.48.refs_8_), channel_id=1, source_target_pairs={{2,0},{3,1},{0,2},{1,3},{6,4},{7,5},{4,6},{5,7},{10,8},{11,9},{8,1... | collective-permute-start | bytes 122888 | tf_op jit(solution)/shard_map/ppermute | solution.py:822
  26.6 4.5 %collective-permute-start = (bf16[80,256]{1,0:T(8,128)(2,1)S(1)}, bf16[80,256]{1,0:T(8,128)(2,1)S(1)}, u32[]{:S(2)}, u32[]{:S(2)}) collective-permute-start(bf16[80,256]{1,0:T(8,128)(2,1)S(1)} %get-tuple-element.48.refs_8_), channel_id=1, source_target_pairs={{1,0},{2,1},{3,2},{0,3},{5,4},{6,5},{7,6},{4,7},{9,8},{10,9},{11,1... | collective-permute-start | bytes 122888 | tf_op jit(solution)/shard_map/ppermute | solution.py:822
  32.3 17.6 %all-to-all-start.2 = ((bf16[16,32,256]{2,1,0:T(8,128)(2,1)}), bf16[16,32,256]{2,1,0:T(8,128)(2,1)S(1)}, u32[]{:S(2)}, u32[]{:S(2)}) async-start(bf16[16,32,256]{2,1,0:T(8,128)(2,1)} %get-tuple-element.53), calls=%async_computation.2 | async-start | bytes 524288 | tf_op jit(solution)/shard_map/all_to_all | solution.py:860
  40.1 7.9 %collective-permute-start.5 = (bf16[208,256]{1,0:T(8,128)(2,1)}, bf16[208,256]{1,0:T(8,128)(2,1)S(1)}, u32[]{:S(2)}, u32[]{:S(2)}) collective-permute-start(bf16[208,256]{1,0:T(8,128)(2,1)} %get-tuple-element.49.token_ref.refs_0_), channel_id=1, source_target_pairs={{8,0},{16,8},{24,16},{0,24},{9,1},{17,9},{25,17},{1,25},{10,2},{18... | collective-permute-start | bytes 319496 | tf_op jit(solution)/shard_map/ppermute | solution.py:822
  42.9 6.2 %collective-permute-start.4 = (bf16[208,256]{1,0:T(8,128)(2,1)}, bf16[208,256]{1,0:T(8,128)(2,1)S(1)}, u32[]{:S(2)}, u32[]{:S(2)}) collective-permute-start(bf16[208,256]{1,0:T(8,128)(2,1)} %get-tuple-element.49.token_ref.refs_0_), channel_id=1, source_target_pairs={{16,0},{24,8},{0,16},{8,24},{17,1},{25,9},{1,17},{9,25},{18,2},{26... | collective-permute-start | bytes 319496 | tf_op jit(solution)/shard_map/ppermute | solution.py:822
  43.5 6.4 %collective-permute-start.3 = (bf16[208,256]{1,0:T(8,128)(2,1)}, bf16[208,256]{1,0:T(8,128)(2,1)S(1)}, u32[]{:S(2)}, u32[]{:S(2)}) collective-permute-start(bf16[208,256]{1,0:T(8,128)(2,1)} %get-tuple-element.49.token_ref.refs_0_), channel_id=1, source_target_pairs={{24,0},{0,8},{8,16},{16,24},{25,1},{1,9},{9,17},{17,25},{26,2},{2,... | collective-permute-start | bytes 319496 | tf_op jit(solution)/shard_map/ppermute | solution.py:822
  57.8 2.0 %collective-permute-start.6 = (bf16[256,1024]{1,0:T(8,128)(2,1)S(1)}, bf16[256,1024]{1,0:T(8,128)(2,1)S(1)}, u32[]{:S(2)}, u32[]{:S(2)}) collective-permute-start(bf16[256,1024]{1,0:T(8,128)(2,1)S(1)} %get-tuple-element.55), channel_id=1, source_target_pairs={{0,4},{4,0},{1,5},{5,1},{2,6},{6,2},{3,7},{7,3},{8,12},{12,8},{9,1... | collective-permute-start | bytes 1572872 | tf_op jit(solution)/shard_map/ppermute | solution.py:950
